TPU v7x, 32 devices: a whole 2x2x4 slice. The times are simulated.
32 devices in a mesh: row: 4 (over y, core), kv: 8 (over z, x).
Axes of the slice: x: 2, y: 2, z: 4, core: 2. Of those that a mesh axis runs over, the one named last changes fastest.
Arguments:
- tokens: bfloat16 [4, 4096, 2048], P('row', 'kv'), may hold values from -6 to 6
- lengths: int32 [4, 8], P('row'), may hold values from 0 to 4096, as said below
- cotangent: bfloat16 [4, 4096, 2048], P('row', 'kv'), may hold values from -6 to 6
- w_query: bfloat16 [2048, 2048], P(('row', 'kv')), may hold values from -0.1875 to 0.1875
- w_key: bfloat16 [2048, 2048], P(('row', 'kv')), may hold values from -0.1875 to 0.1875
- w_value: bfloat16 [2048, 2048], P(('row', 'kv')), may hold values from -0.125 to 0.125
- w_out: bfloat16 [2048, 2048], P(('row', 'kv')), may hold values from -0.25 to 0.25
- w_gate: bfloat16 [2048, 8192], P(None, ('row', 'kv')), may hold values from -0.125 to 0.125
- w_up: bfloat16 [2048, 8192], P(None, ('row', 'kv')), may hold values from -0.125 to 0.125
- w_down: bfloat16 [8192, 2048], P(('row', 'kv')), may hold values from -0.0625 to 0.0625
- gain_attn: bfloat16 [2048], P(('row', 'kv')), may hold values from 0.099609375 to 1.8984375
- gain_mlp: bfloat16 [2048], P(('row', 'kv')), may hold values from 0.099609375 to 1.8984375
Outputs:
- mixed: bfloat16 [4, 4096, 2048], P('row', 'kv')
- grad_tokens: float32 [4, 4096, 2048], P('row', 'kv')
- grad_query: float32 [2048, 2048], P(('row', 'kv'))
- grad_key: float32 [2048, 2048], P(('row', 'kv'))
- grad_value: float32 [2048, 2048], P(('row', 'kv'))
- grad_out: float32 [2048, 2048], P(('row', 'kv'))
- grad_gate: float32 [2048, 8192], P(None, ('row', 'kv'))
- grad_up: float32 [2048, 8192], P(None, ('row', 'kv'))
- grad_down: float32 [8192, 2048], P(('row', 'kv'))
- grad_gain_attn: float32 [2048], P(('row', 'kv'))
- grad_gain_mlp: float32 [2048], P(('row', 'kv'))
Inputs may be any that keep to these rules, and one draw needn't show every extreme that they name: Each row of 4096 positions holds its documents in the order of lengths, then unused positions; the lengths of a row sum to at most 4096; a length of 0 is an empty slot.
All inputs are finite; a program needn't handle non-finite values.
Results may differ from a plain program's by a relative error of at most 0.02.
Values may be sent and summed in bfloat16 or wider, within the bound.
A program may use at most 320 MiB of HBM per device.

v0:
```python
import math

import jax
import jax.numpy as jnp
from jax import lax
from jax.sharding import PartitionSpec as P

H = 16
HD = 128
LEN = 4096


EPSILON = 1e-05


def contract_rows(left, right):
    return lax.dot_general(
        left, right, (((0,), (0,)), ((), ())), preferred_element_type=jnp.float32
    )


def contract_cols(left, right):
    return lax.dot_general(
        left, right, (((1,), (1,)), ((), ())), preferred_element_type=jnp.float32
    )


def norm_forward(value, gain):
    inverse = lax.rsqrt(jnp.mean(value * value, axis=-1, keepdims=True) + EPSILON)
    return (value * inverse * gain.astype(jnp.float32), inverse)


def norm_backward(value, inverse, gain, upstream):
    scaled = upstream * gain.astype(jnp.float32)
    inner = jnp.mean(scaled * value, axis=-1, keepdims=True)
    back = inverse * scaled - value * (inverse * inverse * inverse) * inner
    gain_term = jnp.sum(upstream * value * inverse, axis=0)
    return (back, gain_term)


def segment_table(lengths):
    ends = jnp.cumsum(lengths, axis=-1)
    places = jnp.arange(LEN, dtype=jnp.int32)
    segment = jnp.sum((ends[:, None, :] <= places[None, :, None]).astype(jnp.int32), axis=-1)
    valid = places[None, :] < ends[:, -1:]
    return (segment, valid)


def score_block(
    query_rows, key_heads, query_segment, key_segment, key_valid, query_start, key_places
):
    count = query_rows.shape[0]
    query_heads = query_rows.reshape(count, H, HD)
    raw = jnp.einsum("qhd,khd->hqk", query_heads, key_heads, preferred_element_type=jnp.float32)
    scores = raw * (1.0 / math.sqrt(HD)) - math.log(LEN)
    places = query_start + jnp.arange(count, dtype=jnp.int32)
    allowed = (
        (key_places[None, :] <= places[:, None])
        & (key_segment[None, :] == query_segment[:, None])
        & key_valid[None, :]
    )
    return (jax.nn.sigmoid(scores), allowed.astype(jnp.float32)[None])


def gate_backward(d_hidden, gate, up_part, sigmoid_gate):
    d_gate = (d_hidden * up_part * sigmoid_gate * (1.0 + gate * (1.0 - sigmoid_gate))).astype(
        jnp.bfloat16
    )
    d_up = (d_hidden * gate * sigmoid_gate).astype(jnp.bfloat16)
    return (d_gate, d_up)


def body(
    tokens,
    lengths,
    cotangent,
    w_query,
    w_key,
    w_value,
    w_out,
    w_gate,
    w_up,
    w_down,
    gain_attn,
    gain_mlp,
):
    rows_here, block, width = tokens.shape
    count = rows_here * block
    scale = 1.0 / math.sqrt(HD)
    kv_place = lax.axis_index("kv")
    key_places = kv_place * block + jnp.arange(block, dtype=jnp.int32)
    attn_set = (
        lax.all_gather(w_query, ("row", "kv"), axis=0, tiled=True),
        lax.all_gather(w_key, ("row", "kv"), axis=0, tiled=True),
        lax.all_gather(w_value, ("row", "kv"), axis=0, tiled=True),
        lax.all_gather(w_out, ("row", "kv"), axis=0, tiled=True),
        lax.all_gather(gain_attn, ("row", "kv"), axis=0, tiled=True),
        lax.all_gather(gain_mlp, ("row", "kv"), axis=0, tiled=True),
    )
    full_query, full_key, full_value, full_out, full_gain_attn, full_gain_mlp = attn_set
    flat = tokens.reshape(count, width).astype(jnp.float32)
    normed_attn, inverse_attn = norm_forward(flat, full_gain_attn)
    normed_attn_low = normed_attn.astype(jnp.bfloat16)
    query_low = jnp.dot(normed_attn_low, full_query, preferred_element_type=jnp.float32).astype(
        jnp.bfloat16
    )
    key_low = jnp.dot(normed_attn_low, full_key, preferred_element_type=jnp.float32).astype(
        jnp.bfloat16
    )
    value_low = jnp.dot(normed_attn_low, full_value, preferred_element_type=jnp.float32).astype(
        jnp.bfloat16
    )
    key_heads = key_low.reshape(rows_here, block, H, HD)
    value_heads = value_low.reshape(rows_here, block, H, HD)
    segment, valid = segment_table(lengths)
    key_segment = lax.dynamic_slice_in_dim(segment, kv_place * block, block, 1)
    key_valid = lax.dynamic_slice_in_dim(valid, kv_place * block, block, 1)
    queries_all = lax.all_gather(
        query_low.reshape(rows_here, block, width), "kv", axis=1, tiled=True
    )
    which = 0
    query_rows = queries_all[which]
    query_segment = segment[which]
    sigmoid_part, allowed = score_block(
        query_rows,
        key_heads[which],
        query_segment,
        key_segment[which],
        key_valid[which],
        jnp.int32(0),
        key_places,
    )
    weight = (sigmoid_part * allowed).astype(jnp.bfloat16)
    summed = jnp.einsum(
        "hqk,khd->qhd", weight, value_heads[which], preferred_element_type=jnp.float32
    )
    pieces = [
        lax.psum_scatter(
            summed.reshape(lax.axis_size("kv") * block, width).astype(jnp.bfloat16),
            "kv",
            scatter_dimension=0,
            tiled=True,
        ).astype(jnp.float32)
    ]
    attended_low = jnp.stack(pieces).reshape(count, width).astype(jnp.bfloat16)
    resid = flat + jnp.dot(attended_low, full_out, preferred_element_type=jnp.float32)
    normed_mlp, inverse_mlp = norm_forward(resid, full_gain_mlp)
    normed_mlp_low = normed_mlp.astype(jnp.bfloat16)
    upstream_low = cotangent.reshape(count, width)
    upstream = upstream_low.astype(jnp.float32)
    slice_gate, slice_up, slice_down = (
        lax.all_gather(w_gate, "row", axis=1, tiled=True),
        lax.all_gather(w_up, "row", axis=1, tiled=True),
        lax.all_gather(w_down, "row", axis=0, tiled=True),
    )
    row_normed, row_upstream = (
        lax.all_gather(normed_mlp_low.reshape(rows_here, block, width), "kv", axis=1, tiled=True),
        lax.all_gather(cotangent, "kv", axis=1, tiled=True),
    )
    normed_rows = row_normed.reshape(rows_here * LEN, width)
    upstream_rows = row_upstream.reshape(rows_here * LEN, width)
    gate = jnp.dot(normed_rows, slice_gate, preferred_element_type=jnp.float32)
    up_part = jnp.dot(normed_rows, slice_up, preferred_element_type=jnp.float32)
    sigmoid_gate = jax.nn.sigmoid(gate)
    hidden_low = (gate * sigmoid_gate * up_part).astype(jnp.bfloat16)
    hidden_rows = hidden_low.reshape(rows_here, LEN, hidden_low.shape[1])
    which = 0
    hidden_part = hidden_rows[which]
    outputs = [
        lax.psum_scatter(
            jnp.dot(hidden_part, slice_down, preferred_element_type=jnp.float32).astype(
                jnp.bfloat16
            ),
            "kv",
            scatter_dimension=0,
            tiled=True,
        ).astype(jnp.float32)
    ]
    result = resid + jnp.stack(outputs).reshape(count, width)
    d_hidden = contract_cols(upstream_rows, slice_down)
    d_gate, d_up = gate_backward(d_hidden, gate, up_part, sigmoid_gate)
    partial_normed = contract_cols(d_gate, slice_gate) + contract_cols(d_up, slice_up)
    d_normed_mlp = (
        lax.psum_scatter(
            partial_normed.reshape(rows_here, LEN, width).astype(jnp.bfloat16),
            "kv",
            scatter_dimension=1,
            tiled=True,
        )
        .astype(jnp.float32)
        .reshape(count, width)
    )
    grad_gate, grad_up, grad_down = (
        lax.psum_scatter(
            contract_rows(normed_rows, d_gate).astype(jnp.bfloat16),
            "row",
            scatter_dimension=1,
            tiled=True,
        ).astype(jnp.float32),
        lax.psum_scatter(
            contract_rows(normed_rows, d_up).astype(jnp.bfloat16),
            "row",
            scatter_dimension=1,
            tiled=True,
        ).astype(jnp.float32),
        lax.psum_scatter(
            contract_rows(hidden_low, upstream_rows).astype(jnp.bfloat16),
            "row",
            scatter_dimension=0,
            tiled=True,
        ).astype(jnp.float32),
    )
    mixed = result.astype(jnp.bfloat16).reshape(rows_here, block, width)
    back_mlp, gain_mlp_term = norm_backward(resid, inverse_mlp, full_gain_mlp, d_normed_mlp)
    d_resid = upstream + back_mlp
    d_resid_low = d_resid.astype(jnp.bfloat16)
    d_attended = contract_cols(d_resid_low, full_out).astype(jnp.bfloat16)
    grads_all = lax.all_gather(
        d_attended.reshape(rows_here, block, width), "kv", axis=1, tiled=True
    )
    query_block = min(512, LEN)
    block_count = LEN // query_block
    which = 0

    def sweep(carry, index, which=which):
        key_total, value_total = carry
        start = index * query_block
        query_rows = lax.dynamic_slice_in_dim(queries_all[which], start, query_block, 0)
        grad_rows = lax.dynamic_slice_in_dim(grads_all[which], start, query_block, 0)
        query_segment = lax.dynamic_slice_in_dim(segment[which], start, query_block, 0)
        sigmoid_part, allowed = score_block(
            query_rows,
            key_heads[which],
            query_segment,
            key_segment[which],
            key_valid[which],
            start,
            key_places,
        )
        weight = (sigmoid_part * allowed).astype(jnp.bfloat16)
        grad_heads = grad_rows.reshape(query_block, H, HD)
        value_total = value_total + jnp.einsum(
            "hqk,qhd->khd", weight, grad_heads, preferred_element_type=jnp.float32
        )
        d_weight = jnp.einsum(
            "qhd,khd->hqk", grad_heads, value_heads[which], preferred_element_type=jnp.float32
        )
        d_score = (d_weight * sigmoid_part * (1.0 - sigmoid_part) * allowed).astype(jnp.bfloat16)
        query_part = (
            jnp.einsum(
                "hqk,khd->qhd", d_score, key_heads[which], preferred_element_type=jnp.float32
            )
            * scale
        )
        key_total = (
            key_total
            + jnp.einsum(
                "hqk,qhd->khd",
                d_score,
                query_rows.reshape(query_block, H, HD),
                preferred_element_type=jnp.float32,
            )
            * scale
        )
        return ((key_total, value_total), query_part.reshape(query_block, width))

    zeros = jnp.zeros((block, H, HD), jnp.float32)
    totals, query_parts = lax.scan(sweep, (zeros, zeros), jnp.arange(block_count, dtype=jnp.int32))
    query_terms = [query_parts.reshape(LEN, width)]
    key_grads = [totals[0].reshape(block, width)]
    value_grads = [totals[1].reshape(block, width)]
    query_local = lax.psum_scatter(
        jnp.stack(query_terms).astype(jnp.bfloat16), "kv", scatter_dimension=1, tiled=True
    ).astype(jnp.float32)
    d_query_low = query_local.reshape(count, width).astype(jnp.bfloat16)
    d_key_low = jnp.stack(key_grads).reshape(count, width).astype(jnp.bfloat16)
    d_value_low = jnp.stack(value_grads).reshape(count, width).astype(jnp.bfloat16)
    d_normed_attn = (
        contract_cols(d_query_low, full_query)
        + contract_cols(d_key_low, full_key)
        + contract_cols(d_value_low, full_value)
    )
    back_attn, gain_attn_term = norm_backward(flat, inverse_attn, full_gain_attn, d_normed_attn)
    grad_tokens = (d_resid + back_attn).reshape(rows_here, block, width)
    projected_low = jnp.concatenate((d_query_low, d_key_low, d_value_low), axis=1)
    grad_projections = lax.psum_scatter(
        contract_rows(normed_attn_low, projected_low),
        ("row", "kv"),
        scatter_dimension=0,
        tiled=True,
    )
    out_term = contract_rows(attended_low, d_resid_low)
    grad_out, grad_gain_attn, grad_gain_mlp = (
        lax.psum_scatter(out_term, ("row", "kv"), scatter_dimension=0, tiled=True),
        lax.psum_scatter(gain_attn_term, ("row", "kv"), scatter_dimension=0, tiled=True),
        lax.psum_scatter(gain_mlp_term, ("row", "kv"), scatter_dimension=0, tiled=True),
    )
    grad_query = grad_projections[:, :width]
    grad_key = grad_projections[:, width : 2 * width]
    grad_value = grad_projections[:, 2 * width :]
    return (
        mixed,
        grad_tokens,
        grad_query,
        grad_key,
        grad_value,
        grad_out,
        grad_gate,
        grad_up,
        grad_down,
        grad_gain_attn,
        grad_gain_mlp,
    )


def solution(mesh):
    return jax.shard_map(
        body,
        mesh=mesh,
        in_specs=(
            P("row", "kv", None),
            P("row", None),
            P("row", "kv", None),
            P(("row", "kv"), None),
            P(("row", "kv"), None),
            P(("row", "kv"), None),
            P(("row", "kv"), None),
            P(None, ("row", "kv")),
            P(None, ("row", "kv")),
            P(("row", "kv"), None),
            P(("row", "kv")),
            P(("row", "kv")),
        ),
        out_specs=(
            P("row", "kv", None),
            P("row", "kv", None),
            P(("row", "kv"), None),
            P(("row", "kv"), None),
            P(("row", "kv"), None),
            P(("row", "kv"), None),
            P(None, ("row", "kv")),
            P(None, ("row", "kv")),
            P(("row", "kv"), None),
            P(("row", "kv")),
            P(("row", "kv")),
        ),
        check_vma=False,
    )
```

profile of v0, /device:TPU:0, one launch (start us, length us, event | category | flops | bytes accessed | tf_op | source)
XLA Modules:
  0.0 4016.5 jit_solution(7247933420828728869)
XLA Ops:
  11.2 43.3 %all-reduce.5 = (bf16[2048]{0:T(1024)(128)(2,1)S(1)}, bf16[2048]{0:T(1024)(128)(2,1)}) all-reduce(bf16[2048]{0:T(1024)(128)(2,1)S(1)} %dynamic-update-slice, bf16[2048]{0:T(1024)(128)(2,1)S(1)} %dynamic-update-slice.1), channel_id=1, replica_groups=mesh['row'=4,'kv'=8] {'row','kv'}, use_global_device_ids=true, to_apply=%add | all-reduce | flops 4096 | bytes 16384
  57.2 34.2 all-gather.17.cloned.1.call-done
  91.4 9.9 convolution_convert_fusion.5
  108.3 62.1 %all-gather.15.cloned.1.call-done = bf16[2048,2048]{1,0:T(8,128)(2,1)} async-done(((bf16[64,2048]{1,0:T(8,128)(2,1)}), bf16[2048,2048]{1,0:T(8,128)(2,1)}) %all-gather.15.cloned.1.call-update) | async-done | bytes 8388624 | tf_op jit(solution)/shard_map/all_gather | solution.py:95
  181.6 67.8 %all-gather.19.cloned.1.call-done = bf16[2048,2048]{1,0:T(8,128)(2,1)} async-done(((bf16[64,2048]{1,0:T(8,128)(2,1)}), bf16[2048,2048]{1,0:T(8,128)(2,1)}) %all-gather.19.cloned.1.call-update) | async-done | bytes 8388624 | tf_op jit(solution)/shard_map/all_gather | solution.py:94
  249.5 9.9 convolution_convert_fusion.4
  259.3 218.9 %all-gather.31.cloned.1.call-done = bf16[4096,2048]{1,0:T(8,128)(2,1)} async-done(((bf16[512,2048]{1,0:T(8,128)(2,1)}), bf16[4096,2048]{1,0:T(8,128)(2,1)}) %all-gather.31.cloned.1.call-update) | async-done | bytes 16777232 | tf_op jit(solution)/shard_map/all_gather | solution.py:118
  478.2 68.0 %fusion.18 = bf16[16,128,4096]{2,1,0:T(8,128)(2,1)} fusion(bf16[512,16,128]{0,2,1:T(8,128)(2,1)} %bitcast.191, f32[4096,512]{1,0:T(8,128)} %fusion.23, bf16[4096,2048]{1,0:T(8,128)(2,1)} %all-gather.31.cloned.1.call-done, bf16[512,2048]{1,0:T(8,128)(2,1)} %convolution_convert_fusion.4), kind=kOutput, calls=%fused_computation.34 | convolution fusion | flops 17423138816 | bytes 46137344 | tf_op jit(solution)/shard_map/hqk,khd->qhd/dot_general | solution.py:134
  547.1 10.0 all-gather.21.cloned.1.call-done
  557.0 284.8 %reduce-scatter.10.cloned.1.call-done = bf16[512,2048]{0,1:T(8,128)(2,1)} async-done(((bf16[4096,2048]{0,1:T(8,128)(2,1)}), bf16[512,2048]{0,1:T(8,128)(2,1)}) %reduce-scatter.10.cloned.1.call-update) | async-done | bytes 2097168 | tf_op jit(solution)/shard_map/reduce_scatter | solution.py:138
  855.5 22.1 all-gather.25.cloned.1.call-done
  877.6 230.6 %all-gather.33.cloned.1.call-done = bf16[4096,2048]{1,0:T(8,128)(2,1)} async-done(((bf16[512,2048]{1,0:T(8,128)(2,1)}), bf16[4096,2048]{1,0:T(8,128)(2,1)}) %all-gather.33.cloned.1.call-update) | async-done | bytes 16777232 | tf_op jit(solution)/shard_map/all_gather | solution.py:157
  1108.1 23.8 fusion.71
  1132.0 11.1 all-gather.23.cloned.1.call-done
  1143.0 23.4 fusion.70
  1166.4 12.6 all-gather.27.cloned.1.call-done
  1179.0 230.0 %all-gather.29.cloned.1.call-done = bf16[1,4096,2048]{2,1,0:T(8,128)(2,1)} async-done(((bf16[1,512,2048]{2,1,0:T(8,128)(2,1)}), bf16[1,4096,2048]{2,1,0:T(8,128)(2,1)}) %all-gather.29.cloned.1.call-update) | async-done | bytes 16777232 | tf_op jit(solution)/shard_map/all_gather | solution.py:158
  1409.0 36.0 multiply_convert_fusion.7
  1445.1 25.5 fusion.72
  1470.6 26.6 fusion.17
  1497.2 23.7 convolution_convert_fusion
  1521.0 257.3 %reduce-scatter.14.cloned.1.call-done = bf16[1,512,2048]{2,1,0:T(8,128)(2,1)} async-done(((bf16[1,4096,2048]{2,1,0:T(8,128)(2,1)}), bf16[1,512,2048]{2,1,0:T(8,128)(2,1)}) %reduce-scatter.14.cloned.1.call-update) | async-done | bytes 2097168 | tf_op jit(solution)/shard_map/reduce_scatter | solution.py:184
  1783.1 280.7 %reduce-scatter.12.cloned.1.call-done = bf16[512,2048]{1,0:T(8,128)(2,1)} async-done(((bf16[4096,2048]{1,0:T(8,128)(2,1)}), bf16[512,2048]{1,0:T(8,128)(2,1)}) %reduce-scatter.12.cloned.1.call-update) | async-done | bytes 2097168 | tf_op jit(solution)/shard_map/reduce_scatter | solution.py:170
  2071.1 9.3 convolution_convert_fusion.3
  2084.1 223.2 %all-gather.35.cloned.1.call-done = bf16[4096,2048]{1,0:T(8,128)(2,1)} async-done(((bf16[512,2048]{1,0:T(8,128)(2,1)}), bf16[4096,2048]{1,0:T(8,128)(2,1)}) %all-gather.35.cloned.1.call-update) | async-done | bytes 16777232 | tf_op jit(solution)/shard_map/all_gather | solution.py:218
  2307.3 482.0 %while.17 = (s32[]{:T(128)}, f32[512,16,128]{0,2,1:T(8,128)}, f32[512,16,128]{0,2,1:T(8,128)}, bf16[8,512,2048]{2,1,0:T(8,128)(2,1)}, s32[8]{0:T(128)S(1)}, /*in...) while((s32[]{:T(128)}, f32[512,16,128]{0,2,1:T(8,128)}, ...), condition=%wide.region_9.10_spmd.clone, body=%wide.region_8.9_spmd.clone.sunk | while | flops 5427692544 | bytes 187713376 | solution.py:268
  2318.9 10.1 add_divide_fusion.3
  2329.1 9.8 bitcast_add_fusion.5
  2338.9 9.9 multiply_convert_fusion.18
  2377.1 10.1 add_divide_fusion.3
  2387.2 11.0 bitcast_add_fusion.5
  2398.2 9.9 multiply_convert_fusion.18
  2437.6 10.1 add_divide_fusion.3
  2447.7 11.0 bitcast_add_fusion.5
  2458.7 9.9 multiply_convert_fusion.18
  2498.2 10.1 add_divide_fusion.3
  2508.3 11.0 bitcast_add_fusion.5
  2519.3 9.9 multiply_convert_fusion.18
  2558.8 10.1 add_divide_fusion.3
  2568.9 11.0 bitcast_add_fusion.5
  2579.9 9.9 multiply_convert_fusion.18
  2589.8 8.7 bitcast_add_fusion.4
  2619.3 10.1 add_divide_fusion.3
  2629.5 11.0 bitcast_add_fusion.5
  2640.4 9.9 multiply_convert_fusion.18
  2679.9 10.1 add_divide_fusion.3
  2690.0 11.0 bitcast_add_fusion.5
  2701.0 9.9 multiply_convert_fusion.18
  2740.4 10.1 add_divide_fusion.3
  2750.5 11.0 bitcast_add_fusion.5
  2761.5 9.9 multiply_convert_fusion.18
  2789.4 24.0 fusion.47
  2813.5 23.9 convolution_convert_fusion.1
  2837.4 23.8 convolution_convert_fusion.2
  2874.7 195.6 %reduce-scatter.16.cloned.1.call-done = bf16[1,512,2048]{2,1,0:T(8,128)(2,1)} async-done(((bf16[1,4096,2048]{2,1,0:T(8,128)(2,1)}), bf16[1,512,2048]{2,1,0:T(8,128)(2,1)}) %reduce-scatter.16.cloned.1.call-update) | async-done | bytes 2097168 | tf_op jit(solution)/shard_map/reduce_scatter | solution.py:272
  3070.4 26.3 fusion.24
  3096.7 13.1 fusion.55
  3119.2 44.3 %reduce-scatter.24.cloned.1.call-done = bf16[2048,256]{1,0:T(8,128)(2,1)} async-done(((bf16[2048,1024]{1,0:T(8,128)(2,1)}), bf16[2048,256]{1,0:T(8,128)(2,1)}) %reduce-scatter.24.cloned.1.call-update) | async-done | bytes 1048592 | tf_op jit(solution)/shard_map/reduce_scatter | solution.py:200
  3166.2 44.2 %reduce-scatter.22.cloned.1.call-done = bf16[2048,256]{1,0:T(8,128)(2,1)} async-done(((bf16[2048,1024]{1,0:T(8,128)(2,1)}), bf16[2048,256]{1,0:T(8,128)(2,1)}) %reduce-scatter.22.cloned.1.call-update) | async-done | bytes 1048592 | tf_op jit(solution)/shard_map/reduce_scatter | solution.py:194
  3221.2 10.7 fusion.59
  3231.8 13.7 fusion.46
  3245.5 39.3 all-reduce.4
  3292.6 356.9 %reduce-scatter.18.cloned.1.call-done = f32[64,6144]{1,0:T(8,128)} async-done(((f32[2048,6144]{1,0:T(8,128)}), f32[64,6144]{1,0:T(8,128)}) %reduce-scatter.18.cloned.1.call-update) | async-done | bytes 1572880 | tf_op jit(solution)/shard_map/reduce_scatter | solution.py:286
  3652.1 357.4 %reduce-scatter.20.cloned.1.call-done = f32[64,2048]{1,0:T(8,128)} async-done(((f32[2048,2048]{1,0:T(8,128)}), f32[64,2048]{1,0:T(8,128)}) %reduce-scatter.20.cloned.1.call-update) | async-done | bytes 524304 | tf_op jit(solution)/shard_map/reduce_scatter | solution.py:294
  (280 shorter events, 322.8 us)
Async XLA Ops:
  7.2 84.2 %all-gather.17.cloned.1.call-start = ((), (), s32[]{:S(2)}) async-start(), calls=%async_computation.10 | async-start | bytes 8650752 | tf_op jit(solution)/shard_map/all_gather | solution.py:93
  7.9 162.5 %all-gather.15.cloned.1.call-start = ((), (), s32[]{:S(2)}) async-start(), calls=%async_computation.9 | async-start | bytes 8650752 | tf_op jit(solution)/shard_map/all_gather | solution.py:95
  8.7 240.8 %all-gather.19.cloned.1.call-start = ((), (), s32[]{:S(2)}) async-start(), calls=%async_computation.11 | async-start | bytes 8650752 | tf_op jit(solution)/shard_map/all_gather | solution.py:94
  9.4 468.8 %all-gather.31.cloned.1.call-start = ((), (), s32[]{:S(2)}) async-start(), calls=%async_computation.26 | async-start | bytes 18874368 | tf_op jit(solution)/shard_map/all_gather | solution.py:118
  54.5 195.0 %copy-start.13 = (f32[2048]{0:T(1024)}, f32[2048]{0:T(1024)S(1)}, u32[]{:S(2)}) copy-start(f32[2048]{0:T(1024)S(1)} %convert_element_type.171) | copy-start | bytes 24580
  57.2 192.3 %copy-start.15 = (f32[512]{0:T(512)}, f32[512]{0:T(512)S(1)}, u32[]{:S(2)}) copy-start(f32[512]{0:T(512)S(1)} %get-tuple-element.321) | copy-start | bytes 6148
  91.4 10.7 copy-start.29
  101.3 455.7 %all-gather.21.cloned.1.call-start = ((), (), s32[]{:S(2)}) async-start(), calls=%async_computation.13 | async-start | bytes 8650752 | tf_op jit(solution)/shard_map/all_gather | solution.py:96
  101.9 739.9 %reduce-scatter.10.cloned.1.call-start = ((), (), s32[]{:S(2)}) async-start(), calls=%async_computation.12 | async-start | bytes 18874368 | tf_op jit(solution)/shard_map/reduce_scatter | solution.py:138
  179.0 80.4 %copy-start.1 = (bf16[512,2048]{1,0:T(8,128)(2,1)}, bf16[512,2048]{1,0:T(8,128)(2,1)S(1)}, u32[]{:S(2)}) copy-start(bf16[512,2048]{1,0:T(8,128)(2,1)S(1)} %convolution_convert_fusion.6) | copy-start | bytes 6291460
  546.2 295.6 %copy-start.4 = (bf16[1,512,2048]{2,1,0:T(8,128)(2,1)S(1)}, bf16[1,512,2048]{2,1,0:T(8,128)(2,1)}, u32[]{:S(2)}) copy-start(bf16[1,512,2048]{2,1,0:T(8,128)(2,1)} %param.14) | copy-start | bytes 6291460
  546.2 331.4 %all-gather.25.cloned.1.call-start = ((), (), s32[]{:S(2)}) async-start(), calls=%async_computation.15 | async-start | bytes 5242880 | tf_op jit(solution)/shard_map/all_gather | solution.py:153
  547.0 561.2 %all-gather.33.cloned.1.call-start = ((), (), s32[]{:S(2)}) async-start(), calls=%async_computation.27 | async-start | bytes 18874368 | tf_op jit(solution)/shard_map/all_gather | solution.py:157
  547.0 303.2 %copy-start.17 = (f32[2048]{0:T(1024)}, f32[2048]{0:T(1024)S(1)}, u32[]{:S(2)}) copy-start(f32[2048]{0:T(1024)S(1)} %convert_element_type.182) | copy-start | bytes 24580
  853.4 289.7 %all-gather.23.cloned.1.call-start = ((), (), s32[]{:S(2)}) async-start(), calls=%async_computation.14 | async-start | bytes 5242880 | tf_op jit(solution)/shard_map/all_gather | solution.py:152
  854.1 324.9 %all-gather.27.cloned.1.call-start = ((), (), s32[]{:S(2)}) async-start(), calls=%async_computation.16 | async-start | bytes 5242880 | tf_op jit(solution)/shard_map/all_gather | solution.py:154
  854.7 554.3 %all-gather.29.cloned.1.call-start = ((), (), s32[]{:S(2)}) async-start(), calls=%async_computation.18 | async-start | bytes 18874368 | tf_op jit(solution)/shard_map/all_gather | solution.py:158
  855.4 922.9 %reduce-scatter.14.cloned.1.call-start = ((), (), s32[]{:S(2)}) async-start(), calls=%async_computation.19 | async-start | bytes 18874368 | tf_op jit(solution)/shard_map/reduce_scatter | solution.py:184
  1445.1 25.5 copy-start.28
  1497.2 566.6 %reduce-scatter.12.cloned.1.call-start = ((), (), s32[]{:S(2)}) async-start(), calls=%async_computation.17 | async-start | bytes 18874368 | tf_op jit(solution)/shard_map/reduce_scatter | solution.py:170
  1520.9 257.5 %copy-start.18 = (f32[2048]{0:T(1024)S(1)}, f32[2048]{0:T(1024)}, u32[]{:S(2)}) copy-start(f32[2048]{0:T(1024)} %copy-done.17) | copy-start | bytes 24580
  1520.9 257.5 %copy-start.23 = (f32[512]{0:T(512)S(1)}, f32[512]{0:T(512)}, u32[]{:S(2)}) copy-start(f32[512]{0:T(512)} %copy-done.22) | copy-start | bytes 6148
  1521.0 542.9 %copy-start.7 = (bf16[1,512,2048]{2,1,0:T(8,128)(2,1)S(1)}, bf16[1,512,2048]{2,1,0:T(8,128)(2,1)}, u32[]{:S(2)}) copy-start(bf16[1,512,2048]{2,1,0:T(8,128)(2,1)} %param.16) | copy-start | bytes 6291460
  1521.0 542.9 %copy-start.26 = (f32[512]{0:T(512)S(1)}, f32[512]{0:T(512)}, u32[]{:S(2)}) copy-start(f32[512]{0:T(512)} %get-tuple-element.322) | copy-start | bytes 6148
  1521.0 786.4 %all-gather.35.cloned.1.call-start = ((), (), s32[]{:S(2)}) async-start(), calls=%async_computation.28 | async-start | bytes 18874368 | tf_op jit(solution)/shard_map/all_gather | solution.py:218
  2071.1 10.1 copy-start.11
  2080.5 226.9 %copy-start.21 = (s32[512]{0:T(512)S(1)}, s32[512]{0:T(512)}, u32[]{:S(2)}) copy-start(s32[512]{0:T(512)} %copy-done.20) | copy-start | bytes 6148
  2080.5 989.9 %reduce-scatter.16.cloned.1.call-start = ((), (), s32[]{:S(2)}) async-start(), calls=%async_computation.20 | async-start | bytes 18874368 | tf_op jit(solution)/shard_map/reduce_scatter | solution.py:272
  2329.1 9.8 copy-start.2
  2348.7 7.5 copy-start
  2348.7 8.2 copy-start.12
  2387.2 11.0 copy-start.2
  2408.1 8.7 copy-start
  2408.1 9.4 copy-start.12
  2447.7 11.0 copy-start.2
  2468.6 8.7 copy-start
  2468.6 9.4 copy-start.12
  2508.3 11.0 copy-start.2
  2529.2 8.7 copy-start
  2529.2 9.4 copy-start.12
  2568.9 11.0 copy-start.2
  2589.8 8.7 copy-start
  2589.8 9.4 copy-start.12
  2629.5 11.0 copy-start.2
  2650.3 8.7 copy-start
  2650.3 9.4 copy-start.12
  2690.0 11.0 copy-start.2
  2710.9 8.7 copy-start
  2710.9 9.4 copy-start.12
  2750.5 11.0 copy-start.2
  2771.4 8.7 copy-start
  2771.4 9.4 copy-start.12
  2789.4 327.0 %reduce-scatter.26.cloned.1.call-start = ((), (), s32[]{:S(2)}) async-start(), calls=%async_computation.25 | async-start | bytes 5242880 | tf_op jit(solution)/shard_map/reduce_scatter | solution.py:206
  2813.4 350.0 %reduce-scatter.24.cloned.1.call-start = ((), (), s32[]{:S(2)}) async-start(), calls=%async_computation.24 | async-start | bytes 5242880 | tf_op jit(solution)/shard_map/reduce_scatter | solution.py:200
  2837.4 373.0 %reduce-scatter.22.cloned.1.call-start = ((), (), s32[]{:S(2)}) async-start(), calls=%async_computation.23 | async-start | bytes 5242880 | tf_op jit(solution)/shard_map/reduce_scatter | solution.py:194
  2861.3 788.3 %reduce-scatter.18.cloned.1.call-start = ((), (), s32[]{:S(2)}) async-start(), calls=%async_computation.21 | async-start | bytes 51904512 | tf_op jit(solution)/shard_map/reduce_scatter | solution.py:286
  2866.6 203.8 %copy-start.5 = (bf16[1,512,2048]{2,1,0:T(8,128)(2,1)S(1)}, bf16[1,512,2048]{2,1,0:T(8,128)(2,1)}, u32[]{:S(2)}) copy-start(bf16[1,512,2048]{2,1,0:T(8,128)(2,1)} %param.14) | copy-start | bytes 6291460
  2866.6 203.8 %copy-start.14 = (f32[2048]{0:T(1024)S(1)}, f32[2048]{0:T(1024)}, u32[]{:S(2)}) copy-start(f32[2048]{0:T(1024)} %copy-done.13) | copy-start | bytes 24580
  2866.6 203.8 %copy-start.16 = (f32[512]{0:T(512)S(1)}, f32[512]{0:T(512)}, u32[]{:S(2)}) copy-start(f32[512]{0:T(512)} %copy-done.15) | copy-start | bytes 6148
  3096.7 912.8 %reduce-scatter.20.cloned.1.call-start = ((), (), s32[]{:S(2)}) async-start(), calls=%async_computation.22 | async-start | bytes 17301504 | tf_op jit(solution)/shard_map/reduce_scatter | solution.py:294
  3213.1 8.0 copy-start.10
  3221.2 10.7 copy-start.8
  3231.8 13.7 copy-start.24
  3231.8 54.2 %copy-start.25 = (f32[512]{0:T(512)S(1)}, f32[512]{0:T(512)}, u32[]{:S(2)}) copy-start(f32[512]{0:T(512)} %get-tuple-element.320) | copy-start | bytes 6148
  (7 other events, 18.7 us)
Sparse Core Ops, SparseCore 0:
  11.0 80.3 all-gather.16
  94.4 75.9 all-gather.14
  173.4 75.9 all-gather.18
  252.0 226.1 all-gather.30
  481.1 75.9 all-gather.20
  560.7 281.0 reduce-scatter.9
  843.4 34.1 all-gather.24
  880.5 227.5 all-gather.32
  1109.8 33.2 all-gather.22
  1144.5 34.4 all-gather.26
  1181.4 227.5 all-gather.28
  1497.3 281.0 reduce-scatter.13
  1782.2 281.6 reduce-scatter.11
  2080.6 226.6 all-gather.34
  2789.5 280.8 reduce-scatter.15
  3072.7 43.5 reduce-scatter.25
  3118.9 44.5 reduce-scatter.23
  3165.9 44.5 reduce-scatter.21
  3218.0 431.4 reduce-scatter.17
  3652.3 357.0 reduce-scatter.19
where the time goes:
time: 4020 us
  waiting for transfers between devices  2960 us (74%)
  matrix products  764 us (19%)
  local copies, waits for them, and re-layouts  147 us (4%)
  blocking collectives  82.6 us (2%)
  other arithmetic  45.3 us (1%)
    reduce_scatter x1, waiting for transfers between devices, body(): lax.psum_scatter(out_term, ('row', 'kv'), scatter_dimension=0, tiled=True)  357 us
    reduce_scatter x1, waiting for transfers between devices, body(): lax.psum_scatter(contract_rows(normed_attn_low, projected_low), ('row', '...  357 us
    reduce_scatter x1, waiting for transfers between devices, body(): lax.psum_scatter(summed.reshape(lax.axis_size('kv') * block, width).astyp...  285 us
    reduce_scatter x1, waiting for transfers between devices, body(): lax.psum_scatter(jnp.dot(hidden_part, slice_down, preferred_element_type=...  281 us
    reduce_scatter x1, waiting for transfers between devices, body(): lax.psum_scatter(partial_normed.reshape(rows_here, LEN, width).astype(jnp...  257 us
    all_gather x1, waiting for transfers between devices, body(): lax.all_gather(normed_mlp_low.reshape(rows_here, block, width), 'kv', axi...  231 us
    all_gather x1, waiting for transfers between devices, body(): lax.all_gather(cotangent, 'kv', axis=1, tiled=True)  230 us
    all_gather x1, waiting for transfers between devices, body(): lax.all_gather(d_attended.reshape(rows_here, block, width), 'kv', axis=1,...  223 us
  transfers between devices with their start and end apart: 20, of which 20 were waited for; matrix products, arithmetic and copies ran while one was open for 9% of the time, Pallas kernels for 0%

commit v1 on v0

--- a/solution.py
+++ b/solution.py
@@ -1,9 +1,12 @@
+import functools
 import math
 
 import jax
 import jax.numpy as jnp
 from jax import lax
-from jax.sharding import PartitionSpec as P
+from jax.experimental import pallas as pl
+from jax.experimental.pallas import tpu as pltpu
+from jax.sharding import Mesh, PartitionSpec as P
 
 H = 16
 HD = 128
@@ -70,7 +73,285 @@
     return (d_gate, d_up)
 
 
-def body(
+TILE = 512
+LOW = jnp.bfloat16
+VMEM_LIMIT = 60 * 1024 * 1024
+
+
+def doc_start(ends, place):
+    start = jnp.zeros_like(place)
+    for k in range(8):
+        start = jnp.where(ends[k] <= place, ends[k], start)
+    return jnp.where(place < ends[7], start, LEN)
+
+
+def doc_end(ends, place):
+    end = ends[7]
+    for k in range(6, -1, -1):
+        end = jnp.where(ends[k] > place, ends[k], end)
+    return end
+
+
+def sigmoid_of(raw):
+    return pl.reciprocal(1.0 + jnp.exp2(math.log2(LEN) - raw * (math.log2(math.e) / math.sqrt(HD))), approx=True)
+
+
+def dot_nt(left, right):
+    return lax.dot_general(left, right, (((1,), (1,)), ((), ())), preferred_element_type=jnp.float32)
+
+
+def attend_kernel(ends, qkv, out, total):
+    head, i = pl.program_id(0), pl.program_id(1)
+    column = pl.multiple_of(head * HD, HD)
+    width = qkv.shape[1] // 3
+    first = i * TILE
+    query = qkv[pl.ds(pl.multiple_of(first, TILE), TILE), pl.ds(column, HD)]
+    total[...] = jnp.zeros_like(total)
+    begin = jnp.minimum(doc_start(ends, first), first) // TILE
+    latest = doc_start(ends, first + TILE - 1)
+
+    def step(j, carry):
+        here = pl.ds(pl.multiple_of(j * TILE, TILE), TILE)
+        key = qkv[here, pl.ds(pl.multiple_of(column + width, HD), HD)]
+        value = qkv[here, pl.ds(pl.multiple_of(column + 2 * width, HD), HD)]
+        plain = (j < i) & (j * TILE >= latest)
+
+        @pl.when(plain)
+        def _():
+            weight = sigmoid_of(dot_nt(query, key)).astype(LOW)
+            total[...] += jnp.dot(weight, value, preferred_element_type=jnp.float32)
+
+        @pl.when(jnp.logical_not(plain))
+        def _():
+            q_place = first + lax.broadcasted_iota(jnp.int32, (TILE, 1), 0)
+            k_place = j * TILE + lax.broadcasted_iota(jnp.int32, (1, TILE), 1)
+            allowed = (k_place <= q_place) & (k_place >= doc_start(ends, q_place))
+            weight = jnp.where(allowed, sigmoid_of(dot_nt(query, key)), 0.0).astype(LOW)
+            total[...] += jnp.dot(weight, value, preferred_element_type=jnp.float32)
+
+        return carry
+
+    lax.fori_loop(begin, i + 1, step, 0)
+    out[pl.ds(pl.multiple_of(first, TILE), TILE), pl.ds(column, HD)] = total[...].astype(LOW)
+
+
+def attend_back_kernel(ends, qkv, grads, out, query_total, key_total, value_total):
+    head, j = pl.program_id(0), pl.program_id(1)
+    column = pl.multiple_of(head * HD, HD)
+    width = qkv.shape[1] // 3
+    first = j * TILE
+    here = pl.ds(pl.multiple_of(first, TILE), TILE)
+    key_column = pl.multiple_of(column + width, HD)
+    value_column = pl.multiple_of(column + 2 * width, HD)
+    key = qkv[here, pl.ds(key_column, HD)]
+    value = qkv[here, pl.ds(value_column, HD)]
+    key_turned = key.T
+    key_total[...] = jnp.zeros_like(key_total)
+    value_total[...] = jnp.zeros_like(value_total)
+
+    @pl.when(j == 0)
+    def _():
+        query_total[...] = jnp.zeros_like(query_total)
+
+    end = pl.cdiv(doc_end(ends, first + TILE - 1), TILE)
+
+    def step(i, carry):
+        there = pl.ds(pl.multiple_of(i * TILE, TILE), TILE)
+        query = qkv[there, pl.ds(column, HD)]
+        grad = grads[there, pl.ds(column, HD)]
+        plain = (j < i) & (first >= doc_start(ends, i * TILE + TILE - 1))
+
+        def finish(sig):
+            value_total[...] += jnp.dot(sig.astype(LOW), grad, preferred_element_type=jnp.float32)
+            d_score = (dot_nt(value, grad) * (sig * (1.0 - sig))).astype(LOW)
+            key_total[...] += jnp.dot(d_score, query, preferred_element_type=jnp.float32)
+            query_total[:, there] += jnp.dot(key_turned, d_score, preferred_element_type=jnp.float32)
+
+        @pl.when(plain)
+        def _():
+            finish(sigmoid_of(dot_nt(key, query)))
+
+        @pl.when(jnp.logical_not(plain))
+        def _():
+            q_place = i * TILE + lax.broadcasted_iota(jnp.int32, (1, TILE), 1)
+            k_place = first + lax.broadcasted_iota(jnp.int32, (TILE, 1), 0)
+            allowed = (k_place <= q_place) & (k_place >= doc_start(ends, q_place))
+            finish(jnp.where(allowed, sigmoid_of(dot_nt(key, query)), 0.0))
+
+        return carry
+
+    lax.fori_loop(j, end, step, 0)
+    scale = 1.0 / math.sqrt(HD)
+    out[here, pl.ds(key_column, HD)] = (key_total[...] * scale).astype(LOW)
+    out[here, pl.ds(value_column, HD)] = value_total[...].astype(LOW)
+
+    @pl.when(j == pl.num_programs(1) - 1)
+    def _():
+        for t in range(LEN // TILE):
+            out[t * TILE : (t + 1) * TILE, pl.ds(column, HD)] = (
+                (query_total[:, t * TILE : (t + 1) * TILE] * scale).T.astype(LOW)
+            )
+
+
+def attend(ends, qkv):
+    places, width = qkv.shape
+    heads = width // (3 * HD)
+    return pl.pallas_call(
+        attend_kernel,
+        out_shape=jax.ShapeDtypeStruct((places, width // 3), LOW),
+        grid_spec=pltpu.PrefetchScalarGridSpec(
+            num_scalar_prefetch=1,
+            grid=(heads, places // TILE),
+            in_specs=[pl.BlockSpec((places, width), lambda h, i, ends: (0, 0))],
+            out_specs=pl.BlockSpec((places, width // 3), lambda h, i, ends: (0, 0)),
+            scratch_shapes=[pltpu.VMEM((TILE, HD), jnp.float32)],
+        ),
+        compiler_params=pltpu.CompilerParams(vmem_limit_bytes=VMEM_LIMIT),
+        cost_estimate=pl.CostEstimate(
+            flops=4 * heads * places * places * HD // 2, bytes_accessed=8 * places * width // 3, transcendentals=heads * places * places // 2
+        ),
+    )(ends, qkv)
+
+
+def attend_back(ends, qkv, grads):
+    places, width = qkv.shape
+    heads = width // (3 * HD)
+    whole = lambda columns: pl.BlockSpec((places, columns), lambda h, j, ends: (0, 0))
+    return pl.pallas_call(
+        attend_back_kernel,
+        out_shape=jax.ShapeDtypeStruct((places, width), LOW),
+        grid_spec=pltpu.PrefetchScalarGridSpec(
+            num_scalar_prefetch=1,
+            grid=(heads, places // TILE),
+            in_specs=[whole(width), whole(width // 3)],
+            out_specs=whole(width),
+            scratch_shapes=[
+                pltpu.VMEM((HD, places), jnp.float32),
+                pltpu.VMEM((TILE, HD), jnp.float32),
+                pltpu.VMEM((TILE, HD), jnp.float32),
+            ],
+        ),
+        compiler_params=pltpu.CompilerParams(vmem_limit_bytes=VMEM_LIMIT),
+        cost_estimate=pl.CostEstimate(
+            flops=10 * heads * places * places * HD // 2, bytes_accessed=14 * places * width // 3, transcendentals=heads * places * places // 2
+        ),
+    )(ends, qkv, grads)
+
+
+LAYER = ("y", "c", "x")
+ALL = ("y", "c", "z", "x")
+
+
+def gather_layer(part):
+    return lax.all_gather(part, LAYER, axis=0, tiled=True)
+
+
+def scatter_layer(whole):
+    return lax.psum_scatter(whole.astype(LOW), LAYER, scatter_dimension=0, tiled=True).astype(jnp.float32)
+
+
+def swap_rows(part):
+    return lax.all_to_all(part.reshape(4, -1, part.shape[1]), "z", 0, 0).reshape(part.shape)
+
+
+def dot_wide(left, right):
+    return jnp.dot(left, right, preferred_element_type=jnp.float32)
+
+
+def body_layers(
+    tokens, lengths, cotangent, w_query, w_key, w_value, w_out, w_gate, w_up, w_down, gain_attn, gain_mlp
+):
+    rows_here, block, width = tokens.shape
+    members = lax.axis_size(LAYER)
+    layers = lax.axis_size("z")
+    shard = w_query.shape[0]
+    owned = width // members
+    gains = lax.all_gather(jnp.stack((gain_attn, gain_mlp), axis=1), ALL, axis=0, tiled=True)
+    full_gain_attn, full_gain_mlp = gains[:, 0], gains[:, 1]
+    ends = jnp.cumsum(lax.all_gather(lengths, ("y", "c"), axis=0, tiled=True), axis=-1)
+    ends = lax.dynamic_slice_in_dim(ends, lax.axis_index("z"), 1, 0)[0]
+
+    flat = tokens.reshape(block, width).astype(jnp.float32)
+    normed_attn, inverse_attn = norm_forward(flat, full_gain_attn)
+    layer_normed = gather_layer(normed_attn.astype(LOW))
+    qkv_shards = jnp.stack((w_query, w_key, w_value), axis=1).reshape(shard, 3, members, owned)
+    qkv_shards = qkv_shards.transpose(2, 0, 1, 3).reshape(members, shard, 3 * owned)
+    qkv_shards = lax.all_to_all(qkv_shards, LAYER, 0, 0)
+    w_qkv = lax.all_gather(qkv_shards, "z", axis=0)
+    w_qkv = w_qkv.reshape(layers, 4, 2 * shard, 3 * owned).transpose(1, 0, 2, 3).reshape(width, 3 * owned)
+    out_rows = lax.all_gather(w_out, ("z", "x"), axis=0, tiled=True)
+    w_out_own = lax.dynamic_slice_in_dim(out_rows, lax.axis_index("x") * owned, owned, 0)
+
+    qkv = swap_rows(dot_wide(layer_normed, w_qkv).astype(LOW))
+    attended = swap_rows(attend(ends, qkv))
+    resid = flat + scatter_layer(dot_wide(attended, w_out_own))
+
+    normed_mlp, inverse_mlp = norm_forward(resid, full_gain_mlp)
+    own_gate = lax.all_gather(w_gate, "z", axis=1, tiled=True)
+    own_up = lax.all_gather(w_up, "z", axis=1, tiled=True)
+    own_down = lax.all_gather(w_down, "z", axis=0, tiled=True)
+    upstream_low = cotangent.reshape(block, width)
+    upstream = upstream_low.astype(jnp.float32)
+    layer_upstream = gather_layer(upstream_low)
+    layer_mlp = gather_layer(normed_mlp.astype(LOW))
+    gate = dot_wide(layer_mlp, own_gate)
+    up_part = dot_wide(layer_mlp, own_up)
+    sigmoid_gate = jax.nn.sigmoid(gate)
+    hidden = (gate * sigmoid_gate * up_part).astype(LOW)
+    result = resid + scatter_layer(dot_wide(hidden, own_down))
+    d_hidden = contract_cols(layer_upstream, own_down)
+    d_gate, d_up = gate_backward(d_hidden, gate, up_part, sigmoid_gate)
+    d_normed_mlp = scatter_layer(contract_cols(d_gate, own_gate) + contract_cols(d_up, own_up))
+
+    def scatter_layers(whole, axis):
+        return lax.psum_scatter(whole.astype(LOW), "z", scatter_dimension=axis, tiled=True).astype(jnp.float32)
+
+    grad_gate = scatter_layers(contract_rows(layer_mlp, d_gate), 1)
+    grad_up = scatter_layers(contract_rows(layer_mlp, d_up), 1)
+    grad_down = scatter_layers(contract_rows(hidden, layer_upstream), 0)
+    mixed = result.astype(LOW).reshape(rows_here, block, width)
+
+    back_mlp, gain_mlp_term = norm_backward(resid, inverse_mlp, full_gain_mlp, d_normed_mlp)
+    d_resid = upstream + back_mlp
+    layer_d_resid = gather_layer(d_resid.astype(LOW))
+    d_attended = swap_rows(contract_cols(layer_d_resid, w_out_own).astype(LOW))
+    d_qkv = swap_rows(attend_back(ends, qkv, d_attended))
+    d_normed_attn = scatter_layer(contract_cols(d_qkv, w_qkv))
+    out_term = contract_rows(attended, layer_d_resid)
+    qkv_term = contract_rows(layer_normed, d_qkv)
+
+    back_attn, gain_attn_term = norm_backward(flat, inverse_attn, full_gain_attn, d_normed_attn)
+    grad_tokens = (d_resid + back_attn).reshape(rows_here, block, width)
+
+    out_term = lax.dynamic_update_slice_in_dim(
+        jnp.zeros((2 * owned, width), LOW), out_term.astype(LOW), lax.axis_index("x") * owned, 0
+    )
+    grad_out = lax.psum_scatter(out_term, ("z", "x"), scatter_dimension=0, tiled=True).astype(jnp.float32)
+    qkv_term = qkv_term.reshape(4, layers, 2 * shard, 3 * owned).transpose(1, 0, 2, 3)
+    qkv_term = qkv_term.reshape(layers * members * shard, 3 * owned)
+    qkv_term = lax.psum_scatter(qkv_term.astype(LOW), "z", scatter_dimension=0, tiled=True)
+    qkv_term = lax.all_to_all(qkv_term.reshape(members, shard, 3 * owned), LAYER, 0, 0)
+    qkv_term = qkv_term.reshape(members, shard, 3, owned).transpose(2, 1, 0, 3).astype(jnp.float32)
+    grad_query, grad_key, grad_value = qkv_term.reshape(3, shard, width)
+    gain_terms = lax.psum_scatter(
+        jnp.stack((gain_attn_term, gain_mlp_term), axis=1), ALL, scatter_dimension=0, tiled=True
+    )
+    return (
+        mixed,
+        grad_tokens,
+        grad_query,
+        grad_key,
+        grad_value,
+        grad_out,
+        grad_gate,
+        grad_up,
+        grad_down,
+        gain_terms[:, 0],
+        gain_terms[:, 1],
+    )
+
+
+def body_any(
     tokens,
     lengths,
     cotangent,
@@ -314,35 +595,19 @@
 
 
 def solution(mesh):
+    rows, columns = mesh.shape["row"], mesh.shape["kv"]
+    if rows == 4 and columns == 2 * rows:
+        mesh = Mesh(mesh.devices.reshape(2, 2, rows, 2), ("y", "c", "z", "x"))
+        row, kv, run = ("y", "c"), ("z", "x"), body_layers
+    else:
+        row, kv, run = "row", "kv", body_any
+    both = ("y", "c", "z", "x") if run is body_layers else ("row", "kv")
+    tall, wide, flat = P(both, None), P(None, both), P(both)
+    tokens = P(row, kv, None)
     return jax.shard_map(
-        body,
+        run,
         mesh=mesh,
-        in_specs=(
-            P("row", "kv", None),
-            P("row", None),
-            P("row", "kv", None),
-            P(("row", "kv"), None),
-            P(("row", "kv"), None),
-            P(("row", "kv"), None),
-            P(("row", "kv"), None),
-            P(None, ("row", "kv")),
-            P(None, ("row", "kv")),
-            P(("row", "kv"), None),
-            P(("row", "kv")),
-            P(("row", "kv")),
-        ),
-        out_specs=(
-            P("row", "kv", None),
-            P("row", "kv", None),
-            P(("row", "kv"), None),
-            P(("row", "kv"), None),
-            P(("row", "kv"), None),
-            P(("row", "kv"), None),
-            P(None, ("row", "kv")),
-            P(None, ("row", "kv")),
-            P(("row", "kv"), None),
-            P(("row", "kv")),
-            P(("row", "kv")),
-        ),
+        in_specs=(tokens, P(row, None), tokens, tall, tall, tall, tall, wide, wide, tall, flat, flat),
+        out_specs=(tokens, tokens, tall, tall, tall, tall, wide, wide, tall, flat, flat),
         check_vma=False,
     )

time: 4020 us -> 2410 us (0.60)
  waiting for transfers between devices: 2960 us -> 1680 us
  matrix products: 764 us -> 322 us
  Pallas kernels: 0 us -> 135 us
  local copies, waits for them, and re-layouts: 147 us -> 50.9 us
  blocking collectives: 82.6 us -> 143 us
    reduce_scatter x9, waiting for transfers between devices: 1830 us -> 681 us  [the longest x4 452 us: scatter_layer(): lax.psum_scatter(whole.astype(LOW), LAYER, scatter_dimension=0, tiled=True)]
    all_gather x11 -> x9, waiting for transfers between devices: 1120 us -> 543 us  [the longest x4 354 us: gather_layer(): return lax.all_gather(part, LAYER, axis=0, tiled=True)]
    dot_general x48 -> x5, matrix products: 523 us -> 102 us  [dot_wide(): return jnp.dot(left, right, preferred_element_type=jnp.float32)]
    all_to_all x0 -> x4, waiting for transfers between devices: none -> 322 us  [the longest x3 322 us: swap_rows(): lax.all_to_all(part.reshape(4, -1, part.shape[1]), 'z', 0, 0)]
    pallas_call x0 -> x2, Pallas kernels: none -> 135 us  [the longest x1 82.2 us: attend_back(): pl.pallas_call(attend_back_kernel, out_shape=jax.ShapeDtypeStruct((places...]
    unnamed x20, waiting for transfers between devices: 5.38 us -> 133 us
    dynamic_slice x40 -> x0, local copies, waits for them, and re-layouts: 84.9 us -> none  [the longest x16 54.9 us: sweep(): lax.dynamic_slice_in_dim(grads_all[which], start, query_block, 0)]
    unnamed x2 -> x0, blocking collectives: 82.6 us -> none
  transfers between devices with their start and end apart: 20 -> 23, of which waited for: 20 -> 19; matrix products, arithmetic and copies ran while one was open for 9% -> 10% of each run, Pallas kernels for 0% -> 2%
where the time goes in v1:
time: 2410 us
  waiting for transfers between devices  1680 us (70%)
  matrix products  322 us (13%)
  blocking collectives  143 us (6%)
  Pallas kernels  135 us (6%)
  local copies, waits for them, and re-layouts  50.9 us (2%)
  other arithmetic  39 us (2%)
    reduce_scatter x4, waiting for transfers between devices, scatter_layer(): lax.psum_scatter(whole.astype(LOW), LAYER, scatter_dimension=0, tiled=True)  452 us
    all_gather x4, waiting for transfers between devices, gather_layer(): return lax.all_gather(part, LAYER, axis=0, tiled=True)  354 us
    all_to_all x3, waiting for transfers between devices, swap_rows(): lax.all_to_all(part.reshape(4, -1, part.shape[1]), 'z', 0, 0)  322 us
    reduce_scatter x3, waiting for transfers between devices, scatter_layers(): lax.psum_scatter(whole.astype(LOW), 'z', scatter_dimension=axis, tiled=True)  159 us
    unnamed x20, waiting for transfers between devices  133 us
    dot_general x5, matrix products, contract_cols(): lax.dot_general(left, right, (((1,), (1,)), ((), ())), preferred_element_...  119 us
    dot_general x5, matrix products, dot_wide(): return jnp.dot(left, right, preferred_element_type=jnp.float32)  102 us
    dot_general x5, matrix products, contract_rows(): lax.dot_general(left, right, (((0,), (0,)), ((), ())), preferred_element_...  101 us
  transfers between devices with their start and end apart: 23, of which 19 were waited for; matrix products, arithmetic and copies ran while one was open for 10% of the time, Pallas kernels for 2%

profile of v1, /device:TPU:0, one launch (start us, length us, event | category | flops | bytes accessed | tf_op | source)
XLA Modules:
  0.0 2407.7 jit_solution(12649190280232843361)
XLA Ops:
  12.5 1.8 maximum_bitcast_fusion
  14.3 1.7 reshape.141
  16.0 17.3 all_to_all.30
  33.4 68.0 %all-gather.3 = bf16[32,64,2]{1,2,0:T(2,128)(2,1)S(1)} all-gather(bf16[1,64,2]{1,2,0:T(2,128)(2,1)S(1)} %maximum_bitcast_fusion.1), channel_id=1, replica_groups=mesh['y'=2,'c'=2,'z'=4,'x'=2] {'y','c','z','x'}, dimensions={0}, use_global_device_ids=true | all-gather | bytes 8448 | tf_op jit(solution)/shard_map/all_gather | solution.py:269
  103.2 1.9 fusion.17
  105.1 3.9 copy.54
  109.0 82.9 %all-gather.14.cloned.1.call-done = bf16[4096,2048]{1,0:T(8,128)(2,1)} async-done(((bf16[512,2048]{1,0:T(8,128)(2,1)}), bf16[4096,2048]{1,0:T(8,128)(2,1)}) %all-gather.14.cloned.1.call-update) | async-done | bytes 16777232 | tf_op jit(solution)/shard_map/all_gather | solution.py:246
  191.9 19.4 convolution_convert_fusion.3
  211.3 5.4 all-to-all-start.1
  217.3 5.0 all-gather.2
  223.0 157.8 %all-to-all-done.1 = bf16[4,1024,768]{2,1,0:T(8,128)(2,1)} async-done(((bf16[4,1024,768]{2,1,0:T(8,128)(2,1)}), bf16[4,1024,768]{2,1,0:T(8,128)(2,1)}, u32[]{:S(2)}, u32[]{:S(2)}) %all-to-all-start.1) | async-done | bytes 6291488 | tf_op jit(solution)/shard_map/all_to_all | solution.py:254
  380.8 52.6 %shard_map.203 = bf16[4096,256]{1,0:T(8,128)(2,1)} custom-call(s32[8]{0:T(128)} %fusion.31.ends, bf16[4096,768]{1,0:T(8,128)(2,1)} %bitcast.14.qkv), custom_call_target="tpu_custom_call" | custom-call | flops 8589934592 | bytes 8388608 | tf_op jit(solution)/shard_map/pallas_call | solution.py:199
  433.4 6.9 all-to-all-start.2
  440.6 47.7 %all-to-all-done.2 = bf16[4,1024,256]{2,1,0:T(8,128)(2,1)} async-done(((bf16[4,1024,256]{2,1,0:T(8,128)(2,1)}), bf16[4,1024,256]{2,1,0:T(8,128)(2,1)}, u32[]{:S(2)}, u32[]{:S(2)}) %all-to-all-start.2) | async-done | bytes 2097184 | tf_op jit(solution)/shard_map/all_to_all | solution.py:254
  488.2 12.1 convolution_convert_fusion.2
  501.0 113.6 %reduce-scatter.13.cloned.1.call-done = bf16[512,2048]{1,0:T(8,128)(2,1)} async-done(((bf16[4096,2048]{1,0:T(8,128)(2,1)}), bf16[512,2048]{1,0:T(8,128)(2,1)}) %reduce-scatter.13.cloned.1.call-update) | async-done | bytes 2097168 | tf_op jit(solution)/shard_map/reduce_scatter | solution.py:250
  614.7 2.5 multiply_reduce_fusion
  618.3 2.4 multiply_convert_fusion.3
  623.3 73.4 %all-gather.22.cloned.1.call-done = bf16[2048,1024]{1,0:T(8,128)(2,1)} async-done(((bf16[2048,256]{1,0:T(8,128)(2,1)}), bf16[2048,1024]{1,0:T(8,128)(2,1)}) %all-gather.22.cloned.1.call-update) | async-done | bytes 4194320 | tf_op jit(solution)/shard_map/all_gather | solution.py:291
  696.7 90.4 %all-gather.18.cloned.1.call-done = bf16[4096,2048]{1,0:T(8,128)(2,1)} async-done(((bf16[512,2048]{1,0:T(8,128)(2,1)}), bf16[4096,2048]{1,0:T(8,128)(2,1)}) %all-gather.18.cloned.1.call-update) | async-done | bytes 16777232 | tf_op jit(solution)/shard_map/all_gather | solution.py:246
  787.0 23.4 fusion.36
  810.5 58.6 %all-gather.20.cloned.1.call-done = bf16[2048,1024]{1,0:T(8,128)(2,1)} async-done(((bf16[2048,256]{1,0:T(8,128)(2,1)}), bf16[2048,1024]{1,0:T(8,128)(2,1)}) %all-gather.20.cloned.1.call-update) | async-done | bytes 4194320 | tf_op jit(solution)/shard_map/all_gather | solution.py:290
  869.1 23.4 fusion.35
  892.4 57.2 %all-gather.24.cloned.1.call-done = bf16[1024,2048]{1,0:T(8,128)(2,1)} async-done(((bf16[256,2048]{1,0:T(8,128)(2,1)}), bf16[1024,2048]{1,0:T(8,128)(2,1)}) %all-gather.24.cloned.1.call-update) | async-done | bytes 4194320 | tf_op jit(solution)/shard_map/all_gather | solution.py:292
  949.6 90.3 %all-gather.30.cloned.1.call-done = bf16[1,4096,2048]{2,1,0:T(8,128)(2,1)} async-done(((bf16[1,512,2048]{2,1,0:T(8,128)(2,1)}), bf16[1,4096,2048]{2,1,0:T(8,128)(2,1)}) %all-gather.30.cloned.1.call-update) | async-done | bytes 16777232 | tf_op jit(solution)/shard_map/all_gather | solution.py:246
  1039.9 36.1 %multiply_convert_fusion = (bf16[4096,1024]{1,0:T(8,128)(2,1)}, bf16[4096,1024]{1,0:T(8,128)(2,1)}, bf16[4096,1024]{1,0:T(8,128)(2,1)}) fusion(f32[4096,1024]{1,0:T(8,128)} %fusion.35, f32[4096,1024]{1,0:T(8,128)} %fusion.36, bf16[1024,2048]{1,0:T(8,128)(2,1)} %all-gather.24.cloned.1.call-done, bf16[1,4096,2048]{2,1,0:T(8,128)(2,1)} %all-gather.30.cloned.1.call-done), kind=kOutput, calls=%fused_computation.5 | convolution fusion | flops 17246978048 | bytes 79691776 | tf_op jit(solution)/shard_map/dot_general | solution.py:26
  1076.0 25.6 %fusion.37 = f32[4096,2048]{1,0:T(8,128)} fusion(bf16[4096,1024]{1,0:T(8,128)(2,1)} %get-tuple-element.16, bf16[2048,1024]{1,0:T(8,128)(2,1)} %all-gather.20.cloned.1.call-done), kind=kOutput, calls=%fused_computation.73 | convolution fusion | flops 17179869184 | bytes 46137344 | tf_op jit(solution)/shard_map/dot_general | solution.py:26
  1101.6 26.6 %add_convert_fusion = bf16[4096,2048]{1,0:T(8,128)(2,1)} fusion(f32[4096,2048]{1,0:T(8,128)} %fusion.37, bf16[4096,1024]{1,0:T(8,128)(2,1)} %get-tuple-element.15, bf16[2048,1024]{1,0:T(8,128)(2,1)S(1)} %copy-done.25), kind=kOutput, calls=%fused_computation | convolution fusion | flops 17196646400 | bytes 62914560 | tf_op jit(solution)/shard_map/dot_general | solution.py:26
  1128.2 116.1 %reduce-scatter.17.cloned.1.call-done = bf16[512,2048]{1,0:T(8,128)(2,1)} async-done(((bf16[4096,2048]{1,0:T(8,128)(2,1)}), bf16[512,2048]{1,0:T(8,128)(2,1)}) %reduce-scatter.17.cloned.1.call-update) | async-done | bytes 2097168 | tf_op jit(solution)/shard_map/reduce_scatter | solution.py:250
  1244.3 4.5 fusion.14
  1249.5 3.1 fusion.32
  1252.6 90.0 %all-gather.26.cloned.1.call-done = bf16[4096,2048]{1,0:T(8,128)(2,1)} async-done(((bf16[512,2048]{1,0:T(8,128)(2,1)}), bf16[4096,2048]{1,0:T(8,128)(2,1)}) %all-gather.26.cloned.1.call-update) | async-done | bytes 16777232 | tf_op jit(solution)/shard_map/all_gather | solution.py:246
  1342.6 10.6 convolution_convert_fusion.4
  1353.2 53.1 %all_to_all.31 = bf16[4,1024,256]{2,1,0:T(8,128)(2,1)} all-to-all(bf16[4,1024,256]{2,1,0:T(8,128)(2,1)S(1)} %bitcast.137), channel_id=1, replica_groups=mesh['y'=2,'c'=2,'z'=4,'x'=2] {'z'}, dimensions={0} | all-to-all | bytes 4194304 | tf_op jit(solution)/shard_map/all_to_all | solution.py:254
  1406.3 82.2 %shard_map.204 = bf16[4096,768]{1,0:T(8,128)(2,1)} custom-call(s32[8]{0:T(128)} %fusion.31.ends, bf16[4096,768]{1,0:T(8,128)(2,1)} %bitcast.14.qkv, bf16[4096,256]{1,0:T(8,128)(2,1)} %bitcast.136), custom_call_target="tpu_custom_call" | custom-call | flops 21474836480 | bytes 14680064 | tf_op jit(solution)/shard_map/pallas_call | solution.py:220
  1488.5 5.3 all-to-all-start.4
  1493.8 21.1 copy.61
  1514.9 116.5 %all-to-all-done.4 = bf16[4,1024,768]{2,1,0:T(8,128)(2,1)} async-done(((bf16[4,1024,768]{2,1,0:T(8,128)(2,1)}), bf16[4,1024,768]{2,1,0:T(8,128)(2,1)}, u32[]{:S(2)}, u32[]{:S(2)}) %all-to-all-start.4) | async-done | bytes 6291488 | tf_op jit(solution)/shard_map/all_to_all | solution.py:254
  1631.5 18.5 convert_bitcast_fusion
  1650.0 2.0 copy.56
  1652.1 24.2 %fusion.22 = bf16[1024,2048]{1,0:T(8,128)(2,1)} fusion(bf16[4096,1024]{1,0:T(8,128)(2,1)} %get-tuple-element.17, bf16[1,4096,2048]{2,1,0:T(8,128)(2,1)} %all-gather.30.cloned.1.call-done), kind=kOutput, calls=%fused_computation.44 | convolution fusion | flops 17181966336 | bytes 29360128 | tf_op jit(solution)/shard_map/dot_general | solution.py:20
  1676.4 23.8 convolution_convert_fusion.5
  1700.3 24.0 convolution_convert_fusion.6
  1724.5 11.0 fusion.25
  1735.6 1.3 copy-done.7
  1736.9 20.2 convolution_convert_fusion
  1757.2 23.6 convolution_convert_fusion.1
  1780.8 3.6 all-to-all-start.5
  1784.6 5.0 reduce-scatter.29.cloned.1.call-done
  1789.6 2.8 convert_element_type.161
  1792.4 76.9 %reduce-scatter.27.cloned.1.call-done = bf16[2048,256]{1,0:T(8,128)(2,1)} async-done(((bf16[2048,1024]{1,0:T(8,128)(2,1)}), bf16[2048,256]{1,0:T(8,128)(2,1)}) %reduce-scatter.27.cloned.1.call-update) | async-done | bytes 1048592 | tf_op jit(solution)/shard_map/reduce_scatter | solution.py:307
  1869.3 2.7 convert_element_type.159
  1872.0 77.3 %reduce-scatter.25.cloned.1.call-done = bf16[2048,256]{1,0:T(8,128)(2,1)} async-done(((bf16[2048,1024]{1,0:T(8,128)(2,1)}), bf16[2048,256]{1,0:T(8,128)(2,1)}) %reduce-scatter.25.cloned.1.call-update) | async-done | bytes 1048592 | tf_op jit(solution)/shard_map/reduce_scatter | solution.py:307
  1949.3 2.7 convert_element_type.157
  1952.0 70.1 %reduce-scatter.23.cloned.1.call-done = bf16[64,2048]{1,0:T(8,128)(2,1)} async-done(((bf16[512,2048]{1,0:T(8,128)(2,1)}), bf16[64,2048]{1,0:T(8,128)(2,1)}) %reduce-scatter.23.cloned.1.call-update) | async-done | bytes 262160 | tf_op jit(solution)/shard_map/reduce_scatter | solution.py:329
  2022.1 1.8 convert_element_type.155
  2023.9 1.8 reshape.159
  2025.7 4.7 fusion.33
  2034.3 106.6 %reduce-scatter.19.cloned.1.call-done = bf16[512,2048]{1,0:T(8,128)(2,1)} async-done(((bf16[4096,2048]{1,0:T(8,128)(2,1)}), bf16[512,2048]{1,0:T(8,128)(2,1)}) %reduce-scatter.19.cloned.1.call-update) | async-done | bytes 2097168 | tf_op jit(solution)/shard_map/reduce_scatter | solution.py:250
  2140.9 3.2 fusion.21
  2144.1 1.4 copy.62
  2145.5 115.2 %reduce-scatter.15.cloned.1.call-done = bf16[512,2048]{1,0:T(8,128)(2,1)} async-done(((bf16[4096,2048]{1,0:T(8,128)(2,1)}), bf16[512,2048]{1,0:T(8,128)(2,1)}) %reduce-scatter.15.cloned.1.call-update) | async-done | bytes 2097168 | tf_op jit(solution)/shard_map/reduce_scatter | solution.py:250
  2260.7 7.8 fusion.9
  2268.5 129.4 %reduce-scatter.31.cloned.1.call-done = f32[64,2]{1,0:T(8,128)} async-done(((f32[2048,2]{1,0:T(8,128)}), f32[64,2]{1,0:T(8,128)}) %reduce-scatter.31.cloned.1.call-update) | async-done | bytes 528
  (125 shorter events, 19.7 us)
Async XLA Ops:
  8.0 97.1 %all-gather.28.cloned.1.call-start = ((), (), s32[]{:S(2)}) async-start(), calls=%async_computation.32 | async-start | bytes 3932160 | tf_op jit(solution)/shard_map/all_gather | solution.py:280
  10.9 22.5 copy-start.26
  10.9 22.5 copy-start.27
  10.9 90.6 %copy-start = (bf16[1,512,2048]{2,1,0:T(8,128)(2,1)S(1)}, bf16[1,512,2048]{2,1,0:T(8,128)(2,1)}, u32[]{:S(2)}) copy-start(bf16[1,512,2048]{2,1,0:T(8,128)(2,1)} %param.12) | copy-start | bytes 6291460
  33.4 158.5 %all-gather.14.cloned.1.call-start = ((), (), s32[]{:S(2)}) async-start(), calls=%async_computation.16 | async-start | bytes 18874368 | tf_op jit(solution)/shard_map/all_gather | solution.py:246
  102.6 0.6 copy-start.16
  102.6 0.6 copy-start.11
  102.6 515.1 %copy-start.8 = (f32[2048,1]{0,1:T(1,128)}, f32[2048,1]{0,1:T(1,128)S(1)}, u32[]{:S(2)}) copy-start(f32[2048,1]{0,1:T(1,128)S(1)} %get-tuple-element.25) | copy-start | bytes 24580
  211.3 6.0 copy-start.24
  211.3 169.5 %all-to-all-start.1 = ((bf16[4,1024,768]{2,1,0:T(8,128)(2,1)}), bf16[4,1024,768]{2,1,0:T(8,128)(2,1)}, u32[]{:S(2)}, u32[]{:S(2)}) async-start(bf16[4,1024,768]{2,1,0:T(8,128)(2,1)} %bitcast.130), calls=%async_computation.1 | async-start | bytes 12582912 | tf_op jit(solution)/shard_map/all_to_all | solution.py:254
  216.7 223.8 %all-gather.16.cloned.1.call-start = ((), (), s32[]{:S(2)}) async-start(), calls=%async_computation.17 | async-start | bytes 2359296 | tf_op jit(solution)/shard_map/all_gather | solution.py:282
  433.4 54.8 %all-to-all-start.2 = ((bf16[4,1024,256]{2,1,0:T(8,128)(2,1)}), bf16[4,1024,256]{2,1,0:T(8,128)(2,1)}, u32[]{:S(2)}, u32[]{:S(2)}) async-start(bf16[4,1024,256]{2,1,0:T(8,128)(2,1)} %bitcast.135), calls=%async_computation.2 | async-start | bytes 4194304 | tf_op jit(solution)/shard_map/all_to_all | solution.py:254
  440.3 174.4 %reduce-scatter.13.cloned.1.call-start = ((), (), s32[]{:S(2)}) async-start(), calls=%async_computation.18 | async-start | bytes 18874368 | tf_op jit(solution)/shard_map/reduce_scatter | solution.py:250
  500.4 196.3 %all-gather.22.cloned.1.call-start = ((), (), s32[]{:S(2)}) async-start(), calls=%async_computation.21 | async-start | bytes 5242880 | tf_op jit(solution)/shard_map/all_gather | solution.py:291
  501.0 286.1 %all-gather.18.cloned.1.call-start = ((), (), s32[]{:S(2)}) async-start(), calls=%async_computation.19 | async-start | bytes 18874368 | tf_op jit(solution)/shard_map/all_gather | solution.py:246
  614.6 3.7 copy-start.3
  617.8 0.6 copy-start.13
  620.7 248.3 %all-gather.20.cloned.1.call-start = ((), (), s32[]{:S(2)}) async-start(), calls=%async_computation.20 | async-start | bytes 5242880 | tf_op jit(solution)/shard_map/all_gather | solution.py:290
  621.3 328.3 %all-gather.24.cloned.1.call-start = ((), (), s32[]{:S(2)}) async-start(), calls=%async_computation.22 | async-start | bytes 5242880 | tf_op jit(solution)/shard_map/all_gather | solution.py:292
  622.1 417.9 %all-gather.30.cloned.1.call-start = ((), (), s32[]{:S(2)}) async-start(), calls=%async_computation.33 | async-start | bytes 18874368 | tf_op jit(solution)/shard_map/all_gather | solution.py:246
  622.8 621.5 %reduce-scatter.17.cloned.1.call-start = ((), (), s32[]{:S(2)}) async-start(), calls=%async_computation.24 | async-start | bytes 18874368 | tf_op jit(solution)/shard_map/reduce_scatter | solution.py:250
  1076.0 25.6 %copy-start.25 = (bf16[2048,1024]{1,0:T(8,128)(2,1)S(1)}, bf16[2048,1024]{1,0:T(8,128)(2,1)}, u32[]{:S(2)}) copy-start(bf16[2048,1024]{1,0:T(8,128)(2,1)} %all-gather.22.cloned.1.call-done) | copy-start | bytes 12582916
  1128.2 116.2 %copy-start.1 = (bf16[1,512,2048]{2,1,0:T(8,128)(2,1)S(1)}, bf16[1,512,2048]{2,1,0:T(8,128)(2,1)}, u32[]{:S(2)}) copy-start(bf16[1,512,2048]{2,1,0:T(8,128)(2,1)} %param.12) | copy-start | bytes 6291460
  1128.2 116.2 %copy-start.9 = (f32[2048,1]{0,1:T(1,128)S(1)}, f32[2048,1]{0,1:T(1,128)}, u32[]{:S(2)}) copy-start(f32[2048,1]{0,1:T(1,128)} %copy-done.8) | copy-start | bytes 24580
  1128.2 116.2 %copy-start.14 = (f32[512]{0:T(512)S(1)}, f32[512]{0:T(512)}, u32[]{:S(2)}) copy-start(f32[512]{0:T(512)} %copy-done.13) | copy-start | bytes 6148
  1128.2 121.3 %copy-start.19 = (f32[512]{0:T(512)S(1)}, f32[512]{0:T(512)}, u32[]{:S(2)}) copy-start(f32[512]{0:T(512)} %get-tuple-element.29) | copy-start | bytes 6148
  1128.2 214.4 %all-gather.26.cloned.1.call-start = ((), (), s32[]{:S(2)}) async-start(), calls=%async_computation.25 | async-start | bytes 18874368 | tf_op jit(solution)/shard_map/all_gather | solution.py:246
  1244.3 5.2 copy-start.4
  1244.3 5.2 copy-start.5
  1244.3 5.1 copy-start.6
  1248.9 0.6 copy-start.21
  1488.5 143.0 %all-to-all-start.4 = ((bf16[4,1024,768]{2,1,0:T(8,128)(2,1)}), bf16[4,1024,768]{2,1,0:T(8,128)(2,1)}, u32[]{:S(2)}, u32[]{:S(2)}) async-start(bf16[4,1024,768]{2,1,0:T(8,128)(2,1)} %bitcast.131), calls=%async_computation.7 | async-start | bytes 12582912 | tf_op jit(solution)/shard_map/all_to_all | solution.py:254
  1493.8 287.0 %reduce-scatter.21.cloned.1.call-start = ((), (), s32[]{:S(2)}) async-start(), calls=%async_computation.27 | async-start | bytes 3932160 | tf_op jit(solution)/shard_map/reduce_scatter | solution.py:332
  1652.1 137.5 %reduce-scatter.29.cloned.1.call-start = ((), (), s32[]{:S(2)}) async-start(), calls=%async_computation.31 | async-start | bytes 5242880 | tf_op jit(solution)/shard_map/reduce_scatter | solution.py:307
  1676.4 192.9 %reduce-scatter.27.cloned.1.call-start = ((), (), s32[]{:S(2)}) async-start(), calls=%async_computation.30 | async-start | bytes 5242880 | tf_op jit(solution)/shard_map/reduce_scatter | solution.py:307
  1700.2 249.1 %reduce-scatter.25.cloned.1.call-start = ((), (), s32[]{:S(2)}) async-start(), calls=%async_computation.29 | async-start | bytes 5242880 | tf_op jit(solution)/shard_map/reduce_scatter | solution.py:307
  1724.2 297.9 %reduce-scatter.23.cloned.1.call-start = ((), (), s32[]{:S(2)}) async-start(), calls=%async_computation.28 | async-start | bytes 2359296 | tf_op jit(solution)/shard_map/reduce_scatter | solution.py:329
  1735.5 1.3 copy-start.7
  1736.9 404.0 %reduce-scatter.19.cloned.1.call-start = ((), (), s32[]{:S(2)}) async-start(), calls=%async_computation.26 | async-start | bytes 18874368 | tf_op jit(solution)/shard_map/reduce_scatter | solution.py:250
  1757.2 503.5 %reduce-scatter.15.cloned.1.call-start = ((), (), s32[]{:S(2)}) async-start(), calls=%async_computation.23 | async-start | bytes 18874368 | tf_op jit(solution)/shard_map/reduce_scatter | solution.py:250
  1780.8 243.1 %all-to-all-start.5 = ((bf16[8,64,768]{2,1,0:T(8,128)(2,1)}), bf16[8,64,768]{2,1,0:T(8,128)(2,1)S(1)}, u32[]{:S(2)}, u32[]{:S(2)}) async-start(bf16[8,64,768]{2,1,0:T(8,128)(2,1)} %bitcast.144), calls=%async_computation.10 | async-start | bytes 1572864 | tf_op jit(solution)/shard_map/all_to_all | solution.py:333
  1784.4 613.5 %reduce-scatter.31.cloned.1.call-start = ((), (), s32[]{:S(2)}) async-start(), calls=%async_computation.34 | async-start | bytes 1081344
  2025.7 115.2 %copy-start.2 = (bf16[1,512,2048]{2,1,0:T(8,128)(2,1)S(1)}, bf16[1,512,2048]{2,1,0:T(8,128)(2,1)}, u32[]{:S(2)}) copy-start(bf16[1,512,2048]{2,1,0:T(8,128)(2,1)} %param.12) | copy-start | bytes 6291460
  2025.7 115.2 %copy-start.12 = (f32[2048,1]{0,1:T(1,128)S(1)}, f32[2048,1]{0,1:T(1,128)}, u32[]{:S(2)}) copy-start(f32[2048,1]{0,1:T(1,128)} %copy-done.11) | copy-start | bytes 24580
  2025.7 115.2 %copy-start.17 = (f32[512]{0:T(512)S(1)}, f32[512]{0:T(512)}, u32[]{:S(2)}) copy-start(f32[512]{0:T(512)} %copy-done.16) | copy-start | bytes 6148
  2031.7 112.4 %copy-start.18 = (f32[2048]{0:T(1024)S(1)}, f32[2048]{0:T(1024)}, u32[]{:S(2)}) copy-start(f32[2048]{0:T(1024)} %get-tuple-element.11) | copy-start | bytes 24580
  2033.0 227.7 %copy-start.10 = (f32[2048,1]{0,1:T(1,128)S(1)}, f32[2048,1]{0,1:T(1,128)}, u32[]{:S(2)}) copy-start(f32[2048,1]{0,1:T(1,128)} %copy-done.8) | copy-start | bytes 24580
  2033.0 227.7 %copy-start.15 = (f32[512]{0:T(512)S(1)}, f32[512]{0:T(512)}, u32[]{:S(2)}) copy-start(f32[512]{0:T(512)} %copy-done.13) | copy-start | bytes 6148
  2033.0 227.7 %copy-start.20 = (f32[512]{0:T(512)S(1)}, f32[512]{0:T(512)}, u32[]{:S(2)}) copy-start(f32[512]{0:T(512)} %get-tuple-element.29) | copy-start | bytes 6148
  2033.0 227.7 %copy-start.22 = (f32[512]{0:T(512)S(1)}, f32[512]{0:T(512)}, u32[]{:S(2)}) copy-start(f32[512]{0:T(512)} %copy-done.21) | copy-start | bytes 6148
  2033.0 227.7 %copy-start.23 = (f32[512]{0:T(512)S(1)}, f32[512]{0:T(512)}, u32[]{:S(2)}) copy-start(f32[512]{0:T(512)} %get-tuple-element.27) | copy-start | bytes 6148
Sparse Core Ops, SparseCore 0:
  33.5 63.7 all-gather.27
  105.2 86.6 all-gather.13
  500.5 114.1 reduce-scatter.12
  616.1 80.5 all-gather.21
  699.0 88.0 all-gather.17
  788.5 80.5 all-gather.19
  870.6 78.9 all-gather.23
  951.5 88.3 all-gather.29
  1128.3 115.9 reduce-scatter.16
  1252.7 89.8 all-gather.25
  1652.2 58.3 reduce-scatter.20
  1712.8 76.7 reduce-scatter.28
  1792.0 77.2 reduce-scatter.26
  1872.0 77.2 reduce-scatter.24
  1953.7 68.3 reduce-scatter.22
  2025.9 114.9 reduce-scatter.18
  2144.7 115.9 reduce-scatter.14
  2262.9 134.9 reduce-scatter.30
Sparse Core Ops, SparseCore 1:
  219.3 88.7 all-gather.15

commit v2 on v1

--- a/solution.py
+++ b/solution.py
@@ -100,18 +100,23 @@
     return lax.dot_general(left, right, (((1,), (1,)), ((), ())), preferred_element_type=jnp.float32)
 
 
+def rows_of(ends, block):
+    z, x = block // 2, block % 2
+    return pl.ds(pl.multiple_of((4 * ((z + ends[8]) % 2) + 2 * (z // 2) + x) * TILE, TILE), TILE)
+
+
 def attend_kernel(ends, qkv, out, total):
     head, i = pl.program_id(0), pl.program_id(1)
     column = pl.multiple_of(head * HD, HD)
     width = qkv.shape[1] // 3
     first = i * TILE
-    query = qkv[pl.ds(pl.multiple_of(first, TILE), TILE), pl.ds(column, HD)]
+    query = qkv[rows_of(ends, i), pl.ds(column, HD)]
     total[...] = jnp.zeros_like(total)
     begin = jnp.minimum(doc_start(ends, first), first) // TILE
     latest = doc_start(ends, first + TILE - 1)
 
     def step(j, carry):
-        here = pl.ds(pl.multiple_of(j * TILE, TILE), TILE)
+        here = rows_of(ends, j)
         key = qkv[here, pl.ds(pl.multiple_of(column + width, HD), HD)]
         value = qkv[here, pl.ds(pl.multiple_of(column + 2 * width, HD), HD)]
         plain = (j < i) & (j * TILE >= latest)
@@ -132,7 +137,7 @@
         return carry
 
     lax.fori_loop(begin, i + 1, step, 0)
-    out[pl.ds(pl.multiple_of(first, TILE), TILE), pl.ds(column, HD)] = total[...].astype(LOW)
+    out[rows_of(ends, i), pl.ds(column, HD)] = total[...].astype(LOW)
 
 
 def attend_back_kernel(ends, qkv, grads, out, query_total, key_total, value_total):
@@ -140,7 +145,7 @@
     column = pl.multiple_of(head * HD, HD)
     width = qkv.shape[1] // 3
     first = j * TILE
-    here = pl.ds(pl.multiple_of(first, TILE), TILE)
+    here = rows_of(ends, j)
     key_column = pl.multiple_of(column + width, HD)
     value_column = pl.multiple_of(column + 2 * width, HD)
     key = qkv[here, pl.ds(key_column, HD)]
@@ -156,7 +161,8 @@
     end = pl.cdiv(doc_end(ends, first + TILE - 1), TILE)
 
     def step(i, carry):
-        there = pl.ds(pl.multiple_of(i * TILE, TILE), TILE)
+        there = rows_of(ends, i)
+        turned = pl.ds(pl.multiple_of(i * TILE, TILE), TILE)
         query = qkv[there, pl.ds(column, HD)]
         grad = grads[there, pl.ds(column, HD)]
         plain = (j < i) & (first >= doc_start(ends, i * TILE + TILE - 1))
@@ -165,7 +171,7 @@
             value_total[...] += jnp.dot(sig.astype(LOW), grad, preferred_element_type=jnp.float32)
             d_score = (dot_nt(value, grad) * (sig * (1.0 - sig))).astype(LOW)
             key_total[...] += jnp.dot(d_score, query, preferred_element_type=jnp.float32)
-            query_total[:, there] += jnp.dot(key_turned, d_score, preferred_element_type=jnp.float32)
+            query_total[:, turned] += jnp.dot(key_turned, d_score, preferred_element_type=jnp.float32)
 
         @pl.when(plain)
         def _():
@@ -188,7 +194,7 @@
     @pl.when(j == pl.num_programs(1) - 1)
     def _():
         for t in range(LEN // TILE):
-            out[t * TILE : (t + 1) * TILE, pl.ds(column, HD)] = (
+            out[rows_of(ends, t), pl.ds(column, HD)] = (
                 (query_total[:, t * TILE : (t + 1) * TILE] * scale).T.astype(LOW)
             )
 
@@ -250,8 +256,16 @@
     return lax.psum_scatter(whole.astype(LOW), LAYER, scatter_dimension=0, tiled=True).astype(jnp.float32)
 
 
-def swap_rows(part):
-    return lax.all_to_all(part.reshape(4, -1, part.shape[1]), "z", 0, 0).reshape(part.shape)
+def trade(part, back=False):
+    pairs = []
+    for y in range(2):
+        for c in range(2):
+            for z in range(4):
+                for x in range(2):
+                    owner = ((y * 2 + c) * 4 + z) * 2 + x
+                    worker = ((((z + c) % 2) * 2 + z // 2) * 4 + 2 * y + c) * 2 + x
+                    pairs.append((worker, owner) if back else (owner, worker))
+    return lax.ppermute(part, ALL, pairs)
 
 
 def dot_wide(left, right):
@@ -268,10 +282,9 @@
     owned = width // members
     gains = lax.all_gather(jnp.stack((gain_attn, gain_mlp), axis=1), ALL, axis=0, tiled=True)
     full_gain_attn, full_gain_mlp = gains[:, 0], gains[:, 1]
-    ends = jnp.cumsum(lax.all_gather(lengths, ("y", "c"), axis=0, tiled=True), axis=-1)
-    ends = lax.dynamic_slice_in_dim(ends, lax.axis_index("z"), 1, 0)[0]
-
-    flat = tokens.reshape(block, width).astype(jnp.float32)
+    parity = (lax.axis_index("z") % 2).astype(jnp.int32)
+    ends = jnp.concatenate((jnp.cumsum(trade(lengths)[0]), parity[None]))
+    flat = trade(tokens).reshape(block, width).astype(jnp.float32)
     normed_attn, inverse_attn = norm_forward(flat, full_gain_attn)
     layer_normed = gather_layer(normed_attn.astype(LOW))
     qkv_shards = jnp.stack((w_query, w_key, w_value), axis=1).reshape(shard, 3, members, owned)
@@ -282,15 +295,15 @@
     out_rows = lax.all_gather(w_out, ("z", "x"), axis=0, tiled=True)
     w_out_own = lax.dynamic_slice_in_dim(out_rows, lax.axis_index("x") * owned, owned, 0)
 
-    qkv = swap_rows(dot_wide(layer_normed, w_qkv).astype(LOW))
-    attended = swap_rows(attend(ends, qkv))
+    qkv = dot_wide(layer_normed, w_qkv).astype(LOW)
+    attended = attend(ends, qkv)
     resid = flat + scatter_layer(dot_wide(attended, w_out_own))
 
     normed_mlp, inverse_mlp = norm_forward(resid, full_gain_mlp)
     own_gate = lax.all_gather(w_gate, "z", axis=1, tiled=True)
     own_up = lax.all_gather(w_up, "z", axis=1, tiled=True)
     own_down = lax.all_gather(w_down, "z", axis=0, tiled=True)
-    upstream_low = cotangent.reshape(block, width)
+    upstream_low = trade(cotangent).reshape(block, width)
     upstream = upstream_low.astype(jnp.float32)
     layer_upstream = gather_layer(upstream_low)
     layer_mlp = gather_layer(normed_mlp.astype(LOW))
@@ -309,19 +322,20 @@
     grad_gate = scatter_layers(contract_rows(layer_mlp, d_gate), 1)
     grad_up = scatter_layers(contract_rows(layer_mlp, d_up), 1)
     grad_down = scatter_layers(contract_rows(hidden, layer_upstream), 0)
-    mixed = result.astype(LOW).reshape(rows_here, block, width)
+    mixed = trade(result.astype(LOW).reshape(rows_here, block, width), back=True)
 
     back_mlp, gain_mlp_term = norm_backward(resid, inverse_mlp, full_gain_mlp, d_normed_mlp)
     d_resid = upstream + back_mlp
     layer_d_resid = gather_layer(d_resid.astype(LOW))
-    d_attended = swap_rows(contract_cols(layer_d_resid, w_out_own).astype(LOW))
-    d_qkv = swap_rows(attend_back(ends, qkv, d_attended))
+    d_attended = contract_cols(layer_d_resid, w_out_own).astype(LOW)
+    d_qkv = attend_back(ends, qkv, d_attended)
     d_normed_attn = scatter_layer(contract_cols(d_qkv, w_qkv))
     out_term = contract_rows(attended, layer_d_resid)
     qkv_term = contract_rows(layer_normed, d_qkv)
 
     back_attn, gain_attn_term = norm_backward(flat, inverse_attn, full_gain_attn, d_normed_attn)
-    grad_tokens = (d_resid + back_attn).reshape(rows_here, block, width)
+    grad_tokens = (d_resid + back_attn).astype(LOW).reshape(rows_here, block, width)
+    grad_tokens = trade(grad_tokens, back=True).astype(jnp.float32)
 
     out_term = lax.dynamic_update_slice_in_dim(
         jnp.zeros((2 * owned, width), LOW), out_term.astype(LOW), lax.axis_index("x") * owned, 0

time: 2410 us -> 2300 us (0.954)
  waiting for transfers between devices: 1680 us -> 1450 us
  blocking collectives: 143 us -> 216 us
  starting transfers between devices: 22.7 us -> 65.5 us
    all_to_all x3 -> x0, waiting for transfers between devices: 322 us -> none  [swap_rows(): lax.all_to_all(part.reshape(4, -1, part.shape[1]), 'z', 0, 0)]
    all_gather x1, blocking collectives: 68 us -> 199 us  [body_layers(): lax.all_gather(jnp.stack((gain_attn, gain_mlp), axis=1), ALL, axis=0, til...]
    reduce_scatter x4, waiting for transfers between devices: 452 us -> 330 us  [scatter_layer(): lax.psum_scatter(whole.astype(LOW), LAYER, scatter_dimension=0, tiled=True)]
    reduce_scatter x3, waiting for transfers between devices: 159 us -> 260 us  [scatter_layers(): lax.psum_scatter(whole.astype(LOW), 'z', scatter_dimension=axis, tiled=True)]
    all_gather x1, waiting for transfers between devices: 73.4 us -> 149 us  [body_layers(): own_up = lax.all_gather(w_up, 'z', axis=1, tiled=True)]
    all_to_all x1 -> x0, blocking collectives: 53.1 us -> none  [swap_rows(): lax.all_to_all(part.reshape(4, -1, part.shape[1]), 'z', 0, 0)]
    reduce_scatter x1, waiting for transfers between devices: 0.02 us -> 47.1 us  [body_layers(): lax.psum_scatter(qkv_term.astype(LOW), 'z', scatter_dimension=0, tiled=True)]
    ppermute x0 -> x5, starting transfers between devices: none -> 39.6 us  [trade(): return lax.ppermute(part, ALL, pairs)]
  transfers between devices with their start and end apart: 23 -> 25, of which waited for: 19 -> 16; matrix products, arithmetic and copies ran while one was open for 10% -> 11% of each run, Pallas kernels for 2% -> 3%
where the time goes in v2:
time: 2300 us; the launch traced here: 2290 us
  waiting for transfers between devices  1450 us (63%)
  matrix products  327 us (14%)
  blocking collectives  216 us (9%)
  Pallas kernels  143 us (6%)
  starting transfers between devices  65.5 us (3%)
  other arithmetic  44.1 us (2%)
  local copies, waits for them, and re-layouts  28.9 us (1%)
    all_gather x4, waiting for transfers between devices, gather_layer(): return lax.all_gather(part, LAYER, axis=0, tiled=True)  351 us
    reduce_scatter x4, waiting for transfers between devices, scatter_layer(): lax.psum_scatter(whole.astype(LOW), LAYER, scatter_dimension=0, tiled=True)  330 us
    reduce_scatter x3, waiting for transfers between devices, scatter_layers(): lax.psum_scatter(whole.astype(LOW), 'z', scatter_dimension=axis, tiled=True)  260 us
    all_gather x1, blocking collectives, body_layers(): lax.all_gather(jnp.stack((gain_attn, gain_mlp), axis=1), ALL, axis=0, til...  199 us
    all_gather x1, waiting for transfers between devices, body_layers(): own_up = lax.all_gather(w_up, 'z', axis=1, tiled=True)  149 us
    unnamed x20, waiting for transfers between devices  131 us
    dot_general x5, matrix products, contract_cols(): lax.dot_general(left, right, (((1,), (1,)), ((), ())), preferred_element_...  119 us
    dot_general x5, matrix products, contract_rows(): lax.dot_general(left, right, (((0,), (0,)), ((), ())), preferred_element_...  105 us
  transfers between devices with their start and end apart: 25, of which 16 were waited for; matrix products, arithmetic and copies ran while one was open for 11% of the time, Pallas kernels for 3%

profile of v2, /device:TPU:0, one launch (start us, length us, event | category | flops | bytes accessed | tf_op | source)
XLA Modules:
  0.0 2292.5 jit_solution(12952796718217208759)
XLA Ops:
  7.2 1.0 copy.59
  8.6 1.0 copy.60
  10.1 1.0 copy.61
  11.5 1.8 maximum_bitcast_fusion
  14.3 17.1 all_to_all.10
  31.5 2.3 collective-permute-start
  33.8 198.9 %all-gather.2 = bf16[32,64,2]{1,2,0:T(2,128)(2,1)S(1)} all-gather(bf16[1,64,2]{1,2,0:T(2,128)(2,1)S(1)} %maximum_bitcast_fusion.1), channel_id=1, replica_groups=mesh['y'=2,'c'=2,'z'=4,'x'=2] {'y','c','z','x'}, dimensions={0}, use_global_device_ids=true | all-gather | bytes 8448 | tf_op jit(solution)/shard_map/all_gather | solution.py:283
  234.7 1.9 fusion.17
  238.5 4.4 copy.50
  242.8 79.6 %all-gather.13.cloned.1.call-done = bf16[4096,2048]{1,0:T(8,128)(2,1)} async-done(((bf16[512,2048]{1,0:T(8,128)(2,1)}), bf16[4096,2048]{1,0:T(8,128)(2,1)}) %all-gather.13.cloned.1.call-update) | async-done | bytes 16777232 | tf_op jit(solution)/shard_map/all_gather | solution.py:252
  322.5 19.5 convolution_convert_fusion.3.qkv
  341.9 58.7 %shard_map.203 = bf16[4096,256]{1,0:T(8,128)(2,1)} custom-call(s32[9]{0:T(128)} %pad_add_fusion.ends, bf16[4096,768]{1,0:T(8,128)(2,1)} %convolution_convert_fusion.3.qkv), custom_call_target="tpu_custom_call" | custom-call | flops 8589934592 | bytes 8388608 | tf_op jit(solution)/shard_map/pallas_call | solution.py:205
  400.6 12.2 convolution_convert_fusion.2
  413.5 115.5 %reduce-scatter.13.cloned.1.call-done = bf16[512,2048]{1,0:T(8,128)(2,1)} async-done(((bf16[4096,2048]{1,0:T(8,128)(2,1)}), bf16[512,2048]{1,0:T(8,128)(2,1)}) %reduce-scatter.13.cloned.1.call-update) | async-done | bytes 2097168 | tf_op jit(solution)/shard_map/reduce_scatter | solution.py:256
  528.9 2.5 multiply_reduce_fusion
  532.6 2.4 multiply_convert_fusion.3
  536.6 2.5 collective-permute-start.3
  539.1 1.3 copy-done.5
  540.5 148.7 %all-gather.21.cloned.1.call-done = bf16[2048,1024]{1,0:T(8,128)(2,1)} async-done(((bf16[2048,256]{1,0:T(8,128)(2,1)}), bf16[2048,1024]{1,0:T(8,128)(2,1)}) %all-gather.21.cloned.1.call-update) | async-done | bytes 4194320 | tf_op jit(solution)/shard_map/all_gather | solution.py:304
  689.2 90.6 %all-gather.17.cloned.1.call-done = bf16[4096,2048]{1,0:T(8,128)(2,1)} async-done(((bf16[512,2048]{1,0:T(8,128)(2,1)}), bf16[4096,2048]{1,0:T(8,128)(2,1)}) %all-gather.17.cloned.1.call-update) | async-done | bytes 16777232 | tf_op jit(solution)/shard_map/all_gather | solution.py:252
  779.7 23.6 %fusion.36 = f32[4096,1024]{1,0:T(8,128)} fusion(bf16[4096,2048]{1,0:T(8,128)(2,1)} %all-gather.17.cloned.1.call-done, bf16[2048,1024]{1,0:T(8,128)(2,1)} %all-gather.21.cloned.1.call-done), kind=kOutput, calls=%fused_computation.72 | convolution fusion | flops 17179869184 | bytes 37748736 | tf_op jit(solution)/shard_map/dot_general | solution.py:272
  803.3 58.6 %all-gather.19.cloned.1.call-done = bf16[2048,1024]{1,0:T(8,128)(2,1)} async-done(((bf16[2048,256]{1,0:T(8,128)(2,1)}), bf16[2048,1024]{1,0:T(8,128)(2,1)}) %all-gather.19.cloned.1.call-update) | async-done | bytes 4194320 | tf_op jit(solution)/shard_map/all_gather | solution.py:303
  861.9 23.4 %fusion.35 = f32[4096,1024]{1,0:T(8,128)} fusion(bf16[4096,2048]{1,0:T(8,128)(2,1)} %all-gather.17.cloned.1.call-done, bf16[2048,1024]{1,0:T(8,128)(2,1)} %all-gather.19.cloned.1.call-done), kind=kOutput, calls=%fused_computation.71 | convolution fusion | flops 17179869184 | bytes 37748736 | tf_op jit(solution)/shard_map/dot_general | solution.py:272
  885.3 57.2 %all-gather.23.cloned.1.call-done = bf16[1024,2048]{1,0:T(8,128)(2,1)} async-done(((bf16[256,2048]{1,0:T(8,128)(2,1)}), bf16[1024,2048]{1,0:T(8,128)(2,1)}) %all-gather.23.cloned.1.call-update) | async-done | bytes 4194320 | tf_op jit(solution)/shard_map/all_gather | solution.py:305
  942.4 90.9 %all-gather.29.cloned.1.call-done = bf16[1,4096,2048]{2,1,0:T(8,128)(2,1)} async-done(((bf16[1,512,2048]{2,1,0:T(8,128)(2,1)}), bf16[1,4096,2048]{2,1,0:T(8,128)(2,1)}) %all-gather.29.cloned.1.call-update) | async-done | bytes 16777232 | tf_op jit(solution)/shard_map/all_gather | solution.py:252
  1033.3 36.1 %multiply_convert_fusion = (bf16[4096,1024]{1,0:T(8,128)(2,1)}, bf16[4096,1024]{1,0:T(8,128)(2,1)}, bf16[4096,1024]{1,0:T(8,128)(2,1)}) fusion(f32[4096,1024]{1,0:T(8,128)} %fusion.35, f32[4096,1024]{1,0:T(8,128)} %fusion.36, bf16[1024,2048]{1,0:T(8,128)(2,1)} %all-gather.23.cloned.1.call-done, bf16[1,4096,2048]{2,1,0:T(8,128)(2,1)} %all-gather.29.cloned.1.call-done), kind=kOutput, calls=%fused_computation.5 | convolution fusion | flops 17246978048 | bytes 79691776 | tf_op jit(solution)/shard_map/dot_general | solution.py:26
  1069.4 25.6 %fusion.37 = f32[4096,2048]{1,0:T(8,128)} fusion(bf16[4096,1024]{1,0:T(8,128)(2,1)} %get-tuple-element.16, bf16[2048,1024]{1,0:T(8,128)(2,1)} %all-gather.19.cloned.1.call-done), kind=kOutput, calls=%fused_computation.73 | convolution fusion | flops 17179869184 | bytes 46137344 | tf_op jit(solution)/shard_map/dot_general | solution.py:26
  1095.0 26.6 %add_convert_fusion = bf16[4096,2048]{1,0:T(8,128)(2,1)} fusion(f32[4096,2048]{1,0:T(8,128)} %fusion.37, bf16[4096,1024]{1,0:T(8,128)(2,1)} %get-tuple-element.15, bf16[2048,1024]{1,0:T(8,128)(2,1)S(1)} %copy-done.25), kind=kOutput, calls=%fused_computation | convolution fusion | flops 17196646400 | bytes 62914560 | tf_op jit(solution)/shard_map/dot_general | solution.py:26
  1121.7 116.1 %reduce-scatter.17.cloned.1.call-done = bf16[512,2048]{1,0:T(8,128)(2,1)} async-done(((bf16[4096,2048]{1,0:T(8,128)(2,1)}), bf16[512,2048]{1,0:T(8,128)(2,1)}) %reduce-scatter.17.cloned.1.call-update) | async-done | bytes 2097168 | tf_op jit(solution)/shard_map/reduce_scatter | solution.py:256
  1237.8 4.5 fusion.14
  1242.9 3.3 fusion.32
  1246.2 90.0 %all-gather.25.cloned.1.call-done = bf16[4096,2048]{1,0:T(8,128)(2,1)} async-done(((bf16[512,2048]{1,0:T(8,128)(2,1)}), bf16[4096,2048]{1,0:T(8,128)(2,1)}) %all-gather.25.cloned.1.call-update) | async-done | bytes 16777232 | tf_op jit(solution)/shard_map/all_gather | solution.py:252
  1336.2 11.9 convolution_convert_fusion.4.grads
  1348.1 84.4 %shard_map.204 = bf16[4096,768]{1,0:T(8,128)(2,1)} custom-call(s32[9]{0:T(128)} %pad_add_fusion.ends, bf16[4096,768]{1,0:T(8,128)(2,1)} %convolution_convert_fusion.3.qkv, bf16[4096,256]{1,0:T(8,128)(2,1)} %convolution_convert_fusion.4.grads), custom_call_target="tpu_custom_call" | custom-call | flops 21474836480 | bytes 14680064 | tf_op jit(solution)/shard_map/pallas_call | solution.py:226
  1432.4 18.8 convolution_convert_fusion
  1451.4 24.3 %convolution_convert_fusion.1 = bf16[4096,2048]{1,0:T(8,128)(2,1)} fusion(bf16[4096,1024]{1,0:T(8,128)(2,1)} %get-tuple-element.17, bf16[1024,2048]{1,0:T(8,128)(2,1)} %all-gather.23.cloned.1.call-done), kind=kOutput, calls=%fused_computation.10 | convolution fusion | flops 17188257792 | bytes 29360128 | tf_op jit(solution)/shard_map/dot_general | solution.py:272
  1475.7 19.9 convolution_convert_fusion.7
  1495.6 1.8 copy.51
  1497.5 24.4 %fusion.22 = bf16[1024,2048]{1,0:T(8,128)(2,1)} fusion(bf16[4096,1024]{1,0:T(8,128)(2,1)} %get-tuple-element.17, bf16[1,4096,2048]{2,1,0:T(8,128)(2,1)} %all-gather.29.cloned.1.call-done), kind=kOutput, calls=%fused_computation.44 | convolution fusion | flops 17181966336 | bytes 29360128 | tf_op jit(solution)/shard_map/dot_general | solution.py:20
  1522.0 24.0 %convolution_convert_fusion.5 = bf16[2048,1024]{1,0:T(8,128)(2,1)} fusion(bf16[4096,2048]{1,0:T(8,128)(2,1)} %all-gather.17.cloned.1.call-done, bf16[4096,1024]{1,0:T(8,128)(2,1)} %get-tuple-element.15), kind=kOutput, calls=%fused_computation.45 | convolution fusion | flops 17181966336 | bytes 29360128 | tf_op jit(solution)/shard_map/dot_general | solution.py:20
  1546.1 24.0 %convolution_convert_fusion.6 = bf16[2048,1024]{1,0:T(8,128)(2,1)} fusion(bf16[4096,2048]{1,0:T(8,128)(2,1)} %all-gather.17.cloned.1.call-done, bf16[4096,1024]{1,0:T(8,128)(2,1)} %get-tuple-element.16), kind=kOutput, calls=%fused_computation.46 | convolution fusion | flops 17181966336 | bytes 29360128 | tf_op jit(solution)/shard_map/dot_general | solution.py:20
  1570.4 1.6 broadcast_in_dim.5
  1572.1 13.1 fusion.25
  1585.3 3.5 fusion.21
  1588.8 98.2 %reduce-scatter.15.cloned.1.call-done = bf16[512,2048]{1,0:T(8,128)(2,1)} async-done(((bf16[4096,2048]{1,0:T(8,128)(2,1)}), bf16[512,2048]{1,0:T(8,128)(2,1)}) %reduce-scatter.15.cloned.1.call-update) | async-done | bytes 2097168 | tf_op jit(solution)/shard_map/reduce_scatter | solution.py:256
  1687.0 7.5 fusion.27
  1694.5 17.1 collective-permute-start.4
  1711.6 17.1 collective-permute-start.2
  1728.7 47.1 %reduce-scatter.21.cloned.1.call-done = bf16[512,768]{1,0:T(8,128)(2,1)} async-done(((bf16[2048,768]{1,0:T(8,128)(2,1)}), bf16[512,768]{1,0:T(8,128)(2,1)}) %reduce-scatter.21.cloned.1.call-update) | async-done | bytes 786448 | tf_op jit(solution)/shard_map/reduce_scatter | solution.py:346
  1775.8 24.6 %all-to-all-start.1 = ((bf16[8,64,768]{2,1,0:T(8,128)(2,1)}), bf16[8,64,768]{2,1,0:T(8,128)(2,1)S(1)}, u32[]{:S(2)}, u32[]{:S(2)}) async-start(bf16[8,64,768]{2,1,0:T(8,128)(2,1)} %bitcast.124), calls=%async_computation.6 | async-start | bytes 1572864 | tf_op jit(solution)/shard_map/all_to_all | solution.py:347
  1800.5 100.6 %reduce-scatter.29.cloned.1.call-done = bf16[256,2048]{1,0:T(8,128)(2,1)} async-done(((bf16[1024,2048]{1,0:T(8,128)(2,1)}), bf16[256,2048]{1,0:T(8,128)(2,1)}) %reduce-scatter.29.cloned.1.call-update) | async-done | bytes 1048592 | tf_op jit(solution)/shard_map/reduce_scatter | solution.py:320
  1901.1 2.8 convert_element_type.173
  1903.9 81.9 %reduce-scatter.27.cloned.1.call-done = bf16[2048,256]{1,0:T(8,128)(2,1)} async-done(((bf16[2048,1024]{1,0:T(8,128)(2,1)}), bf16[2048,256]{1,0:T(8,128)(2,1)}) %reduce-scatter.27.cloned.1.call-update) | async-done | bytes 1048592 | tf_op jit(solution)/shard_map/reduce_scatter | solution.py:320
  1985.7 2.7 convert_element_type.171
  1988.4 77.3 %reduce-scatter.25.cloned.1.call-done = bf16[2048,256]{1,0:T(8,128)(2,1)} async-done(((bf16[2048,1024]{1,0:T(8,128)(2,1)}), bf16[2048,256]{1,0:T(8,128)(2,1)}) %reduce-scatter.25.cloned.1.call-update) | async-done | bytes 1048592 | tf_op jit(solution)/shard_map/reduce_scatter | solution.py:320
  2065.7 2.7 convert_element_type.169
  2068.4 69.4 %reduce-scatter.23.cloned.1.call-done = bf16[64,2048]{1,0:T(8,128)(2,1)} async-done(((bf16[512,2048]{1,0:T(8,128)(2,1)}), bf16[64,2048]{1,0:T(8,128)(2,1)}) %reduce-scatter.23.cloned.1.call-update) | async-done | bytes 262160 | tf_op jit(solution)/shard_map/reduce_scatter | solution.py:343
  2137.8 1.8 convert_element_type.167
  2140.5 1.3 copy.55
  2141.9 1.5 fusion.33
  2143.7 1.0 copy.64
  2147.2 128.9 %reduce-scatter.31.cloned.1.call-done = f32[64,2]{1,0:T(8,128)} async-done(((f32[2048,2]{1,0:T(8,128)}), f32[64,2]{1,0:T(8,128)}) %reduce-scatter.31.cloned.1.call-update) | async-done | bytes 528
  2278.2 4.1 convert_element_type.158
  2282.3 3.2 copy.67
  (130 shorter events, 16.7 us)
Async XLA Ops:
  7.2 231.3 %all-gather.27.cloned.1.call-start = ((), (), s32[]{:S(2)}) async-start(), calls=%async_computation.28 | async-start | bytes 3932160 | tf_op jit(solution)/shard_map/all_gather | solution.py:293
  10.1 23.7 %copy-start.26 = (bf16[64]{0:T(256)(128)(2,1)S(1)}, bf16[64]{0:T(256)(128)(2,1)}, u32[]{:S(2)}) copy-start(bf16[64]{0:T(256)(128)(2,1)} %param.23) | copy-start | bytes 388
  10.1 23.7 %copy-start.27 = (bf16[64]{0:T(256)(128)(2,1)S(1)}, bf16[64]{0:T(256)(128)(2,1)}, u32[]{:S(2)}) copy-start(bf16[64]{0:T(256)(128)(2,1)} %param.22) | copy-start | bytes 388
  31.4 291.0 %all-gather.13.cloned.1.call-start = ((), (), s32[]{:S(2)}) async-start(), calls=%async_computation.12 | async-start | bytes 18874368 | tf_op jit(solution)/shard_map/all_gather | solution.py:252
  31.5 201.3 %collective-permute-start = (bf16[1,512,2048]{2,1,0:T(8,128)(2,1)}, bf16[1,512,2048]{2,1,0:T(8,128)(2,1)S(1)}, u32[]{:S(2)}, u32[]{:S(2)}) collective-permute-start(bf16[1,512,2048]{2,1,0:T(8,128)(2,1)} %param.12), channel_id=1, source_target_pairs={{0,0},{1,1},{2,16},{3,17},{4,8},{5,9},{6,24},{7,25},{8,18},{9,19},... | collective-permute-start | bytes 6291464 | tf_op jit(solution)/shard_map/ppermute | solution.py:268
  232.8 1.3 copy-start.12
  232.8 299.2 %copy-start.9 = (f32[2048,1]{0,1:T(1,128)}, f32[2048,1]{0,1:T(1,128)S(1)}, u32[]{:S(2)}) copy-start(f32[2048,1]{0,1:T(1,128)S(1)} %get-tuple-element.25) | copy-start | bytes 24580
  232.8 3.8 copy-start.28
  232.8 299.2 %copy-start = (bf16[1,512,2048]{2,1,0:T(8,128)(2,1)}, bf16[1,512,2048]{2,1,0:T(8,128)(2,1)S(1)}, u32[]{:S(2)}) copy-start(bf16[1,512,2048]{2,1,0:T(8,128)(2,1)S(1)} %collective-permute-done) | copy-start | bytes 6291460
  234.1 0.6 copy-start.17
  236.6 164.1 %all-gather.15.cloned.1.call-start = ((), (), s32[]{:S(2)}) async-start(), calls=%async_computation.13 | async-start | bytes 2359296 | tf_op jit(solution)/shard_map/all_gather | solution.py:295
  236.6 1.1 collective-permute-start.1
  237.3 291.6 %reduce-scatter.13.cloned.1.call-start = ((), (), s32[]{:S(2)}) async-start(), calls=%async_computation.14 | async-start | bytes 18874368 | tf_op jit(solution)/shard_map/reduce_scatter | solution.py:256
  412.8 276.3 %all-gather.21.cloned.1.call-start = ((), (), s32[]{:S(2)}) async-start(), calls=%async_computation.17 | async-start | bytes 5242880 | tf_op jit(solution)/shard_map/all_gather | solution.py:304
  413.4 366.3 %all-gather.17.cloned.1.call-start = ((), (), s32[]{:S(2)}) async-start(), calls=%async_computation.15 | async-start | bytes 18874368 | tf_op jit(solution)/shard_map/all_gather | solution.py:252
  528.9 3.7 copy-start.3
  532.0 0.6 copy-start.14
  535.0 326.9 %all-gather.19.cloned.1.call-start = ((), (), s32[]{:S(2)}) async-start(), calls=%async_computation.16 | async-start | bytes 5242880 | tf_op jit(solution)/shard_map/all_gather | solution.py:303
  535.8 406.7 %all-gather.23.cloned.1.call-start = ((), (), s32[]{:S(2)}) async-start(), calls=%async_computation.18 | async-start | bytes 5242880 | tf_op jit(solution)/shard_map/all_gather | solution.py:305
  536.5 496.8 %all-gather.29.cloned.1.call-start = ((), (), s32[]{:S(2)}) async-start(), calls=%async_computation.29 | async-start | bytes 18874368 | tf_op jit(solution)/shard_map/all_gather | solution.py:252
  536.6 2.5 collective-permute-start.3
  539.1 1.3 copy-start.5
  540.4 697.4 %reduce-scatter.17.cloned.1.call-start = ((), (), s32[]{:S(2)}) async-start(), calls=%async_computation.20 | async-start | bytes 18874368 | tf_op jit(solution)/shard_map/reduce_scatter | solution.py:256
  1069.4 25.6 %copy-start.25 = (bf16[2048,1024]{1,0:T(8,128)(2,1)S(1)}, bf16[2048,1024]{1,0:T(8,128)(2,1)}, u32[]{:S(2)}) copy-start(bf16[2048,1024]{1,0:T(8,128)(2,1)} %all-gather.21.cloned.1.call-done) | copy-start | bytes 12582916
  1121.6 116.2 %copy-start.1 = (bf16[1,512,2048]{2,1,0:T(8,128)(2,1)S(1)}, bf16[1,512,2048]{2,1,0:T(8,128)(2,1)}, u32[]{:S(2)}) copy-start(bf16[1,512,2048]{2,1,0:T(8,128)(2,1)} %copy-done) | copy-start | bytes 6291460
  1121.6 116.2 %copy-start.10 = (f32[2048,1]{0,1:T(1,128)S(1)}, f32[2048,1]{0,1:T(1,128)}, u32[]{:S(2)}) copy-start(f32[2048,1]{0,1:T(1,128)} %copy-done.9) | copy-start | bytes 24580
  1121.6 116.2 %copy-start.15 = (f32[512]{0:T(512)S(1)}, f32[512]{0:T(512)}, u32[]{:S(2)}) copy-start(f32[512]{0:T(512)} %copy-done.14) | copy-start | bytes 6148
  1121.6 121.2 %copy-start.20 = (f32[512]{0:T(512)S(1)}, f32[512]{0:T(512)}, u32[]{:S(2)}) copy-start(f32[512]{0:T(512)} %get-tuple-element.29) | copy-start | bytes 6148
  1121.6 214.6 %all-gather.25.cloned.1.call-start = ((), (), s32[]{:S(2)}) async-start(), calls=%async_computation.21 | async-start | bytes 18874368 | tf_op jit(solution)/shard_map/all_gather | solution.py:252
  1237.8 5.1 copy-start.4
  1237.8 5.1 copy-start.6
  1237.8 5.1 copy-start.7
  1242.3 0.5 copy-start.22
  1246.2 339.0 %reduce-scatter.19.cloned.1.call-start = ((), (), s32[]{:S(2)}) async-start(), calls=%async_computation.22 | async-start | bytes 18874368 | tf_op jit(solution)/shard_map/reduce_scatter | solution.py:256
  1348.1 84.4 %copy-start.8 = (bf16[4,4,128,768]{3,2,1,0:T(8,128)(2,1)S(1)}, bf16[4,4,128,768]{3,2,1,0:T(8,128)(2,1)}, u32[]{:S(2)}) copy-start(bf16[4,4,128,768]{3,2,1,0:T(8,128)(2,1)} %copy.50) | copy-start | bytes 9437188
  1451.3 235.7 %reduce-scatter.15.cloned.1.call-start = ((), (), s32[]{:S(2)}) async-start(), calls=%async_computation.19 | async-start | bytes 18874368 | tf_op jit(solution)/shard_map/reduce_scatter | solution.py:256
  1475.6 300.2 %reduce-scatter.21.cloned.1.call-start = ((), (), s32[]{:S(2)}) async-start(), calls=%async_computation.23 | async-start | bytes 3932160 | tf_op jit(solution)/shard_map/reduce_scatter | solution.py:346
  1497.5 403.6 %reduce-scatter.29.cloned.1.call-start = ((), (), s32[]{:S(2)}) async-start(), calls=%async_computation.27 | async-start | bytes 5242880 | tf_op jit(solution)/shard_map/reduce_scatter | solution.py:320
  1521.9 463.8 %reduce-scatter.27.cloned.1.call-start = ((), (), s32[]{:S(2)}) async-start(), calls=%async_computation.26 | async-start | bytes 5242880 | tf_op jit(solution)/shard_map/reduce_scatter | solution.py:320
  1546.0 519.7 %reduce-scatter.25.cloned.1.call-start = ((), (), s32[]{:S(2)}) async-start(), calls=%async_computation.25 | async-start | bytes 5242880 | tf_op jit(solution)/shard_map/reduce_scatter | solution.py:320
  1570.1 567.7 %reduce-scatter.23.cloned.1.call-start = ((), (), s32[]{:S(2)}) async-start(), calls=%async_computation.24 | async-start | bytes 2359296 | tf_op jit(solution)/shard_map/reduce_scatter | solution.py:343
  1572.0 13.2 copy-start.2
  1572.0 13.2 copy-start.13
  1572.1 13.2 copy-start.18
  1585.1 101.9 %copy-start.11 = (f32[2048,1]{0,1:T(1,128)S(1)}, f32[2048,1]{0,1:T(1,128)}, u32[]{:S(2)}) copy-start(f32[2048,1]{0,1:T(1,128)} %copy-done.9) | copy-start | bytes 24580
  1585.1 101.9 %copy-start.16 = (f32[512]{0:T(512)S(1)}, f32[512]{0:T(512)}, u32[]{:S(2)}) copy-start(f32[512]{0:T(512)} %copy-done.14) | copy-start | bytes 6148
  1585.1 101.9 %copy-start.21 = (f32[512]{0:T(512)S(1)}, f32[512]{0:T(512)}, u32[]{:S(2)}) copy-start(f32[512]{0:T(512)} %get-tuple-element.29) | copy-start | bytes 6148
  1585.2 101.9 %copy-start.23 = (f32[512]{0:T(512)S(1)}, f32[512]{0:T(512)}, u32[]{:S(2)}) copy-start(f32[512]{0:T(512)} %copy-done.22) | copy-start | bytes 6148
  1585.2 101.9 %copy-start.24 = (f32[512]{0:T(512)S(1)}, f32[512]{0:T(512)}, u32[]{:S(2)}) copy-start(f32[512]{0:T(512)} %get-tuple-element.27) | copy-start | bytes 6148
  1694.5 583.7 %collective-permute-start.4 = (bf16[1,512,2048]{2,1,0:T(8,128)(2,1)}, bf16[1,512,2048]{2,1,0:T(8,128)(2,1)}, u32[]{:S(2)}, u32[]{:S(2)}) collective-permute-start(bf16[1,512,2048]{2,1,0:T(8,128)(2,1)} %get-tuple-element.18), channel_id=1, source_target_pairs={{0,0},{1,1},{16,2},{17,3},{8,4},{9,5},{24,6},{25,7},{18,8},{19,9},... | collective-permute-start | bytes 6291464 | tf_op jit(solution)/shard_map/ppermute | solution.py:268
  1711.6 570.7 %collective-permute-start.2 = (bf16[1,512,2048]{2,1,0:T(8,128)(2,1)}, bf16[1,512,2048]{2,1,0:T(8,128)(2,1)}, u32[]{:S(2)}, u32[]{:S(2)}) collective-permute-start(bf16[1,512,2048]{2,1,0:T(8,128)(2,1)} %get-tuple-element.19), channel_id=1, source_target_pairs={{0,0},{1,1},{16,2},{17,3},{8,4},{9,5},{24,6},{25,7},{18,8},{19,9},... | collective-permute-start | bytes 6291464 | tf_op jit(solution)/shard_map/ppermute | solution.py:268
  1775.8 363.8 %all-to-all-start.1 = ((bf16[8,64,768]{2,1,0:T(8,128)(2,1)}), bf16[8,64,768]{2,1,0:T(8,128)(2,1)S(1)}, u32[]{:S(2)}, u32[]{:S(2)}) async-start(bf16[8,64,768]{2,1,0:T(8,128)(2,1)} %bitcast.124), calls=%async_computation.6 | async-start | bytes 1572864 | tf_op jit(solution)/shard_map/all_to_all | solution.py:347
  1800.4 475.7 %reduce-scatter.31.cloned.1.call-start = ((), (), s32[]{:S(2)}) async-start(), calls=%async_computation.30 | async-start | bytes 1081344
  1988.4 152.0 %copy-start.19 = (f32[2048]{0:T(1024)S(1)}, f32[2048]{0:T(1024)}, u32[]{:S(2)}) copy-start(f32[2048]{0:T(1024)} %get-tuple-element.11) | copy-start | bytes 24580
Sparse Core Ops, SparseCore 0:
  31.6 127.8 all-gather.26
  236.7 85.7 all-gather.12
  324.6 49.2 all-gather.14
  412.9 115.9 reduce-scatter.12
  530.3 158.7 all-gather.20
  691.5 88.2 all-gather.16
  781.3 80.5 all-gather.18
  863.5 78.9 all-gather.22
  944.9 88.3 all-gather.28
  1121.7 115.9 reduce-scatter.16
  1246.3 89.8 all-gather.24
  1451.4 115.9 reduce-scatter.18
  1571.0 115.9 reduce-scatter.14
  1689.2 86.6 reduce-scatter.20
  1778.0 123.0 reduce-scatter.28
  1903.3 82.3 reduce-scatter.26
  1988.5 77.2 reduce-scatter.24
  2069.5 68.2 reduce-scatter.22
  2142.0 134.0 reduce-scatter.30

commit v3 on v2

--- a/solution.py
+++ b/solution.py
@@ -244,6 +244,601 @@
     )(ends, qkv, grads)
 
 
+def dot_wide(left, right):
+    return jnp.dot(left, right, preferred_element_type=jnp.float32)
+
+
+HALF = TILE // 2
+CHUNK = 32
+MESH_ID = pl.DeviceIdType.MESH
+
+
+def flip(bit, by):
+    return bit + by - 2 * bit * by
+
+
+def spot():
+    return tuple(lax.axis_index(name) for name in ("y", "c", "z", "x"))
+
+
+def near():
+    y, c, z, x = spot()
+    return (y, c, z, 1 - x), (1 - y, c, z, x), (y, 1 - c, z, x)
+
+
+def worker_of(y, c, z, x):
+    return lax.rem(z + c, 2), z // 2, 2 * y + c, x
+
+
+def owner_of(y, c, z, x):
+    row = lax.rem(z, 2)
+    return z // 2, row, 2 * c + lax.rem(y + row, 2), x
+
+
+def place_of(y, c, x, half=None):
+    first = (4 * y + 2 * c + x) * TILE
+    if half is None:
+        return pl.ds(pl.multiple_of(first, TILE), TILE)
+    return pl.ds(pl.multiple_of(first + half * HALF, HALF), HALF)
+
+
+def remote(src, dst, send, recv, peer):
+    return pltpu.make_async_remote_copy(
+        src_ref=src, dst_ref=dst, send_sem=send, recv_sem=recv, device_id=peer, device_id_type=MESH_ID
+    )
+
+
+def greet(peers):
+    barrier = pltpu.get_barrier_semaphore()
+    for peer in peers:
+        pl.semaphore_signal(barrier, inc=1, device_id=peer, device_id_type=MESH_ID)
+    pl.semaphore_wait(barrier, len(peers))
+
+
+class Gather:
+    def __init__(self, own, whole, send, recv):
+        y, c, z, x = spot()
+        across_x, across_y, core = near()
+
+        def from_own(k, half, peer):
+            return remote(own(half), whole.at[place_of(y, c, x, half)], send.at[k], recv.at[k], peer)
+
+        def passed(k, at, peer):
+            return remote(whole.at[at], whole.at[at], send.at[k], recv.at[k], peer)
+
+        self.mine = [
+            [from_own(0, 0, across_x), from_own(1, 0, across_y), from_own(2, 0, core)],
+            [from_own(3, 1, across_x), from_own(4, 1, across_y), from_own(5, 1, core)],
+        ]
+        held_x = [place_of(y, c, 1 - x, half) for half in (0, 1)]
+        held_y = [place_of(1 - y, c, x, half) for half in (0, 1)]
+        far = [place_of(1 - y, c, 1 - x, half) for half in (0, 1)]
+        self.over_y, self.over_x = passed(6, held_x[0], across_y), passed(7, held_y[1], across_x)
+        self.core_x = [passed(8 + half, held_x[half], core) for half in (0, 1)]
+        self.core_y = [passed(10 + half, held_y[half], core) for half in (0, 1)]
+        self.core_far = [passed(12 + half, far[half], core) for half in (0, 1)]
+
+    def start(self, half):
+        for copy in self.mine[half]:
+            copy.start()
+
+    def pass_first(self):
+        self.mine[0][0].wait_recv()
+        self.over_y.start()
+        self.core_x[0].start()
+        self.mine[0][1].wait_recv()
+        self.core_y[0].start()
+
+    def pass_second(self):
+        self.mine[1][1].wait_recv()
+        self.over_x.start()
+        self.core_y[1].start()
+        self.mine[1][0].wait_recv()
+        self.core_x[1].start()
+
+    def pass_far(self):
+        self.over_y.wait_recv()
+        self.core_far[0].start()
+        self.over_x.wait_recv()
+        self.core_far[1].start()
+
+    def finish(self):
+        from_core = [self.mine[0][2], self.mine[1][2]] + self.core_x + self.core_y + self.core_far
+        for copy in from_core:
+            copy.wait_recv()
+        for copy in self.mine[0] + self.mine[1] + [self.over_y, self.over_x] + self.core_x + self.core_y + self.core_far:
+            copy.wait_send()
+
+
+GATHER_COPIES = 14
+
+
+def run_gather(own, whole, send, recv, local):
+    y, c, z, x = spot()
+    keep = pltpu.make_async_copy(own, whole.at[place_of(y, c, x)], local)
+    keep.start()
+    gather = Gather(lambda half: own.at[pl.ds(half * HALF, HALF)], whole, send, recv)
+    gather.start(0)
+    gather.start(1)
+    gather.pass_first()
+    gather.pass_second()
+    gather.pass_far()
+    gather.finish()
+    keep.wait()
+
+
+def add_rows(total, first, term, start, count):
+    def step(i, carry):
+        here = pl.ds(pl.multiple_of(first + i * CHUNK, CHUNK), CHUNK)
+        there = pl.ds(pl.multiple_of(start + i * CHUNK, CHUNK), CHUNK)
+        total[here, :] = (total[here, :].astype(jnp.float32) + term[there, :].astype(jnp.float32)).astype(LOW)
+        return carry
+
+    lax.fori_loop(0, count // CHUNK, step, 0)
+
+
+def scatter_scratch(width):
+    return [
+        pltpu.VMEM((2, TILE, width), LOW),
+        pltpu.VMEM((4, TILE, width), LOW),
+        pltpu.VMEM((4, TILE, width), LOW),
+        pltpu.VMEM((2, HALF, width), LOW),
+        pltpu.VMEM((2, TILE, width), LOW),
+        pltpu.SemaphoreType.DMA((10,)),
+        pltpu.SemaphoreType.DMA((10,)),
+    ]
+
+
+def run_scatter(produce, staged, core_part, total, relayed, landed, send, recv):
+    y, c, z, x = spot()
+    across_x, across_y, core = near()
+    dests = ((1 - y, 1 - x), (y, 1 - x), (1 - y, x), (y, x))
+    first, second = pl.ds(0, HALF), pl.ds(HALF, HALF)
+    to_core = [
+        remote(staged.at[k % 2], core_part.at[k], send.at[k], recv.at[k], core) for k in range(4)
+    ]
+    far_x = remote(total.at[0, first], relayed.at[0], send.at[4], recv.at[4], across_x)
+    far_y = remote(total.at[0, second], relayed.at[1], send.at[5], recv.at[5], across_y)
+    to_x = [
+        remote(total.at[1, at], landed.at[0, at], send.at[6 + half], recv.at[6 + half], across_x)
+        for half, at in enumerate((first, second))
+    ]
+    to_y = [
+        remote(total.at[2, at], landed.at[1, at], send.at[8 + half], recv.at[8 + half], across_y)
+        for half, at in enumerate((first, second))
+    ]
+    for k, (to_row, to_column) in enumerate(dests):
+        if k >= 2:
+            to_core[k - 2].wait_send()
+        produce(2 * k, to_row, 1 - c, to_column, staged.at[k % 2])
+        to_core[k].start()
+        produce(2 * k + 1, to_row, c, to_column, total.at[k])
+        to_core[k].wait_recv()
+        add_rows(total.at[k], 0, core_part.at[k], 0, TILE)
+        if k == 0:
+            far_x.start()
+            far_y.start()
+        if k == 1:
+            to_x[0].start()
+        if k == 2:
+            to_y[1].start()
+    far_y.wait_recv()
+    add_rows(total.at[1], HALF, relayed.at[1], 0, HALF)
+    to_x[1].start()
+    far_x.wait_recv()
+    add_rows(total.at[2], 0, relayed.at[0], 0, HALF)
+    to_y[0].start()
+    for copy in to_x + to_y:
+        copy.wait_recv()
+    for copy in to_core[2:] + [far_x, far_y] + to_x + to_y:
+        copy.wait_send()
+
+
+def begin_kernel(x_own, w_query, w_key, w_value, x_whole, w_qkv, trade_send, trade_recv, gather_send, gather_recv, w_send, w_recv, up_send, up_recv, down_send, down_recv, local):
+    y, c, z, x = spot()
+    row = 2 * y + c
+    last = lax.axis_size("z") - 1
+    worker, owner = worker_of(y, c, z, x), owner_of(y, c, z, x)
+    moves = jnp.logical_not((worker[0] == y) & (worker[1] == c) & (worker[2] == z))
+    layer = [
+        (flip(y, dy), flip(c, dc), z, flip(x, dx)) for dy in (0, 1) for dc in (0, 1) for dx in (0, 1) if dy + dc + dx
+    ]
+    barrier = pltpu.get_barrier_semaphore()
+    for peer in layer:
+        pl.semaphore_signal(barrier, inc=1, device_id=peer, device_id_type=MESH_ID)
+
+    @pl.when(moves)
+    def _():
+        pl.semaphore_signal(barrier, inc=1, device_id=owner, device_id_type=MESH_ID)
+        pl.semaphore_signal(barrier, inc=1, device_id=worker, device_id_type=MESH_ID)
+
+    @pl.when(z > 0)
+    def _():
+        pl.semaphore_signal(barrier, inc=1, device_id=(y, c, z - 1, x), device_id_type=MESH_ID)
+
+    @pl.when(z < last)
+    def _():
+        pl.semaphore_signal(barrier, inc=1, device_id=(y, c, z + 1, x), device_id_type=MESH_ID)
+
+    pl.semaphore_wait(barrier, len(layer) + 2 * moves.astype(jnp.int32) + (z > 0).astype(jnp.int32) + (z < last).astype(jnp.int32))
+
+    shard, width = w_query.shape
+    owned = width // 8
+    trades = [
+        remote(
+            x_own.at[half],
+            x_whole.at[place_of(worker[0], worker[1], worker[3], half)],
+            trade_send.at[half],
+            trade_recv.at[half],
+            worker,
+        )
+        for half in (0, 1)
+    ]
+    keeps = [
+        pltpu.make_async_copy(x_own.at[half], x_whole.at[place_of(y, c, x, half)], trade_recv.at[half]) for half in (0, 1)
+    ]
+
+    @pl.when(moves)
+    def _():
+        for copy in trades:
+            copy.start()
+
+    @pl.when(jnp.logical_not(moves))
+    def _():
+        for copy in keeps:
+            copy.start()
+
+    spread, kept = [], []
+    for m, source in enumerate((w_query, w_key, w_value)):
+        dst = w_qkv.at[row, z, pl.ds(pl.multiple_of(x * shard, shard), shard), pl.ds(m * owned, owned)]
+        for k, peer in enumerate(layer):
+            columns = pl.ds(pl.multiple_of((4 * peer[0] + 2 * peer[1] + peer[3]) * owned, owned), owned)
+            spread.append(remote(source.at[:, columns], dst, w_send.at[m, k], w_recv.at[m, k], peer))
+        columns = pl.ds(pl.multiple_of((4 * y + 2 * c + x) * owned, owned), owned)
+        kept.append(pltpu.make_async_copy(source.at[:, columns], dst, local.at[m]))
+    for copy in spread + kept:
+        copy.start()
+
+    gather = Gather(lambda half: x_whole.at[place_of(y, c, x, half)], x_whole, gather_send, gather_recv)
+    for half in (0, 1):
+
+        @pl.when(moves)
+        def _():
+            trades[half].wait_recv()
+
+        @pl.when(jnp.logical_not(moves))
+        def _():
+            keeps[half].wait()
+
+        gather.start(half)
+
+    for copy in kept:
+        copy.wait()
+    for copy in spread:
+        copy.wait_recv()
+
+    def up(h):
+        slab = w_qkv.at[:, z - h]
+        return remote(slab, slab, up_send.at[h], up_recv.at[h], (y, c, z + 1, x))
+
+    def down(h):
+        slab = w_qkv.at[:, z + h]
+        return remote(slab, slab, down_send.at[h], down_recv.at[h], (y, c, z - 1, x))
+
+    def arrive(h):
+        @pl.when(z - h - 1 >= 0)
+        def _():
+            slab = w_qkv.at[:, z - h - 1]
+            remote(slab, slab, up_send.at[h], up_recv.at[h], (y, c, z, x)).wait_recv()
+            if h < 2:
+
+                @pl.when(z < last)
+                def _():
+                    up(h + 1).start()
+
+        @pl.when(z + h + 1 <= last)
+        def _():
+            slab = w_qkv.at[:, z + h + 1]
+            remote(slab, slab, down_send.at[h], down_recv.at[h], (y, c, z, x)).wait_recv()
+            if h < 2:
+
+                @pl.when(z > 0)
+                def _():
+                    down(h + 1).start()
+
+    @pl.when(z < last)
+    def _():
+        up(0).start()
+
+    @pl.when(z > 0)
+    def _():
+        down(0).start()
+
+    gather.pass_first()
+    arrive(0)
+    gather.pass_second()
+    arrive(1)
+    gather.pass_far()
+    arrive(2)
+    gather.finish()
+
+    @pl.when(moves)
+    def _():
+        for copy in trades:
+            copy.wait_send()
+
+    for copy in spread:
+        copy.wait_send()
+    for h in range(3):
+
+        @pl.when((z < last) & (z - h >= 0))
+        def _():
+            up(h).wait_send()
+
+        @pl.when((z > 0) & (z + h <= last))
+        def _():
+            down(h).wait_send()
+
+
+def anywhere():
+    return pl.BlockSpec(memory_space=pl.ANY)
+
+
+def in_vmem():
+    return pl.BlockSpec(memory_space=pltpu.VMEM)
+
+
+def dma(*shape):
+    return pltpu.SemaphoreType.DMA(shape)
+
+
+def remote_params(number):
+    return pltpu.CompilerParams(collective_id=number, has_side_effects=True, vmem_limit_bytes=VMEM_LIMIT)
+
+
+def begin(x_own, w_query, w_key, w_value):
+    block, width = x_own.shape
+    shard = w_query.shape[0]
+    x_whole, w_qkv = pl.pallas_call(
+        begin_kernel,
+        out_shape=(
+            jax.ShapeDtypeStruct((8 * block, width), LOW),
+            jax.ShapeDtypeStruct((4, 4, 2 * shard, 3 * width // 8), LOW),
+        ),
+        in_specs=[anywhere()] * 4,
+        out_specs=[anywhere()] * 2,
+        scratch_shapes=[
+            dma(2), dma(2), dma(GATHER_COPIES), dma(GATHER_COPIES), dma(3, 7), dma(3, 7), dma(3), dma(3), dma(3), dma(3), dma(3),
+        ],
+        compiler_params=remote_params(1),
+        cost_estimate=pl.CostEstimate(flops=0, bytes_accessed=300_000_000, transcendentals=0),
+    )(x_own.reshape(2, block // 2, width), w_query, w_key, w_value)
+    return x_whole, w_qkv.reshape(width, 3 * width // 8)
+
+
+def summed(total, landed, here):
+    parts = (total[3, here, :], landed[0, here, :], landed[1, here, :])
+    return sum(part.astype(jnp.float32) for part in parts)
+
+
+def over_chunks(work):
+    def step(i, carry):
+        work(pl.ds(pl.multiple_of(i * CHUNK, CHUNK), CHUNK))
+        return carry
+
+    lax.fori_loop(0, TILE // CHUNK, step, 0)
+
+
+def inverse_of(value):
+    return lax.rsqrt(jnp.mean(value * value, axis=-1, keepdims=True) + EPSILON)
+
+
+def close_attention_kernel(attended, w_out, x_own, gain, resid, normed, own, *scratch):
+    scatter, (send, recv, local) = scratch[:7], scratch[7:]
+    width = w_out.shape[1]
+    greet(near())
+
+    def produce(turn, y, c, x, out):
+        at = place_of(y, c, x)
+
+        def step(i, carry):
+            columns = pl.ds(pl.multiple_of(i * TILE, TILE), TILE)
+            out[:, columns] = dot_wide(attended[at, :], w_out[:, columns]).astype(LOW)
+            return carry
+
+        lax.fori_loop(0, width // TILE, step, 0)
+
+    run_scatter(produce, *scatter)
+    total, landed = scatter[2], scatter[4]
+
+    def chunk(here):
+        value = x_own[here, :].astype(jnp.float32) + summed(total, landed, here)
+        resid[here, :] = value
+        own[here, :] = (value * inverse_of(value) * gain[...]).astype(LOW)
+
+    over_chunks(chunk)
+    run_gather(own, normed, send, recv, local.at[0])
+
+
+def close_attention(attended, w_out, x_own, gain):
+    block, width = x_own.shape
+    return pl.pallas_call(
+        close_attention_kernel,
+        out_shape=(
+            jax.ShapeDtypeStruct((block, width), jnp.float32),
+            jax.ShapeDtypeStruct((8 * block, width), LOW),
+        ),
+        in_specs=[in_vmem()] * 4,
+        out_specs=[in_vmem(), anywhere()],
+        scratch_shapes=[pltpu.VMEM((block, width), LOW)]
+        + scatter_scratch(width)
+        + [dma(GATHER_COPIES), dma(GATHER_COPIES), dma(1)],
+        compiler_params=remote_params(2),
+        cost_estimate=pl.CostEstimate(flops=0, bytes_accessed=450_000_000, transcendentals=0),
+    )(attended, w_out, x_own, gain)
+
+
+def norm_back(value, gain, upstream):
+    inverse = inverse_of(value)
+    scaled = upstream * gain
+    inner = jnp.mean(scaled * value, axis=-1, keepdims=True)
+    return inverse * scaled - value * (inverse * inverse * inverse) * inner, upstream * value * inverse
+
+
+def fold_rows(total, terms):
+    for first in range(0, CHUNK, 8):
+        total[...] += terms[first : first + 8, :]
+
+
+def close_mlp_kernel(d_gate, d_up, w_gate, w_up, resid, upstream, gain, d_resid, gain_term, d_resid_whole, own, blocks, *scratch):
+    scatter, (send, recv, local, fetched) = scratch[:7], scratch[7:]
+    y, c, z, x = spot()
+    width = w_gate.shape[0]
+    order = [(r, k, q) for r, q in ((1 - y, 1 - x), (y, 1 - x), (1 - y, x), (y, x)) for k in (1 - c, c)]
+
+    def fetch(turn):
+        at = place_of(*order[turn])
+        slot = turn % 2
+        return [
+            pltpu.make_async_copy(source.at[at], blocks.at[slot, m], fetched.at[slot, m])
+            for m, source in enumerate((d_gate, d_up))
+        ]
+
+    for copy in fetch(0):
+        copy.start()
+    greet(near())
+
+    def produce(turn, to_y, to_c, to_x, out):
+        if turn < 7:
+            for copy in fetch(turn + 1):
+                copy.start()
+        for copy in fetch(turn):
+            copy.wait()
+
+        def step(i, carry):
+            columns = pl.ds(pl.multiple_of(i * TILE, TILE), TILE)
+            part = dot_nt(blocks[turn % 2, 0], w_gate[columns, :]) + dot_nt(blocks[turn % 2, 1], w_up[columns, :])
+            out[:, columns] = part.astype(LOW)
+            return carry
+
+        lax.fori_loop(0, width // TILE, step, 0)
+
+    run_scatter(produce, *scatter)
+    total, landed = scatter[2], scatter[4]
+    gain_term[...] = jnp.zeros_like(gain_term)
+
+    def chunk(here):
+        back, terms = norm_back(resid[here, :], gain[...], summed(total, landed, here))
+        value = upstream[here, :].astype(jnp.float32) + back
+        d_resid[here, :] = value
+        own[here, :] = value.astype(LOW)
+        fold_rows(gain_term, terms)
+
+    over_chunks(chunk)
+    run_gather(own, d_resid_whole, send, recv, local.at[0])
+
+
+def close_mlp(d_gate, d_up, w_gate, w_up, resid, upstream, gain):
+    block, width = resid.shape
+    hidden = d_gate.shape[1]
+    return pl.pallas_call(
+        close_mlp_kernel,
+        out_shape=(
+            jax.ShapeDtypeStruct((block, width), jnp.float32),
+            jax.ShapeDtypeStruct((8, width), jnp.float32),
+            jax.ShapeDtypeStruct((8 * block, width), LOW),
+        ),
+        in_specs=[anywhere()] * 2 + [in_vmem()] * 5,
+        out_specs=[in_vmem(), in_vmem(), anywhere()],
+        scratch_shapes=[pltpu.VMEM((block, width), LOW), pltpu.VMEM((2, 2, block, hidden), LOW)]
+        + scatter_scratch(width)
+        + [dma(GATHER_COPIES), dma(GATHER_COPIES), dma(1), dma(2, 2)],
+        compiler_params=remote_params(3),
+        cost_estimate=pl.CostEstimate(flops=0, bytes_accessed=450_000_000, transcendentals=0),
+    )(d_gate, d_up, w_gate, w_up, resid, upstream, gain)
+
+
+def close_layer_kernel(d_qkv, w_qkv, x_own, d_resid, gain, grad_low, gain_term, own, *scratch):
+    scatter, (send, recv) = scratch[:7], scratch[7:]
+    y, c, z, x = spot()
+    worker, owner = worker_of(y, c, z, x), owner_of(y, c, z, x)
+    moves = jnp.logical_not((worker[0] == y) & (worker[1] == c) & (worker[2] == z))
+    width = w_qkv.shape[0]
+    barrier = pltpu.get_barrier_semaphore()
+
+    @pl.when(moves)
+    def _():
+        pl.semaphore_signal(barrier, inc=1, device_id=owner, device_id_type=MESH_ID)
+        pl.semaphore_signal(barrier, inc=1, device_id=worker, device_id_type=MESH_ID)
+
+    for peer in near():
+        pl.semaphore_signal(barrier, inc=1, device_id=peer, device_id_type=MESH_ID)
+    pl.semaphore_wait(barrier, 3 + 2 * moves.astype(jnp.int32))
+
+    def produce(turn, to_y, to_c, to_x, out):
+        at = place_of(to_y, to_c, to_x)
+
+        def step(i, carry):
+            columns = pl.ds(pl.multiple_of(i * TILE, TILE), TILE)
+            out[:, columns] = dot_nt(d_qkv[at, :], w_qkv[columns, :]).astype(LOW)
+            return carry
+
+        lax.fori_loop(0, width // TILE, step, 0)
+
+    run_scatter(produce, *scatter)
+    total, landed = scatter[2], scatter[4]
+    gain_term[...] = jnp.zeros_like(gain_term)
+    trades = [
+        remote(own.at[pl.ds(half * HALF, HALF)], grad_low.at[pl.ds(half * HALF, HALF)], send.at[half], recv.at[half], owner)
+        for half in (0, 1)
+    ]
+    keeps = [
+        pltpu.make_async_copy(own.at[pl.ds(half * HALF, HALF)], grad_low.at[pl.ds(half * HALF, HALF)], recv.at[half])
+        for half in (0, 1)
+    ]
+    for half in (0, 1):
+
+        def step(i, carry):
+            here = pl.ds(pl.multiple_of(half * HALF + i * CHUNK, CHUNK), CHUNK)
+            back, terms = norm_back(x_own[here, :].astype(jnp.float32), gain[...], summed(total, landed, here))
+            own[here, :] = (d_resid[here, :] + back).astype(LOW)
+            fold_rows(gain_term, terms)
+            return carry
+
+        lax.fori_loop(0, HALF // CHUNK, step, 0)
+
+        @pl.when(moves)
+        def _():
+            trades[half].start()
+
+        @pl.when(jnp.logical_not(moves))
+        def _():
+            keeps[half].start()
+
+    @pl.when(moves)
+    def _():
+        for copy in trades:
+            copy.wait()
+
+    @pl.when(jnp.logical_not(moves))
+    def _():
+        for copy in keeps:
+            copy.wait()
+
+
+def close_layer(d_qkv, w_qkv, x_own, d_resid, gain):
+    block, width = x_own.shape
+    return pl.pallas_call(
+        close_layer_kernel,
+        out_shape=(jax.ShapeDtypeStruct((block, width), LOW), jax.ShapeDtypeStruct((8, width), jnp.float32)),
+        in_specs=[in_vmem()] * 5,
+        out_specs=[anywhere(), in_vmem()],
+        scratch_shapes=[pltpu.VMEM((block, width), LOW)] + scatter_scratch(width) + [dma(2), dma(2)],
+        compiler_params=remote_params(4),
+        cost_estimate=pl.CostEstimate(flops=0, bytes_accessed=350_000_000, transcendentals=0),
+    )(d_qkv, w_qkv, x_own, d_resid, gain)
+
+
 LAYER = ("y", "c", "x")
 ALL = ("y", "c", "z", "x")
 
@@ -268,10 +863,6 @@
     return lax.ppermute(part, ALL, pairs)
 
 
-def dot_wide(left, right):
-    return jnp.dot(left, right, preferred_element_type=jnp.float32)
-
-
 def body_layers(
     tokens, lengths, cotangent, w_query, w_key, w_value, w_out, w_gate, w_up, w_down, gain_attn, gain_mlp
 ):
@@ -280,41 +871,36 @@
     layers = lax.axis_size("z")
     shard = w_query.shape[0]
     owned = width // members
-    gains = lax.all_gather(jnp.stack((gain_attn, gain_mlp), axis=1), ALL, axis=0, tiled=True)
-    full_gain_attn, full_gain_mlp = gains[:, 0], gains[:, 1]
     parity = (lax.axis_index("z") % 2).astype(jnp.int32)
     ends = jnp.concatenate((jnp.cumsum(trade(lengths)[0]), parity[None]))
-    flat = trade(tokens).reshape(block, width).astype(jnp.float32)
-    normed_attn, inverse_attn = norm_forward(flat, full_gain_attn)
-    layer_normed = gather_layer(normed_attn.astype(LOW))
-    qkv_shards = jnp.stack((w_query, w_key, w_value), axis=1).reshape(shard, 3, members, owned)
-    qkv_shards = qkv_shards.transpose(2, 0, 1, 3).reshape(members, shard, 3 * owned)
-    qkv_shards = lax.all_to_all(qkv_shards, LAYER, 0, 0)
-    w_qkv = lax.all_gather(qkv_shards, "z", axis=0)
-    w_qkv = w_qkv.reshape(layers, 4, 2 * shard, 3 * owned).transpose(1, 0, 2, 3).reshape(width, 3 * owned)
+    layer_x, w_qkv = begin(tokens.reshape(block, width), w_query, w_key, w_value)
+    place = (4 * lax.axis_index("y") + 2 * lax.axis_index("c") + lax.axis_index("x")) * block
+    x_own = lax.dynamic_slice_in_dim(layer_x, place, block, 0)
+    full_gain_attn, full_gain_mlp = (
+        lax.all_gather(gain, ALL, axis=0, tiled=True).astype(jnp.float32)[None] for gain in (gain_attn, gain_mlp)
+    )
+    layer_normed = norm_forward(layer_x.astype(jnp.float32), full_gain_attn)[0].astype(LOW)
     out_rows = lax.all_gather(w_out, ("z", "x"), axis=0, tiled=True)
     w_out_own = lax.dynamic_slice_in_dim(out_rows, lax.axis_index("x") * owned, owned, 0)
 
     qkv = dot_wide(layer_normed, w_qkv).astype(LOW)
     attended = attend(ends, qkv)
-    resid = flat + scatter_layer(dot_wide(attended, w_out_own))
-
-    normed_mlp, inverse_mlp = norm_forward(resid, full_gain_mlp)
+    resid, layer_mlp = close_attention(attended, w_out_own, x_own, full_gain_mlp)
+
     own_gate = lax.all_gather(w_gate, "z", axis=1, tiled=True)
     own_up = lax.all_gather(w_up, "z", axis=1, tiled=True)
     own_down = lax.all_gather(w_down, "z", axis=0, tiled=True)
-    upstream_low = trade(cotangent).reshape(block, width)
-    upstream = upstream_low.astype(jnp.float32)
-    layer_upstream = gather_layer(upstream_low)
-    layer_mlp = gather_layer(normed_mlp.astype(LOW))
+    upstream = trade(cotangent).reshape(block, width)
+    layer_upstream = gather_layer(upstream)
     gate = dot_wide(layer_mlp, own_gate)
     up_part = dot_wide(layer_mlp, own_up)
     sigmoid_gate = jax.nn.sigmoid(gate)
     hidden = (gate * sigmoid_gate * up_part).astype(LOW)
     result = resid + scatter_layer(dot_wide(hidden, own_down))
+    mixed = trade(result.astype(LOW).reshape(rows_here, block, width), back=True)
     d_hidden = contract_cols(layer_upstream, own_down)
     d_gate, d_up = gate_backward(d_hidden, gate, up_part, sigmoid_gate)
-    d_normed_mlp = scatter_layer(contract_cols(d_gate, own_gate) + contract_cols(d_up, own_up))
+    d_resid, gain_mlp_term, layer_d_resid = close_mlp(d_gate, d_up, own_gate, own_up, resid, upstream, full_gain_mlp)
 
     def scatter_layers(whole, axis):
         return lax.psum_scatter(whole.astype(LOW), "z", scatter_dimension=axis, tiled=True).astype(jnp.float32)
@@ -322,21 +908,14 @@
     grad_gate = scatter_layers(contract_rows(layer_mlp, d_gate), 1)
     grad_up = scatter_layers(contract_rows(layer_mlp, d_up), 1)
     grad_down = scatter_layers(contract_rows(hidden, layer_upstream), 0)
-    mixed = trade(result.astype(LOW).reshape(rows_here, block, width), back=True)
-
-    back_mlp, gain_mlp_term = norm_backward(resid, inverse_mlp, full_gain_mlp, d_normed_mlp)
-    d_resid = upstream + back_mlp
-    layer_d_resid = gather_layer(d_resid.astype(LOW))
+
     d_attended = contract_cols(layer_d_resid, w_out_own).astype(LOW)
     d_qkv = attend_back(ends, qkv, d_attended)
-    d_normed_attn = scatter_layer(contract_cols(d_qkv, w_qkv))
+    grad_low, gain_attn_term = close_layer(d_qkv, w_qkv, x_own, d_resid, full_gain_attn)
+    grad_tokens = grad_low.astype(jnp.float32).reshape(rows_here, block, width)
+
     out_term = contract_rows(attended, layer_d_resid)
     qkv_term = contract_rows(layer_normed, d_qkv)
-
-    back_attn, gain_attn_term = norm_backward(flat, inverse_attn, full_gain_attn, d_normed_attn)
-    grad_tokens = (d_resid + back_attn).astype(LOW).reshape(rows_here, block, width)
-    grad_tokens = trade(grad_tokens, back=True).astype(jnp.float32)
-
     out_term = lax.dynamic_update_slice_in_dim(
         jnp.zeros((2 * owned, width), LOW), out_term.astype(LOW), lax.axis_index("x") * owned, 0
     )
@@ -347,8 +926,9 @@
     qkv_term = lax.all_to_all(qkv_term.reshape(members, shard, 3 * owned), LAYER, 0, 0)
     qkv_term = qkv_term.reshape(members, shard, 3, owned).transpose(2, 1, 0, 3).astype(jnp.float32)
     grad_query, grad_key, grad_value = qkv_term.reshape(3, shard, width)
-    gain_terms = lax.psum_scatter(
-        jnp.stack((gain_attn_term, gain_mlp_term), axis=1), ALL, scatter_dimension=0, tiled=True
+    grad_gain_attn, grad_gain_mlp = (
+        lax.psum_scatter(jnp.sum(term, axis=0), ALL, scatter_dimension=0, tiled=True)
+        for term in (gain_attn_term, gain_mlp_term)
     )
     return (
         mixed,
@@ -360,8 +940,8 @@
         grad_gate,
         grad_up,
         grad_down,
-        gain_terms[:, 0],
-        gain_terms[:, 1],
+        grad_gain_attn,
+        grad_gain_mlp,
     )
 
 

time: 2300 us -> 1650 us (0.72)
  waiting for transfers between devices: 1450 us -> 88.6 us
  Pallas kernels: 143 us -> 910 us
  blocking collectives: 216 us -> 316 us
  matrix products: 327 us -> 236 us
  starting transfers between devices: 65.5 us -> 24.8 us
    pallas_call x0 -> x4, Pallas kernels: none -> 772 us  [the longest x1 277 us: begin(): pl.pallas_call(begin_kernel, out_shape=(jax.ShapeDtypeStruct((8 * block,...]
    all_gather x4 -> x1, waiting for transfers between devices: 351 us -> 0.01 us  [gather_layer(): return lax.all_gather(part, LAYER, axis=0, tiled=True)]
    reduce_scatter x4 -> x1, waiting for transfers between devices: 330 us -> 0.02 us  [scatter_layer(): lax.psum_scatter(whole.astype(LOW), LAYER, scatter_dimension=0, tiled=True)]
    unnamed x0 -> x2, blocking collectives: none -> 316 us
    all_gather x1 -> x0, blocking collectives: 199 us -> none  [body_layers(): lax.all_gather(jnp.stack((gain_attn, gain_mlp), axis=1), ALL, axis=0, til...]
    reduce_scatter x3, waiting for transfers between devices: 260 us -> 85.9 us  [scatter_layers(): lax.psum_scatter(whole.astype(LOW), 'z', scatter_dimension=axis, tiled=True)]
    all_gather x1, waiting for transfers between devices: 149 us -> 0.01 us  [body_layers(): own_up = lax.all_gather(w_up, 'z', axis=1, tiled=True)]
    unnamed x20 -> x11, waiting for transfers between devices: 131 us -> 2.69 us
  transfers between devices with their start and end apart: 25 -> 15, of which waited for: 16 -> 2; matrix products, arithmetic and copies ran while one was open for 11% -> 14% of each run, Pallas kernels for 3% -> 55%
where the time goes in v3:
time: 1650 us; the launch traced here: 1640 us
  Pallas kernels  910 us (55%)
  blocking collectives  316 us (19%)
  matrix products  236 us (14%)
  waiting for transfers between devices  88.6 us (5%)
  other arithmetic  28.8 us (2%)
  starting transfers between devices  24.8 us (2%)
  local copies, waits for them, and re-layouts  22.4 us (1%)
    unnamed x2, blocking collectives  316 us
    pallas_call x1, Pallas kernels, begin(): pl.pallas_call(begin_kernel, out_shape=(jax.ShapeDtypeStruct((8 * block,...  277 us
    pallas_call x1, Pallas kernels, close_mlp(): pl.pallas_call(close_mlp_kernel, out_shape=(jax.ShapeDtypeStruct((block,...  235 us
    pallas_call x1, Pallas kernels, close_attention(): pl.pallas_call(close_attention_kernel, out_shape=(jax.ShapeDtypeStruct((b...  158 us
    pallas_call x1, Pallas kernels, close_layer(): pl.pallas_call(close_layer_kernel, out_shape=(jax.ShapeDtypeStruct((block...  103 us
    dot_general x5, matrix products, contract_rows(): lax.dot_general(left, right, (((0,), (0,)), ((), ())), preferred_element_...  100 us
    dot_general x4, matrix products, dot_wide(): return jnp.dot(left, right, preferred_element_type=jnp.float32)  89.7 us
    reduce_scatter x3, waiting for transfers between devices, scatter_layers(): lax.psum_scatter(whole.astype(LOW), 'z', scatter_dimension=axis, tiled=True)  85.9 us
  transfers between devices with their start and end apart: 15, of which 2 were waited for; matrix products, arithmetic and copies ran while one was open for 14% of the time, Pallas kernels for 55%

profile of v3, /device:TPU:0, one launch (start us, length us, event | category | flops | bytes accessed | tf_op | source)
XLA Modules:
  0.0 1640.4 jit_solution(9620715444483451830)
XLA Ops:
  7.2 0.7 all-gather.7.cloned.1.call-update
  8.0 0.7 all-gather.9.cloned.1.call-update
  8.7 0.7 all-gather.11.cloned.1.call-update
  9.4 0.5 all-gather.13.cloned.1.call-update
  10.0 2.2 collective-permute-start.2
  12.3 1.3 copy-done.1
  13.6 0.0 reduce-scatter.7.cloned.1.call-start
  13.7 1.3 collective-permute-start
  15.0 0.8 dynamic-update-slice
  15.8 0.8 dynamic-update-slice.1
  16.7 200.9 %all-reduce.5 = (bf16[2048]{0:T(1024)(128)(2,1)S(1)}, bf16[2048]{0:T(1024)(128)(2,1)S(1)}) all-reduce(bf16[2048]{0:T(1024)(128)(2,1)S(1)} %dynamic-update-slice, bf16[2048]{0:T(1024)(128)(2,1)S(1)} %dynamic-update-slice.1), channel_id=1, replica_groups=mesh['y'=2,'c'=2,'z'=4,'x'=2] {'y','c','z','x'}, use_global_device_ids=true, to_apply=%add | all-reduce | flops 4096 | bytes 16384
  217.6 0.6 broadcast_in_dim.20
  218.2 276.6 %shard_map.203 = (bf16[4096,2048]{1,0:T(8,128)(2,1)}, bf16[4,4,128,768]{3,2,1,0:T(8,128)(2,1)}) custom-call(bf16[2,256,2048]{2,1,0:T(8,128)(2,1)} %bitcast.61, bf16[64,2048]{1,0:T(8,128)(2,1)} %w_query.1, bf16[64,2048]{1,0:T(8,128)(2,1)} %w_key.1, bf16[64,2048]{1,0:T(8,128)(2,1)} %w_value.1), custom_call_target="tpu_custom_call" | custom-call | bytes 300000000 | tf_op jit(solution)/shard_map/pallas_call | solution.py:602
  494.8 7.4 fusion
  502.2 3.2 constant_dynamic-slice_fusion.x_own
  505.4 18.9 %convolution_convert_fusion.1.qkv = bf16[4096,768]{1,0:T(8,128)(2,1)} fusion(bf16[2048,768]{1,0:T(8,128)(2,1)S(1)} %bitcast.59, bf16[4096,2048]{1,0:T(8,128)(2,1)} %get-tuple-element.20, f32[2048]{0:T(1024)S(1)} %convert_element_type.81, f32[4096]{0:T(1024)S(1)} %add_rsqrt_fusion), kind=kOutput, calls=%fused_computation.14 | convolution fusion | flops 12921602048 | bytes 26238976 | tf_op jit(solution)/shard_map/dot_general | solution.py:248
  524.3 0.2 reduce-window.9
  524.5 0.6 pad_add_fusion.ends
  525.1 54.2 %shard_map.204.attended = bf16[4096,256]{1,0:T(8,128)(2,1)} custom-call(s32[9]{0:T(128)} %pad_add_fusion.ends, bf16[4096,768]{1,0:T(8,128)(2,1)} %convolution_convert_fusion.1.qkv), custom_call_target="tpu_custom_call" | custom-call | flops 8589934592 | bytes 8388608 | tf_op jit(solution)/shard_map/pallas_call | solution.py:205
  579.3 2.3 constant_dynamic-slice_fusion.1.w_out
  581.6 157.7 %shard_map.205 = (f32[512,2048]{1,0:T(8,128)}, bf16[4096,2048]{1,0:T(8,128)(2,1)}) custom-call(bf16[4096,256]{1,0:T(8,128)(2,1)} %shard_map.204.attended, bf16[256,2048]{1,0:T(8,128)(2,1)} %constant_dynamic-slice_fusion.1.w_out, bf16[512,2048]{1,0:T(8,128)(2,1)} %constant_dynamic-slice_fusion.x_own, f32[1,2048]{1,0:T(1,128)} %bitcast.69), custom_call_target="tpu_custom_call" | custom-call | bytes 450000000 | tf_op jit(solution)/shard_map/pallas_call | solution.py:665
  739.4 23.8 %fusion.19 = f32[4096,1024]{1,0:T(8,128)} fusion(bf16[4096,2048]{1,0:T(8,128)(2,1)} %get-tuple-element.23, bf16[2048,1024]{1,0:T(8,128)(2,1)} %all-gather.9.cloned.1.call-done.w_gate), kind=kOutput, calls=%fused_computation.31 | convolution fusion | flops 17179869184 | bytes 37748736 | tf_op jit(solution)/shard_map/dot_general | solution.py:248
  763.2 23.4 %fusion.20 = f32[4096,1024]{1,0:T(8,128)} fusion(bf16[4096,2048]{1,0:T(8,128)(2,1)} %get-tuple-element.23, bf16[2048,1024]{1,0:T(8,128)(2,1)} %all-gather.11.cloned.1.call-done.w_up), kind=kOutput, calls=%fused_computation.32 | convolution fusion | flops 17179869184 | bytes 37748736 | tf_op jit(solution)/shard_map/dot_general | solution.py:248
  786.6 36.1 %multiply_convert_fusion = (bf16[4096,1024]{1,0:T(8,128)(2,1)}, bf16[4096,1024]{1,0:T(8,128)(2,1)}, bf16[4096,1024]{1,0:T(8,128)(2,1)}) fusion(f32[4096,1024]{1,0:T(8,128)} %fusion.19, f32[4096,1024]{1,0:T(8,128)} %fusion.20, bf16[1024,2048]{1,0:T(8,128)(2,1)} %all-gather.13.cloned.1.call-done, bf16[1,4096,2048]{2,1,0:T(8,128)(2,1)} %all-gather.15.cloned.1.call-done), kind=kOutput, calls=%fused_computation.9 | convolution fusion | flops 17246978048 | bytes 79691776 | tf_op jit(solution)/shard_map/dot_general | solution.py:26
  822.7 23.6 %convolution_convert_fusion = bf16[4096,2048]{1,0:T(8,128)(2,1)} fusion(bf16[4096,1024]{1,0:T(8,128)(2,1)} %get-tuple-element.35, bf16[1024,2048]{1,0:T(8,128)(2,1)} %all-gather.13.cloned.1.call-done), kind=kOutput, calls=%fused_computation.13 | convolution fusion | flops 17188257792 | bytes 29360128 | tf_op jit(solution)/shard_map/dot_general | solution.py:248
  846.3 0.0 reduce-scatter.9.cloned.1.call-start
  846.4 235.0 %shard_map.206 = (f32[512,2048]{1,0:T(8,128)}, f32[8,2048]{1,0:T(8,128)}, bf16[4096,2048]{1,0:T(8,128)(2,1)}) custom-call(bf16[4096,1024]{1,0:T(8,128)(2,1)} %get-tuple-element.34.d_gate, bf16[4096,1024]{1,0:T(8,128)(2,1)} %get-tuple-element.33.d_up, bf16[2048,1024]{1,0:T(8,128)(2,1)} %all-gather.9.cloned.1.call-done.w_gate, ...), custom_call_target="tpu_custom_call" | custom-call | bytes 450000000 | tf_op jit(solution)/shard_map/pallas_call | solution.py:744
  1081.5 9.7 convolution_convert_fusion.2.grads
  1091.2 83.5 %shard_map.207.d_qkv = bf16[4096,768]{1,0:T(8,128)(2,1)} custom-call(s32[9]{0:T(128)} %pad_add_fusion.ends, bf16[4096,768]{1,0:T(8,128)(2,1)} %convolution_convert_fusion.1.qkv, bf16[4096,256]{1,0:T(8,128)(2,1)} %convolution_convert_fusion.2.grads), custom_call_target="tpu_custom_call" | custom-call | flops 21474836480 | bytes 14680064 | tf_op jit(solution)/shard_map/pallas_call | solution.py:226
  1174.6 19.7 %fusion.13 = bf16[2048,768]{1,0:T(8,128)(2,1)S(1)} fusion(bf16[4096,768]{1,0:T(8,128)(2,1)} %shard_map.207.d_qkv, bf16[4096,2048]{1,0:T(8,128)(2,1)} %get-tuple-element.20, f32[2048]{0:T(1024)S(1)} %copy-done.6, f32[4096]{0:T(1024)S(1)} %copy-done.8), kind=kOutput, calls=%fused_computation.21 | convolution fusion | flops 12920029184 | bytes 26238976 | tf_op jit(solution)/shard_map/dot_general | solution.py:20
  1194.3 1.9 copy.28
  1196.2 0.0 reduce-scatter.11.cloned.1.call-start
  1196.3 1.6 broadcast_in_dim.19
  1197.8 9.3 fusion.16
  1207.1 0.0 reduce-scatter.13.cloned.1.call-start
  1207.2 23.9 %convolution_convert_fusion.4 = bf16[2048,1024]{1,0:T(8,128)(2,1)} fusion(bf16[4096,2048]{1,0:T(8,128)(2,1)} %get-tuple-element.23, bf16[4096,1024]{1,0:T(8,128)(2,1)} %get-tuple-element.34.d_gate), kind=kOutput, calls=%fused_computation.20 | convolution fusion | flops 17181966336 | bytes 29360128 | tf_op jit(solution)/shard_map/dot_general | solution.py:20
  1231.1 0.0 reduce-scatter.15.cloned.1.call-start
  1231.1 23.8 %convolution_convert_fusion.3 = bf16[2048,1024]{1,0:T(8,128)(2,1)} fusion(bf16[4096,2048]{1,0:T(8,128)(2,1)} %get-tuple-element.23, bf16[4096,1024]{1,0:T(8,128)(2,1)} %get-tuple-element.33.d_up), kind=kOutput, calls=%fused_computation.19 | convolution fusion | flops 17181966336 | bytes 29360128 | tf_op jit(solution)/shard_map/dot_general | solution.py:20
  1254.9 0.0 reduce-scatter.17.cloned.1.call-start
  1254.9 23.9 %fusion.10 = bf16[1024,2048]{1,0:T(8,128)(2,1)} fusion(bf16[4096,1024]{1,0:T(8,128)(2,1)} %get-tuple-element.35, bf16[1,4096,2048]{2,1,0:T(8,128)(2,1)} %all-gather.15.cloned.1.call-done), kind=kOutput, calls=%fused_computation.18 | convolution fusion | flops 17181966336 | bytes 29360128 | tf_op jit(solution)/shard_map/dot_general | solution.py:20
  1278.9 5.0 fusion.17
  1283.8 17.1 %collective-permute-start.1 = (bf16[1,512,2048]{2,1,0:T(8,128)(2,1)}, bf16[1,512,2048]{2,1,0:T(8,128)(2,1)}, u32[]{:S(2)}, u32[]{:S(2)}) collective-permute-start(bf16[1,512,2048]{2,1,0:T(8,128)(2,1)} %fusion.17), channel_id=1, source_target_pairs={{0,0},{1,1},{16,2},{17,3},{8,4},{9,5},{24,6},{25,7},{18,8},{19,9},... | collective-permute-start | bytes 6291464 | tf_op jit(solution)/shard_map/ppermute | solution.py:863
  1300.9 3.7 all-to-all-start
  1304.6 102.9 %shard_map.208 = (bf16[512,2048]{1,0:T(8,128)(2,1)}, f32[8,2048]{1,0:T(8,128)}) custom-call(bf16[4096,768]{1,0:T(8,128)(2,1)} %shard_map.207.d_qkv, bf16[2048,768]{1,0:T(8,128)(2,1)} %bitcast.58, bf16[512,2048]{1,0:T(8,128)(2,1)} %constant_dynamic-slice_fusion.x_own, f32[512,2048]{1,0:T(8,128)} %get-tuple-element.25.d_resid, f32[1,2048]{1,0:T(1,128)} %bitcast.71), custom_call_target="tpu_custom_call" | custom-call | bytes 350000000 | tf_op jit(solution)/shard_map/pallas_call | solution.py:831
  1407.6 0.9 reduce_sum.28
  1408.5 114.7 %all-reduce.4 = (f32[2048]{0:T(1024)S(1)}, f32[2048]{0:T(1024)S(1)}) all-reduce(f32[2048]{0:T(1024)S(1)} %reduce_sum.28, f32[2048]{0:T(1024)S(1)} %reduce_sum.29), channel_id=9, replica_groups=mesh['y'=2,'c'=2,'z'=4,'x'=2] {'y','c','z','x'}, use_global_device_ids=true, to_apply=%region_9.10.clone | all-reduce | flops 4096 | bytes 32768
  1523.1 0.6 dynamic-slice
  1523.7 0.6 dynamic-slice.1
  1524.3 4.1 bitcast_convert_fusion
  1528.4 1.8 convert_element_type.99
  1530.2 0.9 reshape.101
  1531.1 1.5 fusion.18
  1532.6 0.3 copy.29
  1532.9 1.0 copy.32
  1533.8 0.3 copy.30
  1534.1 1.0 copy.33
  1535.1 0.3 copy.31
  1535.4 1.0 copy.34
  1536.4 2.7 convert_element_type.101
  1539.1 9.0 reduce-scatter.15.cloned.1.call-done
  1548.1 2.7 convert_element_type.103
  1550.8 76.8 %reduce-scatter.17.cloned.1.call-done = bf16[256,2048]{1,0:T(8,128)(2,1)} async-done(((bf16[1024,2048]{1,0:T(8,128)(2,1)}), bf16[256,2048]{1,0:T(8,128)(2,1)}) %reduce-scatter.17.cloned.1.call-update) | async-done | bytes 1048592 | tf_op jit(solution)/shard_map/reduce_scatter | solution.py:906
  1627.7 2.8 convert_element_type.105
  1630.5 3.2 copy.39
  (47 shorter events, 0.4 us)
Async XLA Ops:
  7.2 572.2 %all-gather.7.cloned.1.call-start = ((), (), s32[]{:S(2)}) async-start(), calls=%async_computation.7 | async-start | bytes 2359296 | tf_op jit(solution)/shard_map/all_gather | solution.py:883
  7.9 731.5 %all-gather.9.cloned.1.call-start = ((), (), s32[]{:S(2)}) async-start(), calls=%async_computation.8 | async-start | bytes 5242880 | tf_op jit(solution)/shard_map/all_gather | solution.py:890
  8.7 754.5 %all-gather.11.cloned.1.call-start = ((), (), s32[]{:S(2)}) async-start(), calls=%async_computation.9 | async-start | bytes 5242880 | tf_op jit(solution)/shard_map/all_gather | solution.py:891
  9.4 777.2 %all-gather.13.cloned.1.call-start = ((), (), s32[]{:S(2)}) async-start(), calls=%async_computation.10 | async-start | bytes 5242880 | tf_op jit(solution)/shard_map/all_gather | solution.py:892
  10.0 776.7 %all-gather.15.cloned.1.call-start = ((), (), s32[]{:S(2)}) async-start(), calls=%async_computation.17 | async-start | bytes 18874368 | tf_op jit(solution)/shard_map/all_gather | solution.py:847
  10.0 2.3 collective-permute-start.2
  12.3 1.3 copy-start.1
  13.6 1265.3 %reduce-scatter.7.cloned.1.call-start = ((), (), s32[]{:S(2)}) async-start(), calls=%async_computation.11 | async-start | bytes 18874368 | tf_op jit(solution)/shard_map/reduce_scatter | solution.py:851
  13.7 510.7 %collective-permute-start = (s32[1,8]{1,0:T(1,128)}, s32[1,8]{1,0:T(1,128)S(1)}, u32[]{:S(2)}, u32[]{:S(2)}) collective-permute-start(s32[1,8]{1,0:T(1,128)} %param.13), channel_id=1, source_target_pairs={{0,0},{1,1},{2,16},{3,17},{4,8},{5,9},{6,24},{7,25},{8,18},{9,19},... | collective-permute-start | bytes 104 | tf_op jit(solution)/shard_map/ppermute | solution.py:863
  217.6 287.8 %copy-start.5 = (f32[2048]{0:T(1024)}, f32[2048]{0:T(1024)S(1)}, u32[]{:S(2)}) copy-start(f32[2048]{0:T(1024)S(1)} %convert_element_type.81) | copy-start | bytes 24580
  494.8 10.6 copy-start.3
  502.2 22.1 %copy-start.7 = (f32[4096]{0:T(1024)}, f32[4096]{0:T(1024)S(1)}, u32[]{:S(2)}) copy-start(f32[4096]{0:T(1024)S(1)} %add_rsqrt_fusion) | copy-start | bytes 49156
  846.3 454.6 %reduce-scatter.9.cloned.1.call-start = ((), (), s32[]{:S(2)}) async-start(), calls=%async_computation.12 | async-start | bytes 3932160 | tf_op jit(solution)/shard_map/reduce_scatter | solution.py:925
  846.4 235.1 %copy-start.2 = (bf16[256,2048]{1,0:T(8,128)(2,1)S(1)}, bf16[256,2048]{1,0:T(8,128)(2,1)}, u32[]{:S(2)}) copy-start(bf16[256,2048]{1,0:T(8,128)(2,1)} %constant_dynamic-slice_fusion.1.w_out) | copy-start | bytes 3145732
  1091.2 83.5 %copy-start.6 = (f32[2048]{0:T(1024)S(1)}, f32[2048]{0:T(1024)}, u32[]{:S(2)}) copy-start(f32[2048]{0:T(1024)} %copy-done.5) | copy-start | bytes 24580
  1091.2 83.5 %copy-start.8 = (f32[4096]{0:T(1024)S(1)}, f32[4096]{0:T(1024)}, u32[]{:S(2)}) copy-start(f32[4096]{0:T(1024)} %copy-done.7) | copy-start | bytes 49156
  1194.3 3.6 copy-start
  1196.2 332.2 %reduce-scatter.11.cloned.1.call-start = ((), (), s32[]{:S(2)}) async-start(), calls=%async_computation.13 | async-start | bytes 2359296 | tf_op jit(solution)/shard_map/reduce_scatter | solution.py:922
  1207.1 329.2 %reduce-scatter.13.cloned.1.call-start = ((), (), s32[]{:S(2)}) async-start(), calls=%async_computation.14 | async-start | bytes 5242880 | tf_op jit(solution)/shard_map/reduce_scatter | solution.py:906
  1231.1 317.1 %reduce-scatter.15.cloned.1.call-start = ((), (), s32[]{:S(2)}) async-start(), calls=%async_computation.15 | async-start | bytes 5242880 | tf_op jit(solution)/shard_map/reduce_scatter | solution.py:906
  1254.9 372.8 %reduce-scatter.17.cloned.1.call-start = ((), (), s32[]{:S(2)}) async-start(), calls=%async_computation.16 | async-start | bytes 5242880 | tf_op jit(solution)/shard_map/reduce_scatter | solution.py:906
  1283.8 346.6 %collective-permute-start.1 = (bf16[1,512,2048]{2,1,0:T(8,128)(2,1)}, bf16[1,512,2048]{2,1,0:T(8,128)(2,1)}, u32[]{:S(2)}, u32[]{:S(2)}) collective-permute-start(bf16[1,512,2048]{2,1,0:T(8,128)(2,1)} %fusion.17), channel_id=1, source_target_pairs={{0,0},{1,1},{16,2},{17,3},{8,4},{9,5},{24,6},{25,7},{18,8},{19,9},... | collective-permute-start | bytes 6291464 | tf_op jit(solution)/shard_map/ppermute | solution.py:863
  1300.9 107.5 %copy-start.4 = (f32[8,2048]{1,0:T(8,128)S(1)}, f32[8,2048]{1,0:T(8,128)}, u32[]{:S(2)}) copy-start(f32[8,2048]{1,0:T(8,128)} %get-tuple-element.28) | copy-start | bytes 196612
  1300.9 229.3 %all-to-all-start = ((bf16[8,64,768]{2,1,0:T(8,128)(2,1)}), bf16[8,64,768]{2,1,0:T(8,128)(2,1)S(1)}, u32[]{:S(2)}, u32[]{:S(2)}) async-start(bf16[8,64,768]{2,1,0:T(8,128)(2,1)} %bitcast.65), calls=%async_computation.2 | async-start | bytes 1572864 | tf_op jit(solution)/shard_map/all_to_all | solution.py:926
Sparse Core Ops, SparseCore 0:
  10.1 101.2 all-gather.6
  113.0 89.2 all-gather.8
  203.9 160.4 all-gather.10
  365.8 110.9 all-gather.12
  479.2 88.2 all-gather.14
  846.5 188.3 reduce-scatter.6
  1196.3 63.0 reduce-scatter.8
  1263.6 92.2 reduce-scatter.10
  1358.2 89.6 reduce-scatter.12
  1450.1 97.9 reduce-scatter.14
  1550.4 77.1 reduce-scatter.16

commit v4 on v3

--- a/solution.py
+++ b/solution.py
@@ -353,18 +353,112 @@
 GATHER_COPIES = 14
 
 
-def run_gather(own, whole, send, recv, local):
+def run_gather(own, whole, send, recv, local, beside=lambda h: None):
     y, c, z, x = spot()
     keep = pltpu.make_async_copy(own, whole.at[place_of(y, c, x)], local)
     keep.start()
     gather = Gather(lambda half: own.at[pl.ds(half * HALF, HALF)], whole, send, recv)
     gather.start(0)
     gather.start(1)
+    beside(0)
     gather.pass_first()
     gather.pass_second()
+    beside(1)
     gather.pass_far()
     gather.finish()
+    beside(2)
     keep.wait()
+
+
+class Chain:
+    def __init__(self, own, slab, sems, index):
+        self.own, self.slab, self.sems, self.index = own, slab, sems, index
+        self.last = lax.axis_size("z") - 1
+
+    def move(self, which, h, source, layer, to):
+        y, c, z, x = spot()
+        return remote(
+            source, self.slab(layer), self.sems[2 * which].at[self.index, h], self.sems[2 * which + 1].at[self.index, h], (y, c, to, x)
+        )
+
+    def up(self, h):
+        z = lax.axis_index("z")
+        return self.move(0, h, self.own if h == 0 else self.slab(z - h), z - h, z + 1)
+
+    def down(self, h):
+        z = lax.axis_index("z")
+        return self.move(1, h, self.own if h == 0 else self.slab(z + h), z + h, z - 1)
+
+    def start(self):
+        z = lax.axis_index("z")
+
+        @pl.when(z < self.last)
+        def _():
+            self.up(0).start()
+
+        @pl.when(z > 0)
+        def _():
+            self.down(0).start()
+
+    def arrive(self, h):
+        z = lax.axis_index("z")
+
+        @pl.when(z - h - 1 >= 0)
+        def _():
+            self.move(0, h, self.slab(z - h - 1), z - h - 1, z).wait_recv()
+            if h < 2:
+
+                @pl.when(z < self.last)
+                def _():
+                    self.up(h + 1).start()
+
+        @pl.when(z + h + 1 <= self.last)
+        def _():
+            self.move(1, h, self.slab(z + h + 1), z + h + 1, z).wait_recv()
+            if h < 2:
+
+                @pl.when(z > 0)
+                def _():
+                    self.down(h + 1).start()
+
+    def finish(self):
+        z = lax.axis_index("z")
+        for h in range(3):
+
+            @pl.when((z < self.last) & (z - h >= 0))
+            def _():
+                self.up(h).wait_send()
+
+            @pl.when((z > 0) & (z + h <= self.last))
+            def _():
+                self.down(h).wait_send()
+
+
+def chain_sems(count):
+    return [pltpu.SemaphoreType.DMA((count, 3)) for _ in range(4)]
+
+
+def greet_neighbours(peers):
+    y, c, z, x = spot()
+    last = lax.axis_size("z") - 1
+    barrier = pltpu.get_barrier_semaphore()
+    for peer in peers:
+        pl.semaphore_signal(barrier, inc=1, device_id=peer, device_id_type=MESH_ID)
+
+    @pl.when(z > 0)
+    def _():
+        pl.semaphore_signal(barrier, inc=1, device_id=(y, c, z - 1, x), device_id_type=MESH_ID)
+
+    @pl.when(z < last)
+    def _():
+        pl.semaphore_signal(barrier, inc=1, device_id=(y, c, z + 1, x), device_id_type=MESH_ID)
+
+    return barrier, len(peers) + (z > 0).astype(jnp.int32) + (z < last).astype(jnp.int32)
+
+
+def others():
+    y, c, z, x = spot()
+    return [(flip(y, dy), flip(c, dc), z, flip(x, dx)) for dy in (0, 1) for dc in (0, 1) for dx in (0, 1) if dy + dc + dx]
 
 
 def add_rows(total, first, term, start, count):
@@ -434,33 +528,23 @@
         copy.wait_send()
 
 
-def begin_kernel(x_own, w_query, w_key, w_value, x_whole, w_qkv, trade_send, trade_recv, gather_send, gather_recv, w_send, w_recv, up_send, up_recv, down_send, down_recv, local):
+def begin_kernel(
+    x_own, w_query, w_key, w_value, facts, x_whole, w_qkv, facts_whole,
+    trade_send, trade_recv, gather_send, gather_recv, w_send, w_recv, fact_send, fact_recv, local, *sems
+):
     y, c, z, x = spot()
     row = 2 * y + c
-    last = lax.axis_size("z") - 1
     worker, owner = worker_of(y, c, z, x), owner_of(y, c, z, x)
     moves = jnp.logical_not((worker[0] == y) & (worker[1] == c) & (worker[2] == z))
-    layer = [
-        (flip(y, dy), flip(c, dc), z, flip(x, dx)) for dy in (0, 1) for dc in (0, 1) for dx in (0, 1) if dy + dc + dx
-    ]
-    barrier = pltpu.get_barrier_semaphore()
-    for peer in layer:
-        pl.semaphore_signal(barrier, inc=1, device_id=peer, device_id_type=MESH_ID)
+    layer = others()
+    barrier, count = greet_neighbours(layer)
 
     @pl.when(moves)
     def _():
         pl.semaphore_signal(barrier, inc=1, device_id=owner, device_id_type=MESH_ID)
         pl.semaphore_signal(barrier, inc=1, device_id=worker, device_id_type=MESH_ID)
 
-    @pl.when(z > 0)
-    def _():
-        pl.semaphore_signal(barrier, inc=1, device_id=(y, c, z - 1, x), device_id_type=MESH_ID)
-
-    @pl.when(z < last)
-    def _():
-        pl.semaphore_signal(barrier, inc=1, device_id=(y, c, z + 1, x), device_id_type=MESH_ID)
-
-    pl.semaphore_wait(barrier, len(layer) + 2 * moves.astype(jnp.int32) + (z > 0).astype(jnp.int32) + (z < last).astype(jnp.int32))
+    pl.semaphore_wait(barrier, count + 2 * moves.astype(jnp.int32))
 
     shard, width = w_query.shape
     owned = width // 8
@@ -488,7 +572,10 @@
         for copy in keeps:
             copy.start()
 
-    spread, kept = [], []
+    spread = [
+        remote(facts, facts_whole.at[row, z, x], fact_send.at[k], fact_recv.at[k], peer) for k, peer in enumerate(layer)
+    ]
+    kept = [pltpu.make_async_copy(facts, facts_whole.at[row, z, x], local.at[3])]
     for m, source in enumerate((w_query, w_key, w_value)):
         dst = w_qkv.at[row, z, pl.ds(pl.multiple_of(x * shard, shard), shard), pl.ds(m * owned, owned)]
         for k, peer in enumerate(layer):
@@ -516,44 +603,17 @@
         copy.wait()
     for copy in spread:
         copy.wait_recv()
-
-    def up(h):
-        slab = w_qkv.at[:, z - h]
-        return remote(slab, slab, up_send.at[h], up_recv.at[h], (y, c, z + 1, x))
-
-    def down(h):
-        slab = w_qkv.at[:, z + h]
-        return remote(slab, slab, down_send.at[h], down_recv.at[h], (y, c, z - 1, x))
+    chains = [
+        Chain(facts_whole.at[:, z], lambda at: facts_whole.at[:, at], sems, 0),
+        Chain(w_qkv.at[:, z], lambda at: w_qkv.at[:, at], sems, 1),
+    ]
 
     def arrive(h):
-        @pl.when(z - h - 1 >= 0)
-        def _():
-            slab = w_qkv.at[:, z - h - 1]
-            remote(slab, slab, up_send.at[h], up_recv.at[h], (y, c, z, x)).wait_recv()
-            if h < 2:
-
-                @pl.when(z < last)
-                def _():
-                    up(h + 1).start()
-
-        @pl.when(z + h + 1 <= last)
-        def _():
-            slab = w_qkv.at[:, z + h + 1]
-            remote(slab, slab, down_send.at[h], down_recv.at[h], (y, c, z, x)).wait_recv()
-            if h < 2:
-
-                @pl.when(z > 0)
-                def _():
-                    down(h + 1).start()
-
-    @pl.when(z < last)
-    def _():
-        up(0).start()
-
-    @pl.when(z > 0)
-    def _():
-        down(0).start()
-
+        for chain in chains:
+            chain.arrive(h)
+
+    for chain in chains:
+        chain.start()
     gather.pass_first()
     arrive(0)
     gather.pass_second()
@@ -569,15 +629,8 @@
 
     for copy in spread:
         copy.wait_send()
-    for h in range(3):
-
-        @pl.when((z < last) & (z - h >= 0))
-        def _():
-            up(h).wait_send()
-
-        @pl.when((z > 0) & (z + h <= last))
-        def _():
-            down(h).wait_send()
+    for chain in chains:
+        chain.finish()
 
 
 def anywhere():
@@ -596,24 +649,25 @@
     return pltpu.CompilerParams(collective_id=number, has_side_effects=True, vmem_limit_bytes=VMEM_LIMIT)
 
 
-def begin(x_own, w_query, w_key, w_value):
+def begin(x_own, w_query, w_key, w_value, facts):
     block, width = x_own.shape
     shard = w_query.shape[0]
-    x_whole, w_qkv = pl.pallas_call(
+    x_whole, w_qkv, facts_whole = pl.pallas_call(
         begin_kernel,
         out_shape=(
             jax.ShapeDtypeStruct((8 * block, width), LOW),
             jax.ShapeDtypeStruct((4, 4, 2 * shard, 3 * width // 8), LOW),
+            jax.ShapeDtypeStruct((4, 4, 2, *facts.shape), jnp.float32),
         ),
-        in_specs=[anywhere()] * 4,
-        out_specs=[anywhere()] * 2,
+        in_specs=[anywhere()] * 5,
+        out_specs=[anywhere()] * 3,
         scratch_shapes=[
-            dma(2), dma(2), dma(GATHER_COPIES), dma(GATHER_COPIES), dma(3, 7), dma(3, 7), dma(3), dma(3), dma(3), dma(3), dma(3),
+            dma(2), dma(2), dma(GATHER_COPIES), dma(GATHER_COPIES), dma(3, 7), dma(3, 7), dma(7), dma(7), dma(4), *chain_sems(2)
         ],
         compiler_params=remote_params(1),
-        cost_estimate=pl.CostEstimate(flops=0, bytes_accessed=300_000_000, transcendentals=0),
-    )(x_own.reshape(2, block // 2, width), w_query, w_key, w_value)
-    return x_whole, w_qkv.reshape(width, 3 * width // 8)
+        cost_estimate=pl.CostEstimate(flops=0, bytes_accessed=350_000_000, transcendentals=0),
+    )(x_own.reshape(2, block // 2, width), w_query, w_key, w_value, facts)
+    return x_whole, w_qkv.reshape(width, 3 * width // 8), facts_whole
 
 
 def summed(total, landed, here):
@@ -633,10 +687,27 @@
     return lax.rsqrt(jnp.mean(value * value, axis=-1, keepdims=True) + EPSILON)
 
 
-def close_attention_kernel(attended, w_out, x_own, gain, resid, normed, own, *scratch):
-    scatter, (send, recv, local) = scratch[:7], scratch[7:]
+def close_attention_kernel(attended, w_out, x_own, gain, w_gate, w_up, resid, normed, own_gate, own_up, own, *scratch):
+    scatter, (send, recv, local), sems = scratch[:7], scratch[7:10], scratch[10:]
     width = w_out.shape[1]
-    greet(near())
+    hidden = w_gate.shape[1]
+    z = lax.axis_index("z")
+    barrier, count = greet_neighbours(near())
+    pl.semaphore_wait(barrier, count)
+
+    def slab_of(whole):
+        return lambda at: whole.at[:, pl.ds(pl.multiple_of(at * hidden, hidden), hidden)]
+
+    chains, kept = [], []
+    for k, (part, whole) in enumerate(((w_gate, own_gate), (w_up, own_up))):
+        chains.append(Chain(part, slab_of(whole), sems, k))
+        chains[k].start()
+        kept.append(pltpu.make_async_copy(part, slab_of(whole)(z), local.at[1 + k]))
+        kept[k].start()
+
+    def arrive(h):
+        for chain in chains:
+            chain.arrive(h)
 
     def produce(turn, y, c, x, out):
         at = place_of(y, c, x)
@@ -657,25 +728,32 @@
         own[here, :] = (value * inverse_of(value) * gain[...]).astype(LOW)
 
     over_chunks(chunk)
-    run_gather(own, normed, send, recv, local.at[0])
-
-
-def close_attention(attended, w_out, x_own, gain):
+    run_gather(own, normed, send, recv, local.at[0], arrive)
+    for chain in chains:
+        chain.finish()
+    for copy in kept:
+        copy.wait()
+
+
+def close_attention(attended, w_out, x_own, gain, w_gate, w_up):
     block, width = x_own.shape
+    hidden = w_gate.shape[1]
     return pl.pallas_call(
         close_attention_kernel,
         out_shape=(
             jax.ShapeDtypeStruct((block, width), jnp.float32),
             jax.ShapeDtypeStruct((8 * block, width), LOW),
+            jax.ShapeDtypeStruct((width, 4 * hidden), LOW),
+            jax.ShapeDtypeStruct((width, 4 * hidden), LOW),
         ),
-        in_specs=[in_vmem()] * 4,
-        out_specs=[in_vmem(), anywhere()],
+        in_specs=[in_vmem()] * 4 + [anywhere()] * 2,
+        out_specs=[in_vmem()] + [anywhere()] * 3,
         scratch_shapes=[pltpu.VMEM((block, width), LOW)]
         + scatter_scratch(width)
-        + [dma(GATHER_COPIES), dma(GATHER_COPIES), dma(1)],
+        + [dma(GATHER_COPIES), dma(GATHER_COPIES), dma(3), *chain_sems(2)],
         compiler_params=remote_params(2),
         cost_estimate=pl.CostEstimate(flops=0, bytes_accessed=450_000_000, transcendentals=0),
-    )(attended, w_out, x_own, gain)
+    )(attended, w_out, x_own, gain, w_gate, w_up)
 
 
 def norm_back(value, gain, upstream):
@@ -758,8 +836,8 @@
     )(d_gate, d_up, w_gate, w_up, resid, upstream, gain)
 
 
-def close_layer_kernel(d_qkv, w_qkv, x_own, d_resid, gain, grad_low, gain_term, own, *scratch):
-    scatter, (send, recv) = scratch[:7], scratch[7:]
+def close_layer_kernel(d_qkv, w_qkv, x_own, d_resid, gain, mlp_term, grad_low, gain_grads, own, terms, layer_terms, part, column_terms, *scratch):
+    scatter, (send, recv, term_send, term_recv, line_send, line_recv) = scratch[:7], scratch[7:]
     y, c, z, x = spot()
     worker, owner = worker_of(y, c, z, x), owner_of(y, c, z, x)
     moves = jnp.logical_not((worker[0] == y) & (worker[1] == c) & (worker[2] == z))
@@ -771,9 +849,11 @@
         pl.semaphore_signal(barrier, inc=1, device_id=owner, device_id_type=MESH_ID)
         pl.semaphore_signal(barrier, inc=1, device_id=worker, device_id_type=MESH_ID)
 
-    for peer in near():
+    layer = others()
+    line = [(y, c, lax.rem(z + dz, 4), x) for dz in (1, 2, 3)]
+    for peer in layer + line:
         pl.semaphore_signal(barrier, inc=1, device_id=peer, device_id_type=MESH_ID)
-    pl.semaphore_wait(barrier, 3 + 2 * moves.astype(jnp.int32))
+    pl.semaphore_wait(barrier, len(layer + line) + 2 * moves.astype(jnp.int32))
 
     def produce(turn, to_y, to_c, to_x, out):
         at = place_of(to_y, to_c, to_x)
@@ -787,7 +867,8 @@
 
     run_scatter(produce, *scatter)
     total, landed = scatter[2], scatter[4]
-    gain_term[...] = jnp.zeros_like(gain_term)
+    terms[1] = mlp_term[...]
+    terms[0] = jnp.zeros_like(mlp_term)
     trades = [
         remote(own.at[pl.ds(half * HALF, HALF)], grad_low.at[pl.ds(half * HALF, HALF)], send.at[half], recv.at[half], owner)
         for half in (0, 1)
@@ -800,9 +881,9 @@
 
         def step(i, carry):
             here = pl.ds(pl.multiple_of(half * HALF + i * CHUNK, CHUNK), CHUNK)
-            back, terms = norm_back(x_own[here, :].astype(jnp.float32), gain[...], summed(total, landed, here))
+            back, products = norm_back(x_own[here, :].astype(jnp.float32), gain[...], summed(total, landed, here))
             own[here, :] = (d_resid[here, :] + back).astype(LOW)
-            fold_rows(gain_term, terms)
+            fold_rows(terms.at[0], products)
             return carry
 
         lax.fori_loop(0, HALF // CHUNK, step, 0)
@@ -814,6 +895,32 @@
         @pl.when(jnp.logical_not(moves))
         def _():
             keeps[half].start()
+
+    def columns_of(row, layers):
+        return pl.ds(pl.multiple_of((4 * row) * HD, HD), layers * HD)
+
+    spread = [
+        remote(terms.at[:, :, columns_of(2 * peer[0] + peer[1], 4)], layer_terms.at[k], term_send.at[k], term_recv.at[k], peer)
+        for k, peer in enumerate(layer)
+    ]
+    for copy in spread:
+        copy.start()
+    for copy in spread:
+        copy.wait_recv()
+    part[...] = sum((layer_terms[k] for k in range(7)), terms[:, :, columns_of(2 * y + c, 4)])
+    lines = [
+        remote(
+            part.at[:, :, pl.ds(pl.multiple_of(peer[2] * HD, HD), HD)], column_terms.at[k], line_send.at[k], line_recv.at[k], peer
+        )
+        for k, peer in enumerate(line)
+    ]
+    for copy in lines:
+        copy.start()
+    for copy in lines:
+        copy.wait_recv()
+    gain_grads[...] = sum((column_terms[k] for k in range(3)), part[:, :, pl.ds(pl.multiple_of(z * HD, HD), HD)])
+    for copy in spread + lines:
+        copy.wait_send()
 
     @pl.when(moves)
     def _():
@@ -826,17 +933,25 @@
             copy.wait()
 
 
-def close_layer(d_qkv, w_qkv, x_own, d_resid, gain):
+def close_layer(d_qkv, w_qkv, x_own, d_resid, gain, mlp_term):
     block, width = x_own.shape
     return pl.pallas_call(
         close_layer_kernel,
-        out_shape=(jax.ShapeDtypeStruct((block, width), LOW), jax.ShapeDtypeStruct((8, width), jnp.float32)),
-        in_specs=[in_vmem()] * 5,
+        out_shape=(jax.ShapeDtypeStruct((block, width), LOW), jax.ShapeDtypeStruct((2, 8, width // 16), jnp.float32)),
+        in_specs=[in_vmem()] * 6,
         out_specs=[anywhere(), in_vmem()],
-        scratch_shapes=[pltpu.VMEM((block, width), LOW)] + scatter_scratch(width) + [dma(2), dma(2)],
+        scratch_shapes=[
+            pltpu.VMEM((block, width), LOW),
+            pltpu.VMEM((2, 8, width), jnp.float32),
+            pltpu.VMEM((7, 2, 8, width // 4), jnp.float32),
+            pltpu.VMEM((2, 8, width // 4), jnp.float32),
+            pltpu.VMEM((3, 2, 8, width // 16), jnp.float32),
+        ]
+        + scatter_scratch(width)
+        + [dma(2), dma(2), dma(7), dma(7), dma(3), dma(3)],
         compiler_params=remote_params(4),
         cost_estimate=pl.CostEstimate(flops=0, bytes_accessed=350_000_000, transcendentals=0),
-    )(d_qkv, w_qkv, x_own, d_resid, gain)
+    )(d_qkv, w_qkv, x_own, d_resid, gain, mlp_term)
 
 
 LAYER = ("y", "c", "x")
@@ -863,6 +978,10 @@
     return lax.ppermute(part, ALL, pairs)
 
 
+def after(first, then):
+    return lax.optimization_barrier((first, then))[1]
+
+
 def body_layers(
     tokens, lengths, cotangent, w_query, w_key, w_value, w_out, w_gate, w_up, w_down, gain_attn, gain_mlp
 ):
@@ -871,65 +990,66 @@
     layers = lax.axis_size("z")
     shard = w_query.shape[0]
     owned = width // members
-    parity = (lax.axis_index("z") % 2).astype(jnp.int32)
-    ends = jnp.concatenate((jnp.cumsum(trade(lengths)[0]), parity[None]))
-    layer_x, w_qkv = begin(tokens.reshape(block, width), w_query, w_key, w_value)
+    facts = jnp.zeros((8, 2 * shard), jnp.float32)
+    facts = facts.at[0, :shard].set(gain_attn.astype(jnp.float32)).at[1, :shard].set(gain_mlp.astype(jnp.float32))
+    facts = facts.at[2, : lengths.shape[1]].set(lengths[0].astype(jnp.float32))
+    layer_x, w_qkv, facts = begin(tokens.reshape(block, width), w_query, w_key, w_value, facts)
+    full_gain_attn, full_gain_mlp = facts[:, :, :, 0, :shard].reshape(1, width), facts[:, :, :, 1, :shard].reshape(1, width)
+    layer = lax.axis_index("z")
+    own_lengths = lax.dynamic_index_in_dim(facts[:, 0, 0, 2, : lengths.shape[1]], layer, 0, False).astype(jnp.int32)
+    ends = jnp.concatenate((jnp.cumsum(own_lengths), (layer % 2).astype(jnp.int32)[None]))
     place = (4 * lax.axis_index("y") + 2 * lax.axis_index("c") + lax.axis_index("x")) * block
     x_own = lax.dynamic_slice_in_dim(layer_x, place, block, 0)
-    full_gain_attn, full_gain_mlp = (
-        lax.all_gather(gain, ALL, axis=0, tiled=True).astype(jnp.float32)[None] for gain in (gain_attn, gain_mlp)
-    )
     layer_normed = norm_forward(layer_x.astype(jnp.float32), full_gain_attn)[0].astype(LOW)
-    out_rows = lax.all_gather(w_out, ("z", "x"), axis=0, tiled=True)
+    out_rows = lax.all_gather(after(facts, w_out), ("z", "x"), axis=0, tiled=True)
     w_out_own = lax.dynamic_slice_in_dim(out_rows, lax.axis_index("x") * owned, owned, 0)
 
     qkv = dot_wide(layer_normed, w_qkv).astype(LOW)
     attended = attend(ends, qkv)
-    resid, layer_mlp = close_attention(attended, w_out_own, x_own, full_gain_mlp)
-
-    own_gate = lax.all_gather(w_gate, "z", axis=1, tiled=True)
-    own_up = lax.all_gather(w_up, "z", axis=1, tiled=True)
-    own_down = lax.all_gather(w_down, "z", axis=0, tiled=True)
-    upstream = trade(cotangent).reshape(block, width)
+    resid, layer_mlp, own_gate, own_up = close_attention(attended, w_out_own, x_own, full_gain_mlp, w_gate, w_up)
+
+    own_down = lax.all_gather(after(qkv, w_down), "z", axis=0, tiled=True)
+    upstream = trade(after(facts, cotangent)).reshape(block, width)
     layer_upstream = gather_layer(upstream)
     gate = dot_wide(layer_mlp, own_gate)
     up_part = dot_wide(layer_mlp, own_up)
     sigmoid_gate = jax.nn.sigmoid(gate)
     hidden = (gate * sigmoid_gate * up_part).astype(LOW)
-    result = resid + scatter_layer(dot_wide(hidden, own_down))
-    mixed = trade(result.astype(LOW).reshape(rows_here, block, width), back=True)
+    down_term = contract_rows(hidden, layer_upstream).astype(LOW)
     d_hidden = contract_cols(layer_upstream, own_down)
     d_gate, d_up = gate_backward(d_hidden, gate, up_part, sigmoid_gate)
-    d_resid, gain_mlp_term, layer_d_resid = close_mlp(d_gate, d_up, own_gate, own_up, resid, upstream, full_gain_mlp)
+    gate_term, up_term = contract_rows(layer_mlp, d_gate).astype(LOW), contract_rows(layer_mlp, d_up).astype(LOW)
 
     def scatter_layers(whole, axis):
-        return lax.psum_scatter(whole.astype(LOW), "z", scatter_dimension=axis, tiled=True).astype(jnp.float32)
-
-    grad_gate = scatter_layers(contract_rows(layer_mlp, d_gate), 1)
-    grad_up = scatter_layers(contract_rows(layer_mlp, d_up), 1)
-    grad_down = scatter_layers(contract_rows(hidden, layer_upstream), 0)
-
-    d_attended = contract_cols(layer_d_resid, w_out_own).astype(LOW)
-    d_qkv = attend_back(ends, qkv, d_attended)
-    grad_low, gain_attn_term = close_layer(d_qkv, w_qkv, x_own, d_resid, full_gain_attn)
-    grad_tokens = grad_low.astype(jnp.float32).reshape(rows_here, block, width)
+        return lax.psum_scatter(whole, "z", scatter_dimension=axis, tiled=True).astype(jnp.float32)
+
+    grad_gate, grad_up, grad_down = scatter_layers(gate_term, 1), scatter_layers(up_term, 1), scatter_layers(down_term, 0)
+    d_resid, gain_mlp_term, layer_d_resid = close_mlp(
+        after((gate_term, up_term, down_term), d_gate), d_up, own_gate, own_up, resid, upstream, full_gain_mlp
+    )
+    result = resid + scatter_layer(dot_wide(after(d_resid, hidden), own_down))
+    mixed = trade(result.astype(LOW).reshape(rows_here, block, width), back=True)
 
     out_term = contract_rows(attended, layer_d_resid)
-    qkv_term = contract_rows(layer_normed, d_qkv)
     out_term = lax.dynamic_update_slice_in_dim(
         jnp.zeros((2 * owned, width), LOW), out_term.astype(LOW), lax.axis_index("x") * owned, 0
     )
     grad_out = lax.psum_scatter(out_term, ("z", "x"), scatter_dimension=0, tiled=True).astype(jnp.float32)
+    d_attended = contract_cols(layer_d_resid, w_out_own).astype(LOW)
+    d_qkv = attend_back(ends, qkv, after(out_term, d_attended))
+    qkv_term = contract_rows(layer_normed, d_qkv).astype(LOW)
+    grad_low, gain_grads = close_layer(
+        after(qkv_term, d_qkv), w_qkv, x_own, d_resid, full_gain_attn, gain_mlp_term
+    )
+    grad_tokens = grad_low.astype(jnp.float32).reshape(rows_here, block, width)
+
     qkv_term = qkv_term.reshape(4, layers, 2 * shard, 3 * owned).transpose(1, 0, 2, 3)
     qkv_term = qkv_term.reshape(layers * members * shard, 3 * owned)
-    qkv_term = lax.psum_scatter(qkv_term.astype(LOW), "z", scatter_dimension=0, tiled=True)
+    qkv_term = lax.psum_scatter(qkv_term, "z", scatter_dimension=0, tiled=True)
     qkv_term = lax.all_to_all(qkv_term.reshape(members, shard, 3 * owned), LAYER, 0, 0)
     qkv_term = qkv_term.reshape(members, shard, 3, owned).transpose(2, 1, 0, 3).astype(jnp.float32)
     grad_query, grad_key, grad_value = qkv_term.reshape(3, shard, width)
-    grad_gain_attn, grad_gain_mlp = (
-        lax.psum_scatter(jnp.sum(term, axis=0), ALL, scatter_dimension=0, tiled=True)
-        for term in (gain_attn_term, gain_mlp_term)
-    )
+    gain_grads = lax.dynamic_index_in_dim(jnp.sum(gain_grads, axis=1).reshape(2, 2, shard), lax.axis_index("x"), 1, False)
     return (
         mixed,
         grad_tokens,
@@ -940,8 +1060,8 @@
         grad_gate,
         grad_up,
         grad_down,
-        grad_gain_attn,
-        grad_gain_mlp,
+        gain_grads[0],
+        gain_grads[1],
     )
 
 

time: 1650 us -> 1560 us (0.945)
  blocking collectives: 316 us -> 0 us
  waiting for transfers between devices: 88.6 us -> 254 us
  Pallas kernels: 910 us -> 971 us
    unnamed x2 -> x0, blocking collectives: 316 us -> none
    pallas_call x1, Pallas kernels: 158 us -> 359 us  [close_attention(): pl.pallas_call(close_attention_kernel, out_shape=(jax.ShapeDtypeStruct((b...]
    reduce_scatter x4, waiting for transfers between devices: 85.9 us -> 224 us  [the longest x3 224 us: scatter_layers(): lax.psum_scatter(whole, 'z', scatter_dimension=axis, tiled=True)]
    pallas_call x1, Pallas kernels: 277 us -> 152 us  [begin(): pl.pallas_call(begin_kernel, out_shape=(jax.ShapeDtypeStruct((8 * block,...]
    pallas_call x1, Pallas kernels: 235 us -> 165 us  [close_mlp(): pl.pallas_call(close_mlp_kernel, out_shape=(jax.ShapeDtypeStruct((block,...]
    pallas_call x1, Pallas kernels: 103 us -> 158 us  [close_layer(): pl.pallas_call(close_layer_kernel, out_shape=(jax.ShapeDtypeStruct((block...]
    reduce_scatter x1, waiting for transfers between devices: 0.01 us -> 22.5 us  [body_layers(): lax.psum_scatter(out_term, ('z', 'x'), scatter_dimension=0, tiled=True)]
  transfers between devices with their start and end apart: 15 -> 12, of which waited for: 2 -> 5; matrix products, arithmetic and copies ran while one was open for 14% -> 10% of each run, Pallas kernels for 55% -> 42%
where the time goes in v4:
time: 1560 us
  Pallas kernels  971 us (62%)
  waiting for transfers between devices  254 us (16%)
  matrix products  237 us (15%)
  other arithmetic  30.1 us (2%)
  starting transfers between devices  26.2 us (2%)
  local copies, waits for them, and re-layouts  25.3 us (2%)
    pallas_call x1, Pallas kernels, close_attention(): pl.pallas_call(close_attention_kernel, out_shape=(jax.ShapeDtypeStruct((b...  359 us
    reduce_scatter x3, waiting for transfers between devices, scatter_layers(): lax.psum_scatter(whole, 'z', scatter_dimension=axis, tiled=True)  224 us
    pallas_call x1, Pallas kernels, close_mlp(): pl.pallas_call(close_mlp_kernel, out_shape=(jax.ShapeDtypeStruct((block,...  165 us
    pallas_call x1, Pallas kernels, close_layer(): pl.pallas_call(close_layer_kernel, out_shape=(jax.ShapeDtypeStruct((block...  158 us
    pallas_call x1, Pallas kernels, begin(): pl.pallas_call(begin_kernel, out_shape=(jax.ShapeDtypeStruct((8 * block,...  152 us
    dot_general x5, matrix products, contract_rows(): lax.dot_general(left, right, (((0,), (0,)), ((), ())), preferred_element_...  103 us
    dot_general x4, matrix products, dot_wide(): return jnp.dot(left, right, preferred_element_type=jnp.float32)  87.1 us
    pallas_call x1, Pallas kernels, attend_back(): pl.pallas_call(attend_back_kernel, out_shape=jax.ShapeDtypeStruct((places...  83.6 us
  transfers between devices with their start and end apart: 12, of which 5 were waited for; matrix products, arithmetic and copies ran while one was open for 10% of the time, Pallas kernels for 42%

profile of v4, /device:TPU:0, one launch (start us, length us, event | category | flops | bytes accessed | tf_op | source)
XLA Modules:
  0.0 1558.7 jit_solution(488623641976629307)
XLA Ops:
  7.2 0.7 pad_convert_fusion
  7.9 0.7 bitcast_convert_fusion.1
  8.5 0.7 convert_element_type.86
  9.3 0.2 scatter.20.facts
  9.5 0.6 copy-done.7
  10.1 152.1 %shard_map.203 = (bf16[4096,2048]{1,0:T(8,128)(2,1)}, bf16[4,4,128,768]{3,2,1,0:T(8,128)(2,1)}, f32[4,4,2,8,128]{4,3,2,1,0:T(8,128)}) custom-call(bf16[2,256,2048]{2,1,0:T(8,128)(2,1)} %bitcast.69, bf16[64,2048]{1,0:T(8,128)(2,1)} %w_query.1, bf16[64,2048]{1,0:T(8,128)(2,1)} %w_key.1, bf16[64,2048]{1,0:T(8,128)(2,1)} %w_value.1, f32[8,128]{1,0:T(8,128)} %copy-done.7), custom_call_target="tpu_custom_call" | custom-call | bytes 350000000 | tf_op jit(solution)/shard_map/pallas_call | solution.py:655
  162.3 7.6 fusion
  169.9 1.6 slice_reduce_fusion
  171.7 0.6 copy-done.8
  172.3 19.0 %convolution_convert_fusion.1.qkv = bf16[4096,768]{1,0:T(8,128)(2,1)} fusion(bf16[2048,768]{1,0:T(8,128)(2,1)S(1)} %bitcast.67, bf16[4096,2048]{1,0:T(8,128)(2,1)} %get-tuple-element.67, f32[2048]{0:T(1024)S(1)} %mul.58, f32[4096]{0:T(1024)S(1)} %add_rsqrt_fusion), kind=kOutput, calls=%fused_computation.14 | convolution fusion | flops 12921602048 | bytes 26238976 | tf_op jit(solution)/shard_map/dot_general | solution.py:248
  191.4 2.3 collective-permute-start
  193.6 1.3 copy-done.1
  195.0 0.7 slice.74
  196.0 0.7 reshape_squeeze.6.gain
  196.6 0.6 pad_add_fusion.ends
  197.2 3.2 constant_dynamic-slice_fusion.2.x_own
  200.4 54.2 %shard_map.204.attended = bf16[4096,256]{1,0:T(8,128)(2,1)} custom-call(s32[9]{0:T(128)} %pad_add_fusion.ends, bf16[4096,768]{1,0:T(8,128)(2,1)} %convolution_convert_fusion.1.qkv), custom_call_target="tpu_custom_call" | custom-call | flops 8589934592 | bytes 8388608 | tf_op jit(solution)/shard_map/pallas_call | solution.py:205
  254.6 4.7 all-gather.5.cloned.1.call-done
  259.3 2.3 constant_dynamic-slice_fusion.3.w_out
  261.6 358.9 %shard_map.205 = (f32[512,2048]{1,0:T(8,128)}, bf16[4096,2048]{1,0:T(8,128)(2,1)}, bf16[2048,1024]{1,0:T(8,128)(2,1)}, bf16[2048,1024]{1,0:T(8,128)(2,1)}) custom-call(bf16[4096,256]{1,0:T(8,128)(2,1)} %shard_map.204.attended, bf16[256,2048]{1,0:T(8,128)(2,1)} %constant_dynamic-slice_fusion.3.w_out, bf16[512,2048]{1,0:T(8,128)(2,1)} %constant_dynamic-slice_fusion.2.x_own, ...), custom_call_target="tpu_custom_call" | custom-call | bytes 450000000 | tf_op jit(solution)/shard_map/pallas_call | solution.py:741
  620.6 23.5 %fusion.23 = f32[4096,1024]{1,0:T(8,128)} fusion(bf16[4096,2048]{1,0:T(8,128)(2,1)} %get-tuple-element.71, bf16[2048,1024]{1,0:T(8,128)(2,1)} %get-tuple-element.74.w_up), kind=kOutput, calls=%fused_computation.42 | convolution fusion | flops 17179869184 | bytes 37748736 | tf_op jit(solution)/shard_map/dot_general | solution.py:248
  644.1 20.8 %fusion.24 = f32[4096,1024]{1,0:T(8,128)} fusion(bf16[4096,2048]{1,0:T(8,128)(2,1)S(1)} %copy-done.12, bf16[2048,1024]{1,0:T(8,128)(2,1)S(1)} %copy-done.3), kind=kOutput, calls=%fused_computation.43 | convolution fusion | flops 17179869184 | bytes 37748736 | tf_op jit(solution)/shard_map/dot_general | solution.py:248
  665.0 36.3 %multiply_convert_fusion = (bf16[4096,1024]{1,0:T(8,128)(2,1)}, bf16[4096,1024]{1,0:T(8,128)(2,1)}, bf16[4096,1024]{1,0:T(8,128)(2,1)}) fusion(f32[4096,1024]{1,0:T(8,128)} %fusion.23, f32[4096,1024]{1,0:T(8,128)} %fusion.24, bf16[1024,2048]{1,0:T(8,128)(2,1)} %all-gather.7.cloned.1.call-done, bf16[1,4096,2048]{2,1,0:T(8,128)(2,1)} %all-gather.9.cloned.1.call-done), kind=kOutput, calls=%fused_computation.9 | convolution fusion | flops 17246978048 | bytes 79691776 | tf_op jit(solution)/shard_map/dot_general | solution.py:26
  701.2 23.7 %convolution_convert_fusion.4 = bf16[2048,1024]{1,0:T(8,128)(2,1)} fusion(bf16[4096,2048]{1,0:T(8,128)(2,1)} %get-tuple-element.71, bf16[4096,1024]{1,0:T(8,128)(2,1)} %get-tuple-element.76.d_gate), kind=kOutput, calls=%fused_computation.20 | convolution fusion | flops 17181966336 | bytes 29360128 | tf_op jit(solution)/shard_map/dot_general | solution.py:20
  724.9 23.8 %convolution_convert_fusion.3 = bf16[2048,1024]{1,0:T(8,128)(2,1)} fusion(bf16[4096,2048]{1,0:T(8,128)(2,1)} %get-tuple-element.71, bf16[4096,1024]{1,0:T(8,128)(2,1)} %get-tuple-element.89.d_up), kind=kOutput, calls=%fused_computation.19 | convolution fusion | flops 17181966336 | bytes 29360128 | tf_op jit(solution)/shard_map/dot_general | solution.py:20
  748.7 24.2 %fusion.10 = bf16[1024,2048]{1,0:T(8,128)(2,1)} fusion(bf16[4096,1024]{1,0:T(8,128)(2,1)} %get-tuple-element.78, bf16[1,4096,2048]{2,1,0:T(8,128)(2,1)} %all-gather.9.cloned.1.call-done), kind=kOutput, calls=%fused_computation.18 | convolution fusion | flops 17181966336 | bytes 29360128 | tf_op jit(solution)/shard_map/dot_general | solution.py:20
  772.9 164.8 %shard_map.206 = (f32[512,2048]{1,0:T(8,128)}, f32[8,2048]{1,0:T(8,128)}, bf16[4096,2048]{1,0:T(8,128)(2,1)}) custom-call(bf16[4096,1024]{1,0:T(8,128)(2,1)} %get-tuple-element.76.d_gate, bf16[4096,1024]{1,0:T(8,128)(2,1)} %get-tuple-element.89.d_up, bf16[2048,1024]{1,0:T(8,128)(2,1)} %get-tuple-element.75.w_gate, ...), custom_call_target="tpu_custom_call" | custom-call | bytes 450000000 | tf_op jit(solution)/shard_map/pallas_call | solution.py:822
  937.7 23.7 %convolution_convert_fusion = bf16[4096,2048]{1,0:T(8,128)(2,1)} fusion(bf16[4096,1024]{1,0:T(8,128)(2,1)} %get-tuple-element.78, bf16[1024,2048]{1,0:T(8,128)(2,1)} %all-gather.7.cloned.1.call-done), kind=kOutput, calls=%fused_computation.13 | convolution fusion | flops 17188257792 | bytes 29360128 | tf_op jit(solution)/shard_map/dot_general | solution.py:248
  961.5 1.1 copy-done.4
  962.6 10.9 convolution_convert_fusion.2.grads
  973.5 0.2 broadcast_in_dim.9
  973.8 11.4 fusion.16
  985.3 83.6 %shard_map.207.d_qkv = bf16[4096,768]{1,0:T(8,128)(2,1)} custom-call(s32[9]{0:T(128)} %pad_add_fusion.ends, bf16[4096,768]{1,0:T(8,128)(2,1)} %convolution_convert_fusion.1.qkv, bf16[4096,256]{1,0:T(8,128)(2,1)} %convolution_convert_fusion.2.grads), custom_call_target="tpu_custom_call" | custom-call | flops 21474836480 | bytes 14680064 | tf_op jit(solution)/shard_map/pallas_call | solution.py:226
  1068.9 20.0 %fusion.13 = bf16[2048,768]{1,0:T(8,128)(2,1)S(1)} fusion(bf16[4096,768]{1,0:T(8,128)(2,1)} %shard_map.207.d_qkv, bf16[4096,2048]{1,0:T(8,128)(2,1)} %get-tuple-element.67, f32[2048]{0:T(1024)S(1)} %copy-done.11, f32[4096]{0:T(1024)S(1)} %copy-done.9), kind=kOutput, calls=%fused_computation.21 | convolution fusion | flops 12920029184 | bytes 26238976 | tf_op jit(solution)/shard_map/dot_general | solution.py:20
  1088.9 1.9 copy.24
  1090.9 0.5 reduce-scatter.11.cloned.1.call-update
  1091.5 0.7 reduce-scatter.13.cloned.1.call-update
  1092.2 0.7 reduce-scatter.15.cloned.1.call-update
  1093.0 0.7 reduce-scatter.17.cloned.1.call-update
  1093.7 4.9 fusion.17
  1098.6 17.1 %collective-permute-start.1 = (bf16[1,512,2048]{2,1,0:T(8,128)(2,1)}, bf16[1,512,2048]{2,1,0:T(8,128)(2,1)}, u32[]{:S(2)}, u32[]{:S(2)}) collective-permute-start(bf16[1,512,2048]{2,1,0:T(8,128)(2,1)} %fusion.17), channel_id=1, source_target_pairs={{0,0},{1,1},{16,2},{17,3},{8,4},{9,5},{24,6},{25,7},{18,8},{19,9},... | collective-permute-start | bytes 6291464 | tf_op jit(solution)/shard_map/ppermute | solution.py:978
  1115.7 0.7 reshape_squeeze.7.gain
  1116.4 157.6 %shard_map.208 = (bf16[512,2048]{1,0:T(8,128)(2,1)}, f32[2,8,128]{2,1,0:T(8,128)}) custom-call(bf16[4096,768]{1,0:T(8,128)(2,1)} %shard_map.207.d_qkv, bf16[2048,768]{1,0:T(8,128)(2,1)} %bitcast.66, bf16[512,2048]{1,0:T(8,128)(2,1)} %constant_dynamic-slice_fusion.2.x_own, f32[512,2048]{1,0:T(8,128)} %get-tuple-element.77.d_resid, ...), custom_call_target="tpu_custom_call" | custom-call | bytes 350000000 | tf_op jit(solution)/shard_map/pallas_call | solution.py:938
  1273.9 0.7 reduce_sum.19
  1274.7 6.5 all-to-all-start
  1281.2 0.5 fusion.20
  1281.7 4.1 bitcast_convert_fusion
  1285.9 22.5 %reduce-scatter.11.cloned.1.call-done = bf16[64,2048]{1,0:T(8,128)(2,1)} async-done(((bf16[512,2048]{1,0:T(8,128)(2,1)}), bf16[64,2048]{1,0:T(8,128)(2,1)}) %reduce-scatter.11.cloned.1.call-update) | async-done | bytes 262160 | tf_op jit(solution)/shard_map/reduce_scatter | solution.py:1037
  1308.4 1.8 convert_element_type.107
  1310.2 0.9 reshape.208
  1311.0 1.5 fusion.22
  1312.5 0.3 copy.25
  1312.8 1.0 copy.28
  1313.8 0.3 copy.26
  1314.1 1.0 copy.29
  1315.0 0.3 copy.27
  1315.4 1.0 copy.30
  1316.3 70.2 %reduce-scatter.13.cloned.1.call-done = bf16[2048,256]{1,0:T(8,128)(2,1)} async-done(((bf16[2048,1024]{1,0:T(8,128)(2,1)}), bf16[2048,256]{1,0:T(8,128)(2,1)}) %reduce-scatter.13.cloned.1.call-update) | async-done | bytes 1048592 | tf_op jit(solution)/shard_map/reduce_scatter | solution.py:1024
  1386.5 2.7 convert_element_type.108
  1389.2 77.0 %reduce-scatter.15.cloned.1.call-done = bf16[2048,256]{1,0:T(8,128)(2,1)} async-done(((bf16[2048,1024]{1,0:T(8,128)(2,1)}), bf16[2048,256]{1,0:T(8,128)(2,1)}) %reduce-scatter.15.cloned.1.call-update) | async-done | bytes 1048592 | tf_op jit(solution)/shard_map/reduce_scatter | solution.py:1024
  1466.2 2.7 convert_element_type.109
  1468.9 76.9 %reduce-scatter.17.cloned.1.call-done = bf16[256,2048]{1,0:T(8,128)(2,1)} async-done(((bf16[1024,2048]{1,0:T(8,128)(2,1)}), bf16[256,2048]{1,0:T(8,128)(2,1)}) %reduce-scatter.17.cloned.1.call-update) | async-done | bytes 1048592 | tf_op jit(solution)/shard_map/reduce_scatter | solution.py:1024
  1545.8 2.8 convert_element_type.110
  1548.6 3.2 copy.35
  (49 shorter events, 1.0 us)
Async XLA Ops:
  7.2 252.1 %all-gather.5.cloned.1.call-start = ((), (), s32[]{:S(2)}) async-start(), calls=%async_computation.7 | async-start | bytes 2359296 | tf_op jit(solution)/shard_map/all_gather | solution.py:1004
  9.5 0.6 copy-start.7
  162.2 502.7 %all-gather.7.cloned.1.call-start = ((), (), s32[]{:S(2)}) async-start(), calls=%async_computation.8 | async-start | bytes 5242880 | tf_op jit(solution)/shard_map/all_gather | solution.py:1011
  162.3 10.0 copy-start.5
  171.7 19.6 %copy-start.10 = (f32[2048]{0:T(1024)}, f32[2048]{0:T(1024)S(1)}, u32[]{:S(2)}) copy-start(f32[2048]{0:T(1024)S(1)} %mul.58) | copy-start | bytes 24580
  171.7 0.6 copy-start.8
  191.3 473.6 %all-gather.9.cloned.1.call-start = ((), (), s32[]{:S(2)}) async-start(), calls=%async_computation.15 | async-start | bytes 18874368 | tf_op jit(solution)/shard_map/all_gather | solution.py:962
  191.4 2.3 collective-permute-start
  193.6 1.3 copy-start.1
  195.0 898.7 %reduce-scatter.7.cloned.1.call-start = ((), (), s32[]{:S(2)}) async-start(), calls=%async_computation.9 | async-start | bytes 18874368 | tf_op jit(solution)/shard_map/reduce_scatter | solution.py:966
  620.6 23.6 %copy-start.3 = (bf16[2048,1024]{1,0:T(8,128)(2,1)S(1)}, bf16[2048,1024]{1,0:T(8,128)(2,1)}, u32[]{:S(2)}) copy-start(bf16[2048,1024]{1,0:T(8,128)(2,1)} %get-tuple-element.75.w_gate) | copy-start | bytes 12582916
  620.6 23.6 %copy-start.12 = (bf16[4096,2048]{1,0:T(8,128)(2,1)S(1)}, bf16[4096,2048]{1,0:T(8,128)(2,1)}, u32[]{:S(2)}) copy-start(bf16[4096,2048]{1,0:T(8,128)(2,1)} %get-tuple-element.71) | copy-start | bytes 50331652
  961.4 1.2 copy-start.4
  961.4 313.3 %reduce-scatter.9.cloned.1.call-start = ((), (), s32[]{:S(2)}) async-start(), calls=%async_computation.10 | async-start | bytes 3932160 | tf_op jit(solution)/shard_map/reduce_scatter | solution.py:1048
  962.6 11.2 copy-start
  985.2 83.7 %copy-start.2 = (bf16[512,2048]{1,0:T(8,128)(2,1)}, bf16[512,2048]{1,0:T(8,128)(2,1)S(1)}, u32[]{:S(2)}) copy-start(bf16[512,2048]{1,0:T(8,128)(2,1)S(1)} %fusion.16) | copy-start | bytes 6291460
  985.2 83.7 %copy-start.9 = (f32[4096]{0:T(1024)S(1)}, f32[4096]{0:T(1024)}, u32[]{:S(2)}) copy-start(f32[4096]{0:T(1024)} %copy-done.8) | copy-start | bytes 49156
  985.2 83.6 %copy-start.11 = (f32[2048]{0:T(1024)S(1)}, f32[2048]{0:T(1024)}, u32[]{:S(2)}) copy-start(f32[2048]{0:T(1024)} %copy-done.10) | copy-start | bytes 24580
  1090.8 217.6 %reduce-scatter.11.cloned.1.call-start = ((), (), s32[]{:S(2)}) async-start(), calls=%async_computation.11 | async-start | bytes 2359296 | tf_op jit(solution)/shard_map/reduce_scatter | solution.py:1037
  1091.4 295.1 %reduce-scatter.13.cloned.1.call-start = ((), (), s32[]{:S(2)}) async-start(), calls=%async_computation.12 | async-start | bytes 5242880 | tf_op jit(solution)/shard_map/reduce_scatter | solution.py:1024
  1092.2 23.5 %copy-start.6 = (f32[4,4,2,1,64]{4,3,2,1,0:T(1,128)S(1)}, f32[4,4,2,1,64]{4,3,2,1,0:T(1,128)}, u32[]{:S(2)}) copy-start(f32[4,4,2,1,64]{4,3,2,1,0:T(1,128)} %get-tuple-element.93) | copy-start | bytes 24580
  1092.2 374.0 %reduce-scatter.15.cloned.1.call-start = ((), (), s32[]{:S(2)}) async-start(), calls=%async_computation.13 | async-start | bytes 5242880 | tf_op jit(solution)/shard_map/reduce_scatter | solution.py:1024
  1092.9 452.9 %reduce-scatter.17.cloned.1.call-start = ((), (), s32[]{:S(2)}) async-start(), calls=%async_computation.14 | async-start | bytes 5242880 | tf_op jit(solution)/shard_map/reduce_scatter | solution.py:1024
  1098.6 450.0 %collective-permute-start.1 = (bf16[1,512,2048]{2,1,0:T(8,128)(2,1)}, bf16[1,512,2048]{2,1,0:T(8,128)(2,1)}, u32[]{:S(2)}, u32[]{:S(2)}) collective-permute-start(bf16[1,512,2048]{2,1,0:T(8,128)(2,1)} %fusion.17), channel_id=1, source_target_pairs={{0,0},{1,1},{16,2},{17,3},{8,4},{9,5},{24,6},{25,7},{18,8},{19,9},... | collective-permute-start | bytes 6291464 | tf_op jit(solution)/shard_map/ppermute | solution.py:978
  1274.7 35.4 %all-to-all-start = ((bf16[8,64,768]{2,1,0:T(8,128)(2,1)}), bf16[8,64,768]{2,1,0:T(8,128)(2,1)S(1)}, u32[]{:S(2)}, u32[]{:S(2)}) async-start(bf16[8,64,768]{2,1,0:T(8,128)(2,1)} %bitcast.73), calls=%async_computation.2 | async-start | bytes 1572864 | tf_op jit(solution)/shard_map/all_to_all | solution.py:1049
Sparse Core Ops, SparseCore 0:
  162.4 96.8 all-gather.4
  260.9 103.5 all-gather.6
  366.9 112.0 all-gather.8
  961.5 115.1 reduce-scatter.6
  1091.0 86.3 reduce-scatter.8
  1181.3 127.0 reduce-scatter.10
  1310.7 75.7 reduce-scatter.12
  1388.9 77.2 reduce-scatter.14
  1468.5 77.2 reduce-scatter.16

commit v5 on v4

--- a/solution.py
+++ b/solution.py
@@ -78,170 +78,8 @@
 VMEM_LIMIT = 60 * 1024 * 1024
 
 
-def doc_start(ends, place):
-    start = jnp.zeros_like(place)
-    for k in range(8):
-        start = jnp.where(ends[k] <= place, ends[k], start)
-    return jnp.where(place < ends[7], start, LEN)
-
-
-def doc_end(ends, place):
-    end = ends[7]
-    for k in range(6, -1, -1):
-        end = jnp.where(ends[k] > place, ends[k], end)
-    return end
-
-
-def sigmoid_of(raw):
-    return pl.reciprocal(1.0 + jnp.exp2(math.log2(LEN) - raw * (math.log2(math.e) / math.sqrt(HD))), approx=True)
-
-
 def dot_nt(left, right):
     return lax.dot_general(left, right, (((1,), (1,)), ((), ())), preferred_element_type=jnp.float32)
-
-
-def rows_of(ends, block):
-    z, x = block // 2, block % 2
-    return pl.ds(pl.multiple_of((4 * ((z + ends[8]) % 2) + 2 * (z // 2) + x) * TILE, TILE), TILE)
-
-
-def attend_kernel(ends, qkv, out, total):
-    head, i = pl.program_id(0), pl.program_id(1)
-    column = pl.multiple_of(head * HD, HD)
-    width = qkv.shape[1] // 3
-    first = i * TILE
-    query = qkv[rows_of(ends, i), pl.ds(column, HD)]
-    total[...] = jnp.zeros_like(total)
-    begin = jnp.minimum(doc_start(ends, first), first) // TILE
-    latest = doc_start(ends, first + TILE - 1)
-
-    def step(j, carry):
-        here = rows_of(ends, j)
-        key = qkv[here, pl.ds(pl.multiple_of(column + width, HD), HD)]
-        value = qkv[here, pl.ds(pl.multiple_of(column + 2 * width, HD), HD)]
-        plain = (j < i) & (j * TILE >= latest)
-
-        @pl.when(plain)
-        def _():
-            weight = sigmoid_of(dot_nt(query, key)).astype(LOW)
-            total[...] += jnp.dot(weight, value, preferred_element_type=jnp.float32)
-
-        @pl.when(jnp.logical_not(plain))
-        def _():
-            q_place = first + lax.broadcasted_iota(jnp.int32, (TILE, 1), 0)
-            k_place = j * TILE + lax.broadcasted_iota(jnp.int32, (1, TILE), 1)
-            allowed = (k_place <= q_place) & (k_place >= doc_start(ends, q_place))
-            weight = jnp.where(allowed, sigmoid_of(dot_nt(query, key)), 0.0).astype(LOW)
-            total[...] += jnp.dot(weight, value, preferred_element_type=jnp.float32)
-
-        return carry
-
-    lax.fori_loop(begin, i + 1, step, 0)
-    out[rows_of(ends, i), pl.ds(column, HD)] = total[...].astype(LOW)
-
-
-def attend_back_kernel(ends, qkv, grads, out, query_total, key_total, value_total):
-    head, j = pl.program_id(0), pl.program_id(1)
-    column = pl.multiple_of(head * HD, HD)
-    width = qkv.shape[1] // 3
-    first = j * TILE
-    here = rows_of(ends, j)
-    key_column = pl.multiple_of(column + width, HD)
-    value_column = pl.multiple_of(column + 2 * width, HD)
-    key = qkv[here, pl.ds(key_column, HD)]
-    value = qkv[here, pl.ds(value_column, HD)]
-    key_turned = key.T
-    key_total[...] = jnp.zeros_like(key_total)
-    value_total[...] = jnp.zeros_like(value_total)
-
-    @pl.when(j == 0)
-    def _():
-        query_total[...] = jnp.zeros_like(query_total)
-
-    end = pl.cdiv(doc_end(ends, first + TILE - 1), TILE)
-
-    def step(i, carry):
-        there = rows_of(ends, i)
-        turned = pl.ds(pl.multiple_of(i * TILE, TILE), TILE)
-        query = qkv[there, pl.ds(column, HD)]
-        grad = grads[there, pl.ds(column, HD)]
-        plain = (j < i) & (first >= doc_start(ends, i * TILE + TILE - 1))
-
-        def finish(sig):
-            value_total[...] += jnp.dot(sig.astype(LOW), grad, preferred_element_type=jnp.float32)
-            d_score = (dot_nt(value, grad) * (sig * (1.0 - sig))).astype(LOW)
-            key_total[...] += jnp.dot(d_score, query, preferred_element_type=jnp.float32)
-            query_total[:, turned] += jnp.dot(key_turned, d_score, preferred_element_type=jnp.float32)
-
-        @pl.when(plain)
-        def _():
-            finish(sigmoid_of(dot_nt(key, query)))
-
-        @pl.when(jnp.logical_not(plain))
-        def _():
-            q_place = i * TILE + lax.broadcasted_iota(jnp.int32, (1, TILE), 1)
-            k_place = first + lax.broadcasted_iota(jnp.int32, (TILE, 1), 0)
-            allowed = (k_place <= q_place) & (k_place >= doc_start(ends, q_place))
-            finish(jnp.where(allowed, sigmoid_of(dot_nt(key, query)), 0.0))
-
-        return carry
-
-    lax.fori_loop(j, end, step, 0)
-    scale = 1.0 / math.sqrt(HD)
-    out[here, pl.ds(key_column, HD)] = (key_total[...] * scale).astype(LOW)
-    out[here, pl.ds(value_column, HD)] = value_total[...].astype(LOW)
-
-    @pl.when(j == pl.num_programs(1) - 1)
-    def _():
-        for t in range(LEN // TILE):
-            out[rows_of(ends, t), pl.ds(column, HD)] = (
-                (query_total[:, t * TILE : (t + 1) * TILE] * scale).T.astype(LOW)
-            )
-
-
-def attend(ends, qkv):
-    places, width = qkv.shape
-    heads = width // (3 * HD)
-    return pl.pallas_call(
-        attend_kernel,
-        out_shape=jax.ShapeDtypeStruct((places, width // 3), LOW),
-        grid_spec=pltpu.PrefetchScalarGridSpec(
-            num_scalar_prefetch=1,
-            grid=(heads, places // TILE),
-            in_specs=[pl.BlockSpec((places, width), lambda h, i, ends: (0, 0))],
-            out_specs=pl.BlockSpec((places, width // 3), lambda h, i, ends: (0, 0)),
-            scratch_shapes=[pltpu.VMEM((TILE, HD), jnp.float32)],
-        ),
-        compiler_params=pltpu.CompilerParams(vmem_limit_bytes=VMEM_LIMIT),
-        cost_estimate=pl.CostEstimate(
-            flops=4 * heads * places * places * HD // 2, bytes_accessed=8 * places * width // 3, transcendentals=heads * places * places // 2
-        ),
-    )(ends, qkv)
-
-
-def attend_back(ends, qkv, grads):
-    places, width = qkv.shape
-    heads = width // (3 * HD)
-    whole = lambda columns: pl.BlockSpec((places, columns), lambda h, j, ends: (0, 0))
-    return pl.pallas_call(
-        attend_back_kernel,
-        out_shape=jax.ShapeDtypeStruct((places, width), LOW),
-        grid_spec=pltpu.PrefetchScalarGridSpec(
-            num_scalar_prefetch=1,
-            grid=(heads, places // TILE),
-            in_specs=[whole(width), whole(width // 3)],
-            out_specs=whole(width),
-            scratch_shapes=[
-                pltpu.VMEM((HD, places), jnp.float32),
-                pltpu.VMEM((TILE, HD), jnp.float32),
-                pltpu.VMEM((TILE, HD), jnp.float32),
-            ],
-        ),
-        compiler_params=pltpu.CompilerParams(vmem_limit_bytes=VMEM_LIMIT),
-        cost_estimate=pl.CostEstimate(
-            flops=10 * heads * places * places * HD // 2, bytes_accessed=14 * places * width // 3, transcendentals=heads * places * places // 2
-        ),
-    )(ends, qkv, grads)
 
 
 def dot_wide(left, right):
@@ -266,17 +104,12 @@
     return (y, c, z, 1 - x), (1 - y, c, z, x), (y, 1 - c, z, x)
 
 
-def worker_of(y, c, z, x):
-    return lax.rem(z + c, 2), z // 2, 2 * y + c, x
-
-
-def owner_of(y, c, z, x):
-    row = lax.rem(z, 2)
-    return z // 2, row, 2 * c + lax.rem(y + row, 2), x
+def partner_of(y, c, z, x):
+    return lax.rem(z, 2), z // 2, 2 * c + y, x
 
 
 def place_of(y, c, x, half=None):
-    first = (4 * y + 2 * c + x) * TILE
+    first = (4 * c + 2 * y + x) * TILE
     if half is None:
         return pl.ds(pl.multiple_of(first, TILE), TILE)
     return pl.ds(pl.multiple_of(first + half * HALF, HALF), HALF)
@@ -360,10 +193,9 @@
     gather = Gather(lambda half: own.at[pl.ds(half * HALF, HALF)], whole, send, recv)
     gather.start(0)
     gather.start(1)
-    beside(0)
     gather.pass_first()
+    beside(1)
     gather.pass_second()
-    beside(1)
     gather.pass_far()
     gather.finish()
     beside(2)
@@ -459,6 +291,21 @@
 def others():
     y, c, z, x = spot()
     return [(flip(y, dy), flip(c, dc), z, flip(x, dx)) for dy in (0, 1) for dc in (0, 1) for dx in (0, 1) if dy + dc + dx]
+
+
+def line_of():
+    y, c, z, x = spot()
+    return [(y, c, lax.rem(z + dz, 4), x) for dz in (1, 2, 3)]
+
+
+def spread_columns(whole, parts, send, recv):
+    size = whole.shape[1] // 4
+    return [
+        remote(
+            whole.at[:, pl.ds(pl.multiple_of(peer[2] * size, size), size)], parts.at[k], send.at[k], recv.at[k], peer
+        )
+        for k, peer in enumerate(line_of())
+    ]
 
 
 def add_rows(total, first, term, start, count):
@@ -483,7 +330,7 @@
     ]
 
 
-def run_scatter(produce, staged, core_part, total, relayed, landed, send, recv):
+def run_scatter(produce, staged, core_part, total, relayed, landed, send, recv, beside=lambda: None):
     y, c, z, x = spot()
     across_x, across_y, core = near()
     dests = ((1 - y, 1 - x), (y, 1 - x), (1 - y, x), (y, x))
@@ -522,6 +369,7 @@
     far_x.wait_recv()
     add_rows(total.at[2], 0, relayed.at[0], 0, HALF)
     to_y[0].start()
+    beside()
     for copy in to_x + to_y:
         copy.wait_recv()
     for copy in to_core[2:] + [far_x, far_y] + to_x + to_y:
@@ -534,27 +382,26 @@
 ):
     y, c, z, x = spot()
     row = 2 * y + c
-    worker, owner = worker_of(y, c, z, x), owner_of(y, c, z, x)
-    moves = jnp.logical_not((worker[0] == y) & (worker[1] == c) & (worker[2] == z))
+    partner = partner_of(y, c, z, x)
+    moves = z != 2 * c + y
     layer = others()
     barrier, count = greet_neighbours(layer)
 
     @pl.when(moves)
     def _():
-        pl.semaphore_signal(barrier, inc=1, device_id=owner, device_id_type=MESH_ID)
-        pl.semaphore_signal(barrier, inc=1, device_id=worker, device_id_type=MESH_ID)
-
-    pl.semaphore_wait(barrier, count + 2 * moves.astype(jnp.int32))
+        pl.semaphore_signal(barrier, inc=1, device_id=partner, device_id_type=MESH_ID)
+
+    pl.semaphore_wait(barrier, count + moves.astype(jnp.int32))
 
     shard, width = w_query.shape
     owned = width // 8
     trades = [
         remote(
             x_own.at[half],
-            x_whole.at[place_of(worker[0], worker[1], worker[3], half)],
+            x_whole.at[place_of(partner[0], partner[1], partner[3], half)],
             trade_send.at[half],
             trade_recv.at[half],
-            worker,
+            partner,
         )
         for half in (0, 1)
     ]
@@ -659,7 +506,7 @@
             jax.ShapeDtypeStruct((4, 4, 2 * shard, 3 * width // 8), LOW),
             jax.ShapeDtypeStruct((4, 4, 2, *facts.shape), jnp.float32),
         ),
-        in_specs=[anywhere()] * 5,
+        in_specs=[in_vmem()] + [anywhere()] * 4,
         out_specs=[anywhere()] * 3,
         scratch_shapes=[
             dma(2), dma(2), dma(GATHER_COPIES), dma(GATHER_COPIES), dma(3, 7), dma(3, 7), dma(7), dma(7), dma(4), *chain_sems(2)
@@ -719,7 +566,7 @@
 
         lax.fori_loop(0, width // TILE, step, 0)
 
-    run_scatter(produce, *scatter)
+    run_scatter(produce, *scatter, beside=lambda: arrive(0))
     total, landed = scatter[2], scatter[4]
 
     def chunk(here):
@@ -746,7 +593,7 @@
             jax.ShapeDtypeStruct((width, 4 * hidden), LOW),
             jax.ShapeDtypeStruct((width, 4 * hidden), LOW),
         ),
-        in_specs=[in_vmem()] * 4 + [anywhere()] * 2,
+        in_specs=[in_vmem()] * 6,
         out_specs=[in_vmem()] + [anywhere()] * 3,
         scratch_shapes=[pltpu.VMEM((block, width), LOW)]
         + scatter_scratch(width)
@@ -768,8 +615,10 @@
         total[...] += terms[first : first + 8, :]
 
 
-def close_mlp_kernel(d_gate, d_up, w_gate, w_up, resid, upstream, gain, d_resid, gain_term, d_resid_whole, own, blocks, *scratch):
-    scatter, (send, recv, local, fetched) = scratch[:7], scratch[7:]
+def close_mlp_kernel(
+    d_gate, d_up, w_gate, w_up, resid, upstream, gain, grad, d_resid, gain_term, d_resid_whole, grad_parts, own, blocks, *scratch
+):
+    scatter, (send, recv, local, fetched, line_send, line_recv) = scratch[:7], scratch[7:]
     y, c, z, x = spot()
     width = w_gate.shape[0]
     order = [(r, k, q) for r, q in ((1 - y, 1 - x), (y, 1 - x), (1 - y, x), (y, x)) for k in (1 - c, c)]
@@ -784,7 +633,10 @@
 
     for copy in fetch(0):
         copy.start()
-    greet(near())
+    greet(near() + tuple(line_of()))
+    to_layers = spread_columns(grad, grad_parts, line_send, line_recv)
+    for copy in to_layers:
+        copy.start()
 
     def produce(turn, to_y, to_c, to_x, out):
         if turn < 7:
@@ -814,9 +666,11 @@
 
     over_chunks(chunk)
     run_gather(own, d_resid_whole, send, recv, local.at[0])
-
-
-def close_mlp(d_gate, d_up, w_gate, w_up, resid, upstream, gain):
+    for copy in to_layers:
+        copy.wait()
+
+
+def close_mlp(d_gate, d_up, w_gate, w_up, resid, upstream, gain, grad):
     block, width = resid.shape
     hidden = d_gate.shape[1]
     return pl.pallas_call(
@@ -825,35 +679,35 @@
             jax.ShapeDtypeStruct((block, width), jnp.float32),
             jax.ShapeDtypeStruct((8, width), jnp.float32),
             jax.ShapeDtypeStruct((8 * block, width), LOW),
+            jax.ShapeDtypeStruct((3, width, hidden // 4), LOW),
         ),
-        in_specs=[anywhere()] * 2 + [in_vmem()] * 5,
-        out_specs=[in_vmem(), in_vmem(), anywhere()],
+        in_specs=[anywhere()] * 2 + [in_vmem()] * 5 + [anywhere()],
+        out_specs=[in_vmem(), in_vmem(), anywhere(), anywhere()],
         scratch_shapes=[pltpu.VMEM((block, width), LOW), pltpu.VMEM((2, 2, block, hidden), LOW)]
         + scatter_scratch(width)
-        + [dma(GATHER_COPIES), dma(GATHER_COPIES), dma(1), dma(2, 2)],
+        + [dma(GATHER_COPIES), dma(GATHER_COPIES), dma(1), dma(2, 2), dma(3), dma(3)],
         compiler_params=remote_params(3),
         cost_estimate=pl.CostEstimate(flops=0, bytes_accessed=450_000_000, transcendentals=0),
-    )(d_gate, d_up, w_gate, w_up, resid, upstream, gain)
+    )(d_gate, d_up, w_gate, w_up, resid, upstream, gain, grad)
 
 
 def close_layer_kernel(d_qkv, w_qkv, x_own, d_resid, gain, mlp_term, grad_low, gain_grads, own, terms, layer_terms, part, column_terms, *scratch):
     scatter, (send, recv, term_send, term_recv, line_send, line_recv) = scratch[:7], scratch[7:]
     y, c, z, x = spot()
-    worker, owner = worker_of(y, c, z, x), owner_of(y, c, z, x)
-    moves = jnp.logical_not((worker[0] == y) & (worker[1] == c) & (worker[2] == z))
+    partner = partner_of(y, c, z, x)
+    moves = z != 2 * c + y
     width = w_qkv.shape[0]
     barrier = pltpu.get_barrier_semaphore()
 
     @pl.when(moves)
     def _():
-        pl.semaphore_signal(barrier, inc=1, device_id=owner, device_id_type=MESH_ID)
-        pl.semaphore_signal(barrier, inc=1, device_id=worker, device_id_type=MESH_ID)
+        pl.semaphore_signal(barrier, inc=1, device_id=partner, device_id_type=MESH_ID)
 
     layer = others()
-    line = [(y, c, lax.rem(z + dz, 4), x) for dz in (1, 2, 3)]
+    line = line_of()
     for peer in layer + line:
         pl.semaphore_signal(barrier, inc=1, device_id=peer, device_id_type=MESH_ID)
-    pl.semaphore_wait(barrier, len(layer + line) + 2 * moves.astype(jnp.int32))
+    pl.semaphore_wait(barrier, len(layer + line) + moves.astype(jnp.int32))
 
     def produce(turn, to_y, to_c, to_x, out):
         at = place_of(to_y, to_c, to_x)
@@ -870,7 +724,7 @@
     terms[1] = mlp_term[...]
     terms[0] = jnp.zeros_like(mlp_term)
     trades = [
-        remote(own.at[pl.ds(half * HALF, HALF)], grad_low.at[pl.ds(half * HALF, HALF)], send.at[half], recv.at[half], owner)
+        remote(own.at[pl.ds(half * HALF, HALF)], grad_low.at[pl.ds(half * HALF, HALF)], send.at[half], recv.at[half], partner)
         for half in (0, 1)
     ]
     keeps = [
@@ -954,27 +808,242 @@
     )(d_qkv, w_qkv, x_own, d_resid, gain, mlp_term)
 
 
+def doc_start(ends, place):
+    start = jnp.zeros_like(place)
+    for k in range(8):
+        start = jnp.where(ends[k] <= place, ends[k], start)
+    return jnp.where(place < ends[7], start, LEN)
+
+
+def sigmoid_of(raw):
+    return pl.reciprocal(1.0 + jnp.exp2(math.log2(LEN) - raw * (math.log2(math.e) / math.sqrt(HD))), approx=True)
+
+
+def tile_at(index):
+    return pl.ds(pl.multiple_of(index * TILE, TILE), TILE)
+
+
+def head_of(array, rows, part, head):
+    first = (part * (array.shape[1] // 3) // HD + head) * HD
+    return array[rows, first : first + HD]
+
+
+def attend_kernel(ends, qkv, upstream, out, upstream_whole, total, send, recv, local):
+    i = pl.program_id(0)
+    y, c, z, x = spot()
+    heads = qkv.shape[1] // (3 * HD)
+    gather = Gather(lambda half: upstream.at[pl.ds(half * HALF, HALF)], upstream_whole, send, recv)
+    keep = pltpu.make_async_copy(upstream, upstream_whole.at[place_of(y, c, x)], local.at[0])
+
+    @pl.when(i == 0)
+    def _():
+        greet(near())
+        gather.start(0)
+        gather.start(1)
+        keep.start()
+
+    @pl.when(i == 6)
+    def _():
+        gather.pass_first()
+
+    total[...] = jnp.zeros_like(total)
+    q_place = i * TILE + lax.broadcasted_iota(jnp.int32, (TILE, 1), 0)
+    q_start = doc_start(ends, q_place)
+
+    def tile(j, diagonal):
+        k_place = j * TILE + lax.broadcasted_iota(jnp.int32, (1, TILE), 1)
+        allowed = k_place >= q_start
+        if diagonal:
+            allowed = allowed & (k_place <= q_place)
+        for head in range(heads):
+            raw = dot_nt(head_of(qkv, tile_at(i), 0, head), head_of(qkv, tile_at(j), 1, head))
+            weight = jnp.where(allowed, sigmoid_of(raw), 0.0).astype(LOW)
+            total[head] += dot_wide(weight, head_of(qkv, tile_at(j), 2, head))
+
+    def step(j, carry):
+        tile(j, False)
+        return carry
+
+    lax.fori_loop(0, i, step, 0)
+    tile(i, True)
+    for head in range(heads):
+        out[tile_at(i), head * HD : (head + 1) * HD] = total[head].astype(LOW)
+
+    @pl.when(i == LEN // TILE - 1)
+    def _():
+        gather.pass_second()
+        gather.pass_far()
+        gather.finish()
+        keep.wait()
+
+
+def out_turns():
+    y, c, z, x = spot()
+    owners = [((y, c, 2 * x + j // 2, j % 2), (z == 2 * x + j // 2) & (x == j % 2)) for j in range(4)]
+    holders = [((y, c, j, z // 2), (z == j) & (x == z // 2)) for j in range(4)]
+    return owners, holders
+
+
+def attend_back_kernel(
+    ends, qkv, grads, up_grad, out_grad, out, up_parts, out_parts, query_total, key_total, value_total, line_send, line_recv, send, recv
+):
+    j = pl.program_id(0)
+    y, c, z, x = spot()
+    heads = qkv.shape[1] // (3 * HD)
+    shard = out_grad.shape[0] // 4
+    owners, holders = out_turns()
+    to_layers = spread_columns(up_grad, up_parts, line_send, line_recv)
+
+    def to_owner(turn):
+        return remote(out_grad.at[pl.ds(turn * shard, shard)], out_parts.at[z], send.at[turn], recv.at[z], owners[turn][0])
+
+    def to_self(turn):
+        return pltpu.make_async_copy(out_grad.at[pl.ds(turn * shard, shard)], out_parts.at[z], recv.at[z])
+
+    @pl.when(j == 0)
+    def _():
+        query_total[...] = jnp.zeros_like(query_total)
+        barrier = pltpu.get_barrier_semaphore()
+        for peer in line_of():
+            pl.semaphore_signal(barrier, inc=1, device_id=peer, device_id_type=MESH_ID)
+        for peer, here in holders:
+
+            @pl.when(jnp.logical_not(here))
+            def _():
+                pl.semaphore_signal(barrier, inc=1, device_id=peer, device_id_type=MESH_ID)
+
+        pl.semaphore_wait(barrier, 7 - (x == z // 2).astype(jnp.int32))
+        for copy in to_layers:
+            copy.start()
+        for turn in range(4):
+
+            @pl.when(jnp.logical_not(owners[turn][1]))
+            def _():
+                to_owner(turn).start()
+
+            @pl.when(owners[turn][1])
+            def _():
+                to_self(turn).start()
+
+    key_total[...] = jnp.zeros_like(key_total)
+    value_total[...] = jnp.zeros_like(value_total)
+    here = tile_at(j)
+    k_place = j * TILE + lax.broadcasted_iota(jnp.int32, (TILE, 1), 0)
+    turned = [head_of(qkv, here, 1, head).T for head in range(heads)]
+
+    def tile(i, diagonal):
+        q_place = i * TILE + lax.broadcasted_iota(jnp.int32, (1, TILE), 1)
+        allowed = k_place >= doc_start(ends, q_place)
+        if diagonal:
+            allowed = allowed & (k_place <= q_place)
+        for head in range(heads):
+            query, grad = head_of(qkv, tile_at(i), 0, head), grads[tile_at(i), head * HD : (head + 1) * HD]
+            sig = jnp.where(allowed, sigmoid_of(dot_nt(head_of(qkv, here, 1, head), query)), 0.0)
+            value_total[head] += dot_wide(sig.astype(LOW), grad)
+            d_score = (dot_nt(head_of(qkv, here, 2, head), grad) * (sig * (1.0 - sig))).astype(LOW)
+            key_total[head] += dot_wide(d_score, query)
+            query_total[head, :, tile_at(i)] += dot_wide(turned[head], d_score)
+
+    def step(i, carry):
+        tile(i, False)
+        return carry
+
+    tile(j, True)
+    lax.fori_loop(j + 1, LEN // TILE, step, 0)
+    scale = 1.0 / math.sqrt(HD)
+    for head in range(heads):
+        first = head * HD
+        out[here, heads * HD + first : (heads + 1) * HD + first] = (key_total[head] * scale).astype(LOW)
+        out[here, 2 * heads * HD + first : (2 * heads + 1) * HD + first] = value_total[head].astype(LOW)
+        out[here, first : first + HD] = (query_total[head, :, here] * scale).T.astype(LOW)
+
+    @pl.when(j == LEN // TILE - 1)
+    def _():
+        for copy in to_layers:
+            copy.wait()
+        for turn in range(4):
+
+            @pl.when(jnp.logical_not(owners[turn][1]))
+            def _():
+                to_owner(turn).wait_send()
+
+            @pl.when(jnp.logical_not(holders[turn][1]))
+            def _():
+                landed = out_parts.at[turn]
+                remote(landed, landed, send.at[turn], recv.at[turn], holders[turn][0]).wait_recv()
+
+            @pl.when(owners[turn][1])
+            def _():
+                to_self(turn).wait()
+
+
+def attend(ends, qkv, upstream):
+    places, width = qkv.shape
+    heads = width // (3 * HD)
+    whole = lambda columns: pl.BlockSpec((places, columns), lambda i: (0, 0))
+    return pl.pallas_call(
+        attend_kernel,
+        out_shape=(
+            jax.ShapeDtypeStruct((places, width // 3), LOW),
+            jax.ShapeDtypeStruct((places, upstream.shape[1]), LOW),
+        ),
+        grid=(places // TILE,),
+        in_specs=[
+            pl.BlockSpec(memory_space=pltpu.SMEM),
+            whole(width),
+            pl.BlockSpec(upstream.shape, lambda i: (0, 0)),
+        ],
+        out_specs=[whole(width // 3), anywhere()],
+        scratch_shapes=[pltpu.VMEM((heads, TILE, HD), jnp.float32), dma(GATHER_COPIES), dma(GATHER_COPIES), dma(1)],
+        compiler_params=remote_params(5),
+        cost_estimate=pl.CostEstimate(flops=0, bytes_accessed=200_000_000, transcendentals=0),
+    )(ends, qkv, upstream)
+
+
+def attend_back(ends, qkv, grads, up_grad, out_grad):
+    places, width = qkv.shape
+    heads = width // (3 * HD)
+    whole = lambda columns: pl.BlockSpec((places, columns), lambda j: (0, 0))
+    return pl.pallas_call(
+        attend_back_kernel,
+        out_shape=(
+            jax.ShapeDtypeStruct((places, width), LOW),
+            jax.ShapeDtypeStruct((3, up_grad.shape[0], up_grad.shape[1] // 4), LOW),
+            jax.ShapeDtypeStruct((4, out_grad.shape[0] // 4, out_grad.shape[1]), LOW),
+        ),
+        grid=(places // TILE,),
+        in_specs=[pl.BlockSpec(memory_space=pltpu.SMEM), whole(width), whole(width // 3), anywhere(), anywhere()],
+        out_specs=[whole(width), anywhere(), anywhere()],
+        scratch_shapes=[
+            pltpu.VMEM((heads, HD, places), jnp.float32),
+            pltpu.VMEM((heads, TILE, HD), jnp.float32),
+            pltpu.VMEM((heads, TILE, HD), jnp.float32),
+            dma(3),
+            dma(3),
+            dma(4),
+            dma(4),
+        ],
+        compiler_params=remote_params(6),
+        cost_estimate=pl.CostEstimate(flops=0, bytes_accessed=300_000_000, transcendentals=0),
+    )(ends, qkv, grads, up_grad, out_grad)
+
+
 LAYER = ("y", "c", "x")
+PLACES = ("c", "y", "x")
 ALL = ("y", "c", "z", "x")
 
 
-def gather_layer(part):
-    return lax.all_gather(part, LAYER, axis=0, tiled=True)
-
-
 def scatter_layer(whole):
-    return lax.psum_scatter(whole.astype(LOW), LAYER, scatter_dimension=0, tiled=True).astype(jnp.float32)
-
-
-def trade(part, back=False):
+    return lax.psum_scatter(whole.astype(LOW), PLACES, scatter_dimension=0, tiled=True).astype(jnp.float32)
+
+
+def trade(part):
     pairs = []
     for y in range(2):
         for c in range(2):
             for z in range(4):
                 for x in range(2):
-                    owner = ((y * 2 + c) * 4 + z) * 2 + x
-                    worker = ((((z + c) % 2) * 2 + z // 2) * 4 + 2 * y + c) * 2 + x
-                    pairs.append((worker, owner) if back else (owner, worker))
+                    pairs.append((((y * 2 + c) * 4 + z) * 2 + x, (((z % 2) * 2 + z // 2) * 4 + 2 * c + y) * 2 + x))
     return lax.ppermute(part, ALL, pairs)
 
 
@@ -996,21 +1065,21 @@
     layer_x, w_qkv, facts = begin(tokens.reshape(block, width), w_query, w_key, w_value, facts)
     full_gain_attn, full_gain_mlp = facts[:, :, :, 0, :shard].reshape(1, width), facts[:, :, :, 1, :shard].reshape(1, width)
     layer = lax.axis_index("z")
-    own_lengths = lax.dynamic_index_in_dim(facts[:, 0, 0, 2, : lengths.shape[1]], layer, 0, False).astype(jnp.int32)
-    ends = jnp.concatenate((jnp.cumsum(own_lengths), (layer % 2).astype(jnp.int32)[None]))
-    place = (4 * lax.axis_index("y") + 2 * lax.axis_index("c") + lax.axis_index("x")) * block
+    own_lengths = facts[:, 0, 0, 2, : lengths.shape[1]].reshape(2, 2, -1)
+    own_lengths = lax.dynamic_slice(own_lengths, (layer % 2, layer // 2, 0), (1, 1, own_lengths.shape[2]))[0, 0]
+    ends = jnp.cumsum(own_lengths.astype(jnp.int32))
+    place = (4 * lax.axis_index("c") + 2 * lax.axis_index("y") + lax.axis_index("x")) * block
     x_own = lax.dynamic_slice_in_dim(layer_x, place, block, 0)
     layer_normed = norm_forward(layer_x.astype(jnp.float32), full_gain_attn)[0].astype(LOW)
     out_rows = lax.all_gather(after(facts, w_out), ("z", "x"), axis=0, tiled=True)
     w_out_own = lax.dynamic_slice_in_dim(out_rows, lax.axis_index("x") * owned, owned, 0)
 
     qkv = dot_wide(layer_normed, w_qkv).astype(LOW)
-    attended = attend(ends, qkv)
+    upstream = trade(after(facts, cotangent)).reshape(block, width)
+    attended, layer_upstream = attend(ends, qkv, upstream)
     resid, layer_mlp, own_gate, own_up = close_attention(attended, w_out_own, x_own, full_gain_mlp, w_gate, w_up)
 
-    own_down = lax.all_gather(after(qkv, w_down), "z", axis=0, tiled=True)
-    upstream = trade(after(facts, cotangent)).reshape(block, width)
-    layer_upstream = gather_layer(upstream)
+    own_down = lax.all_gather(after(resid, w_down), "z", axis=0, tiled=True)
     gate = dot_wide(layer_mlp, own_gate)
     up_part = dot_wide(layer_mlp, own_up)
     sigmoid_gate = jax.nn.sigmoid(gate)
@@ -1020,23 +1089,23 @@
     d_gate, d_up = gate_backward(d_hidden, gate, up_part, sigmoid_gate)
     gate_term, up_term = contract_rows(layer_mlp, d_gate).astype(LOW), contract_rows(layer_mlp, d_up).astype(LOW)
 
-    def scatter_layers(whole, axis):
-        return lax.psum_scatter(whole, "z", scatter_dimension=axis, tiled=True).astype(jnp.float32)
-
-    grad_gate, grad_up, grad_down = scatter_layers(gate_term, 1), scatter_layers(up_term, 1), scatter_layers(down_term, 0)
-    d_resid, gain_mlp_term, layer_d_resid = close_mlp(
-        after((gate_term, up_term, down_term), d_gate), d_up, own_gate, own_up, resid, upstream, full_gain_mlp
-    )
+    grad_down = lax.psum_scatter(down_term, "z", scatter_dimension=0, tiled=True)
+    d_resid, gain_mlp_term, layer_d_resid, gate_parts = close_mlp(
+        after((up_term, grad_down), d_gate), d_up, own_gate, own_up, resid, upstream, full_gain_mlp, gate_term
+    )
+
+    def own_part(whole, parts):
+        own = lax.dynamic_slice_in_dim(whole, layer * parts.shape[2], parts.shape[2], 1)
+        return own.astype(jnp.float32) + jnp.sum(parts.astype(jnp.float32), axis=0)
+
     result = resid + scatter_layer(dot_wide(after(d_resid, hidden), own_down))
-    mixed = trade(result.astype(LOW).reshape(rows_here, block, width), back=True)
-
-    out_term = contract_rows(attended, layer_d_resid)
-    out_term = lax.dynamic_update_slice_in_dim(
-        jnp.zeros((2 * owned, width), LOW), out_term.astype(LOW), lax.axis_index("x") * owned, 0
-    )
-    grad_out = lax.psum_scatter(out_term, ("z", "x"), scatter_dimension=0, tiled=True).astype(jnp.float32)
+    mixed = trade(result.astype(LOW).reshape(rows_here, block, width))
+
+    out_term = contract_rows(attended, layer_d_resid).astype(LOW)
     d_attended = contract_cols(layer_d_resid, w_out_own).astype(LOW)
-    d_qkv = attend_back(ends, qkv, after(out_term, d_attended))
+    d_qkv, up_parts, out_parts = attend_back(ends, qkv, d_attended, up_term, out_term)
+    grad_gate, grad_up = own_part(gate_term, gate_parts), own_part(up_term, up_parts)
+    grad_out = jnp.sum(out_parts.astype(jnp.float32), axis=0)
     qkv_term = contract_rows(layer_normed, d_qkv).astype(LOW)
     grad_low, gain_grads = close_layer(
         after(qkv_term, d_qkv), w_qkv, x_own, d_resid, full_gain_attn, gain_mlp_term
@@ -1059,7 +1128,7 @@
         grad_out,
         grad_gate,
         grad_up,
-        grad_down,
+        grad_down.astype(jnp.float32),
         gain_grads[0],
         gain_grads[1],
     )

time: 1560 us -> 1360 us (0.87)
  waiting for transfers between devices: 254 us -> 67.8 us
  Pallas kernels: 971 us -> 945 us
    reduce_scatter x5 -> x2, waiting for transfers between devices: 247 us -> 27.4 us  [the longest x1 27.4 us: body_layers(): lax.psum_scatter(down_term, 'z', scatter_dimension=0, tiled=True)]
    pallas_call x1, Pallas kernels: 359 us -> 158 us  [close_attention(): pl.pallas_call(close_attention_kernel, out_shape=(jax.ShapeDtypeStruct((b...]
    pallas_call x2, Pallas kernels: 138 us -> 271 us  [the longest x1 141 us: attend(): pl.pallas_call(attend_kernel, out_shape=(jax.ShapeDtypeStruct((places, wi...]
    pallas_call x1, Pallas kernels: 158 us -> 218 us  [close_layer(): pl.pallas_call(close_layer_kernel, out_shape=(jax.ShapeDtypeStruct((block...]
    all_gather x2 -> x1, waiting for transfers between devices: 0.01 us -> 36.2 us  [body_layers(): own_down = lax.all_gather(after(resid, w_down), 'z', axis=0, tiled=True)]
    pallas_call x1, Pallas kernels: 152 us -> 130 us  [begin(): pl.pallas_call(begin_kernel, out_shape=(jax.ShapeDtypeStruct((8 * block,...]
  transfers between devices with their start and end apart: 12 -> 8, of which waited for: 5 -> 3; matrix products, arithmetic and copies ran while one was open for 10% -> 15% of each run, Pallas kernels for 42% -> 36%
where the time goes in v5:
time: 1360 us; the launch traced here: 1350 us
  Pallas kernels  945 us (69%)
  matrix products  240 us (18%)
  waiting for transfers between devices  67.8 us (5%)
  other arithmetic  31 us (2%)
  local copies, waits for them, and re-layouts  24.4 us (2%)
  starting transfers between devices  23.1 us (2%)
  between operations  14.3 us (1%)
    pallas_call x1, Pallas kernels, close_layer(): pl.pallas_call(close_layer_kernel, out_shape=(jax.ShapeDtypeStruct((block...  218 us
    pallas_call x1, Pallas kernels, close_mlp(): pl.pallas_call(close_mlp_kernel, out_shape=(jax.ShapeDtypeStruct((block,...  168 us
    pallas_call x1, Pallas kernels, close_attention(): pl.pallas_call(close_attention_kernel, out_shape=(jax.ShapeDtypeStruct((b...  158 us
    pallas_call x1, Pallas kernels, attend(): pl.pallas_call(attend_kernel, out_shape=(jax.ShapeDtypeStruct((places, wi...  141 us
    pallas_call x1, Pallas kernels, attend_back(): pl.pallas_call(attend_back_kernel, out_shape=(jax.ShapeDtypeStruct((place...  130 us
    pallas_call x1, Pallas kernels, begin(): pl.pallas_call(begin_kernel, out_shape=(jax.ShapeDtypeStruct((8 * block,...  130 us
    dot_general x5, matrix products, contract_rows(): lax.dot_general(left, right, (((0,), (0,)), ((), ())), preferred_element_...  104 us
    dot_general x4, matrix products, dot_wide(): return jnp.dot(left, right, preferred_element_type=jnp.float32)  87.7 us
  transfers between devices with their start and end apart: 8, of which 3 were waited for; matrix products, arithmetic and copies ran while one was open for 15% of the time, Pallas kernels for 36%

profile of v5, /device:TPU:0, one launch (start us, length us, event | category | flops | bytes accessed | tf_op | source)
XLA Modules:
  0.0 1345.2 jit_solution(10347978463442058266)
XLA Ops:
  7.2 0.7 convert_element_type.92
  7.9 0.7 bitcast_convert_fusion.1
  8.5 0.7 pad_convert_fusion
  9.2 0.1 scatter.19
  9.3 0.2 scatter.20.facts
  9.5 0.6 copy-done.8
  10.1 129.9 %shard_map.203 = (bf16[4096,2048]{1,0:T(8,128)(2,1)}, bf16[4,4,128,768]{3,2,1,0:T(8,128)(2,1)}, f32[4,4,2,8,128]{4,3,2,1,0:T(8,128)}) custom-call(bf16[2,256,2048]{2,1,0:T(8,128)(2,1)} %bitcast.63, bf16[64,2048]{1,0:T(8,128)(2,1)} %w_query.1, bf16[64,2048]{1,0:T(8,128)(2,1)} %w_key.1, bf16[64,2048]{1,0:T(8,128)(2,1)} %w_value.1, f32[8,128]{1,0:T(8,128)} %copy-done.8), custom_call_target="tpu_custom_call" | custom-call | bytes 350000000 | tf_op jit(solution)/shard_map/pallas_call | solution.py:502
  140.0 0.0 all-gather.5.cloned.1.call-start
  140.1 2.3 collective-permute-start
  142.3 0.7 slice.74
  143.0 1.6 slice_reduce_fusion
  144.7 7.2 fusion
  151.9 0.7 reshape_squeeze.10.gain
  152.6 0.7 reduce-window.9
  153.3 0.1 mul.61
  153.4 3.2 constant_dynamic-slice_fusion.2.x_own
  156.5 19.9 %convolution_convert_fusion.1.qkv = bf16[4096,768]{1,0:T(8,128)(2,1)} fusion(bf16[2048,768]{1,0:T(8,128)(2,1)} %bitcast.60, bf16[4096,2048]{1,0:T(8,128)(2,1)} %get-tuple-element.72, f32[2048]{0:T(1024)S(1)} %mul.61, f32[4096]{0:T(1024)S(1)} %add_rsqrt_fusion), kind=kOutput, calls=%fused_computation.10 | convolution fusion | flops 12921602048 | bytes 26238976 | tf_op jit(solution)/shard_map/dot_general | solution.py:86
  176.5 1.3 copy-done.1
  177.8 141.1 %shard_map.204 = (bf16[4096,256]{1,0:T(8,128)(2,1)}, bf16[4096,2048]{1,0:T(8,128)(2,1)}) custom-call(s32[8]{0:T(128)} %bitcast.73, bf16[4096,768]{1,0:T(8,128)(2,1)} %convolution_convert_fusion.1.qkv, bf16[512,2048]{1,0:T(8,128)(2,1)} %bitcast.57), custom_call_target="tpu_custom_call" | custom-call | bytes 200000000 | tf_op jit(solution)/shard_map/pallas_call | solution.py:984
  318.9 2.3 constant_dynamic-slice_fusion.3.w_out
  321.2 158.4 %shard_map.205 = (f32[512,2048]{1,0:T(8,128)}, bf16[4096,2048]{1,0:T(8,128)(2,1)}, bf16[2048,1024]{1,0:T(8,128)(2,1)}, bf16[2048,1024]{1,0:T(8,128)(2,1)}) custom-call(bf16[4096,256]{1,0:T(8,128)(2,1)} %get-tuple-element.75.attended, bf16[256,2048]{1,0:T(8,128)(2,1)} %constant_dynamic-slice_fusion.3.w_out, ...), custom_call_target="tpu_custom_call" | custom-call | bytes 450000000 | tf_op jit(solution)/shard_map/pallas_call | solution.py:588
  479.6 0.0 reduce-scatter.4.cloned.1.call-start
  479.7 23.5 %fusion.15 = f32[4096,1024]{1,0:T(8,128)} fusion(bf16[4096,2048]{1,0:T(8,128)(2,1)} %get-tuple-element.78, bf16[2048,1024]{1,0:T(8,128)(2,1)} %get-tuple-element.81.w_gate), kind=kOutput, calls=%fused_computation.41 | convolution fusion | flops 17179869184 | bytes 37748736 | tf_op jit(solution)/shard_map/dot_general | solution.py:86
  503.3 20.8 %fusion.16 = f32[4096,1024]{1,0:T(8,128)} fusion(bf16[4096,2048]{1,0:T(8,128)(2,1)S(1)} %copy-done.13, bf16[2048,1024]{1,0:T(8,128)(2,1)S(1)} %copy-done.2), kind=kOutput, calls=%fused_computation.42 | convolution fusion | flops 17179869184 | bytes 37748736 | tf_op jit(solution)/shard_map/dot_general | solution.py:86
  524.1 36.2 %all-gather.5.cloned.1.call-done = bf16[1024,2048]{1,0:T(8,128)(2,1)} async-done(((bf16[256,2048]{1,0:T(8,128)(2,1)}), bf16[1024,2048]{1,0:T(8,128)(2,1)}) %all-gather.5.cloned.1.call-update) | async-done | bytes 4194320 | tf_op jit(solution)/shard_map/all_gather | solution.py:1082
  560.3 36.4 %multiply_convert_fusion = (bf16[4096,1024]{1,0:T(8,128)(2,1)}, bf16[4096,1024]{1,0:T(8,128)(2,1)}, bf16[4096,1024]{1,0:T(8,128)(2,1)}) fusion(f32[4096,1024]{1,0:T(8,128)} %fusion.15, f32[4096,1024]{1,0:T(8,128)} %fusion.16, bf16[4096,2048]{1,0:T(8,128)(2,1)} %get-tuple-element.79, bf16[1024,2048]{1,0:T(8,128)(2,1)} %all-gather.5.cloned.1.call-done), kind=kOutput, calls=%fused_computation.5 | convolution fusion | flops 17246978048 | bytes 79691776 | tf_op jit(solution)/shard_map/dot_general | solution.py:26
  596.7 23.8 %convolution_convert_fusion.4 = bf16[1024,2048]{1,0:T(8,128)(2,1)} fusion(bf16[4096,1024]{1,0:T(8,128)(2,1)} %get-tuple-element.85, bf16[4096,2048]{1,0:T(8,128)(2,1)} %get-tuple-element.79), kind=kOutput, calls=%fused_computation.17 | convolution fusion | flops 17181966336 | bytes 29360128 | tf_op jit(solution)/shard_map/dot_general | solution.py:20
  620.5 0.0 reduce-scatter.6.cloned.1.call-start
  620.6 24.2 %convolution_convert_fusion.5.up_grad = bf16[2048,1024]{1,0:T(8,128)(2,1)} fusion(bf16[4096,2048]{1,0:T(8,128)(2,1)} %get-tuple-element.78, bf16[4096,1024]{1,0:T(8,128)(2,1)} %get-tuple-element.99.d_up), kind=kOutput, calls=%fused_computation.18 | convolution fusion | flops 17181966336 | bytes 29360128 | tf_op jit(solution)/shard_map/dot_general | solution.py:20
  644.8 23.8 %convolution_convert_fusion.3.grad = bf16[2048,1024]{1,0:T(8,128)(2,1)} fusion(bf16[4096,2048]{1,0:T(8,128)(2,1)} %get-tuple-element.78, bf16[4096,1024]{1,0:T(8,128)(2,1)} %get-tuple-element.83.d_gate), kind=kOutput, calls=%fused_computation.16 | convolution fusion | flops 17181966336 | bytes 29360128 | tf_op jit(solution)/shard_map/dot_general | solution.py:20
  668.6 27.4 %reduce-scatter.4.cloned.1.call-done = bf16[256,2048]{1,0:T(8,128)(2,1)} async-done(((bf16[1024,2048]{1,0:T(8,128)(2,1)}), bf16[256,2048]{1,0:T(8,128)(2,1)}) %reduce-scatter.4.cloned.1.call-update) | async-done | bytes 1048592 | tf_op jit(solution)/shard_map/reduce_scatter | solution.py:1092
  696.0 167.7 %shard_map.206 = (f32[512,2048]{1,0:T(8,128)}, f32[8,2048]{1,0:T(8,128)}, bf16[4096,2048]{1,0:T(8,128)(2,1)}, bf16[3,2048,256]{2,1,0:T(8,128)(2,1)}) custom-call(bf16[4096,1024]{1,0:T(8,128)(2,1)} %get-tuple-element.83.d_gate, bf16[4096,1024]{1,0:T(8,128)(2,1)} %get-tuple-element.99.d_up, bf16[2048,1024]{1,0:T(8,128)(2,1)} %get-tuple-element.81.w_gate, ...), custom_call_target="tpu_custom_call" | custom-call | bytes 450000000 | tf_op jit(solution)/shard_map/pallas_call | solution.py:676
  863.7 23.5 %convolution_convert_fusion = bf16[4096,2048]{1,0:T(8,128)(2,1)} fusion(bf16[4096,1024]{1,0:T(8,128)(2,1)} %get-tuple-element.85, bf16[1024,2048]{1,0:T(8,128)(2,1)} %all-gather.5.cloned.1.call-done), kind=kOutput, calls=%fused_computation.9 | convolution fusion | flops 17188257792 | bytes 29360128 | tf_op jit(solution)/shard_map/dot_general | solution.py:86
  887.1 0.0 reduce-scatter.8.cloned.1.call-start
  887.2 1.1 copy-done.3
  888.3 11.6 convolution_convert_fusion.2.grads
  899.9 12.3 convolution_convert_fusion.6.out_grad
  912.2 129.9 %shard_map.207 = (bf16[4096,768]{1,0:T(8,128)(2,1)}, bf16[3,2048,256]{2,1,0:T(8,128)(2,1)}, bf16[4,64,2048]{2,1,0:T(8,128)(2,1)}) custom-call(s32[8]{0:T(128)} %bitcast.74, bf16[4096,768]{1,0:T(8,128)(2,1)} %convolution_convert_fusion.1.qkv, bf16[4096,256]{1,0:T(8,128)(2,1)} %convolution_convert_fusion.2.grads, ...), custom_call_target="tpu_custom_call" | custom-call | bytes 300000000 | tf_op jit(solution)/shard_map/pallas_call | solution.py:1007
  1042.2 20.1 %fusion.6 = bf16[2048,768]{1,0:T(8,128)(2,1)S(1)} fusion(bf16[4096,768]{1,0:T(8,128)(2,1)} %get-tuple-element.88.d_qkv, bf16[4096,2048]{1,0:T(8,128)(2,1)} %get-tuple-element.72, f32[2048]{0:T(1024)S(1)} %copy-done.12, f32[4096]{0:T(1024)S(1)} %copy-done.10), kind=kOutput, calls=%fused_computation.19 | convolution fusion | flops 12920029184 | bytes 26238976 | tf_op jit(solution)/shard_map/dot_general | solution.py:20
  1062.3 1.9 copy.24
  1064.2 0.7 reshape_squeeze.11.gain
  1064.9 217.7 %shard_map.208 = (bf16[512,2048]{1,0:T(8,128)(2,1)}, f32[2,8,128]{2,1,0:T(8,128)}) custom-call(bf16[4096,768]{1,0:T(8,128)(2,1)} %get-tuple-element.88.d_qkv, bf16[2048,768]{1,0:T(8,128)(2,1)} %bitcast.61, bf16[512,2048]{1,0:T(8,128)(2,1)} %constant_dynamic-slice_fusion.2.x_own, f32[512,2048]{1,0:T(8,128)} %get-tuple-element.84.d_resid, ...), custom_call_target="tpu_custom_call" | custom-call | bytes 350000000 | tf_op jit(solution)/shard_map/pallas_call | solution.py:792
  1282.7 0.8 reduce_sum.49
  1283.5 0.1 reshape.202
  1283.6 2.6 convert_reduce_fusion
  1286.2 5.0 fusion.9
  1291.2 17.1 %collective-permute-start.1 = (bf16[1,512,2048]{2,1,0:T(8,128)(2,1)}, bf16[1,512,2048]{2,1,0:T(8,128)(2,1)}, u32[]{:S(2)}, u32[]{:S(2)}) collective-permute-start(bf16[1,512,2048]{2,1,0:T(8,128)(2,1)} %fusion.9), channel_id=1, source_target_pairs={{0,0},{1,1},{2,16},{3,17},{4,8},{5,9},{6,24},{7,25},{8,4},{9,5},{1... | collective-permute-start | bytes 6291464 | tf_op jit(solution)/shard_map/ppermute | solution.py:1047
  1308.3 0.9 convert_reduce_fusion.2
  1309.3 1.8 convert_reduce_fusion.1
  1311.1 2.5 bitcast_convert_fusion
  1313.6 3.5 all-to-all-start
  1317.2 0.5 fusion.12
  1317.7 2.8 convert_element_type.118
  1320.5 4.7 convert_add_fusion
  1325.1 4.1 all-to-all-done
  1329.2 0.9 reshape.206
  1330.1 1.5 fusion.14
  1331.6 0.3 copy.27
  1331.9 1.0 copy.30
  1332.8 0.3 copy.26
  1333.1 1.0 copy.29
  1334.1 0.3 copy.25
  1334.4 1.0 copy.28
  1335.4 3.2 copy.34
  (38 shorter events, 0.2 us)
Async XLA Ops:
  7.2 311.7 %all-gather.3.cloned.1.call-start = ((), (), s32[]{:S(2)}) async-start(), calls=%async_computation.4 | async-start | bytes 2359296 | tf_op jit(solution)/shard_map/all_gather | solution.py:1074
  9.5 0.6 copy-start.8
  140.0 420.3 %all-gather.5.cloned.1.call-start = ((), (), s32[]{:S(2)}) async-start(), calls=%async_computation.5 | async-start | bytes 5242880 | tf_op jit(solution)/shard_map/all_gather | solution.py:1082
  140.1 36.4 %collective-permute-start = (bf16[1,512,2048]{2,1,0:T(8,128)(2,1)}, bf16[1,512,2048]{2,1,0:T(8,128)(2,1)S(1)}, u32[]{:S(2)}, u32[]{:S(2)}) collective-permute-start(bf16[1,512,2048]{2,1,0:T(8,128)(2,1)} %param.20), channel_id=1, source_target_pairs={{0,0},{1,1},{2,16},{3,17},{4,8},{5,9},{6,24},{7,25},{8,4},{9,5},{1... | collective-permute-start | bytes 6291464 | tf_op jit(solution)/shard_map/ppermute | solution.py:1047
  153.4 23.1 %copy-start.11 = (f32[2048]{0:T(1024)}, f32[2048]{0:T(1024)S(1)}, u32[]{:S(2)}) copy-start(f32[2048]{0:T(1024)S(1)} %mul.61) | copy-start | bytes 24580
  153.4 23.1 %copy-start.9 = (f32[4096]{0:T(1024)}, f32[4096]{0:T(1024)S(1)}, u32[]{:S(2)}) copy-start(f32[4096]{0:T(1024)S(1)} %add_rsqrt_fusion) | copy-start | bytes 49156
  176.5 1.3 copy-start.1
  479.6 216.3 %reduce-scatter.4.cloned.1.call-start = ((), (), s32[]{:S(2)}) async-start(), calls=%async_computation.6 | async-start | bytes 5242880 | tf_op jit(solution)/shard_map/reduce_scatter | solution.py:1092
  479.7 23.6 %copy-start.2 = (bf16[2048,1024]{1,0:T(8,128)(2,1)S(1)}, bf16[2048,1024]{1,0:T(8,128)(2,1)}, u32[]{:S(2)}) copy-start(bf16[2048,1024]{1,0:T(8,128)(2,1)} %get-tuple-element.82.w_up) | copy-start | bytes 12582916
  479.7 23.5 %copy-start.13 = (bf16[4096,2048]{1,0:T(8,128)(2,1)S(1)}, bf16[4096,2048]{1,0:T(8,128)(2,1)}, u32[]{:S(2)}) copy-start(bf16[4096,2048]{1,0:T(8,128)(2,1)} %get-tuple-element.78) | copy-start | bytes 50331652
  620.5 665.6 %reduce-scatter.6.cloned.1.call-start = ((), (), s32[]{:S(2)}) async-start(), calls=%async_computation.7 | async-start | bytes 18874368 | tf_op jit(solution)/shard_map/reduce_scatter | solution.py:1037
  887.1 1.2 copy-start.3
  887.1 426.5 %reduce-scatter.8.cloned.1.call-start = ((), (), s32[]{:S(2)}) async-start(), calls=%async_computation.8 | async-start | bytes 3932160 | tf_op jit(solution)/shard_map/reduce_scatter | solution.py:1117
  888.3 11.6 copy-start
  912.2 130.0 %copy-start.10 = (f32[4096]{0:T(1024)S(1)}, f32[4096]{0:T(1024)}, u32[]{:S(2)}) copy-start(f32[4096]{0:T(1024)} %copy-done.9) | copy-start | bytes 49156
  912.2 130.0 %copy-start.12 = (f32[2048]{0:T(1024)S(1)}, f32[2048]{0:T(1024)}, u32[]{:S(2)}) copy-start(f32[2048]{0:T(1024)} %copy-done.11) | copy-start | bytes 24580
  1062.3 1.9 copy-start.7
  1282.7 25.7 %copy-start.6 = (bf16[4,64,2048]{2,1,0:T(8,128)(2,1)S(1)}, bf16[4,64,2048]{2,1,0:T(8,128)(2,1)}, u32[]{:S(2)}) copy-start(bf16[4,64,2048]{2,1,0:T(8,128)(2,1)} %get-tuple-element.91) | copy-start | bytes 3145732
  1286.2 23.1 %copy-start.4 = (bf16[3,2048,256]{2,1,0:T(8,128)(2,1)S(1)}, bf16[3,2048,256]{2,1,0:T(8,128)(2,1)}, u32[]{:S(2)}) copy-start(bf16[3,2048,256]{2,1,0:T(8,128)(2,1)} %get-tuple-element.92) | copy-start | bytes 9437188
  1286.2 24.9 %copy-start.5 = (bf16[512,2048]{1,0:T(8,128)(2,1)S(1)}, bf16[512,2048]{1,0:T(8,128)(2,1)}, u32[]{:S(2)}) copy-start(bf16[512,2048]{1,0:T(8,128)(2,1)} %get-tuple-element.90) | copy-start | bytes 6291460
  1291.2 44.1 %collective-permute-start.1 = (bf16[1,512,2048]{2,1,0:T(8,128)(2,1)}, bf16[1,512,2048]{2,1,0:T(8,128)(2,1)}, u32[]{:S(2)}, u32[]{:S(2)}) collective-permute-start(bf16[1,512,2048]{2,1,0:T(8,128)(2,1)} %fusion.9), channel_id=1, source_target_pairs={{0,0},{1,1},{2,16},{3,17},{4,8},{5,9},{6,24},{7,25},{8,4},{9,5},{1... | collective-permute-start | bytes 6291464 | tf_op jit(solution)/shard_map/ppermute | solution.py:1047
  1313.6 15.6 %all-to-all-start = ((bf16[8,64,768]{2,1,0:T(8,128)(2,1)}), bf16[8,64,768]{2,1,0:T(8,128)(2,1)S(1)}, u32[]{:S(2)}, u32[]{:S(2)}) async-start(bf16[8,64,768]{2,1,0:T(8,128)(2,1)} %bitcast.67), calls=%async_computation.3 | async-start | bytes 1572864 | tf_op jit(solution)/shard_map/all_to_all | solution.py:1118
Sparse Core Ops, SparseCore 0:
  140.1 85.5 all-gather.2
  479.8 80.5 all-gather.4
  620.7 75.2 reduce-scatter.3
  887.3 128.2 reduce-scatter.5
  1064.4 75.0 reduce-scatter.7

commit v6 on v5

--- a/solution.py
+++ b/solution.py
@@ -616,7 +616,7 @@
 
 
 def close_mlp_kernel(
-    d_gate, d_up, w_gate, w_up, resid, upstream, gain, grad, d_resid, gain_term, d_resid_whole, grad_parts, own, blocks, *scratch
+    d_gate, d_up, w_gate, w_up, resid, upstream, gain, grad_a, grad_b, d_resid, gain_term, d_resid_whole, parts_a, parts_b, own, blocks, *scratch
 ):
     scatter, (send, recv, local, fetched, line_send, line_recv) = scratch[:7], scratch[7:]
     y, c, z, x = spot()
@@ -634,7 +634,11 @@
     for copy in fetch(0):
         copy.start()
     greet(near() + tuple(line_of()))
-    to_layers = spread_columns(grad, grad_parts, line_send, line_recv)
+    to_layers = [
+        copy
+        for k, (grad, parts) in enumerate(((grad_a, parts_a), (grad_b, parts_b)))
+        for copy in spread_columns(grad, parts, line_send.at[k], line_recv.at[k])
+    ]
     for copy in to_layers:
         copy.start()
 
@@ -670,7 +674,7 @@
         copy.wait()
 
 
-def close_mlp(d_gate, d_up, w_gate, w_up, resid, upstream, gain, grad):
+def close_mlp(d_gate, d_up, w_gate, w_up, resid, upstream, gain, *grads):
     block, width = resid.shape
     hidden = d_gate.shape[1]
     return pl.pallas_call(
@@ -680,15 +684,16 @@
             jax.ShapeDtypeStruct((8, width), jnp.float32),
             jax.ShapeDtypeStruct((8 * block, width), LOW),
             jax.ShapeDtypeStruct((3, width, hidden // 4), LOW),
+            jax.ShapeDtypeStruct((3, width, hidden // 4), LOW),
         ),
-        in_specs=[anywhere()] * 2 + [in_vmem()] * 5 + [anywhere()],
-        out_specs=[in_vmem(), in_vmem(), anywhere(), anywhere()],
+        in_specs=[anywhere()] * 2 + [in_vmem()] * 5 + [anywhere()] * 2,
+        out_specs=[in_vmem(), in_vmem()] + [anywhere()] * 3,
         scratch_shapes=[pltpu.VMEM((block, width), LOW), pltpu.VMEM((2, 2, block, hidden), LOW)]
         + scatter_scratch(width)
-        + [dma(GATHER_COPIES), dma(GATHER_COPIES), dma(1), dma(2, 2), dma(3), dma(3)],
+        + [dma(GATHER_COPIES), dma(GATHER_COPIES), dma(1), dma(2, 2), dma(2, 3), dma(2, 3)],
         compiler_params=remote_params(3),
         cost_estimate=pl.CostEstimate(flops=0, bytes_accessed=450_000_000, transcendentals=0),
-    )(d_gate, d_up, w_gate, w_up, resid, upstream, gain, grad)
+    )(d_gate, d_up, w_gate, w_up, resid, upstream, gain, *grads)
 
 
 def close_layer_kernel(d_qkv, w_qkv, x_own, d_resid, gain, mlp_term, grad_low, gain_grads, own, terms, layer_terms, part, column_terms, *scratch):
@@ -828,24 +833,9 @@
     return array[rows, first : first + HD]
 
 
-def attend_kernel(ends, qkv, upstream, out, upstream_whole, total, send, recv, local):
+def attend_kernel(ends, qkv, out, total):
     i = pl.program_id(0)
-    y, c, z, x = spot()
     heads = qkv.shape[1] // (3 * HD)
-    gather = Gather(lambda half: upstream.at[pl.ds(half * HALF, HALF)], upstream_whole, send, recv)
-    keep = pltpu.make_async_copy(upstream, upstream_whole.at[place_of(y, c, x)], local.at[0])
-
-    @pl.when(i == 0)
-    def _():
-        greet(near())
-        gather.start(0)
-        gather.start(1)
-        keep.start()
-
-    @pl.when(i == 6)
-    def _():
-        gather.pass_first()
-
     total[...] = jnp.zeros_like(total)
     q_place = i * TILE + lax.broadcasted_iota(jnp.int32, (TILE, 1), 0)
     q_start = doc_start(ends, q_place)
@@ -869,7 +859,36 @@
     for head in range(heads):
         out[tile_at(i), head * HD : (head + 1) * HD] = total[head].astype(LOW)
 
-    @pl.when(i == LEN // TILE - 1)
+
+def open_mlp_kernel(normed, w_gate, w_up, upstream, gate, up, hidden, upstream_whole, send, recv, local):
+    i = pl.program_id(0)
+    y, c, z, x = spot()
+    steps = pl.num_programs(0)
+    gather = Gather(lambda half: upstream.at[pl.ds(half * HALF, HALF)], upstream_whole, send, recv)
+    keep = pltpu.make_async_copy(upstream, upstream_whole.at[place_of(y, c, x)], local.at[0])
+
+    @pl.when(i == 0)
+    def _():
+        greet(near())
+        gather.start(0)
+        gather.start(1)
+        keep.start()
+
+    @pl.when(i == steps - 3)
+    def _():
+        gather.pass_first()
+
+    def step(n, carry):
+        columns = pl.ds(pl.multiple_of(n * HALF, HALF), HALF)
+        gate_part, up_part = dot_wide(normed[...], w_gate[:, columns]), dot_wide(normed[...], w_up[:, columns])
+        gate[:, columns] = gate_part
+        up[:, columns] = up_part
+        hidden[:, columns] = (gate_part * jax.nn.sigmoid(gate_part) * up_part).astype(LOW)
+        return carry
+
+    lax.fori_loop(0, w_gate.shape[1] // HALF, step, 0)
+
+    @pl.when(i == steps - 1)
     def _():
         gather.pass_second()
         gather.pass_far()
@@ -877,6 +896,28 @@
         keep.wait()
 
 
+def open_mlp(normed, w_gate, w_up, upstream):
+    places, width = normed.shape
+    hidden = w_gate.shape[1]
+    rows = lambda columns: pl.BlockSpec((TILE, columns), lambda i: (i, 0))
+    whole = lambda array: pl.BlockSpec(array.shape, lambda i: (0, 0))
+    return pl.pallas_call(
+        open_mlp_kernel,
+        out_shape=(
+            jax.ShapeDtypeStruct((places, hidden), jnp.float32),
+            jax.ShapeDtypeStruct((places, hidden), jnp.float32),
+            jax.ShapeDtypeStruct((places, hidden), LOW),
+            jax.ShapeDtypeStruct((places, width), LOW),
+        ),
+        grid=(places // TILE,),
+        in_specs=[rows(width), whole(w_gate), whole(w_up), whole(upstream)],
+        out_specs=[rows(hidden), rows(hidden), rows(hidden), anywhere()],
+        scratch_shapes=[dma(GATHER_COPIES), dma(GATHER_COPIES), dma(1)],
+        compiler_params=remote_params(5),
+        cost_estimate=pl.CostEstimate(flops=0, bytes_accessed=250_000_000, transcendentals=0),
+    )(normed, w_gate, w_up, upstream)
+
+
 def out_turns():
     y, c, z, x = spot()
     owners = [((y, c, 2 * x + j // 2, j % 2), (z == 2 * x + j // 2) & (x == j % 2)) for j in range(4)]
@@ -885,14 +926,13 @@
 
 
 def attend_back_kernel(
-    ends, qkv, grads, up_grad, out_grad, out, up_parts, out_parts, query_total, key_total, value_total, line_send, line_recv, send, recv
+    ends, qkv, grads, out_grad, out, out_parts, query_total, key_total, value_total, send, recv
 ):
     j = pl.program_id(0)
     y, c, z, x = spot()
     heads = qkv.shape[1] // (3 * HD)
     shard = out_grad.shape[0] // 4
     owners, holders = out_turns()
-    to_layers = spread_columns(up_grad, up_parts, line_send, line_recv)
 
     def to_owner(turn):
         return remote(out_grad.at[pl.ds(turn * shard, shard)], out_parts.at[z], send.at[turn], recv.at[z], owners[turn][0])
@@ -904,17 +944,13 @@
     def _():
         query_total[...] = jnp.zeros_like(query_total)
         barrier = pltpu.get_barrier_semaphore()
-        for peer in line_of():
-            pl.semaphore_signal(barrier, inc=1, device_id=peer, device_id_type=MESH_ID)
         for peer, here in holders:
 
             @pl.when(jnp.logical_not(here))
             def _():
                 pl.semaphore_signal(barrier, inc=1, device_id=peer, device_id_type=MESH_ID)
 
-        pl.semaphore_wait(barrier, 7 - (x == z // 2).astype(jnp.int32))
-        for copy in to_layers:
-            copy.start()
+        pl.semaphore_wait(barrier, 4 - (x == z // 2).astype(jnp.int32))
         for turn in range(4):
 
             @pl.when(jnp.logical_not(owners[turn][1]))
@@ -959,8 +995,6 @@
 
     @pl.when(j == LEN // TILE - 1)
     def _():
-        for copy in to_layers:
-            copy.wait()
         for turn in range(4):
 
             @pl.when(jnp.logical_not(owners[turn][1]))
@@ -977,30 +1011,23 @@
                 to_self(turn).wait()
 
 
-def attend(ends, qkv, upstream):
+def attend(ends, qkv):
     places, width = qkv.shape
     heads = width // (3 * HD)
     whole = lambda columns: pl.BlockSpec((places, columns), lambda i: (0, 0))
     return pl.pallas_call(
         attend_kernel,
-        out_shape=(
-            jax.ShapeDtypeStruct((places, width // 3), LOW),
-            jax.ShapeDtypeStruct((places, upstream.shape[1]), LOW),
-        ),
+        out_shape=jax.ShapeDtypeStruct((places, width // 3), LOW),
         grid=(places // TILE,),
-        in_specs=[
-            pl.BlockSpec(memory_space=pltpu.SMEM),
-            whole(width),
-            pl.BlockSpec(upstream.shape, lambda i: (0, 0)),
-        ],
-        out_specs=[whole(width // 3), anywhere()],
-        scratch_shapes=[pltpu.VMEM((heads, TILE, HD), jnp.float32), dma(GATHER_COPIES), dma(GATHER_COPIES), dma(1)],
-        compiler_params=remote_params(5),
-        cost_estimate=pl.CostEstimate(flops=0, bytes_accessed=200_000_000, transcendentals=0),
-    )(ends, qkv, upstream)
-
-
-def attend_back(ends, qkv, grads, up_grad, out_grad):
+        in_specs=[pl.BlockSpec(memory_space=pltpu.SMEM), whole(width)],
+        out_specs=whole(width // 3),
+        scratch_shapes=[pltpu.VMEM((heads, TILE, HD), jnp.float32)],
+        compiler_params=pltpu.CompilerParams(vmem_limit_bytes=VMEM_LIMIT),
+        cost_estimate=pl.CostEstimate(flops=0, bytes_accessed=150_000_000, transcendentals=0),
+    )(ends, qkv)
+
+
+def attend_back(ends, qkv, grads, out_grad):
     places, width = qkv.shape
     heads = width // (3 * HD)
     whole = lambda columns: pl.BlockSpec((places, columns), lambda j: (0, 0))
@@ -1008,24 +1035,21 @@
         attend_back_kernel,
         out_shape=(
             jax.ShapeDtypeStruct((places, width), LOW),
-            jax.ShapeDtypeStruct((3, up_grad.shape[0], up_grad.shape[1] // 4), LOW),
             jax.ShapeDtypeStruct((4, out_grad.shape[0] // 4, out_grad.shape[1]), LOW),
         ),
         grid=(places // TILE,),
-        in_specs=[pl.BlockSpec(memory_space=pltpu.SMEM), whole(width), whole(width // 3), anywhere(), anywhere()],
-        out_specs=[whole(width), anywhere(), anywhere()],
+        in_specs=[pl.BlockSpec(memory_space=pltpu.SMEM), whole(width), whole(width // 3), anywhere()],
+        out_specs=[whole(width), anywhere()],
         scratch_shapes=[
             pltpu.VMEM((heads, HD, places), jnp.float32),
             pltpu.VMEM((heads, TILE, HD), jnp.float32),
             pltpu.VMEM((heads, TILE, HD), jnp.float32),
-            dma(3),
-            dma(3),
             dma(4),
             dma(4),
         ],
         compiler_params=remote_params(6),
         cost_estimate=pl.CostEstimate(flops=0, bytes_accessed=300_000_000, transcendentals=0),
-    )(ends, qkv, grads, up_grad, out_grad)
+    )(ends, qkv, grads, out_grad)
 
 
 LAYER = ("y", "c", "x")
@@ -1076,22 +1100,18 @@
 
     qkv = dot_wide(layer_normed, w_qkv).astype(LOW)
     upstream = trade(after(facts, cotangent)).reshape(block, width)
-    attended, layer_upstream = attend(ends, qkv, upstream)
+    attended = attend(ends, qkv)
     resid, layer_mlp, own_gate, own_up = close_attention(attended, w_out_own, x_own, full_gain_mlp, w_gate, w_up)
 
     own_down = lax.all_gather(after(resid, w_down), "z", axis=0, tiled=True)
-    gate = dot_wide(layer_mlp, own_gate)
-    up_part = dot_wide(layer_mlp, own_up)
-    sigmoid_gate = jax.nn.sigmoid(gate)
-    hidden = (gate * sigmoid_gate * up_part).astype(LOW)
+    gate, up_part, hidden, layer_upstream = open_mlp(layer_mlp, own_gate, own_up, upstream)
     down_term = contract_rows(hidden, layer_upstream).astype(LOW)
-    d_hidden = contract_cols(layer_upstream, own_down)
-    d_gate, d_up = gate_backward(d_hidden, gate, up_part, sigmoid_gate)
+    d_hidden = contract_cols(after(down_term, layer_upstream), own_down)
+    d_gate, d_up = gate_backward(d_hidden, gate, up_part, jax.nn.sigmoid(gate))
     gate_term, up_term = contract_rows(layer_mlp, d_gate).astype(LOW), contract_rows(layer_mlp, d_up).astype(LOW)
-
     grad_down = lax.psum_scatter(down_term, "z", scatter_dimension=0, tiled=True)
-    d_resid, gain_mlp_term, layer_d_resid, gate_parts = close_mlp(
-        after((up_term, grad_down), d_gate), d_up, own_gate, own_up, resid, upstream, full_gain_mlp, gate_term
+    d_resid, gain_mlp_term, layer_d_resid, gate_parts, up_parts = close_mlp(
+        after(grad_down, d_gate), d_up, own_gate, own_up, resid, upstream, full_gain_mlp, gate_term, up_term
     )
 
     def own_part(whole, parts):
@@ -1103,7 +1123,7 @@
 
     out_term = contract_rows(attended, layer_d_resid).astype(LOW)
     d_attended = contract_cols(layer_d_resid, w_out_own).astype(LOW)
-    d_qkv, up_parts, out_parts = attend_back(ends, qkv, d_attended, up_term, out_term)
+    d_qkv, out_parts = attend_back(ends, qkv, d_attended, out_term)
     grad_gate, grad_up = own_part(gate_term, gate_parts), own_part(up_term, up_parts)
     grad_out = jnp.sum(out_parts.astype(jnp.float32), axis=0)
     qkv_term = contract_rows(layer_normed, d_qkv).astype(LOW)

time: 1360 us -> 1340 us (0.985)
  Pallas kernels: 945 us -> 1030 us
  matrix products: 240 us -> 175 us
  waiting for transfers between devices: 67.8 us -> 7.5 us
  other arithmetic: 31 us -> 51.8 us
    pallas_call x1 -> x2, Pallas kernels: 141 us -> 263 us  [the longest x1 221 us: open_mlp(): pl.pallas_call(open_mlp_kernel, out_shape=(jax.ShapeDtypeStruct((places,...]
    dot_general x4 -> x2, matrix products: 87.7 us -> 42.8 us  [dot_wide(): return jnp.dot(left, right, preferred_element_type=jnp.float32)]
    all_gather x1, waiting for transfers between devices: 36.2 us -> 0.02 us  [body_layers(): own_down = lax.all_gather(after(resid, w_down), 'z', axis=0, tiled=True)]
    pallas_call x1, Pallas kernels: 130 us -> 99.9 us  [attend_back(): pl.pallas_call(attend_back_kernel, out_shape=(jax.ShapeDtypeStruct((place...]
    reduce_scatter x1, waiting for transfers between devices: 27.4 us -> 0.01 us  [body_layers(): lax.psum_scatter(down_term, 'z', scatter_dimension=0, tiled=True)]
    convert_element_type x0 -> x1, other arithmetic: none -> 18.3 us  [gate_backward(): d_up = (d_hidden * gate * sigmoid_gate).astype(jnp.bfloat16)]
    pallas_call x1, Pallas kernels: 218 us -> 203 us  [close_layer(): pl.pallas_call(close_layer_kernel, out_shape=(jax.ShapeDtypeStruct((block...]
    dot_general x2, matrix products: 48 us -> 33.4 us  [contract_cols(): lax.dot_general(left, right, (((1,), (1,)), ((), ())), preferred_element_...]
  transfers between devices with their start and end apart: 8 -> 8, of which waited for: 3 -> 1; matrix products, arithmetic and copies ran while one was open for 15% -> 16% of each run, Pallas kernels for 36% -> 43%
where the time goes in v6:
time: 1340 us; the launch traced here: 1330 us
  Pallas kernels  1030 us (77%)
  matrix products  175 us (13%)
  other arithmetic  51.8 us (4%)
  local copies, waits for them, and re-layouts  24.4 us (2%)
  starting transfers between devices  23.4 us (2%)
  between operations  14.5 us (1%)
    pallas_call x1, Pallas kernels, open_mlp(): pl.pallas_call(open_mlp_kernel, out_shape=(jax.ShapeDtypeStruct((places,...  221 us
    pallas_call x1, Pallas kernels, close_layer(): pl.pallas_call(close_layer_kernel, out_shape=(jax.ShapeDtypeStruct((block...  203 us
    pallas_call x1, Pallas kernels, close_mlp(): pl.pallas_call(close_mlp_kernel, out_shape=(jax.ShapeDtypeStruct((block,...  170 us
    pallas_call x1, Pallas kernels, close_attention(): pl.pallas_call(close_attention_kernel, out_shape=(jax.ShapeDtypeStruct((b...  164 us
    pallas_call x1, Pallas kernels, begin(): pl.pallas_call(begin_kernel, out_shape=(jax.ShapeDtypeStruct((8 * block,...  130 us
    pallas_call x1, Pallas kernels, attend_back(): pl.pallas_call(attend_back_kernel, out_shape=(jax.ShapeDtypeStruct((place...  99.9 us
    dot_general x5, matrix products, contract_rows(): lax.dot_general(left, right, (((0,), (0,)), ((), ())), preferred_element_...  99.1 us
    dot_general x2, matrix products, dot_wide(): return jnp.dot(left, right, preferred_element_type=jnp.float32)  42.8 us
  transfers between devices with their start and end apart: 8, of which 1 were waited for; matrix products, arithmetic and copies ran while one was open for 16% of the time, Pallas kernels for 43%

profile of v6, /device:TPU:0, one launch (start us, length us, event | category | flops | bytes accessed | tf_op | source)
XLA Modules:
  0.0 1326.7 jit_solution(13886677617648112167)
XLA Ops:
  7.2 0.0 all-gather.3.cloned.1.call-start
  7.2 0.7 pad_convert_fusion
  7.9 0.7 bitcast_convert_fusion.1
  8.5 0.7 convert_element_type.89
  9.2 0.1 scatter.19
  9.3 0.2 scatter.20.facts
  9.5 0.6 copy-done.10
  10.1 129.9 %shard_map.203 = (bf16[4096,2048]{1,0:T(8,128)(2,1)}, bf16[4,4,128,768]{3,2,1,0:T(8,128)(2,1)}, f32[4,4,2,8,128]{4,3,2,1,0:T(8,128)}) custom-call(bf16[2,256,2048]{2,1,0:T(8,128)(2,1)} %bitcast.59, bf16[64,2048]{1,0:T(8,128)(2,1)} %w_query.1, bf16[64,2048]{1,0:T(8,128)(2,1)} %w_key.1, bf16[64,2048]{1,0:T(8,128)(2,1)} %w_value.1, f32[8,128]{1,0:T(8,128)} %copy-done.10), custom_call_target="tpu_custom_call" | custom-call | bytes 350000000 | tf_op jit(solution)/shard_map/pallas_call | solution.py:502
  140.0 0.0 all-gather.5.cloned.1.call-start
  140.1 0.7 slice.74
  140.8 1.6 slice_reduce_fusion
  142.4 7.4 fusion
  149.9 0.7 reduce-window.9
  150.6 0.1 mul.55
  150.7 0.7 reshape_squeeze.10.gain
  151.4 19.1 %convolution_convert_fusion.1.qkv = bf16[4096,768]{1,0:T(8,128)(2,1)} fusion(bf16[2048,768]{1,0:T(8,128)(2,1)S(1)} %bitcast.57, bf16[4096,2048]{1,0:T(8,128)(2,1)} %get-tuple-element.75, f32[2048]{0:T(1024)S(1)} %mul.55, f32[4096]{0:T(1024)S(1)} %add_rsqrt_fusion), kind=kOutput, calls=%fused_computation.9 | convolution fusion | flops 12921602048 | bytes 26238976 | tf_op jit(solution)/shard_map/dot_general | solution.py:86
  170.5 42.5 %shard_map.204.attended = bf16[4096,256]{1,0:T(8,128)(2,1)} custom-call(s32[8]{0:T(128)} %bitcast.69, bf16[4096,768]{1,0:T(8,128)(2,1)} %convolution_convert_fusion.1.qkv), custom_call_target="tpu_custom_call" | custom-call | bytes 150000000 | tf_op jit(solution)/shard_map/pallas_call | solution.py:1018
  213.0 3.2 constant_dynamic-slice_fusion.2.x_own
  216.2 2.3 constant_dynamic-slice_fusion.3.w_out
  218.5 164.2 %shard_map.205 = (f32[512,2048]{1,0:T(8,128)}, bf16[4096,2048]{1,0:T(8,128)(2,1)}, bf16[2048,1024]{1,0:T(8,128)(2,1)}, bf16[2048,1024]{1,0:T(8,128)(2,1)}) custom-call(bf16[4096,256]{1,0:T(8,128)(2,1)} %shard_map.204.attended, bf16[256,2048]{1,0:T(8,128)(2,1)} %constant_dynamic-slice_fusion.3.w_out, bf16[512,2048]{1,0:T(8,128)(2,1)} %constant_dynamic-slice_fusion.2.x_own, ...), custom_call_target="tpu_custom_call" | custom-call | bytes 450000000 | tf_op jit(solution)/shard_map/pallas_call | solution.py:588
  382.7 0.0 reduce-scatter.4.cloned.1.call-start
  382.8 2.3 collective-permute-start
  385.0 1.3 copy-done.4
  386.3 220.6 %shard_map.206 = (f32[4096,1024]{1,0:T(8,128)}, f32[4096,1024]{1,0:T(8,128)}, bf16[4096,1024]{1,0:T(8,128)(2,1)}, bf16[4096,2048]{1,0:T(8,128)(2,1)}) custom-call(bf16[4096,2048]{1,0:T(8,128)(2,1)} %get-tuple-element.79.normed, bf16[2048,1024]{1,0:T(8,128)(2,1)} %get-tuple-element.80.w_gate, bf16[2048,1024]{1,0:T(8,128)(2,1)} %get-tuple-element.81.w_up, ...), custom_call_target="tpu_custom_call" | custom-call | bytes 250000000 | tf_op jit(solution)/shard_map/pallas_call | solution.py:904
  606.9 23.8 %convolution_convert_fusion.5 = bf16[1024,2048]{1,0:T(8,128)(2,1)} fusion(bf16[4096,1024]{1,0:T(8,128)(2,1)} %get-tuple-element.91, bf16[4096,2048]{1,0:T(8,128)(2,1)} %get-tuple-element.85), kind=kOutput, calls=%fused_computation.17 | convolution fusion | flops 17181966336 | bytes 29360128 | tf_op jit(solution)/shard_map/dot_general | solution.py:20
  630.8 0.3 reduce-scatter.6.cloned.1.call-start
  631.0 0.0 all-gather.5.cloned.1.call-done
  631.1 23.6 %fusion.15 = f32[4096,1024]{1,0:T(8,128)} fusion(bf16[4096,2048]{1,0:T(8,128)(2,1)} %get-tuple-element.85, bf16[1024,2048]{1,0:T(8,128)(2,1)} %all-gather.5.cloned.1.call-done), kind=kOutput, calls=%fused_computation.40 | convolution fusion | flops 17179869184 | bytes 37748736 | tf_op jit(solution)/shard_map/dot_general | solution.py:26
  654.7 18.3 %multiply_convert_fusion = (bf16[4096,1024]{1,0:T(8,128)(2,1)S(1)}, bf16[4096,1024]{1,0:T(8,128)(2,1)S(1)}) fusion(f32[4096,1024]{1,0:T(8,128)} %fusion.15, f32[4096,1024]{1,0:T(8,128)} %get-tuple-element.88, f32[4096,1024]{1,0:T(8,128)} %get-tuple-element.87), kind=kLoop, calls=%fused_computation.5 | loop fusion | flops 54525952 | bytes 67108864 | tf_op jit(solution)/shard_map/convert_element_type | solution.py:72
  673.0 24.4 %convolution_convert_fusion.4.grad_a = bf16[2048,1024]{1,0:T(8,128)(2,1)} fusion(bf16[4096,2048]{1,0:T(8,128)(2,1)} %get-tuple-element.79.normed, bf16[4096,1024]{1,0:T(8,128)(2,1)S(1)} %get-tuple-element.89.d_gate), kind=kOutput, calls=%fused_computation.16 | convolution fusion | flops 17181966336 | bytes 29360128 | tf_op jit(solution)/shard_map/dot_general | solution.py:20
  697.4 21.6 %convolution_convert_fusion.3.grad_b = bf16[2048,1024]{1,0:T(8,128)(2,1)} fusion(bf16[4096,2048]{1,0:T(8,128)(2,1)} %get-tuple-element.79.normed, bf16[4096,1024]{1,0:T(8,128)(2,1)S(1)} %get-tuple-element.103.d_up), kind=kOutput, calls=%fused_computation.15 | convolution fusion | flops 17181966336 | bytes 29360128 | tf_op jit(solution)/shard_map/dot_general | solution.py:20
  719.1 169.9 %shard_map.207 = (f32[512,2048]{1,0:T(8,128)}, f32[8,2048]{1,0:T(8,128)}, bf16[4096,2048]{1,0:T(8,128)(2,1)}, bf16[3,2048,256]{2,1,0:T(8,128)(2,1)}, bf16[3,2048,256]{2,1,0:T(8,128)(2,1)}) custom-call(bf16[4096,1024]{1,0:T(8,128)(2,1)} %copy-done.1, bf16[4096,1024]{1,0:T(8,128)(2,1)} %copy-done, bf16[2048,1024]{1,0:T(8,128)(2,1)} %get-tuple-element.80.w_gate, ...), custom_call_target="tpu_custom_call" | custom-call | bytes 450000000 | tf_op jit(solution)/shard_map/pallas_call | solution.py:680
  889.0 23.6 %convolution_convert_fusion = bf16[4096,2048]{1,0:T(8,128)(2,1)} fusion(bf16[4096,1024]{1,0:T(8,128)(2,1)} %get-tuple-element.91, bf16[1024,2048]{1,0:T(8,128)(2,1)} %all-gather.5.cloned.1.call-done), kind=kOutput, calls=%fused_computation.8 | convolution fusion | flops 17188257792 | bytes 29360128 | tf_op jit(solution)/shard_map/dot_general | solution.py:86
  912.7 0.0 reduce-scatter.8.cloned.1.call-start
  912.7 1.1 copy-done.5
  913.9 9.8 convolution_convert_fusion.2.grads
  923.7 9.2 convolution_convert_fusion.6.out_grad
  932.9 99.9 %shard_map.208 = (bf16[4096,768]{1,0:T(8,128)(2,1)}, bf16[4,64,2048]{2,1,0:T(8,128)(2,1)}) custom-call(s32[8]{0:T(128)} %bitcast.70, bf16[4096,768]{1,0:T(8,128)(2,1)} %convolution_convert_fusion.1.qkv, bf16[4096,256]{1,0:T(8,128)(2,1)} %convolution_convert_fusion.2.grads, bf16[256,2048]{1,0:T(8,128)(2,1)} %convolution_convert_fusion.6.out_grad), custom_call_target="tpu_custom_call" | custom-call | bytes 300000000 | tf_op jit(solution)/shard_map/pallas_call | solution.py:1034
  1032.9 20.0 %fusion.6 = bf16[2048,768]{1,0:T(8,128)(2,1)S(1)} fusion(bf16[4096,768]{1,0:T(8,128)(2,1)} %get-tuple-element.94.d_qkv, bf16[4096,2048]{1,0:T(8,128)(2,1)} %get-tuple-element.75, f32[2048]{0:T(1024)S(1)} %copy-done.14, f32[4096]{0:T(1024)S(1)} %copy-done.12), kind=kOutput, calls=%fused_computation.18 | convolution fusion | flops 12920029184 | bytes 26238976 | tf_op jit(solution)/shard_map/dot_general | solution.py:20
  1052.9 1.9 copy.24
  1054.8 0.7 reshape_squeeze.11.gain
  1055.5 202.7 %shard_map.209 = (bf16[512,2048]{1,0:T(8,128)(2,1)}, f32[2,8,128]{2,1,0:T(8,128)}) custom-call(bf16[4096,768]{1,0:T(8,128)(2,1)} %get-tuple-element.94.d_qkv, bf16[2048,768]{1,0:T(8,128)(2,1)} %bitcast.56, bf16[512,2048]{1,0:T(8,128)(2,1)} %constant_dynamic-slice_fusion.2.x_own, f32[512,2048]{1,0:T(8,128)} %get-tuple-element.90.d_resid, ...), custom_call_target="tpu_custom_call" | custom-call | bytes 350000000 | tf_op jit(solution)/shard_map/pallas_call | solution.py:797
  1258.2 0.7 reduce_sum.49
  1259.0 0.1 reshape.202
  1259.0 1.6 convert_element_type.114
  1260.6 0.9 convert_reduce_fusion.2
  1261.5 5.5 convert_reduce_fusion
  1267.1 5.0 fusion.9
  1272.1 17.2 %collective-permute-start.1 = (bf16[1,512,2048]{2,1,0:T(8,128)(2,1)}, bf16[1,512,2048]{2,1,0:T(8,128)(2,1)}, u32[]{:S(2)}, u32[]{:S(2)}) collective-permute-start(bf16[1,512,2048]{2,1,0:T(8,128)(2,1)} %fusion.9), channel_id=1, source_target_pairs={{0,0},{1,1},{2,16},{3,17},{4,8},{5,9},{6,24},{7,25},{8,4},{9,5},{1... | collective-permute-start | bytes 6291464 | tf_op jit(solution)/shard_map/ppermute | solution.py:1071
  1289.3 2.8 convert_add_fusion.1
  1292.1 2.7 convert_add_fusion
  1294.8 3.5 all-to-all-start
  1298.4 0.5 fusion.12
  1298.9 4.1 bitcast_convert_fusion
  1303.1 7.4 all-to-all-done
  1310.4 0.9 reshape.206
  1311.3 1.5 fusion.14
  1312.8 0.3 copy.25
  1313.1 1.0 copy.28
  1314.1 0.3 copy.26
  1314.4 1.0 copy.29
  1315.3 0.3 copy.27
  1315.6 1.0 copy.30
  1316.6 3.2 copy.34
  (40 shorter events, 0.2 us)
Async XLA Ops:
  7.2 209.0 %all-gather.3.cloned.1.call-start = ((), (), s32[]{:S(2)}) async-start(), calls=%async_computation.4 | async-start | bytes 2359296 | tf_op jit(solution)/shard_map/all_gather | solution.py:1098
  9.5 0.6 copy-start.10
  140.0 491.0 %all-gather.5.cloned.1.call-start = ((), (), s32[]{:S(2)}) async-start(), calls=%async_computation.6 | async-start | bytes 5242880 | tf_op jit(solution)/shard_map/all_gather | solution.py:1106
  142.4 9.0 copy-start.6
  150.7 19.9 %copy-start.13 = (f32[2048]{0:T(1024)}, f32[2048]{0:T(1024)S(1)}, u32[]{:S(2)}) copy-start(f32[2048]{0:T(1024)S(1)} %mul.55) | copy-start | bytes 24580
  151.4 19.2 %copy-start.11 = (f32[4096]{0:T(1024)}, f32[4096]{0:T(1024)S(1)}, u32[]{:S(2)}) copy-start(f32[4096]{0:T(1024)S(1)} %add_rsqrt_fusion) | copy-start | bytes 49156
  382.7 336.3 %reduce-scatter.4.cloned.1.call-start = ((), (), s32[]{:S(2)}) async-start(), calls=%async_computation.5 | async-start | bytes 5242880 | tf_op jit(solution)/shard_map/reduce_scatter | solution.py:1112
  382.8 2.3 collective-permute-start
  385.0 1.3 copy-start.4
  630.8 636.3 %reduce-scatter.6.cloned.1.call-start = ((), (), s32[]{:S(2)}) async-start(), calls=%async_computation.7 | async-start | bytes 18874368 | tf_op jit(solution)/shard_map/reduce_scatter | solution.py:1061
  673.0 24.5 %copy-start.1 = (bf16[4096,1024]{1,0:T(8,128)(2,1)}, bf16[4096,1024]{1,0:T(8,128)(2,1)S(1)}, u32[]{:S(2)}) copy-start(bf16[4096,1024]{1,0:T(8,128)(2,1)S(1)} %get-tuple-element.89.d_gate) | copy-start | bytes 25165828
  673.0 24.5 %copy-start = (bf16[4096,1024]{1,0:T(8,128)(2,1)}, bf16[4096,1024]{1,0:T(8,128)(2,1)S(1)}, u32[]{:S(2)}) copy-start(bf16[4096,1024]{1,0:T(8,128)(2,1)S(1)} %get-tuple-element.103.d_up) | copy-start | bytes 25165828
  912.6 1.2 copy-start.5
  912.7 382.2 %reduce-scatter.8.cloned.1.call-start = ((), (), s32[]{:S(2)}) async-start(), calls=%async_computation.8 | async-start | bytes 3932160 | tf_op jit(solution)/shard_map/reduce_scatter | solution.py:1137
  913.9 9.8 copy-start.2
  932.9 99.9 %copy-start.12 = (f32[4096]{0:T(1024)S(1)}, f32[4096]{0:T(1024)}, u32[]{:S(2)}) copy-start(f32[4096]{0:T(1024)} %copy-done.11) | copy-start | bytes 49156
  932.9 99.9 %copy-start.14 = (f32[2048]{0:T(1024)S(1)}, f32[2048]{0:T(1024)}, u32[]{:S(2)}) copy-start(f32[2048]{0:T(1024)} %copy-done.13) | copy-start | bytes 24580
  1052.9 1.9 copy-start.9
  1054.8 204.2 %copy-start.7 = (bf16[256,2048]{1,0:T(8,128)(2,1)S(1)}, bf16[256,2048]{1,0:T(8,128)(2,1)}, u32[]{:S(2)}) copy-start(bf16[256,2048]{1,0:T(8,128)(2,1)} %reduce-scatter.4.cloned.1.call-done) | copy-start | bytes 3145732
  1055.5 205.1 %copy-start.8 = (bf16[4,64,2048]{2,1,0:T(8,128)(2,1)S(1)}, bf16[4,64,2048]{2,1,0:T(8,128)(2,1)}, u32[]{:S(2)}) copy-start(bf16[4,64,2048]{2,1,0:T(8,128)(2,1)} %get-tuple-element.97) | copy-start | bytes 3145732
  1267.1 22.2 %copy-start.3 = (f32[2048,256]{1,0:T(8,128)S(1)}, f32[2048,256]{1,0:T(8,128)}, u32[]{:S(2)}) copy-start(f32[2048,256]{1,0:T(8,128)} %get-tuple-element.112) | copy-start | bytes 6291460
  1272.1 44.5 %collective-permute-start.1 = (bf16[1,512,2048]{2,1,0:T(8,128)(2,1)}, bf16[1,512,2048]{2,1,0:T(8,128)(2,1)}, u32[]{:S(2)}, u32[]{:S(2)}) collective-permute-start(bf16[1,512,2048]{2,1,0:T(8,128)(2,1)} %fusion.9), channel_id=1, source_target_pairs={{0,0},{1,1},{2,16},{3,17},{4,8},{5,9},{6,24},{7,25},{8,4},{9,5},{1... | collective-permute-start | bytes 6291464 | tf_op jit(solution)/shard_map/ppermute | solution.py:1071
  1294.8 15.6 %all-to-all-start = ((bf16[8,64,768]{2,1,0:T(8,128)(2,1)}), bf16[8,64,768]{2,1,0:T(8,128)(2,1)S(1)}, u32[]{:S(2)}, u32[]{:S(2)}) async-start(bf16[8,64,768]{2,1,0:T(8,128)(2,1)} %bitcast.63), calls=%async_computation.3 | async-start | bytes 1572864 | tf_op jit(solution)/shard_map/all_to_all | solution.py:1138
Sparse Core Ops, SparseCore 0:
  140.1 53.3 all-gather.2
  382.8 136.1 all-gather.4
  630.9 75.4 reduce-scatter.3
  912.8 151.3 reduce-scatter.5
  1066.4 60.2 reduce-scatter.7

commit v7 on v6

--- a/solution.py
+++ b/solution.py
@@ -318,62 +318,85 @@
     lax.fori_loop(0, count // CHUNK, step, 0)
 
 
-def scatter_scratch(width):
+def scatter_scratch(width, parts=1):
     return [
         pltpu.VMEM((2, TILE, width), LOW),
         pltpu.VMEM((4, TILE, width), LOW),
         pltpu.VMEM((4, TILE, width), LOW),
         pltpu.VMEM((2, HALF, width), LOW),
         pltpu.VMEM((2, TILE, width), LOW),
-        pltpu.SemaphoreType.DMA((10,)),
-        pltpu.SemaphoreType.DMA((10,)),
+        pltpu.SemaphoreType.DMA((parts, 10)),
+        pltpu.SemaphoreType.DMA((parts, 10)),
     ]
 
 
-def run_scatter(produce, staged, core_part, total, relayed, landed, send, recv, beside=lambda: None):
-    y, c, z, x = spot()
-    across_x, across_y, core = near()
-    dests = ((1 - y, 1 - x), (y, 1 - x), (1 - y, x), (y, x))
-    first, second = pl.ds(0, HALF), pl.ds(HALF, HALF)
-    to_core = [
-        remote(staged.at[k % 2], core_part.at[k], send.at[k], recv.at[k], core) for k in range(4)
-    ]
-    far_x = remote(total.at[0, first], relayed.at[0], send.at[4], recv.at[4], across_x)
-    far_y = remote(total.at[0, second], relayed.at[1], send.at[5], recv.at[5], across_y)
-    to_x = [
-        remote(total.at[1, at], landed.at[0, at], send.at[6 + half], recv.at[6 + half], across_x)
-        for half, at in enumerate((first, second))
-    ]
-    to_y = [
-        remote(total.at[2, at], landed.at[1, at], send.at[8 + half], recv.at[8 + half], across_y)
-        for half, at in enumerate((first, second))
-    ]
-    for k, (to_row, to_column) in enumerate(dests):
-        if k >= 2:
-            to_core[k - 2].wait_send()
-        produce(2 * k, to_row, 1 - c, to_column, staged.at[k % 2])
-        to_core[k].start()
-        produce(2 * k + 1, to_row, c, to_column, total.at[k])
-        to_core[k].wait_recv()
-        add_rows(total.at[k], 0, core_part.at[k], 0, TILE)
-        if k == 0:
-            far_x.start()
-            far_y.start()
-        if k == 1:
-            to_x[0].start()
-        if k == 2:
-            to_y[1].start()
-    far_y.wait_recv()
-    add_rows(total.at[1], HALF, relayed.at[1], 0, HALF)
-    to_x[1].start()
-    far_x.wait_recv()
-    add_rows(total.at[2], 0, relayed.at[0], 0, HALF)
-    to_y[0].start()
+class Scatter:
+    def __init__(self, produce, staged, core_part, total, relayed, landed, send, recv, part=0, start=0, size=TILE):
+        across_x, across_y, core = near()
+        self.produce, self.staged, self.core_part, self.total, self.relayed = produce, staged, core_part, total, relayed
+        self.start, self.size, self.half = start, size, size // 2
+        send, recv = send.at[part], recv.at[part]
+        rows = pl.ds(start, size)
+        halves = (pl.ds(start, self.half), pl.ds(start + self.half, self.half))
+        self.relay_row = start // 2
+        passing = pl.ds(self.relay_row, self.half)
+        self.to_core = [
+            remote(staged.at[k % 2, rows], core_part.at[k, rows], send.at[k], recv.at[k], core) for k in range(4)
+        ]
+        self.far_x = remote(total.at[0, halves[0]], relayed.at[0, passing], send.at[4], recv.at[4], across_x)
+        self.far_y = remote(total.at[0, halves[1]], relayed.at[1, passing], send.at[5], recv.at[5], across_y)
+        self.to_x = [
+            remote(total.at[1, at], landed.at[0, at], send.at[6 + half], recv.at[6 + half], across_x)
+            for half, at in enumerate(halves)
+        ]
+        self.to_y = [
+            remote(total.at[2, at], landed.at[1, at], send.at[8 + half], recv.at[8 + half], across_y)
+            for half, at in enumerate(halves)
+        ]
+
+    def begin(self):
+        y, c, z, x = spot()
+        rows = pl.ds(self.start, self.size)
+        for k, (to_row, to_column) in enumerate(((1 - y, 1 - x), (y, 1 - x), (1 - y, x), (y, x))):
+            if k >= 2:
+                self.to_core[k - 2].wait_send()
+            self.produce(2 * k, to_row, 1 - c, to_column, self.staged.at[k % 2, rows])
+            self.to_core[k].start()
+            self.produce(2 * k + 1, to_row, c, to_column, self.total.at[k, rows])
+            self.to_core[k].wait_recv()
+            add_rows(self.total.at[k], self.start, self.core_part.at[k], self.start, self.size)
+            if k == 0:
+                self.far_x.start()
+                self.far_y.start()
+            if k == 1:
+                self.to_x[0].start()
+            if k == 2:
+                self.to_y[1].start()
+
+    def relay(self):
+        self.far_y.wait_recv()
+        add_rows(self.total.at[1], self.start + self.half, self.relayed.at[1], self.relay_row, self.half)
+        self.to_x[1].start()
+        self.far_x.wait_recv()
+        add_rows(self.total.at[2], self.start, self.relayed.at[0], self.relay_row, self.half)
+        self.to_y[0].start()
+
+    def arrive(self):
+        for copy in self.to_x + self.to_y:
+            copy.wait_recv()
+
+    def finish(self):
+        for copy in self.to_core[2:] + [self.far_x, self.far_y] + self.to_x + self.to_y:
+            copy.wait_send()
+
+
+def run_scatter(produce, *scratch, beside=lambda: None):
+    scatter = Scatter(produce, *scratch)
+    scatter.begin()
+    scatter.relay()
     beside()
-    for copy in to_x + to_y:
-        copy.wait_recv()
-    for copy in to_core[2:] + [far_x, far_y] + to_x + to_y:
-        copy.wait_send()
+    scatter.arrive()
+    scatter.finish()
 
 
 def begin_kernel(
@@ -714,17 +737,23 @@
         pl.semaphore_signal(barrier, inc=1, device_id=peer, device_id_type=MESH_ID)
     pl.semaphore_wait(barrier, len(layer + line) + moves.astype(jnp.int32))
 
-    def produce(turn, to_y, to_c, to_x, out):
-        at = place_of(to_y, to_c, to_x)
-
-        def step(i, carry):
-            columns = pl.ds(pl.multiple_of(i * TILE, TILE), TILE)
-            out[:, columns] = dot_nt(d_qkv[at, :], w_qkv[columns, :]).astype(LOW)
-            return carry
-
-        lax.fori_loop(0, width // TILE, step, 0)
-
-    run_scatter(produce, *scatter)
+    def part_of(half):
+        def produce(turn, to_y, to_c, to_x, out):
+            at = place_of(to_y, to_c, to_x, half)
+
+            def step(i, carry):
+                columns = pl.ds(pl.multiple_of(i * TILE, TILE), TILE)
+                out[:, columns] = dot_nt(d_qkv[at, :], w_qkv[columns, :]).astype(LOW)
+                return carry
+
+            lax.fori_loop(0, width // TILE, step, 0)
+
+        return Scatter(produce, *scatter, part=half, start=half * HALF, size=HALF)
+
+    sums = [part_of(half) for half in (0, 1)]
+    sums[0].begin()
+    sums[0].relay()
+    sums[1].begin()
     total, landed = scatter[2], scatter[4]
     terms[1] = mlp_term[...]
     terms[0] = jnp.zeros_like(mlp_term)
@@ -737,6 +766,9 @@
         for half in (0, 1)
     ]
     for half in (0, 1):
+        if half == 1:
+            sums[1].relay()
+        sums[half].arrive()
 
         def step(i, carry):
             here = pl.ds(pl.multiple_of(half * HALF + i * CHUNK, CHUNK), CHUNK)
@@ -780,6 +812,8 @@
     gain_grads[...] = sum((column_terms[k] for k in range(3)), part[:, :, pl.ds(pl.multiple_of(z * HD, HD), HD)])
     for copy in spread + lines:
         copy.wait_send()
+    for half in (0, 1):
+        sums[half].finish()
 
     @pl.when(moves)
     def _():
@@ -806,7 +840,7 @@
             pltpu.VMEM((2, 8, width // 4), jnp.float32),
             pltpu.VMEM((3, 2, 8, width // 16), jnp.float32),
         ]
-        + scatter_scratch(width)
+        + scatter_scratch(width, 2)
         + [dma(2), dma(2), dma(7), dma(7), dma(3), dma(3)],
         compiler_params=remote_params(4),
         cost_estimate=pl.CostEstimate(flops=0, bytes_accessed=350_000_000, transcendentals=0),
@@ -926,13 +960,17 @@
 
 
 def attend_back_kernel(
-    ends, qkv, grads, out_grad, out, out_parts, query_total, key_total, value_total, send, recv
+    ends, qkv, grads, out_grad, mixed, out, out_parts, mixed_home, query_total, key_total, value_total, send, recv, trade_send, trade_recv
 ):
     j = pl.program_id(0)
     y, c, z, x = spot()
     heads = qkv.shape[1] // (3 * HD)
     shard = out_grad.shape[0] // 4
     owners, holders = out_turns()
+    partner = partner_of(y, c, z, x)
+    moves = z != 2 * c + y
+    trade_copy = remote(mixed, mixed_home, trade_send.at[0], trade_recv.at[0], partner)
+    keep = pltpu.make_async_copy(mixed, mixed_home, trade_recv.at[0])
 
     def to_owner(turn):
         return remote(out_grad.at[pl.ds(turn * shard, shard)], out_parts.at[z], send.at[turn], recv.at[z], owners[turn][0])
@@ -950,7 +988,20 @@
             def _():
                 pl.semaphore_signal(barrier, inc=1, device_id=peer, device_id_type=MESH_ID)
 
-        pl.semaphore_wait(barrier, 4 - (x == z // 2).astype(jnp.int32))
+        @pl.when(moves)
+        def _():
+            pl.semaphore_signal(barrier, inc=1, device_id=partner, device_id_type=MESH_ID)
+
+        pl.semaphore_wait(barrier, 4 - (x == z // 2).astype(jnp.int32) + moves.astype(jnp.int32))
+
+        @pl.when(moves)
+        def _():
+            trade_copy.start()
+
+        @pl.when(jnp.logical_not(moves))
+        def _():
+            keep.start()
+
         for turn in range(4):
 
             @pl.when(jnp.logical_not(owners[turn][1]))
@@ -1009,6 +1060,14 @@
             @pl.when(owners[turn][1])
             def _():
                 to_self(turn).wait()
+
+        @pl.when(moves)
+        def _():
+            trade_copy.wait()
+
+        @pl.when(jnp.logical_not(moves))
+        def _():
+            keep.wait()
 
 
 def attend(ends, qkv):
@@ -1027,7 +1086,7 @@
     )(ends, qkv)
 
 
-def attend_back(ends, qkv, grads, out_grad):
+def attend_back(ends, qkv, grads, out_grad, mixed):
     places, width = qkv.shape
     heads = width // (3 * HD)
     whole = lambda columns: pl.BlockSpec((places, columns), lambda j: (0, 0))
@@ -1036,29 +1095,28 @@
         out_shape=(
             jax.ShapeDtypeStruct((places, width), LOW),
             jax.ShapeDtypeStruct((4, out_grad.shape[0] // 4, out_grad.shape[1]), LOW),
+            jax.ShapeDtypeStruct(mixed.shape, LOW),
         ),
         grid=(places // TILE,),
-        in_specs=[pl.BlockSpec(memory_space=pltpu.SMEM), whole(width), whole(width // 3), anywhere()],
-        out_specs=[whole(width), anywhere()],
+        in_specs=[pl.BlockSpec(memory_space=pltpu.SMEM), whole(width), whole(width // 3), anywhere(), pl.BlockSpec(mixed.shape, lambda j: (0, 0))],
+        out_specs=[whole(width), anywhere(), anywhere()],
         scratch_shapes=[
             pltpu.VMEM((heads, HD, places), jnp.float32),
             pltpu.VMEM((heads, TILE, HD), jnp.float32),
             pltpu.VMEM((heads, TILE, HD), jnp.float32),
             dma(4),
             dma(4),
+            dma(1),
+            dma(1),
         ],
         compiler_params=remote_params(6),
         cost_estimate=pl.CostEstimate(flops=0, bytes_accessed=300_000_000, transcendentals=0),
-    )(ends, qkv, grads, out_grad)
+    )(ends, qkv, grads, out_grad, mixed)
 
 
 LAYER = ("y", "c", "x")
 PLACES = ("c", "y", "x")
 ALL = ("y", "c", "z", "x")
-
-
-def scatter_layer(whole):
-    return lax.psum_scatter(whole.astype(LOW), PLACES, scatter_dimension=0, tiled=True).astype(jnp.float32)
 
 
 def trade(part):
@@ -1101,29 +1159,38 @@
     qkv = dot_wide(layer_normed, w_qkv).astype(LOW)
     upstream = trade(after(facts, cotangent)).reshape(block, width)
     attended = attend(ends, qkv)
-    resid, layer_mlp, own_gate, own_up = close_attention(attended, w_out_own, x_own, full_gain_mlp, w_gate, w_up)
+    resid, layer_mlp, own_gate, own_up = close_attention(after(upstream, attended), w_out_own, x_own, full_gain_mlp, w_gate, w_up)
 
     own_down = lax.all_gather(after(resid, w_down), "z", axis=0, tiled=True)
     gate, up_part, hidden, layer_upstream = open_mlp(layer_mlp, own_gate, own_up, upstream)
-    down_term = contract_rows(hidden, layer_upstream).astype(LOW)
+    part = dot_wide(hidden, own_down).astype(LOW)
+    mixed_sum = lax.psum_scatter(part, PLACES, scatter_dimension=0, tiled=True)
+    down_term = contract_rows(after(part, hidden), layer_upstream).astype(LOW)
+    down_rows = w_down.shape[0]
+    down_parts = []
+    for up in range(1, 4):
+        layers_pairs = [(at, (at + up) % 4) for at in range(4)]
+        slab = lax.dynamic_slice_in_dim(down_term, (layer + up) % 4 * down_rows, down_rows, 0)
+        down_parts.append(lax.ppermute(slab, "z", layers_pairs))
     d_hidden = contract_cols(after(down_term, layer_upstream), own_down)
     d_gate, d_up = gate_backward(d_hidden, gate, up_part, jax.nn.sigmoid(gate))
     gate_term, up_term = contract_rows(layer_mlp, d_gate).astype(LOW), contract_rows(layer_mlp, d_up).astype(LOW)
-    grad_down = lax.psum_scatter(down_term, "z", scatter_dimension=0, tiled=True)
     d_resid, gain_mlp_term, layer_d_resid, gate_parts, up_parts = close_mlp(
-        after(grad_down, d_gate), d_up, own_gate, own_up, resid, upstream, full_gain_mlp, gate_term, up_term
+        after((mixed_sum, *down_parts), d_gate), d_up, own_gate, own_up, resid, upstream, full_gain_mlp, gate_term, up_term
     )
 
     def own_part(whole, parts):
         own = lax.dynamic_slice_in_dim(whole, layer * parts.shape[2], parts.shape[2], 1)
         return own.astype(jnp.float32) + jnp.sum(parts.astype(jnp.float32), axis=0)
 
-    result = resid + scatter_layer(dot_wide(after(d_resid, hidden), own_down))
-    mixed = trade(result.astype(LOW).reshape(rows_here, block, width))
+    mixed = (resid + after(layer_d_resid, mixed_sum).astype(jnp.float32)).astype(LOW)
+    grad_down = lax.dynamic_slice_in_dim(down_term, layer * down_rows, down_rows, 0).astype(jnp.float32)
+    grad_down = grad_down + sum(slab.astype(jnp.float32) for slab in down_parts)
 
     out_term = contract_rows(attended, layer_d_resid).astype(LOW)
     d_attended = contract_cols(layer_d_resid, w_out_own).astype(LOW)
-    d_qkv, out_parts = attend_back(ends, qkv, d_attended, out_term)
+    d_qkv, out_parts, mixed = attend_back(ends, qkv, d_attended, out_term, mixed)
+    mixed = mixed.reshape(rows_here, block, width)
     grad_gate, grad_up = own_part(gate_term, gate_parts), own_part(up_term, up_parts)
     grad_out = jnp.sum(out_parts.astype(jnp.float32), axis=0)
     qkv_term = contract_rows(layer_normed, d_qkv).astype(LOW)
@@ -1148,7 +1215,7 @@
         grad_out,
         grad_gate,
         grad_up,
-        grad_down.astype(jnp.float32),
+        grad_down,
         gain_grads[0],
         gain_grads[1],
     )

time: 1340 us -> 1160 us (0.87)
  Pallas kernels: 1030 us -> 863 us
  starting transfers between devices: 23.4 us -> 9.98 us
    pallas_call x1, Pallas kernels: 221 us -> 82.5 us  [open_mlp(): pl.pallas_call(open_mlp_kernel, out_shape=(jax.ShapeDtypeStruct((places,...]
    pallas_call x1, Pallas kernels: 203 us -> 137 us  [close_layer(): pl.pallas_call(close_layer_kernel, out_shape=(jax.ShapeDtypeStruct((block...]
    pallas_call x1, Pallas kernels: 99.9 us -> 128 us  [attend_back(): pl.pallas_call(attend_back_kernel, out_shape=(jax.ShapeDtypeStruct((place...]
    ppermute x2 -> x1, starting transfers between devices: 19.4 us -> 2.25 us  [trade(): return lax.ppermute(part, ALL, pairs)]
  transfers between devices with their start and end apart: 8 -> 9, of which waited for: 1 -> 2; matrix products, arithmetic and copies ran while one was open for 16% -> 15% of each run, Pallas kernels for 43% -> 23%
where the time goes in v7:
time: 1160 us; the launch traced here: 1150 us
  Pallas kernels  863 us (74%)
  matrix products  171 us (15%)
  other arithmetic  49.6 us (4%)
  local copies, waits for them, and re-layouts  25.8 us (2%)
  waiting for transfers between devices  15.7 us (1%)
  between operations  14.6 us (1%)
    pallas_call x1, Pallas kernels, close_attention(): pl.pallas_call(close_attention_kernel, out_shape=(jax.ShapeDtypeStruct((b...  172 us
    pallas_call x1, Pallas kernels, close_mlp(): pl.pallas_call(close_mlp_kernel, out_shape=(jax.ShapeDtypeStruct((block,...  171 us
    pallas_call x1, Pallas kernels, close_layer(): pl.pallas_call(close_layer_kernel, out_shape=(jax.ShapeDtypeStruct((block...  137 us
    pallas_call x1, Pallas kernels, begin(): pl.pallas_call(begin_kernel, out_shape=(jax.ShapeDtypeStruct((8 * block,...  130 us
    pallas_call x1, Pallas kernels, attend_back(): pl.pallas_call(attend_back_kernel, out_shape=(jax.ShapeDtypeStruct((place...  128 us
    dot_general x5, matrix products, contract_rows(): lax.dot_general(left, right, (((0,), (0,)), ((), ())), preferred_element_...  95.3 us
    pallas_call x1, Pallas kernels, open_mlp(): pl.pallas_call(open_mlp_kernel, out_shape=(jax.ShapeDtypeStruct((places,...  82.5 us
    dot_general x2, matrix products, dot_wide(): return jnp.dot(left, right, preferred_element_type=jnp.float32)  43.5 us
  transfers between devices with their start and end apart: 9, of which 2 were waited for; matrix products, arithmetic and copies ran while one was open for 15% of the time, Pallas kernels for 23%

profile of v7, /device:TPU:0, one launch (start us, length us, event | category | flops | bytes accessed | tf_op | source)
XLA Modules:
  0.0 1150.2 jit_solution(11568496142600869936)
XLA Ops:
  7.2 0.7 pad_convert_fusion
  7.9 0.7 bitcast_convert_fusion.1
  8.5 0.7 convert_element_type.98
  9.2 0.1 scatter.19
  9.3 0.2 scatter.20.facts
  9.5 0.6 copy-done.13
  10.1 129.9 %shard_map.203 = (bf16[4096,2048]{1,0:T(8,128)(2,1)}, bf16[4,4,128,768]{3,2,1,0:T(8,128)(2,1)}, f32[4,4,2,8,128]{4,3,2,1,0:T(8,128)}) custom-call(bf16[2,256,2048]{2,1,0:T(8,128)(2,1)} %bitcast.58, bf16[64,2048]{1,0:T(8,128)(2,1)} %w_query.1, bf16[64,2048]{1,0:T(8,128)(2,1)} %w_key.1, bf16[64,2048]{1,0:T(8,128)(2,1)} %w_value.1, f32[8,128]{1,0:T(8,128)} %copy-done.13), custom_call_target="tpu_custom_call" | custom-call | bytes 350000000 | tf_op jit(solution)/shard_map/pallas_call | solution.py:525
  140.0 2.3 collective-permute-start
  142.3 0.0 all-gather.5.cloned.1.call-start
  142.3 0.7 slice.74
  143.0 1.6 slice_reduce_fusion
  144.7 7.2 fusion
  151.9 0.7 reduce-window.9
  152.6 0.1 mul.68
  152.7 0.7 reshape_squeeze.10.gain
  153.4 20.1 %convolution_convert_fusion.1.qkv = bf16[4096,768]{1,0:T(8,128)(2,1)} fusion(bf16[2048,768]{1,0:T(8,128)(2,1)} %bitcast.55, bf16[4096,2048]{1,0:T(8,128)(2,1)} %get-tuple-element.78, f32[2048]{0:T(1024)S(1)} %mul.68, f32[4096]{0:T(1024)S(1)} %add_rsqrt_fusion), kind=kOutput, calls=%fused_computation.9 | convolution fusion | flops 12921602048 | bytes 26238976 | tf_op jit(solution)/shard_map/dot_general | solution.py:86
  173.5 42.4 %shard_map.204.attended = bf16[4096,256]{1,0:T(8,128)(2,1)} custom-call(s32[8]{0:T(128)} %bitcast.69, bf16[4096,768]{1,0:T(8,128)(2,1)} %convolution_convert_fusion.1.qkv), custom_call_target="tpu_custom_call" | custom-call | bytes 150000000 | tf_op jit(solution)/shard_map/pallas_call | solution.py:1077
  215.8 3.2 constant_dynamic-slice_fusion.5.x_own
  219.0 6.6 all-gather.3.cloned.1.call-done
  225.6 2.3 constant_dynamic-slice_fusion.6.w_out
  227.9 172.3 %shard_map.205 = (f32[512,2048]{1,0:T(8,128)}, bf16[4096,2048]{1,0:T(8,128)(2,1)}, bf16[2048,1024]{1,0:T(8,128)(2,1)}, bf16[2048,1024]{1,0:T(8,128)(2,1)}) custom-call(bf16[4096,256]{1,0:T(8,128)(2,1)} %shard_map.204.attended, bf16[256,2048]{1,0:T(8,128)(2,1)} %constant_dynamic-slice_fusion.6.w_out, bf16[512,2048]{1,0:T(8,128)(2,1)} %constant_dynamic-slice_fusion.5.x_own, ...), custom_call_target="tpu_custom_call" | custom-call | bytes 450000000 | tf_op jit(solution)/shard_map/pallas_call | solution.py:611
  400.3 0.0 reduce-scatter.3.cloned.1.call-start
  400.4 82.5 %shard_map.206 = (f32[4096,1024]{1,0:T(8,128)}, f32[4096,1024]{1,0:T(8,128)}, bf16[4096,1024]{1,0:T(8,128)(2,1)}, bf16[4096,2048]{1,0:T(8,128)(2,1)}) custom-call(bf16[4096,2048]{1,0:T(8,128)(2,1)} %get-tuple-element.83.normed, bf16[2048,1024]{1,0:T(8,128)(2,1)} %get-tuple-element.84.w_gate, bf16[2048,1024]{1,0:T(8,128)(2,1)} %get-tuple-element.85.w_up, ...), custom_call_target="tpu_custom_call" | custom-call | bytes 250000000 | tf_op jit(solution)/shard_map/pallas_call | solution.py:938
  482.9 23.5 %convolution_convert_fusion = bf16[4096,2048]{1,0:T(8,128)(2,1)} fusion(bf16[4096,1024]{1,0:T(8,128)(2,1)} %get-tuple-element.89, bf16[1024,2048]{1,0:T(8,128)(2,1)} %all-gather.5.cloned.1.call-done), kind=kOutput, calls=%fused_computation.8 | convolution fusion | flops 17188257792 | bytes 29360128 | tf_op jit(solution)/shard_map/dot_general | solution.py:86
  506.4 0.0 reduce-scatter.5.cloned.1.call-start
  506.5 23.6 %convolution_convert_fusion.5 = bf16[1024,2048]{1,0:T(8,128)(2,1)S(1)} fusion(bf16[4096,1024]{1,0:T(8,128)(2,1)} %get-tuple-element.89, bf16[4096,2048]{1,0:T(8,128)(2,1)} %get-tuple-element.91), kind=kOutput, calls=%fused_computation.17 | convolution fusion | flops 17181966336 | bytes 29360128 | tf_op jit(solution)/shard_map/dot_general | solution.py:20
  530.1 2.1 copy-done.6
  532.2 1.7 constant_dynamic-slice_fusion.2
  533.9 4.0 collective-permute-start.3
  538.0 22.6 %fusion.14 = f32[4096,1024]{1,0:T(8,128)} fusion(bf16[4096,2048]{1,0:T(8,128)(2,1)} %get-tuple-element.91, bf16[1024,2048]{1,0:T(8,128)(2,1)S(1)} %copy-done.18), kind=kOutput, calls=%fused_computation.43 | convolution fusion | flops 17179869184 | bytes 37748736 | tf_op jit(solution)/shard_map/dot_general | solution.py:26
  560.6 19.4 %multiply_convert_fusion = (bf16[4096,1024]{1,0:T(8,128)(2,1)S(1)}, bf16[4096,1024]{1,0:T(8,128)(2,1)S(1)}) fusion(f32[4096,1024]{1,0:T(8,128)} %fusion.14, f32[4096,1024]{1,0:T(8,128)} %get-tuple-element.93, f32[4096,1024]{1,0:T(8,128)} %get-tuple-element.92), kind=kLoop, calls=%fused_computation.5 | loop fusion | flops 54525952 | bytes 67108864 | tf_op jit(solution)/shard_map/convert_element_type | solution.py:72
  580.0 24.4 %convolution_convert_fusion.4.grad_a = bf16[2048,1024]{1,0:T(8,128)(2,1)} fusion(bf16[4096,2048]{1,0:T(8,128)(2,1)} %get-tuple-element.83.normed, bf16[4096,1024]{1,0:T(8,128)(2,1)S(1)} %get-tuple-element.94.d_gate), kind=kOutput, calls=%fused_computation.16 | convolution fusion | flops 17181966336 | bytes 29360128 | tf_op jit(solution)/shard_map/dot_general | solution.py:20
  604.4 21.9 %convolution_convert_fusion.3.grad_b = bf16[2048,1024]{1,0:T(8,128)(2,1)} fusion(bf16[4096,2048]{1,0:T(8,128)(2,1)} %get-tuple-element.83.normed, bf16[4096,1024]{1,0:T(8,128)(2,1)S(1)} %get-tuple-element.109.d_up), kind=kOutput, calls=%fused_computation.15 | convolution fusion | flops 17181966336 | bytes 29360128 | tf_op jit(solution)/shard_map/dot_general | solution.py:20
  626.4 171.0 %shard_map.207 = (f32[512,2048]{1,0:T(8,128)}, f32[8,2048]{1,0:T(8,128)}, bf16[4096,2048]{1,0:T(8,128)(2,1)}, bf16[3,2048,256]{2,1,0:T(8,128)(2,1)}, bf16[3,2048,256]{2,1,0:T(8,128)(2,1)}) custom-call(bf16[4096,1024]{1,0:T(8,128)(2,1)} %copy-done.1, bf16[4096,1024]{1,0:T(8,128)(2,1)} %copy-done, bf16[2048,1024]{1,0:T(8,128)(2,1)} %get-tuple-element.84.w_gate, ...), custom_call_target="tpu_custom_call" | custom-call | bytes 450000000 | tf_op jit(solution)/shard_map/pallas_call | solution.py:703
  797.4 10.0 convolution_convert_fusion.2.grads
  807.4 1.3 copy-done.2
  808.7 0.6 copy-done.3
  809.3 5.5 convolution_convert_fusion.6.out_grad
  814.8 2.1 add_convert_fusion.mixed
  816.9 128.4 %shard_map.208 = (bf16[4096,768]{1,0:T(8,128)(2,1)}, bf16[4,64,2048]{2,1,0:T(8,128)(2,1)}, bf16[512,2048]{1,0:T(8,128)(2,1)}) custom-call(s32[8]{0:T(128)} %bitcast.70, bf16[4096,768]{1,0:T(8,128)(2,1)} %convolution_convert_fusion.1.qkv, bf16[4096,256]{1,0:T(8,128)(2,1)} %convolution_convert_fusion.2.grads, ...), custom_call_target="tpu_custom_call" | custom-call | bytes 300000000 | tf_op jit(solution)/shard_map/pallas_call | solution.py:1093
  945.3 19.9 %fusion.6 = bf16[2048,768]{1,0:T(8,128)(2,1)S(1)} fusion(bf16[4096,768]{1,0:T(8,128)(2,1)} %get-tuple-element.99.d_qkv, bf16[4096,2048]{1,0:T(8,128)(2,1)} %get-tuple-element.78, f32[2048]{0:T(1024)S(1)} %copy-done.17, f32[4096]{0:T(1024)S(1)} %copy-done.15), kind=kOutput, calls=%fused_computation.18 | convolution fusion | flops 12920029184 | bytes 26238976 | tf_op jit(solution)/shard_map/dot_general | solution.py:20
  965.2 1.9 copy.24
  967.1 0.7 reshape_squeeze.11.gain
  967.8 3.5 add_add_fusion
  971.3 136.6 %shard_map.209 = (bf16[512,2048]{1,0:T(8,128)(2,1)}, f32[2,8,128]{2,1,0:T(8,128)}) custom-call(bf16[4096,768]{1,0:T(8,128)(2,1)} %get-tuple-element.99.d_qkv, bf16[2048,768]{1,0:T(8,128)(2,1)} %bitcast.56, bf16[512,2048]{1,0:T(8,128)(2,1)} %constant_dynamic-slice_fusion.5.x_own, f32[512,2048]{1,0:T(8,128)} %get-tuple-element.100.d_resid, ...), custom_call_target="tpu_custom_call" | custom-call | bytes 350000000 | tf_op jit(solution)/shard_map/pallas_call | solution.py:831
  1107.8 0.7 reduce_sum.49
  1108.5 0.1 reshape.202
  1108.6 2.2 convert_reduce_fusion.2
  1110.8 3.5 convert_reduce_fusion
  1114.3 3.0 convert_add_fusion.1
  1117.3 2.8 convert_add_fusion
  1120.1 3.5 all-to-all-start
  1123.7 0.5 fusion.11
  1124.2 2.5 bitcast_convert_fusion
  1126.7 9.0 all-to-all-done
  1135.7 0.9 reshape.206
  1136.6 1.5 fusion.13
  1138.1 0.3 copy.25
  1138.4 1.0 copy.28
  1139.3 0.3 copy.26
  1139.7 1.0 copy.29
  1140.6 0.3 copy.27
  1140.9 1.0 copy.30
  1141.9 1.3 copy.34
  (50 shorter events, 0.3 us)
Async XLA Ops:
  7.2 218.5 %all-gather.3.cloned.1.call-start = ((), (), s32[]{:S(2)}) async-start(), calls=%async_computation.3 | async-start | bytes 2359296 | tf_op jit(solution)/shard_map/all_gather | solution.py:1156
  9.5 0.6 copy-start.13
  140.0 79.0 %collective-permute-start = (bf16[1,512,2048]{2,1,0:T(8,128)(2,1)}, bf16[1,512,2048]{2,1,0:T(8,128)(2,1)S(1)}, u32[]{:S(2)}, u32[]{:S(2)}) collective-permute-start(bf16[1,512,2048]{2,1,0:T(8,128)(2,1)} %param.20), channel_id=1, source_target_pairs={{0,0},{1,1},{2,16},{3,17},{4,8},{5,9},{6,24},{7,25},{8,4},{9,5},{1... | collective-permute-start | bytes 6291464 | tf_op jit(solution)/shard_map/ppermute | solution.py:1129
  142.3 340.6 %all-gather.5.cloned.1.call-start = ((), (), s32[]{:S(2)}) async-start(), calls=%async_computation.4 | async-start | bytes 5242880 | tf_op jit(solution)/shard_map/all_gather | solution.py:1164
  152.7 20.8 %copy-start.16 = (f32[2048]{0:T(1024)}, f32[2048]{0:T(1024)S(1)}, u32[]{:S(2)}) copy-start(f32[2048]{0:T(1024)S(1)} %mul.68) | copy-start | bytes 24580
  153.4 20.1 %copy-start.14 = (f32[4096]{0:T(1024)}, f32[4096]{0:T(1024)S(1)}, u32[]{:S(2)}) copy-start(f32[4096]{0:T(1024)S(1)} %add_rsqrt_fusion) | copy-start | bytes 49156
  219.0 181.3 %copy-start.5 = (bf16[1,512,2048]{2,1,0:T(8,128)(2,1)}, bf16[1,512,2048]{2,1,0:T(8,128)(2,1)S(1)}, u32[]{:S(2)}) copy-start(bf16[1,512,2048]{2,1,0:T(8,128)(2,1)S(1)} %collective-permute-done) | copy-start | bytes 6291460
  400.3 226.1 %reduce-scatter.3.cloned.1.call-start = ((), (), s32[]{:S(2)}) async-start(), calls=%async_computation.5 | async-start | bytes 18874368 | tf_op jit(solution)/shard_map/reduce_scatter | solution.py:1167
  506.4 613.8 %reduce-scatter.5.cloned.1.call-start = ((), (), s32[]{:S(2)}) async-start(), calls=%async_computation.6 | async-start | bytes 3932160 | tf_op jit(solution)/shard_map/reduce_scatter | solution.py:1204
  530.1 2.1 copy-start.6
  532.2 5.8 copy-start.18
  533.9 92.4 %collective-permute-start.1 = (bf16[256,2048]{1,0:T(8,128)(2,1)}, bf16[256,2048]{1,0:T(8,128)(2,1)S(1)}, u32[]{:S(2)}, u32[]{:S(2)}) collective-permute-start(bf16[256,2048]{1,0:T(8,128)(2,1)} %get-tuple-element.113), channel_id=1, source_target_pairs={{0,2},{2,4},{4,6},{6,0},{1,3},{3,5},{5,7},{7,1},{8,10},{10,12},{12... | collective-permute-start | bytes 3145736 | tf_op jit(solution)/shard_map/ppermute | solution.py:1174
  533.9 92.4 %collective-permute-start.2 = (bf16[256,2048]{1,0:T(8,128)(2,1)}, bf16[256,2048]{1,0:T(8,128)(2,1)S(1)}, u32[]{:S(2)}, u32[]{:S(2)}) collective-permute-start(bf16[256,2048]{1,0:T(8,128)(2,1)} %get-tuple-element.112), channel_id=1, source_target_pairs={{0,4},{2,6},{4,0},{6,2},{1,5},{3,7},{5,1},{7,3},{8,12},{10,14},{12... | collective-permute-start | bytes 3145736 | tf_op jit(solution)/shard_map/ppermute | solution.py:1174
  533.9 92.4 %collective-permute-start.3 = (bf16[256,2048]{1,0:T(8,128)(2,1)}, bf16[256,2048]{1,0:T(8,128)(2,1)}, u32[]{:S(2)}, u32[]{:S(2)}) collective-permute-start(bf16[256,2048]{1,0:T(8,128)(2,1)} %get-tuple-element.111), channel_id=1, source_target_pairs={{0,6},{2,0},{4,2},{6,4},{1,7},{3,1},{5,3},{7,5},{8,14},{10,8},{12,... | collective-permute-start | bytes 3145736 | tf_op jit(solution)/shard_map/ppermute | solution.py:1174
  580.0 24.5 %copy-start.1 = (bf16[4096,1024]{1,0:T(8,128)(2,1)}, bf16[4096,1024]{1,0:T(8,128)(2,1)S(1)}, u32[]{:S(2)}) copy-start(bf16[4096,1024]{1,0:T(8,128)(2,1)S(1)} %get-tuple-element.94.d_gate) | copy-start | bytes 25165828
  580.0 24.5 %copy-start = (bf16[4096,1024]{1,0:T(8,128)(2,1)}, bf16[4096,1024]{1,0:T(8,128)(2,1)S(1)}, u32[]{:S(2)}) copy-start(bf16[4096,1024]{1,0:T(8,128)(2,1)S(1)} %get-tuple-element.109.d_up) | copy-start | bytes 25165828
  626.4 171.0 %copy-start.7 = (bf16[256,2048]{1,0:T(8,128)(2,1)S(1)}, bf16[256,2048]{1,0:T(8,128)(2,1)}, u32[]{:S(2)}) copy-start(bf16[256,2048]{1,0:T(8,128)(2,1)} %constant_dynamic-slice_fusion.6.w_out) | copy-start | bytes 3145732
  797.4 11.3 copy-start.2
  797.4 11.9 %copy-start.3 = (bf16[4096,256]{1,0:T(8,128)(2,1)S(1)}, bf16[4096,256]{1,0:T(8,128)(2,1)}, u32[]{:S(2)}) copy-start(bf16[4096,256]{1,0:T(8,128)(2,1)} %shard_map.204.attended) | copy-start | bytes 6291460
  809.3 5.5 copy-start.4
  809.3 5.5 copy-start.11
  816.9 128.4 %copy-start.15 = (f32[4096]{0:T(1024)S(1)}, f32[4096]{0:T(1024)}, u32[]{:S(2)}) copy-start(f32[4096]{0:T(1024)} %copy-done.14) | copy-start | bytes 49156
  816.9 128.4 %copy-start.17 = (f32[2048]{0:T(1024)S(1)}, f32[2048]{0:T(1024)}, u32[]{:S(2)}) copy-start(f32[2048]{0:T(1024)} %copy-done.16) | copy-start | bytes 24580
  965.2 1.9 copy-start.12
  971.3 139.6 %copy-start.8 = (bf16[3,2048,256]{2,1,0:T(8,128)(2,1)S(1)}, bf16[3,2048,256]{2,1,0:T(8,128)(2,1)}, u32[]{:S(2)}) copy-start(bf16[3,2048,256]{2,1,0:T(8,128)(2,1)} %get-tuple-element.104) | copy-start | bytes 9437188
  1114.3 9.9 copy-start.9
  1120.1 15.6 %all-to-all-start = ((bf16[8,64,768]{2,1,0:T(8,128)(2,1)}), bf16[8,64,768]{2,1,0:T(8,128)(2,1)S(1)}, u32[]{:S(2)}, u32[]{:S(2)}) async-start(bf16[8,64,768]{2,1,0:T(8,128)(2,1)} %bitcast.63), calls=%async_computation.2 | async-start | bytes 1572864 | tf_op jit(solution)/shard_map/all_to_all | solution.py:1205
  1136.6 5.3 copy-start.10
Sparse Core Ops, SparseCore 0:
  142.4 83.2 all-gather.2
  400.4 78.0 all-gather.4
  506.5 113.2 reduce-scatter.2
  967.2 61.6 reduce-scatter.4

commit v8 on v7

--- a/solution.py
+++ b/solution.py
@@ -115,6 +115,10 @@
     return pl.ds(pl.multiple_of(first + half * HALF, HALF), HALF)
 
 
+def quarter_of(y, c, x, half, quarter):
+    return pl.ds(pl.multiple_of((4 * c + 2 * y + x) * TILE + half * HALF + quarter * (HALF // 2), HALF // 2), HALF // 2)
+
+
 def remote(src, dst, send, recv, peer):
     return pltpu.make_async_remote_copy(
         src_ref=src, dst_ref=dst, send_sem=send, recv_sem=recv, device_id=peer, device_id_type=MESH_ID
@@ -129,6 +133,64 @@
 
 
 class Gather:
+    def __init__(self, own, whole, send, recv):
+        y, c, z, x = spot()
+        across_x, across_y, core = near()
+
+        def passed(k, at, peer):
+            return remote(whole.at[at], whole.at[at], send.at[k], recv.at[k], peer)
+
+        self.halves = []
+        for half in (0, 1):
+            k, at = 9 * half, place_of(y, c, x, half)
+            mine = [
+                remote(own(half), whole.at[at], send.at[k + m], recv.at[k + m], peer)
+                for m, peer in enumerate((across_x, across_y, core))
+            ]
+            held_x, held_y = (y, c, 1 - x), (1 - y, c, x)
+            far = (1 - y, c, 1 - x)
+            self.halves.append(
+                (
+                    mine,
+                    passed(k + 3, quarter_of(*held_x, half, 0), across_y),
+                    passed(k + 4, quarter_of(*held_y, half, 1), across_x),
+                    [passed(k + 5, place_of(*held_x, half), core), passed(k + 6, place_of(*held_y, half), core)],
+                    [passed(k + 7 + q, quarter_of(*far, half, q), core) for q in (0, 1)],
+                )
+            )
+
+    def start(self, half):
+        for copy in self.halves[half][0]:
+            copy.start()
+
+    def pass_near(self, half):
+        mine, over_y, over_x, from_near, from_far = self.halves[half]
+        mine[0].wait_recv()
+        over_y.start()
+        from_near[0].start()
+        mine[1].wait_recv()
+        over_x.start()
+        from_near[1].start()
+
+    def pass_far(self, half):
+        mine, over_y, over_x, from_near, from_far = self.halves[half]
+        over_y.wait_recv()
+        from_far[0].start()
+        over_x.wait_recv()
+        from_far[1].start()
+
+    def finish(self):
+        for mine, over_y, over_x, from_near, from_far in self.halves:
+            for copy in [mine[2]] + from_near + from_far:
+                copy.wait_recv()
+            for copy in mine + [over_y, over_x] + from_near + from_far:
+                copy.wait_send()
+
+
+GATHER_COPIES = 18
+
+
+class GatherWhole:
     def __init__(self, own, whole, send, recv):
         y, c, z, x = spot()
         across_x, across_y, core = near()
@@ -183,23 +245,102 @@
             copy.wait_send()
 
 
-GATHER_COPIES = 14
-
-
-def run_gather(own, whole, send, recv, local, beside=lambda h: None):
-    y, c, z, x = spot()
-    keep = pltpu.make_async_copy(own, whole.at[place_of(y, c, x)], local)
-    keep.start()
-    gather = Gather(lambda half: own.at[pl.ds(half * HALF, HALF)], whole, send, recv)
-    gather.start(0)
-    gather.start(1)
-    gather.pass_first()
-    beside(1)
-    gather.pass_second()
-    gather.pass_far()
-    gather.finish()
-    beside(2)
-    keep.wait()
+class Trade:
+    def __init__(self, sources, dst, held, send, recv, held_recv, pass_send, detour=True):
+        y, c, z, x = spot()
+        self.detour = detour
+        across_y = (1 - y, c, z, x)
+        self.moves = z != 2 * c + y
+        self.away = (y == c) & (z == 1 + y)
+        self.straight = self.moves & jnp.logical_not(self.away) if detour else self.moves
+        self.passes = (1 - y == c) & (z == 2 - y)
+        partner = partner_of(y, c, z, x)
+        comes_by = ((partner[0] == partner[1]) & (partner[2] == 1 + partner[0])).astype(jnp.int32)
+        self.sender = (flip(partner[0], comes_by), partner[1], partner[2], x) if detour else partner
+        self.across_y = across_y
+        target = partner_of(*across_y)
+        self.direct, self.keep, self.out, self.onward = [], [], [], []
+        for h, source in enumerate(sources):
+            self.direct.append(remote(source, dst(h, partner), send.at[h], recv.at[h], partner))
+            self.keep.append(pltpu.make_async_copy(source, dst(h, (y, c, z, x)), recv.at[h]))
+            self.out.append(remote(source, held.at[h], send.at[h], held_recv.at[h], across_y))
+            self.onward.append(remote(held.at[h], dst(h, target), pass_send.at[h], recv.at[h], target))
+
+    def greet(self, barrier, neighbours_greet):
+        @pl.when(self.moves)
+        def _():
+            pl.semaphore_signal(barrier, inc=1, device_id=self.sender, device_id_type=MESH_ID)
+
+        count = self.straight.astype(jnp.int32)
+        if not self.detour:
+            return count
+        count = count + self.passes.astype(jnp.int32)
+        if not neighbours_greet:
+
+            @pl.when(self.passes)
+            def _():
+                pl.semaphore_signal(barrier, inc=1, device_id=self.across_y, device_id_type=MESH_ID)
+
+            count = count + self.away.astype(jnp.int32)
+        return count
+
+    def start(self, h):
+        @pl.when(self.straight)
+        def _():
+            self.direct[h].start()
+
+        if self.detour:
+
+            @pl.when(self.away)
+            def _():
+                self.out[h].start()
+
+        @pl.when(jnp.logical_not(self.moves))
+        def _():
+            self.keep[h].start()
+
+    def wait_sent(self, h):
+        @pl.when(self.straight)
+        def _():
+            self.direct[h].wait_send()
+
+        if self.detour:
+
+            @pl.when(self.away)
+            def _():
+                self.out[h].wait_send()
+
+    def forward(self, h):
+        if self.detour:
+
+            @pl.when(self.passes)
+            def _():
+                self.out[h].wait_recv()
+                self.onward[h].start()
+
+    def arrive(self, h):
+        @pl.when(self.moves)
+        def _():
+            self.direct[h].wait_recv()
+
+        @pl.when(jnp.logical_not(self.moves))
+        def _():
+            self.keep[h].wait()
+
+    def finish(self, first=0):
+        for h in range(len(self.direct)):
+            if h >= first:
+                self.wait_sent(h)
+
+            if self.detour:
+
+                @pl.when(self.passes)
+                def _():
+                    self.onward[h].wait_send()
+
+
+def trade_scratch(pieces, rows, width):
+    return [pltpu.VMEM((pieces, rows, width), LOW)] + [pltpu.SemaphoreType.DMA((pieces,)) for _ in range(4)]
 
 
 class Chain:
@@ -298,14 +439,49 @@
     return [(y, c, lax.rem(z + dz, 4), x) for dz in (1, 2, 3)]
 
 
-def spread_columns(whole, parts, send, recv):
-    size = whole.shape[1] // 4
-    return [
-        remote(
-            whole.at[:, pl.ds(pl.multiple_of(peer[2] * size, size), size)], parts.at[k], send.at[k], recv.at[k], peer
-        )
-        for k, peer in enumerate(line_of())
-    ]
+class Fold:
+    def __init__(self, whole, far, near_part, cross, mine, theirs, send, recv, local):
+        y, c, z, x = spot()
+        a, b = z // 2, lax.rem(z, 2)
+        size = whole.shape[1] // 4
+
+        def slab(at):
+            return whole.at[:, pl.ds(pl.multiple_of(at * size, size), size)]
+
+        pair, middle = (y, c, 2 * a + 1 - b, x), (y, c, 2 * (1 - a) + b, x)
+        self.far = remote(slab(2 * (1 - a) + 1 - b), far, send.at[0], recv.at[0], pair)
+        self.near = remote(slab(2 * a + 1 - b), near_part, send.at[1], recv.at[1], pair)
+        self.cross = remote(mine, cross, send.at[2], recv.at[2], middle)
+        self.fetches = [
+            pltpu.make_async_copy(slab(2 * (1 - a) + b), mine, local.at[0]),
+            pltpu.make_async_copy(far, theirs, local.at[1]),
+        ]
+        self.mine, self.theirs = mine, theirs
+
+    def start(self):
+        self.far.start()
+        self.fetches[0].start()
+
+    def fold(self):
+        self.far.wait_recv()
+        self.fetches[1].start()
+        for copy in self.fetches:
+            copy.wait()
+        add_rows(self.mine, 0, self.theirs, 0, self.mine.shape[0])
+        self.cross.start()
+        self.near.start()
+
+    def finish(self):
+        for copy in (self.near, self.cross):
+            copy.wait_recv()
+        for copy in (self.far, self.near, self.cross):
+            copy.wait_send()
+
+
+def fold_peers():
+    y, c, z, x = spot()
+    a, b = z // 2, lax.rem(z, 2)
+    return ((y, c, 2 * a + 1 - b, x), (y, c, 2 * (1 - a) + b, x))
 
 
 def add_rows(total, first, term, start, count):
@@ -390,58 +566,49 @@
             copy.wait_send()
 
 
-def run_scatter(produce, *scratch, beside=lambda: None):
-    scatter = Scatter(produce, *scratch)
-    scatter.begin()
-    scatter.relay()
-    beside()
-    scatter.arrive()
-    scatter.finish()
+def sum_and_gather(part_of, rows_of_half, gather, beside):
+    sums = [part_of(half) for half in (0, 1)]
+    sums[0].begin()
+    sums[0].relay()
+    sums[1].begin()
+    sums[0].arrive()
+    rows_of_half(0)
+    gather.start(0)
+    beside(0)
+    sums[1].relay()
+    beside(1)
+    sums[1].arrive()
+    rows_of_half(1)
+    gather.start(1)
+    gather.pass_near(0)
+    beside(2)
+    gather.pass_near(1)
+    gather.pass_far(0)
+    gather.pass_far(1)
+    gather.finish()
+    beside(3)
+    for half in (0, 1):
+        sums[half].finish()
 
 
 def begin_kernel(
     x_own, w_query, w_key, w_value, facts, x_whole, w_qkv, facts_whole,
-    trade_send, trade_recv, gather_send, gather_recv, w_send, w_recv, fact_send, fact_recv, local, *sems
+    gather_send, gather_recv, w_send, w_recv, fact_send, fact_recv, local, *scratch
 ):
     y, c, z, x = spot()
     row = 2 * y + c
-    partner = partner_of(y, c, z, x)
-    moves = z != 2 * c + y
     layer = others()
+    trade_parts, sems = scratch[:5], scratch[5:]
+    trade = Trade(
+        [x_own.at[half] for half in (0, 1)], lambda half, at: x_whole.at[place_of(at[0], at[1], at[3], half)], *trade_parts, detour=False
+    )
     barrier, count = greet_neighbours(layer)
-
-    @pl.when(moves)
-    def _():
-        pl.semaphore_signal(barrier, inc=1, device_id=partner, device_id_type=MESH_ID)
-
-    pl.semaphore_wait(barrier, count + moves.astype(jnp.int32))
+    pl.semaphore_wait(barrier, count + trade.greet(barrier, True))
 
     shard, width = w_query.shape
     owned = width // 8
-    trades = [
-        remote(
-            x_own.at[half],
-            x_whole.at[place_of(partner[0], partner[1], partner[3], half)],
-            trade_send.at[half],
-            trade_recv.at[half],
-            partner,
-        )
-        for half in (0, 1)
-    ]
-    keeps = [
-        pltpu.make_async_copy(x_own.at[half], x_whole.at[place_of(y, c, x, half)], trade_recv.at[half]) for half in (0, 1)
-    ]
-
-    @pl.when(moves)
-    def _():
-        for copy in trades:
-            copy.start()
-
-    @pl.when(jnp.logical_not(moves))
-    def _():
-        for copy in keeps:
-            copy.start()
-
+    for half in (0, 1):
+        trade.start(half)
     spread = [
         remote(facts, facts_whole.at[row, z, x], fact_send.at[k], fact_recv.at[k], peer) for k, peer in enumerate(layer)
     ]
@@ -456,17 +623,10 @@
     for copy in spread + kept:
         copy.start()
 
-    gather = Gather(lambda half: x_whole.at[place_of(y, c, x, half)], x_whole, gather_send, gather_recv)
+    gather = GatherWhole(lambda half: x_whole.at[place_of(y, c, x, half)], x_whole, gather_send, gather_recv)
     for half in (0, 1):
-
-        @pl.when(moves)
-        def _():
-            trades[half].wait_recv()
-
-        @pl.when(jnp.logical_not(moves))
-        def _():
-            keeps[half].wait()
-
+        trade.forward(half)
+        trade.arrive(half)
         gather.start(half)
 
     for copy in kept:
@@ -491,12 +651,7 @@
     gather.pass_far()
     arrive(2)
     gather.finish()
-
-    @pl.when(moves)
-    def _():
-        for copy in trades:
-            copy.wait_send()
-
+    trade.finish()
     for copy in spread:
         copy.wait_send()
     for chain in chains:
@@ -532,7 +687,8 @@
         in_specs=[in_vmem()] + [anywhere()] * 4,
         out_specs=[anywhere()] * 3,
         scratch_shapes=[
-            dma(2), dma(2), dma(GATHER_COPIES), dma(GATHER_COPIES), dma(3, 7), dma(3, 7), dma(7), dma(7), dma(4), *chain_sems(2)
+            dma(GATHER_COPIES), dma(GATHER_COPIES), dma(3, 7), dma(3, 7), dma(7), dma(7), dma(4),
+            *trade_scratch(2, block // 2, width), *chain_sems(2),
         ],
         compiler_params=remote_params(1),
         cost_estimate=pl.CostEstimate(flops=0, bytes_accessed=350_000_000, transcendentals=0),
@@ -545,12 +701,16 @@
     return sum(part.astype(jnp.float32) for part in parts)
 
 
-def over_chunks(work):
+def over_chunks(work, half):
     def step(i, carry):
-        work(pl.ds(pl.multiple_of(i * CHUNK, CHUNK), CHUNK))
+        work(pl.ds(pl.multiple_of(half * HALF + i * CHUNK, CHUNK), CHUNK))
         return carry
 
-    lax.fori_loop(0, TILE // CHUNK, step, 0)
+    lax.fori_loop(0, HALF // CHUNK, step, 0)
+
+
+def own_halves(own):
+    return lambda half: own.at[pl.ds(half * HALF, HALF)]
 
 
 def inverse_of(value):
@@ -579,17 +739,19 @@
         for chain in chains:
             chain.arrive(h)
 
-    def produce(turn, y, c, x, out):
-        at = place_of(y, c, x)
-
-        def step(i, carry):
-            columns = pl.ds(pl.multiple_of(i * TILE, TILE), TILE)
-            out[:, columns] = dot_wide(attended[at, :], w_out[:, columns]).astype(LOW)
-            return carry
-
-        lax.fori_loop(0, width // TILE, step, 0)
-
-    run_scatter(produce, *scatter, beside=lambda: arrive(0))
+    def part_of(half):
+        def produce(turn, y, c, x, out):
+            at = place_of(y, c, x, half)
+
+            def step(i, carry):
+                columns = pl.ds(pl.multiple_of(i * TILE, TILE), TILE)
+                out[:, columns] = dot_wide(attended[at, :], w_out[:, columns]).astype(LOW)
+                return carry
+
+            lax.fori_loop(0, width // TILE, step, 0)
+
+        return Scatter(produce, *scatter, part=half, start=half * HALF, size=HALF)
+
     total, landed = scatter[2], scatter[4]
 
     def chunk(here):
@@ -597,11 +759,17 @@
         resid[here, :] = value
         own[here, :] = (value * inverse_of(value) * gain[...]).astype(LOW)
 
-    over_chunks(chunk)
-    run_gather(own, normed, send, recv, local.at[0], arrive)
+    def rows_of_half(half):
+        over_chunks(chunk, half)
+
+    y, c, z, x = spot()
+    gather = Gather(own_halves(own), normed, send, recv)
+    sum_and_gather(part_of, rows_of_half, gather, lambda turn: arrive(turn - 1) if turn > 0 else None)
+    keep = pltpu.make_async_copy(own, normed.at[place_of(y, c, x)], local.at[0])
+    keep.start()
     for chain in chains:
         chain.finish()
-    for copy in kept:
+    for copy in kept + [keep]:
         copy.wait()
 
 
@@ -619,7 +787,7 @@
         in_specs=[in_vmem()] * 6,
         out_specs=[in_vmem()] + [anywhere()] * 3,
         scratch_shapes=[pltpu.VMEM((block, width), LOW)]
-        + scatter_scratch(width)
+        + scatter_scratch(width, 2)
         + [dma(GATHER_COPIES), dma(GATHER_COPIES), dma(3), *chain_sems(2)],
         compiler_params=remote_params(2),
         cost_estimate=pl.CostEstimate(flops=0, bytes_accessed=450_000_000, transcendentals=0),
@@ -639,48 +807,55 @@
 
 
 def close_mlp_kernel(
-    d_gate, d_up, w_gate, w_up, resid, upstream, gain, grad_a, grad_b, d_resid, gain_term, d_resid_whole, parts_a, parts_b, own, blocks, *scratch
+    d_gate, d_up, w_gate, w_up, resid, upstream, gain, grad_a, grad_b, d_resid, gain_term, d_resid_whole,
+    far_a, near_a, cross_a, far_b, near_b, cross_b, own, blocks, *scratch
 ):
-    scatter, (send, recv, local, fetched, line_send, line_recv) = scratch[:7], scratch[7:]
+    scatter, (send, recv, local, fetched, fold_send, fold_recv, fold_local, mine, theirs) = scratch[:7], scratch[7:]
     y, c, z, x = spot()
     width = w_gate.shape[0]
-    order = [(r, k, q) for r, q in ((1 - y, 1 - x), (y, 1 - x), (1 - y, x), (y, x)) for k in (1 - c, c)]
+    order = [
+        place_of(r, k, q, half)
+        for half in (0, 1)
+        for r, q in ((1 - y, 1 - x), (y, 1 - x), (1 - y, x), (y, x))
+        for k in (1 - c, c)
+    ]
 
     def fetch(turn):
-        at = place_of(*order[turn])
         slot = turn % 2
         return [
-            pltpu.make_async_copy(source.at[at], blocks.at[slot, m], fetched.at[slot, m])
+            pltpu.make_async_copy(source.at[order[turn]], blocks.at[slot, m], fetched.at[slot, m])
             for m, source in enumerate((d_gate, d_up))
         ]
 
     for copy in fetch(0):
         copy.start()
-    greet(near() + tuple(line_of()))
-    to_layers = [
-        copy
-        for k, (grad, parts) in enumerate(((grad_a, parts_a), (grad_b, parts_b)))
-        for copy in spread_columns(grad, parts, line_send.at[k], line_recv.at[k])
+    greet(near() + fold_peers())
+    folds = [
+        Fold(*refs, mine.at[k], theirs, fold_send.at[k], fold_recv.at[k], fold_local.at[k])
+        for k, refs in enumerate(((grad_a, far_a, near_a, cross_a), (grad_b, far_b, near_b, cross_b)))
     ]
-    for copy in to_layers:
-        copy.start()
-
-    def produce(turn, to_y, to_c, to_x, out):
-        if turn < 7:
-            for copy in fetch(turn + 1):
-                copy.start()
-        for copy in fetch(turn):
-            copy.wait()
-
-        def step(i, carry):
-            columns = pl.ds(pl.multiple_of(i * TILE, TILE), TILE)
-            part = dot_nt(blocks[turn % 2, 0], w_gate[columns, :]) + dot_nt(blocks[turn % 2, 1], w_up[columns, :])
-            out[:, columns] = part.astype(LOW)
-            return carry
-
-        lax.fori_loop(0, width // TILE, step, 0)
-
-    run_scatter(produce, *scatter)
+    for fold in folds:
+        fold.start()
+
+    def part_of(half):
+        def produce(turn, to_y, to_c, to_x, out):
+            turn = turn + 8 * half
+            if turn < 15:
+                for copy in fetch(turn + 1):
+                    copy.start()
+            for copy in fetch(turn):
+                copy.wait()
+
+            def step(i, carry):
+                columns = pl.ds(pl.multiple_of(i * TILE, TILE), TILE)
+                part = dot_nt(blocks[turn % 2, 0], w_gate[columns, :]) + dot_nt(blocks[turn % 2, 1], w_up[columns, :])
+                out[:, columns] = part.astype(LOW)
+                return carry
+
+            lax.fori_loop(0, width // TILE, step, 0)
+
+        return Scatter(produce, *scatter, part=half, start=half * HALF, size=HALF)
+
     total, landed = scatter[2], scatter[4]
     gain_term[...] = jnp.zeros_like(gain_term)
 
@@ -691,10 +866,16 @@
         own[here, :] = value.astype(LOW)
         fold_rows(gain_term, terms)
 
-    over_chunks(chunk)
-    run_gather(own, d_resid_whole, send, recv, local.at[0])
-    for copy in to_layers:
-        copy.wait()
+    def rows_of_half(half):
+        over_chunks(chunk, half)
+
+    gather = Gather(own_halves(own), d_resid_whole, send, recv)
+    sum_and_gather(part_of, rows_of_half, gather, lambda turn: folds[turn].fold() if turn < 2 else None)
+    keep = pltpu.make_async_copy(own, d_resid_whole.at[place_of(y, c, x)], local.at[0])
+    keep.start()
+    for fold in folds:
+        fold.finish()
+    keep.wait()
 
 
 def close_mlp(d_gate, d_up, w_gate, w_up, resid, upstream, gain, *grads):
@@ -706,14 +887,14 @@
             jax.ShapeDtypeStruct((block, width), jnp.float32),
             jax.ShapeDtypeStruct((8, width), jnp.float32),
             jax.ShapeDtypeStruct((8 * block, width), LOW),
-            jax.ShapeDtypeStruct((3, width, hidden // 4), LOW),
-            jax.ShapeDtypeStruct((3, width, hidden // 4), LOW),
+            *[jax.ShapeDtypeStruct((width, hidden // 4), LOW)] * 6,
         ),
         in_specs=[anywhere()] * 2 + [in_vmem()] * 5 + [anywhere()] * 2,
-        out_specs=[in_vmem(), in_vmem()] + [anywhere()] * 3,
-        scratch_shapes=[pltpu.VMEM((block, width), LOW), pltpu.VMEM((2, 2, block, hidden), LOW)]
-        + scatter_scratch(width)
-        + [dma(GATHER_COPIES), dma(GATHER_COPIES), dma(1), dma(2, 2), dma(2, 3), dma(2, 3)],
+        out_specs=[in_vmem(), in_vmem()] + [anywhere()] * 7,
+        scratch_shapes=[pltpu.VMEM((block, width), LOW), pltpu.VMEM((2, 2, block // 2, hidden), LOW)]
+        + scatter_scratch(width, 2)
+        + [dma(GATHER_COPIES), dma(GATHER_COPIES), dma(1), dma(2, 2), dma(2, 3), dma(2, 3), dma(2, 2)]
+        + [pltpu.VMEM((2, width, hidden // 4), LOW), pltpu.VMEM((width, hidden // 4), LOW)],
         compiler_params=remote_params(3),
         cost_estimate=pl.CostEstimate(flops=0, bytes_accessed=450_000_000, transcendentals=0),
     )(d_gate, d_up, w_gate, w_up, resid, upstream, gain, *grads)
@@ -908,10 +1089,6 @@
         gather.start(1)
         keep.start()
 
-    @pl.when(i == steps - 3)
-    def _():
-        gather.pass_first()
-
     def step(n, carry):
         columns = pl.ds(pl.multiple_of(n * HALF, HALF), HALF)
         gate_part, up_part = dot_wide(normed[...], w_gate[:, columns]), dot_wide(normed[...], w_up[:, columns])
@@ -924,8 +1101,10 @@
 
     @pl.when(i == steps - 1)
     def _():
-        gather.pass_second()
-        gather.pass_far()
+        for half in (0, 1):
+            gather.pass_near(half)
+        for half in (0, 1):
+            gather.pass_far(half)
         gather.finish()
         keep.wait()
 
@@ -960,17 +1139,16 @@
 
 
 def attend_back_kernel(
-    ends, qkv, grads, out_grad, mixed, out, out_parts, mixed_home, query_total, key_total, value_total, send, recv, trade_send, trade_recv
+    ends, qkv, grads, out_grad, mixed, out, out_parts, mixed_home, query_total, key_total, value_total, send, recv, *trade_parts
 ):
     j = pl.program_id(0)
     y, c, z, x = spot()
     heads = qkv.shape[1] // (3 * HD)
     shard = out_grad.shape[0] // 4
     owners, holders = out_turns()
-    partner = partner_of(y, c, z, x)
-    moves = z != 2 * c + y
-    trade_copy = remote(mixed, mixed_home, trade_send.at[0], trade_recv.at[0], partner)
-    keep = pltpu.make_async_copy(mixed, mixed_home, trade_recv.at[0])
+    trade = Trade(
+        [mixed.at[pl.ds(half * HALF, HALF)] for half in (0, 1)], lambda half, at: mixed_home.at[pl.ds(half * HALF, HALF)], *trade_parts
+    )
 
     def to_owner(turn):
         return remote(out_grad.at[pl.ds(turn * shard, shard)], out_parts.at[z], send.at[turn], recv.at[z], owners[turn][0])
@@ -988,20 +1166,9 @@
             def _():
                 pl.semaphore_signal(barrier, inc=1, device_id=peer, device_id_type=MESH_ID)
 
-        @pl.when(moves)
-        def _():
-            pl.semaphore_signal(barrier, inc=1, device_id=partner, device_id_type=MESH_ID)
-
-        pl.semaphore_wait(barrier, 4 - (x == z // 2).astype(jnp.int32) + moves.astype(jnp.int32))
-
-        @pl.when(moves)
-        def _():
-            trade_copy.start()
-
-        @pl.when(jnp.logical_not(moves))
-        def _():
-            keep.start()
-
+        pl.semaphore_wait(barrier, 4 - (x == z // 2).astype(jnp.int32) + trade.greet(barrier, False))
+        for half in (0, 1):
+            trade.start(half)
         for turn in range(4):
 
             @pl.when(jnp.logical_not(owners[turn][1]))
@@ -1061,13 +1228,41 @@
             def _():
                 to_self(turn).wait()
 
-        @pl.when(moves)
-        def _():
-            trade_copy.wait()
-
-        @pl.when(jnp.logical_not(moves))
-        def _():
-            keep.wait()
+        for half in (0, 1):
+            trade.arrive(half)
+        trade.finish()
+
+    @pl.when(j == 1)
+    def _():
+        for half in (0, 1):
+            trade.forward(half)
+
+
+def back_mlp_kernel(upstream, w_down, gate, up, d_gate, d_up):
+    def step(n, carry):
+        columns = pl.ds(pl.multiple_of(n * HALF, HALF), HALF)
+        d_hidden = dot_nt(upstream[...], w_down[columns, :])
+        d_gate[:, columns], d_up[:, columns] = gate_backward(
+            d_hidden, gate[:, columns], up[:, columns], jax.nn.sigmoid(gate[:, columns])
+        )
+        return carry
+
+    lax.fori_loop(0, gate.shape[1] // HALF, step, 0)
+
+
+def back_mlp(upstream, w_down, gate, up):
+    places, width = upstream.shape
+    hidden = gate.shape[1]
+    rows = lambda size: pl.BlockSpec((TILE, size), lambda i: (i, 0))
+    return pl.pallas_call(
+        back_mlp_kernel,
+        out_shape=(jax.ShapeDtypeStruct((places, hidden), LOW), jax.ShapeDtypeStruct((places, hidden), LOW)),
+        grid=(places // TILE,),
+        in_specs=[rows(width), pl.BlockSpec(w_down.shape, lambda i: (0, 0)), rows(hidden), rows(hidden)],
+        out_specs=[rows(hidden), rows(hidden)],
+        compiler_params=pltpu.CompilerParams(vmem_limit_bytes=VMEM_LIMIT),
+        cost_estimate=pl.CostEstimate(flops=0, bytes_accessed=90_000_000, transcendentals=0),
+    )(upstream, w_down, gate, up)
 
 
 def attend(ends, qkv):
@@ -1106,8 +1301,7 @@
             pltpu.VMEM((heads, TILE, HD), jnp.float32),
             dma(4),
             dma(4),
-            dma(1),
-            dma(1),
+            *trade_scratch(2, HALF, mixed.shape[1]),
         ],
         compiler_params=remote_params(6),
         cost_estimate=pl.CostEstimate(flops=0, bytes_accessed=300_000_000, transcendentals=0),
@@ -1156,8 +1350,8 @@
     out_rows = lax.all_gather(after(facts, w_out), ("z", "x"), axis=0, tiled=True)
     w_out_own = lax.dynamic_slice_in_dim(out_rows, lax.axis_index("x") * owned, owned, 0)
 
+    upstream = trade(after(facts, cotangent)).reshape(block, width)
     qkv = dot_wide(layer_normed, w_qkv).astype(LOW)
-    upstream = trade(after(facts, cotangent)).reshape(block, width)
     attended = attend(ends, qkv)
     resid, layer_mlp, own_gate, own_up = close_attention(after(upstream, attended), w_out_own, x_own, full_gain_mlp, w_gate, w_up)
 
@@ -1172,16 +1366,15 @@
         layers_pairs = [(at, (at + up) % 4) for at in range(4)]
         slab = lax.dynamic_slice_in_dim(down_term, (layer + up) % 4 * down_rows, down_rows, 0)
         down_parts.append(lax.ppermute(slab, "z", layers_pairs))
-    d_hidden = contract_cols(after(down_term, layer_upstream), own_down)
-    d_gate, d_up = gate_backward(d_hidden, gate, up_part, jax.nn.sigmoid(gate))
+    d_gate, d_up = back_mlp(after(down_term, layer_upstream), own_down, gate, up_part)
     gate_term, up_term = contract_rows(layer_mlp, d_gate).astype(LOW), contract_rows(layer_mlp, d_up).astype(LOW)
-    d_resid, gain_mlp_term, layer_d_resid, gate_parts, up_parts = close_mlp(
+    d_resid, gain_mlp_term, layer_d_resid, *parts = close_mlp(
         after((mixed_sum, *down_parts), d_gate), d_up, own_gate, own_up, resid, upstream, full_gain_mlp, gate_term, up_term
     )
 
-    def own_part(whole, parts):
-        own = lax.dynamic_slice_in_dim(whole, layer * parts.shape[2], parts.shape[2], 1)
-        return own.astype(jnp.float32) + jnp.sum(parts.astype(jnp.float32), axis=0)
+    def own_part(whole, near_part, cross):
+        own = lax.dynamic_slice_in_dim(whole, layer * cross.shape[1], cross.shape[1], 1)
+        return own.astype(jnp.float32) + near_part.astype(jnp.float32) + cross.astype(jnp.float32)
 
     mixed = (resid + after(layer_d_resid, mixed_sum).astype(jnp.float32)).astype(LOW)
     grad_down = lax.dynamic_slice_in_dim(down_term, layer * down_rows, down_rows, 0).astype(jnp.float32)
@@ -1191,7 +1384,7 @@
     d_attended = contract_cols(layer_d_resid, w_out_own).astype(LOW)
     d_qkv, out_parts, mixed = attend_back(ends, qkv, d_attended, out_term, mixed)
     mixed = mixed.reshape(rows_here, block, width)
-    grad_gate, grad_up = own_part(gate_term, gate_parts), own_part(up_term, up_parts)
+    grad_gate, grad_up = own_part(gate_term, *parts[1:3]), own_part(up_term, *parts[4:6])
     grad_out = jnp.sum(out_parts.astype(jnp.float32), axis=0)
     qkv_term = contract_rows(layer_normed, d_qkv).astype(LOW)
     grad_low, gain_grads = close_layer(

time: 1160 us -> 1110 us (0.957)
  other arithmetic: 49.6 us -> 26.3 us
  matrix products: 171 us -> 148 us
    pallas_call x0 -> x1, Pallas kernels: none -> 35.4 us  [back_mlp(): pl.pallas_call(back_mlp_kernel, out_shape=(jax.ShapeDtypeStruct((places,...]
    pallas_call x1, Pallas kernels: 128 us -> 93.5 us  [attend_back(): pl.pallas_call(attend_back_kernel, out_shape=(jax.ShapeDtypeStruct((place...]
    dot_general x2 -> x1, matrix products: 32.6 us -> 9.83 us  [contract_cols(): lax.dot_general(left, right, (((1,), (1,)), ((), ())), preferred_element_...]
    convert_element_type x1 -> x0, other arithmetic: 19.4 us -> none  [gate_backward(): d_up = (d_hidden * gate * sigmoid_gate).astype(jnp.bfloat16)]
  transfers between devices with their start and end apart: 9 -> 9, of which waited for: 2 -> 3; matrix products, arithmetic and copies ran while one was open for 15% -> 11% of each run, Pallas kernels for 23% -> 27%
where the time goes in v8:
time: 1110 us; the launch traced here: 1100 us
  Pallas kernels  860 us (77%)
  matrix products  148 us (13%)
  other arithmetic  26.3 us (2%)
  local copies, waits for them, and re-layouts  26 us (2%)
  waiting for transfers between devices  14.6 us (1%)
  between operations  14.3 us (1%)
    pallas_call x1, Pallas kernels, close_attention(): pl.pallas_call(close_attention_kernel, out_shape=(jax.ShapeDtypeStruct((b...  168 us
    pallas_call x1, Pallas kernels, close_mlp(): pl.pallas_call(close_mlp_kernel, out_shape=(jax.ShapeDtypeStruct((block,...  168 us
    pallas_call x1, Pallas kernels, close_layer(): pl.pallas_call(close_layer_kernel, out_shape=(jax.ShapeDtypeStruct((block...  143 us
    pallas_call x1, Pallas kernels, begin(): pl.pallas_call(begin_kernel, out_shape=(jax.ShapeDtypeStruct((8 * block,...  130 us
    dot_general x5, matrix products, contract_rows(): lax.dot_general(left, right, (((0,), (0,)), ((), ())), preferred_element_...  94.5 us
    pallas_call x1, Pallas kernels, attend_back(): pl.pallas_call(attend_back_kernel, out_shape=(jax.ShapeDtypeStruct((place...  93.5 us
    pallas_call x1, Pallas kernels, open_mlp(): pl.pallas_call(open_mlp_kernel, out_shape=(jax.ShapeDtypeStruct((places,...  80.8 us
    dot_general x2, matrix products, dot_wide(): return jnp.dot(left, right, preferred_element_type=jnp.float32)  43.5 us
  transfers between devices with their start and end apart: 9, of which 3 were waited for; matrix products, arithmetic and copies ran while one was open for 11% of the time, Pallas kernels for 27%

profile of v8, /device:TPU:0, one launch (start us, length us, event | category | flops | bytes accessed | tf_op | source)
XLA Modules:
  0.0 1099.2 jit_solution(14603305366631402902)
XLA Ops:
  7.2 0.0 all-gather.3.cloned.1.call-start
  7.2 0.7 pad_convert_fusion
  7.9 0.7 bitcast_convert_fusion.1
  8.5 0.7 convert_element_type.98
  9.2 0.1 scatter.19
  9.3 0.2 scatter.20.facts
  9.5 0.6 copy-done.13
  10.1 130.0 %shard_map.203 = (bf16[4096,2048]{1,0:T(8,128)(2,1)}, bf16[4,4,128,768]{3,2,1,0:T(8,128)(2,1)}, f32[4,4,2,8,128]{4,3,2,1,0:T(8,128)}) custom-call(bf16[2,256,2048]{2,1,0:T(8,128)(2,1)} %bitcast.56, bf16[64,2048]{1,0:T(8,128)(2,1)} %w_query.1, bf16[64,2048]{1,0:T(8,128)(2,1)} %w_key.1, bf16[64,2048]{1,0:T(8,128)(2,1)} %w_value.1, f32[8,128]{1,0:T(8,128)} %copy-done.13), custom_call_target="tpu_custom_call" | custom-call | bytes 350000000 | tf_op jit(solution)/shard_map/pallas_call | solution.py:680
  140.1 2.3 collective-permute-start
  142.4 0.0 all-gather.5.cloned.1.call-start
  142.4 0.7 slice.74
  143.1 1.6 slice_reduce_fusion
  144.8 7.2 fusion
  152.0 0.7 reduce-window.9
  152.7 0.1 mul.50
  152.8 0.7 reshape_squeeze.10.gain
  153.5 20.1 %convolution_convert_fusion.1.qkv = bf16[4096,768]{1,0:T(8,128)(2,1)} fusion(bf16[2048,768]{1,0:T(8,128)(2,1)} %bitcast.53, bf16[4096,2048]{1,0:T(8,128)(2,1)} %get-tuple-element.82, f32[2048]{0:T(1024)S(1)} %mul.50, f32[4096]{0:T(1024)S(1)} %add_rsqrt_fusion), kind=kOutput, calls=%fused_computation.6 | convolution fusion | flops 12921602048 | bytes 26238976 | tf_op jit(solution)/shard_map/dot_general | solution.py:86
  173.6 42.4 %shard_map.204.attended = bf16[4096,256]{1,0:T(8,128)(2,1)} custom-call(s32[8]{0:T(128)} %bitcast.67, bf16[4096,768]{1,0:T(8,128)(2,1)} %convolution_convert_fusion.1.qkv), custom_call_target="tpu_custom_call" | custom-call | bytes 150000000 | tf_op jit(solution)/shard_map/pallas_call | solution.py:1272
  215.9 3.2 constant_dynamic-slice_fusion.5.x_own
  219.1 6.6 all-gather.3.cloned.1.call-done
  225.8 2.3 constant_dynamic-slice_fusion.6.w_out
  228.1 167.9 %shard_map.205 = (f32[512,2048]{1,0:T(8,128)}, bf16[4096,2048]{1,0:T(8,128)(2,1)}, bf16[2048,1024]{1,0:T(8,128)(2,1)}, bf16[2048,1024]{1,0:T(8,128)(2,1)}) custom-call(bf16[4096,256]{1,0:T(8,128)(2,1)} %shard_map.204.attended, bf16[256,2048]{1,0:T(8,128)(2,1)} %constant_dynamic-slice_fusion.6.w_out, bf16[512,2048]{1,0:T(8,128)(2,1)} %constant_dynamic-slice_fusion.5.x_own, ...), custom_call_target="tpu_custom_call" | custom-call | bytes 450000000 | tf_op jit(solution)/shard_map/pallas_call | solution.py:779
  396.0 0.0 reduce-scatter.3.cloned.1.call-start
  396.1 80.8 %shard_map.206 = (f32[4096,1024]{1,0:T(8,128)}, f32[4096,1024]{1,0:T(8,128)}, bf16[4096,1024]{1,0:T(8,128)(2,1)}, bf16[4096,2048]{1,0:T(8,128)(2,1)}) custom-call(bf16[4096,2048]{1,0:T(8,128)(2,1)} %get-tuple-element.87.normed, bf16[2048,1024]{1,0:T(8,128)(2,1)} %get-tuple-element.88.w_gate, bf16[2048,1024]{1,0:T(8,128)(2,1)} %get-tuple-element.89.w_up, ...), custom_call_target="tpu_custom_call" | custom-call | bytes 250000000 | tf_op jit(solution)/shard_map/pallas_call | solution.py:1117
  476.9 23.5 %convolution_convert_fusion = bf16[4096,2048]{1,0:T(8,128)(2,1)} fusion(bf16[4096,1024]{1,0:T(8,128)(2,1)} %get-tuple-element.93, bf16[1024,2048]{1,0:T(8,128)(2,1)} %all-gather.5.cloned.1.call-done.w_down), kind=kOutput, calls=%fused_computation.5 | convolution fusion | flops 17188257792 | bytes 29360128 | tf_op jit(solution)/shard_map/dot_general | solution.py:86
  500.4 0.0 reduce-scatter.5.cloned.1.call-start
  500.5 23.5 %convolution_convert_fusion.5 = bf16[1024,2048]{1,0:T(8,128)(2,1)S(1)} fusion(bf16[4096,1024]{1,0:T(8,128)(2,1)} %get-tuple-element.93, bf16[4096,2048]{1,0:T(8,128)(2,1)} %get-tuple-element.95.upstream), kind=kOutput, calls=%fused_computation.12 | convolution fusion | flops 17181966336 | bytes 29360128 | tf_op jit(solution)/shard_map/dot_general | solution.py:20
  524.0 2.0 copy-done.5
  526.0 1.8 constant_dynamic-slice_fusion.2
  527.8 0.9 collective-permute-start.2
  528.8 3.0 collective-permute-start.3
  531.8 35.4 %shard_map.207 = (bf16[4096,1024]{1,0:T(8,128)(2,1)}, bf16[4096,1024]{1,0:T(8,128)(2,1)}) custom-call(bf16[4096,2048]{1,0:T(8,128)(2,1)} %get-tuple-element.95.upstream, bf16[1024,2048]{1,0:T(8,128)(2,1)} %all-gather.5.cloned.1.call-done.w_down, f32[4096,1024]{1,0:T(8,128)} %get-tuple-element.96.gate, f32[4096,1024]{1,0:T(8,128)} %get-tuple-element.97.up), custom_call_target="tpu_custom_call" | custom-call | bytes 90000000 | tf_op jit(solution)/shard_map/pallas_call | solution.py:1257
  567.2 24.4 %convolution_convert_fusion.4.grad_a = bf16[2048,1024]{1,0:T(8,128)(2,1)} fusion(bf16[4096,2048]{1,0:T(8,128)(2,1)} %get-tuple-element.87.normed, bf16[4096,1024]{1,0:T(8,128)(2,1)} %get-tuple-element.99.d_gate), kind=kOutput, calls=%fused_computation.11 | convolution fusion | flops 17181966336 | bytes 29360128 | tf_op jit(solution)/shard_map/dot_general | solution.py:20
  591.6 21.3 %convolution_convert_fusion.3.grad_b = bf16[2048,1024]{1,0:T(8,128)(2,1)} fusion(bf16[4096,2048]{1,0:T(8,128)(2,1)} %get-tuple-element.87.normed, bf16[4096,1024]{1,0:T(8,128)(2,1)S(1)} %copy-done.3), kind=kOutput, calls=%fused_computation.10 | convolution fusion | flops 17181966336 | bytes 29360128 | tf_op jit(solution)/shard_map/dot_general | solution.py:20
  612.9 1.2 reduce-scatter.3.cloned.1.call-done
  614.1 167.5 %shard_map.208 = (f32[512,2048]{1,0:T(8,128)}, f32[8,2048]{1,0:T(8,128)}, bf16[4096,2048]{1,0:T(8,128)(2,1)}, bf16[2048,256]{1,0:T(8,128)(2,1)}, bf16[2048,256]{...) custom-call(bf16[4096,1024]{1,0:T(8,128)(2,1)} %get-tuple-element.99, ...), custom_call_target="tpu_custom_call" | custom-call | bytes 450000000 | tf_op jit(solution)/shard_map/pallas_call | solution.py:884
  781.7 9.8 convolution_convert_fusion.2.grads
  791.5 1.4 copy-done
  792.9 0.6 copy-done.1
  793.5 5.5 convolution_convert_fusion.6.out_grad
  799.0 2.1 add_convert_fusion.mixed
  801.1 93.5 %shard_map.209 = (bf16[4096,768]{1,0:T(8,128)(2,1)}, bf16[4,64,2048]{2,1,0:T(8,128)(2,1)}, bf16[512,2048]{1,0:T(8,128)(2,1)}) custom-call(s32[8]{0:T(128)} %bitcast.68, bf16[4096,768]{1,0:T(8,128)(2,1)} %convolution_convert_fusion.1.qkv, bf16[4096,256]{1,0:T(8,128)(2,1)} %convolution_convert_fusion.2.grads, ...), custom_call_target="tpu_custom_call" | custom-call | bytes 300000000 | tf_op jit(solution)/shard_map/pallas_call | solution.py:1288
  894.6 19.8 %fusion.6 = bf16[2048,768]{1,0:T(8,128)(2,1)S(1)} fusion(bf16[4096,768]{1,0:T(8,128)(2,1)} %get-tuple-element.105.d_qkv, bf16[4096,2048]{1,0:T(8,128)(2,1)} %get-tuple-element.82, f32[2048]{0:T(1024)S(1)} %copy-done.17, f32[4096]{0:T(1024)S(1)} %copy-done.15), kind=kOutput, calls=%fused_computation.13 | convolution fusion | flops 12920029184 | bytes 26238976 | tf_op jit(solution)/shard_map/dot_general | solution.py:20
  914.5 1.9 copy.24
  916.5 0.7 reshape_squeeze.11.gain
  917.1 3.5 add_add_fusion
  920.6 142.7 %shard_map.210 = (bf16[512,2048]{1,0:T(8,128)(2,1)}, f32[2,8,128]{2,1,0:T(8,128)}) custom-call(bf16[4096,768]{1,0:T(8,128)(2,1)} %get-tuple-element.105.d_qkv, bf16[2048,768]{1,0:T(8,128)(2,1)} %bitcast.54, bf16[512,2048]{1,0:T(8,128)(2,1)} %constant_dynamic-slice_fusion.5.x_own, f32[512,2048]{1,0:T(8,128)} %get-tuple-element.106.d_resid, ...), custom_call_target="tpu_custom_call" | custom-call | bytes 350000000 | tf_op jit(solution)/shard_map/pallas_call | solution.py:1012
  1063.4 0.7 reduce_sum.29
  1064.1 0.1 reshape.202
  1064.2 0.9 convert_reduce_fusion
  1065.1 4.3 bitcast_convert_fusion
  1069.4 3.5 all-to-all-start
  1073.0 0.5 fusion.11
  1073.5 4.9 convert_add_fusion
  1078.4 6.6 all-to-all-done
  1085.0 0.9 reshape.206
  1085.9 1.5 fusion.13
  1087.4 0.3 copy.25
  1087.7 1.0 copy.28
  1088.6 0.3 copy.26
  1089.0 1.0 copy.29
  1089.9 0.3 copy.27
  1090.2 1.0 copy.30
  1091.2 1.3 copy.34
  (45 shorter events, 0.2 us)
Async XLA Ops:
  7.2 218.6 %all-gather.3.cloned.1.call-start = ((), (), s32[]{:S(2)}) async-start(), calls=%async_computation.3 | async-start | bytes 2359296 | tf_op jit(solution)/shard_map/all_gather | solution.py:1350
  9.5 0.6 copy-start.13
  140.1 79.0 %collective-permute-start = (bf16[1,512,2048]{2,1,0:T(8,128)(2,1)}, bf16[1,512,2048]{2,1,0:T(8,128)(2,1)S(1)}, u32[]{:S(2)}, u32[]{:S(2)}) collective-permute-start(bf16[1,512,2048]{2,1,0:T(8,128)(2,1)} %param.20), channel_id=1, source_target_pairs={{0,0},{1,1},{2,16},{3,17},{4,8},{5,9},{6,24},{7,25},{8,4},{9,5},{1... | collective-permute-start | bytes 6291464 | tf_op jit(solution)/shard_map/ppermute | solution.py:1323
  142.4 334.5 %all-gather.5.cloned.1.call-start = ((), (), s32[]{:S(2)}) async-start(), calls=%async_computation.4 | async-start | bytes 5242880 | tf_op jit(solution)/shard_map/all_gather | solution.py:1358
  152.8 20.8 %copy-start.16 = (f32[2048]{0:T(1024)}, f32[2048]{0:T(1024)S(1)}, u32[]{:S(2)}) copy-start(f32[2048]{0:T(1024)S(1)} %mul.50) | copy-start | bytes 24580
  153.5 20.1 %copy-start.14 = (f32[4096]{0:T(1024)}, f32[4096]{0:T(1024)S(1)}, u32[]{:S(2)}) copy-start(f32[4096]{0:T(1024)S(1)} %add_rsqrt_fusion) | copy-start | bytes 49156
  219.1 176.9 %copy-start.4 = (bf16[1,512,2048]{2,1,0:T(8,128)(2,1)}, bf16[1,512,2048]{2,1,0:T(8,128)(2,1)S(1)}, u32[]{:S(2)}) copy-start(bf16[1,512,2048]{2,1,0:T(8,128)(2,1)S(1)} %collective-permute-done) | copy-start | bytes 6291460
  396.0 218.0 %reduce-scatter.3.cloned.1.call-start = ((), (), s32[]{:S(2)}) async-start(), calls=%async_computation.5 | async-start | bytes 18874368 | tf_op jit(solution)/shard_map/reduce_scatter | solution.py:1361
  500.4 569.0 %reduce-scatter.5.cloned.1.call-start = ((), (), s32[]{:S(2)}) async-start(), calls=%async_computation.6 | async-start | bytes 3932160 | tf_op jit(solution)/shard_map/reduce_scatter | solution.py:1397
  524.0 2.0 copy-start.5
  527.8 85.0 %collective-permute-start.1 = (bf16[256,2048]{1,0:T(8,128)(2,1)}, bf16[256,2048]{1,0:T(8,128)(2,1)S(1)}, u32[]{:S(2)}, u32[]{:S(2)}) collective-permute-start(bf16[256,2048]{1,0:T(8,128)(2,1)} %get-tuple-element.119), channel_id=1, source_target_pairs={{0,2},{2,4},{4,6},{6,0},{1,3},{3,5},{5,7},{7,1},{8,10},{10,12},{12... | collective-permute-start | bytes 3145736 | tf_op jit(solution)/shard_map/ppermute | solution.py:1368
  527.8 85.0 %collective-permute-start.2 = (bf16[256,2048]{1,0:T(8,128)(2,1)}, bf16[256,2048]{1,0:T(8,128)(2,1)S(1)}, u32[]{:S(2)}, u32[]{:S(2)}) collective-permute-start(bf16[256,2048]{1,0:T(8,128)(2,1)} %get-tuple-element.118), channel_id=1, source_target_pairs={{0,4},{2,6},{4,0},{6,2},{1,5},{3,7},{5,1},{7,3},{8,12},{10,14},{12... | collective-permute-start | bytes 3145736 | tf_op jit(solution)/shard_map/ppermute | solution.py:1368
  528.8 84.1 %collective-permute-start.3 = (bf16[256,2048]{1,0:T(8,128)(2,1)}, bf16[256,2048]{1,0:T(8,128)(2,1)}, u32[]{:S(2)}, u32[]{:S(2)}) collective-permute-start(bf16[256,2048]{1,0:T(8,128)(2,1)} %get-tuple-element.117), channel_id=1, source_target_pairs={{0,6},{2,0},{4,2},{6,4},{1,7},{3,1},{5,3},{7,5},{8,14},{10,8},{12,... | collective-permute-start | bytes 3145736 | tf_op jit(solution)/shard_map/ppermute | solution.py:1368
  567.2 24.4 %copy-start.3 = (bf16[4096,1024]{1,0:T(8,128)(2,1)S(1)}, bf16[4096,1024]{1,0:T(8,128)(2,1)}, u32[]{:S(2)}) copy-start(bf16[4096,1024]{1,0:T(8,128)(2,1)} %get-tuple-element.100.d_up) | copy-start | bytes 25165828
  612.9 168.8 %copy-start.6 = (bf16[256,2048]{1,0:T(8,128)(2,1)S(1)}, bf16[256,2048]{1,0:T(8,128)(2,1)}, u32[]{:S(2)}) copy-start(bf16[256,2048]{1,0:T(8,128)(2,1)} %constant_dynamic-slice_fusion.6.w_out) | copy-start | bytes 3145732
  781.6 11.3 %copy-start = (bf16[4096,2048]{1,0:T(8,128)(2,1)S(1)}, bf16[4096,2048]{1,0:T(8,128)(2,1)}, u32[]{:S(2)}) copy-start(bf16[4096,2048]{1,0:T(8,128)(2,1)} %get-tuple-element.101) | copy-start | bytes 50331652
  781.7 11.9 %copy-start.1 = (bf16[4096,256]{1,0:T(8,128)(2,1)S(1)}, bf16[4096,256]{1,0:T(8,128)(2,1)}, u32[]{:S(2)}) copy-start(bf16[4096,256]{1,0:T(8,128)(2,1)} %shard_map.204.attended) | copy-start | bytes 6291460
  793.5 5.5 copy-start.2
  793.5 5.5 copy-start.8
  801.1 93.5 %copy-start.15 = (f32[4096]{0:T(1024)S(1)}, f32[4096]{0:T(1024)}, u32[]{:S(2)}) copy-start(f32[4096]{0:T(1024)} %copy-done.14) | copy-start | bytes 49156
  801.1 93.5 %copy-start.17 = (f32[2048]{0:T(1024)S(1)}, f32[2048]{0:T(1024)}, u32[]{:S(2)}) copy-start(f32[2048]{0:T(1024)} %copy-done.16) | copy-start | bytes 24580
  914.5 2.0 copy-start.12
  920.6 143.5 %copy-start.9 = (bf16[4,64,2048]{2,1,0:T(8,128)(2,1)S(1)}, bf16[4,64,2048]{2,1,0:T(8,128)(2,1)}, u32[]{:S(2)}) copy-start(bf16[4,64,2048]{2,1,0:T(8,128)(2,1)} %get-tuple-element.109) | copy-start | bytes 3145732
  1065.1 8.4 copy-start.10
  1065.1 8.4 copy-start.11
  1069.4 15.6 %all-to-all-start = ((bf16[8,64,768]{2,1,0:T(8,128)(2,1)}), bf16[8,64,768]{2,1,0:T(8,128)(2,1)S(1)}, u32[]{:S(2)}, u32[]{:S(2)}) async-start(bf16[8,64,768]{2,1,0:T(8,128)(2,1)} %bitcast.61), calls=%async_computation.2 | async-start | bytes 1572864 | tf_op jit(solution)/shard_map/all_to_all | solution.py:1398
  1085.9 5.3 copy-start.7
Sparse Core Ops, SparseCore 0:
  142.5 83.2 all-gather.2
  396.2 78.5 all-gather.4
  500.5 113.5 reduce-scatter.2
  916.6 67.1 reduce-scatter.4

commit v9 on v8

--- a/solution.py
+++ b/solution.py
@@ -87,6 +87,7 @@
 
 
 HALF = TILE // 2
+PIECES = 4
 CHUNK = 32
 MESH_ID = pl.DeviceIdType.MESH
 
@@ -717,8 +718,11 @@
     return lax.rsqrt(jnp.mean(value * value, axis=-1, keepdims=True) + EPSILON)
 
 
-def close_attention_kernel(attended, w_out, x_own, gain, w_gate, w_up, resid, normed, own_gate, own_up, own, *scratch):
+def close_attention_kernel(attended, w_out, x_whole, gain, w_gate, w_up, resid, normed, own_gate, own_up, own, x_own, *scratch):
     scatter, (send, recv, local), sems = scratch[:7], scratch[7:10], scratch[10:]
+    y, c, z, x = spot()
+    fetch_x = pltpu.make_async_copy(x_whole.at[place_of(y, c, x)], x_own, local.at[0])
+    fetch_x.start()
     width = w_out.shape[1]
     hidden = w_gate.shape[1]
     z = lax.axis_index("z")
@@ -760,9 +764,10 @@
         own[here, :] = (value * inverse_of(value) * gain[...]).astype(LOW)
 
     def rows_of_half(half):
+        if half == 0:
+            fetch_x.wait()
         over_chunks(chunk, half)
 
-    y, c, z, x = spot()
     gather = Gather(own_halves(own), normed, send, recv)
     sum_and_gather(part_of, rows_of_half, gather, lambda turn: arrive(turn - 1) if turn > 0 else None)
     keep = pltpu.make_async_copy(own, normed.at[place_of(y, c, x)], local.at[0])
@@ -773,8 +778,8 @@
         copy.wait()
 
 
-def close_attention(attended, w_out, x_own, gain, w_gate, w_up):
-    block, width = x_own.shape
+def close_attention(attended, w_out, x_whole, gain, w_gate, w_up):
+    block, width = x_whole.shape[0] // 8, x_whole.shape[1]
     hidden = w_gate.shape[1]
     return pl.pallas_call(
         close_attention_kernel,
@@ -784,14 +789,14 @@
             jax.ShapeDtypeStruct((width, 4 * hidden), LOW),
             jax.ShapeDtypeStruct((width, 4 * hidden), LOW),
         ),
-        in_specs=[in_vmem()] * 6,
+        in_specs=[in_vmem(), in_vmem(), anywhere()] + [in_vmem()] * 3,
         out_specs=[in_vmem()] + [anywhere()] * 3,
-        scratch_shapes=[pltpu.VMEM((block, width), LOW)]
+        scratch_shapes=[pltpu.VMEM((block, width), LOW)] * 2
         + scatter_scratch(width, 2)
         + [dma(GATHER_COPIES), dma(GATHER_COPIES), dma(3), *chain_sems(2)],
         compiler_params=remote_params(2),
         cost_estimate=pl.CostEstimate(flops=0, bytes_accessed=450_000_000, transcendentals=0),
-    )(attended, w_out, x_own, gain, w_gate, w_up)
+    )(attended, w_out, x_whole, gain, w_gate, w_up)
 
 
 def norm_back(value, gain, upstream):
@@ -900,9 +905,11 @@
     )(d_gate, d_up, w_gate, w_up, resid, upstream, gain, *grads)
 
 
-def close_layer_kernel(d_qkv, w_qkv, x_own, d_resid, gain, mlp_term, grad_low, gain_grads, own, terms, layer_terms, part, column_terms, *scratch):
-    scatter, (send, recv, term_send, term_recv, line_send, line_recv) = scratch[:7], scratch[7:]
+def close_layer_kernel(d_qkv, w_qkv, x_whole, d_resid, gain, mlp_term, grad_low, gain_grads, own, terms, layer_terms, part, column_terms, *scratch):
+    scatter, (send, recv, term_send, term_recv, line_send, line_recv, x_own, x_sem) = scratch[:7], scratch[7:]
     y, c, z, x = spot()
+    fetch_x = pltpu.make_async_copy(x_whole.at[place_of(y, c, x)], x_own, x_sem.at[0])
+    fetch_x.start()
     partner = partner_of(y, c, z, x)
     moves = z != 2 * c + y
     width = w_qkv.shape[0]
@@ -918,9 +925,11 @@
         pl.semaphore_signal(barrier, inc=1, device_id=peer, device_id_type=MESH_ID)
     pl.semaphore_wait(barrier, len(layer + line) + moves.astype(jnp.int32))
 
-    def part_of(half):
+    size = TILE // PIECES
+
+    def part_of(piece):
         def produce(turn, to_y, to_c, to_x, out):
-            at = place_of(to_y, to_c, to_x, half)
+            at = quarter_of(to_y, to_c, to_x, piece // 2, piece % 2)
 
             def step(i, carry):
                 columns = pl.ds(pl.multiple_of(i * TILE, TILE), TILE)
@@ -929,44 +938,43 @@
 
             lax.fori_loop(0, width // TILE, step, 0)
 
-        return Scatter(produce, *scatter, part=half, start=half * HALF, size=HALF)
-
-    sums = [part_of(half) for half in (0, 1)]
+        return Scatter(produce, *scatter, part=piece, start=piece * size, size=size)
+
+    sums = [part_of(piece) for piece in range(PIECES)]
     sums[0].begin()
     sums[0].relay()
     sums[1].begin()
     total, landed = scatter[2], scatter[4]
     terms[1] = mlp_term[...]
     terms[0] = jnp.zeros_like(mlp_term)
-    trades = [
-        remote(own.at[pl.ds(half * HALF, HALF)], grad_low.at[pl.ds(half * HALF, HALF)], send.at[half], recv.at[half], partner)
-        for half in (0, 1)
-    ]
-    keeps = [
-        pltpu.make_async_copy(own.at[pl.ds(half * HALF, HALF)], grad_low.at[pl.ds(half * HALF, HALF)], recv.at[half])
-        for half in (0, 1)
-    ]
-    for half in (0, 1):
-        if half == 1:
-            sums[1].relay()
-        sums[half].arrive()
+    pieces = [pl.ds(piece * size, size) for piece in range(PIECES)]
+    trades = [remote(own.at[at], grad_low.at[at], send.at[k], recv.at[k], partner) for k, at in enumerate(pieces)]
+    keeps = [pltpu.make_async_copy(own.at[at], grad_low.at[at], recv.at[k]) for k, at in enumerate(pieces)]
+    fetch_x.wait()
+    for piece in range(PIECES):
+        sums[piece].arrive()
 
         def step(i, carry):
-            here = pl.ds(pl.multiple_of(half * HALF + i * CHUNK, CHUNK), CHUNK)
+            here = pl.ds(pl.multiple_of(piece * size + i * CHUNK, CHUNK), CHUNK)
             back, products = norm_back(x_own[here, :].astype(jnp.float32), gain[...], summed(total, landed, here))
             own[here, :] = (d_resid[here, :] + back).astype(LOW)
             fold_rows(terms.at[0], products)
             return carry
 
-        lax.fori_loop(0, HALF // CHUNK, step, 0)
+        lax.fori_loop(0, size // CHUNK, step, 0)
 
         @pl.when(moves)
         def _():
-            trades[half].start()
+            trades[piece].start()
 
         @pl.when(jnp.logical_not(moves))
         def _():
-            keeps[half].start()
+            keeps[piece].start()
+
+        if piece + 1 < PIECES:
+            sums[piece + 1].relay()
+        if piece + 2 < PIECES:
+            sums[piece + 2].begin()
 
     def columns_of(row, layers):
         return pl.ds(pl.multiple_of((4 * row) * HD, HD), layers * HD)
@@ -993,8 +1001,8 @@
     gain_grads[...] = sum((column_terms[k] for k in range(3)), part[:, :, pl.ds(pl.multiple_of(z * HD, HD), HD)])
     for copy in spread + lines:
         copy.wait_send()
-    for half in (0, 1):
-        sums[half].finish()
+    for part_sum in sums:
+        part_sum.finish()
 
     @pl.when(moves)
     def _():
@@ -1007,12 +1015,12 @@
             copy.wait()
 
 
-def close_layer(d_qkv, w_qkv, x_own, d_resid, gain, mlp_term):
-    block, width = x_own.shape
+def close_layer(d_qkv, w_qkv, x_whole, d_resid, gain, mlp_term):
+    block, width = d_resid.shape
     return pl.pallas_call(
         close_layer_kernel,
         out_shape=(jax.ShapeDtypeStruct((block, width), LOW), jax.ShapeDtypeStruct((2, 8, width // 16), jnp.float32)),
-        in_specs=[in_vmem()] * 6,
+        in_specs=[in_vmem(), in_vmem(), anywhere()] + [in_vmem()] * 3,
         out_specs=[anywhere(), in_vmem()],
         scratch_shapes=[
             pltpu.VMEM((block, width), LOW),
@@ -1021,11 +1029,11 @@
             pltpu.VMEM((2, 8, width // 4), jnp.float32),
             pltpu.VMEM((3, 2, 8, width // 16), jnp.float32),
         ]
-        + scatter_scratch(width, 2)
-        + [dma(2), dma(2), dma(7), dma(7), dma(3), dma(3)],
+        + scatter_scratch(width, PIECES)
+        + [dma(PIECES), dma(PIECES), dma(7), dma(7), dma(3), dma(3), pltpu.VMEM((block, width), LOW), dma(1)],
         compiler_params=remote_params(4),
         cost_estimate=pl.CostEstimate(flops=0, bytes_accessed=350_000_000, transcendentals=0),
-    )(d_qkv, w_qkv, x_own, d_resid, gain, mlp_term)
+    )(d_qkv, w_qkv, x_whole, d_resid, gain, mlp_term)
 
 
 def doc_start(ends, place):
@@ -1090,14 +1098,14 @@
         keep.start()
 
     def step(n, carry):
-        columns = pl.ds(pl.multiple_of(n * HALF, HALF), HALF)
+        columns = pl.ds(pl.multiple_of(n * TILE, TILE), TILE)
         gate_part, up_part = dot_wide(normed[...], w_gate[:, columns]), dot_wide(normed[...], w_up[:, columns])
         gate[:, columns] = gate_part
         up[:, columns] = up_part
         hidden[:, columns] = (gate_part * jax.nn.sigmoid(gate_part) * up_part).astype(LOW)
         return carry
 
-    lax.fori_loop(0, w_gate.shape[1] // HALF, step, 0)
+    lax.fori_loop(0, w_gate.shape[1] // TILE, step, 0)
 
     @pl.when(i == steps - 1)
     def _():
@@ -1240,14 +1248,14 @@
 
 def back_mlp_kernel(upstream, w_down, gate, up, d_gate, d_up):
     def step(n, carry):
-        columns = pl.ds(pl.multiple_of(n * HALF, HALF), HALF)
+        columns = pl.ds(pl.multiple_of(n * TILE, TILE), TILE)
         d_hidden = dot_nt(upstream[...], w_down[columns, :])
         d_gate[:, columns], d_up[:, columns] = gate_backward(
             d_hidden, gate[:, columns], up[:, columns], jax.nn.sigmoid(gate[:, columns])
         )
         return carry
 
-    lax.fori_loop(0, gate.shape[1] // HALF, step, 0)
+    lax.fori_loop(0, gate.shape[1] // TILE, step, 0, unroll=2)
 
 
 def back_mlp(upstream, w_down, gate, up):
@@ -1344,16 +1352,18 @@
     own_lengths = facts[:, 0, 0, 2, : lengths.shape[1]].reshape(2, 2, -1)
     own_lengths = lax.dynamic_slice(own_lengths, (layer % 2, layer // 2, 0), (1, 1, own_lengths.shape[2]))[0, 0]
     ends = jnp.cumsum(own_lengths.astype(jnp.int32))
-    place = (4 * lax.axis_index("c") + 2 * lax.axis_index("y") + lax.axis_index("x")) * block
-    x_own = lax.dynamic_slice_in_dim(layer_x, place, block, 0)
     layer_normed = norm_forward(layer_x.astype(jnp.float32), full_gain_attn)[0].astype(LOW)
-    out_rows = lax.all_gather(after(facts, w_out), ("z", "x"), axis=0, tiled=True)
-    w_out_own = lax.dynamic_slice_in_dim(out_rows, lax.axis_index("x") * owned, owned, 0)
-
+    line = lax.all_gather(after(facts, w_out), "z", axis=0)
+    qkv = dot_wide(layer_normed, w_qkv).astype(LOW)
+    here = lax.axis_index("x")
+    line = after(qkv, line)
+    to_neighbour = lax.dynamic_slice_in_dim(line, 2 * (1 - here), 2, 0)
+    mine, theirs = lax.dynamic_slice_in_dim(line, 2 * here, 2, 0), lax.ppermute(to_neighbour, "x", [(0, 1), (1, 0)])
+    w_out_own = jnp.stack((jnp.where(here == 0, mine, theirs), jnp.where(here == 0, theirs, mine)), axis=1)
+    w_out_own = w_out_own.reshape(owned, width)
     upstream = trade(after(facts, cotangent)).reshape(block, width)
-    qkv = dot_wide(layer_normed, w_qkv).astype(LOW)
-    attended = attend(ends, qkv)
-    resid, layer_mlp, own_gate, own_up = close_attention(after(upstream, attended), w_out_own, x_own, full_gain_mlp, w_gate, w_up)
+    attended = attend(ends, after(to_neighbour, qkv))
+    resid, layer_mlp, own_gate, own_up = close_attention(after(upstream, attended), w_out_own, layer_x, full_gain_mlp, w_gate, w_up)
 
     own_down = lax.all_gather(after(resid, w_down), "z", axis=0, tiled=True)
     gate, up_part, hidden, layer_upstream = open_mlp(layer_mlp, own_gate, own_up, upstream)
@@ -1388,7 +1398,7 @@
     grad_out = jnp.sum(out_parts.astype(jnp.float32), axis=0)
     qkv_term = contract_rows(layer_normed, d_qkv).astype(LOW)
     grad_low, gain_grads = close_layer(
-        after(qkv_term, d_qkv), w_qkv, x_own, d_resid, full_gain_attn, gain_mlp_term
+        after(qkv_term, d_qkv), w_qkv, layer_x, d_resid, full_gain_attn, gain_mlp_term
     )
     grad_tokens = grad_low.astype(jnp.float32).reshape(rows_here, block, width)
 

time: 1110 us -> 1130 us (1.018)
  waiting for transfers between devices: 14.6 us -> 49.6 us
  Pallas kernels: 860 us -> 843 us
    all_gather x1, waiting for transfers between devices: 6.62 us -> 38.9 us  [body_layers(): line = lax.all_gather(after(facts, w_out), 'z', axis=0)]
    pallas_call x1, Pallas kernels: 168 us -> 154 us  [close_attention(): pl.pallas_call(close_attention_kernel, out_shape=(jax.ShapeDtypeStruct((b...]
  transfers between devices with their start and end apart: 9 -> 10, of which waited for: 3 -> 3; matrix products, arithmetic and copies ran while one was open for 11% -> 11% of each run, Pallas kernels for 27% -> 27%
where the time goes in v9:
time: 1130 us; the launch traced here: 1120 us
  Pallas kernels  843 us (75%)
  matrix products  147 us (13%)
  waiting for transfers between devices  49.6 us (4%)
  other arithmetic  29.1 us (3%)
  local copies, waits for them, and re-layouts  22 us (2%)
  between operations  14.4 us (1%)
  starting transfers between devices  12.1 us (1%)
    pallas_call x1, Pallas kernels, close_mlp(): pl.pallas_call(close_mlp_kernel, out_shape=(jax.ShapeDtypeStruct((block,...  167 us
    pallas_call x1, Pallas kernels, close_attention(): pl.pallas_call(close_attention_kernel, out_shape=(jax.ShapeDtypeStruct((b...  154 us
    pallas_call x1, Pallas kernels, close_layer(): pl.pallas_call(close_layer_kernel, out_shape=(jax.ShapeDtypeStruct((block...  142 us
    pallas_call x1, Pallas kernels, begin(): pl.pallas_call(begin_kernel, out_shape=(jax.ShapeDtypeStruct((8 * block,...  130 us
    dot_general x5, matrix products, contract_rows(): lax.dot_general(left, right, (((0,), (0,)), ((), ())), preferred_element_...  94.4 us
    pallas_call x1, Pallas kernels, attend_back(): pl.pallas_call(attend_back_kernel, out_shape=(jax.ShapeDtypeStruct((place...  92.9 us
    pallas_call x1, Pallas kernels, open_mlp(): pl.pallas_call(open_mlp_kernel, out_shape=(jax.ShapeDtypeStruct((places,...  80.6 us
    pallas_call x1, Pallas kernels, attend(): pl.pallas_call(attend_kernel, out_shape=jax.ShapeDtypeStruct((places, wid...  42.5 us
  transfers between devices with their start and end apart: 10, of which 3 were waited for; matrix products, arithmetic and copies ran while one was open for 11% of the time, Pallas kernels for 27%

profile of v9, /device:TPU:0, one launch (start us, length us, event | category | flops | bytes accessed | tf_op | source)
XLA Modules:
  0.0 1116.8 jit_solution(4472130850640423992)
XLA Ops:
  7.2 0.7 pad_convert_fusion
  7.9 0.7 bitcast_convert_fusion.1
  8.5 0.7 convert_element_type.98
  9.2 0.1 scatter.19
  9.3 0.2 scatter.20.facts
  9.5 0.6 copy-done.15
  10.1 130.0 %shard_map.203 = (bf16[4096,2048]{1,0:T(8,128)(2,1)}, bf16[4,4,128,768]{3,2,1,0:T(8,128)(2,1)}, f32[4,4,2,8,128]{4,3,2,1,0:T(8,128)}) custom-call(bf16[2,256,2048]{2,1,0:T(8,128)(2,1)} %bitcast.66, bf16[64,2048]{1,0:T(8,128)(2,1)} %w_query.1, bf16[64,2048]{1,0:T(8,128)(2,1)} %w_key.1, bf16[64,2048]{1,0:T(8,128)(2,1)} %w_value.1, f32[8,128]{1,0:T(8,128)} %copy-done.15), custom_call_target="tpu_custom_call" | custom-call | bytes 350000000 | tf_op jit(solution)/shard_map/pallas_call | solution.py:681
  140.1 2.3 collective-permute-start
  142.4 1.6 slice_reduce_fusion
  144.1 0.1 mul.44
  144.1 7.4 fusion
  151.6 19.0 %convolution_convert_fusion.1.qkv = bf16[4096,768]{1,0:T(8,128)(2,1)} fusion(bf16[2048,768]{1,0:T(8,128)(2,1)S(1)} %bitcast.64, bf16[4096,2048]{1,0:T(8,128)(2,1)} %get-tuple-element.84.x_whole, f32[2048]{0:T(1024)S(1)} %mul.44, f32[4096]{0:T(1024)S(1)} %add_rsqrt_fusion), kind=kOutput, calls=%fused_computation.6 | convolution fusion | flops 12921602048 | bytes 26238976 | tf_op jit(solution)/shard_map/dot_general | solution.py:86
  170.6 38.9 %all-gather.6.cloned.1.call-done = bf16[256,2048]{1,0:T(8,128)(2,1)} async-done(((bf16[64,2048]{1,0:T(8,128)(2,1)}), bf16[256,2048]{1,0:T(8,128)(2,1)}) %all-gather.6.cloned.1.call-update) | async-done | bytes 1048592 | tf_op jit(solution)/shard_map/all_gather | solution.py:1356
  209.5 1.9 constant_dynamic-slice_fusion.5
  211.4 1.4 collective-permute-start.1
  212.8 0.7 slice.74
  213.5 0.7 reduce-window.9
  214.2 0.7 reshape_squeeze.10.gain
  214.9 42.5 %shard_map.204.attended = bf16[4096,256]{1,0:T(8,128)(2,1)} custom-call(s32[8]{0:T(128)} %bitcast.79, bf16[4096,768]{1,0:T(8,128)(2,1)} %convolution_convert_fusion.1.qkv), custom_call_target="tpu_custom_call" | custom-call | bytes 150000000 | tf_op jit(solution)/shard_map/pallas_call | solution.py:1280
  257.4 1.5 select_bitcast_fusion.1
  258.9 1.1 pad_maximum_fusion
  260.0 154.1 %shard_map.205 = (f32[512,2048]{1,0:T(8,128)}, bf16[4096,2048]{1,0:T(8,128)(2,1)}, bf16[2048,1024]{1,0:T(8,128)(2,1)}, bf16[2048,1024]{1,0:T(8,128)(2,1)}) custom-call(bf16[4096,256]{1,0:T(8,128)(2,1)} %shard_map.204.attended, bf16[256,2048]{1,0:T(8,128)(2,1)} %bitcast.61, bf16[4096,2048]{1,0:T(8,128)(2,1)} %get-tuple-element.84.x_whole, ...), custom_call_target="tpu_custom_call" | custom-call | bytes 450000000 | tf_op jit(solution)/shard_map/pallas_call | solution.py:784
  414.1 0.0 reduce-scatter.3.cloned.1.call-start
  414.2 80.6 %shard_map.206 = (f32[4096,1024]{1,0:T(8,128)}, f32[4096,1024]{1,0:T(8,128)}, bf16[4096,1024]{1,0:T(8,128)(2,1)}, bf16[4096,2048]{1,0:T(8,128)(2,1)}) custom-call(bf16[4096,2048]{1,0:T(8,128)(2,1)} %get-tuple-element.91.normed, bf16[2048,1024]{1,0:T(8,128)(2,1)} %get-tuple-element.92.w_gate, bf16[2048,1024]{1,0:T(8,128)(2,1)} %get-tuple-element.93.w_up, ...), custom_call_target="tpu_custom_call" | custom-call | bytes 250000000 | tf_op jit(solution)/shard_map/pallas_call | solution.py:1125
  494.8 23.5 %convolution_convert_fusion = bf16[4096,2048]{1,0:T(8,128)(2,1)} fusion(bf16[4096,1024]{1,0:T(8,128)(2,1)} %get-tuple-element.97, bf16[1024,2048]{1,0:T(8,128)(2,1)} %all-gather.4.cloned.1.call-done.w_down), kind=kOutput, calls=%fused_computation.5 | convolution fusion | flops 17188257792 | bytes 29360128 | tf_op jit(solution)/shard_map/dot_general | solution.py:86
  518.3 23.4 %convolution_convert_fusion.5 = bf16[1024,2048]{1,0:T(8,128)(2,1)S(1)} fusion(bf16[4096,1024]{1,0:T(8,128)(2,1)} %get-tuple-element.97, bf16[4096,2048]{1,0:T(8,128)(2,1)} %get-tuple-element.99.upstream), kind=kOutput, calls=%fused_computation.12 | convolution fusion | flops 17181966336 | bytes 29360128 | tf_op jit(solution)/shard_map/dot_general | solution.py:20
  541.8 2.0 copy-done.6
  543.8 1.7 constant_dynamic-slice_fusion.2
  545.5 0.8 collective-permute-start.2
  546.3 1.3 collective-permute-start.3
  547.6 2.3 collective-permute-start.4
  549.9 33.3 %shard_map.207 = (bf16[4096,1024]{1,0:T(8,128)(2,1)}, bf16[4096,1024]{1,0:T(8,128)(2,1)}) custom-call(bf16[4096,2048]{1,0:T(8,128)(2,1)} %get-tuple-element.99.upstream, bf16[1024,2048]{1,0:T(8,128)(2,1)} %all-gather.4.cloned.1.call-done.w_down, f32[4096,1024]{1,0:T(8,128)} %get-tuple-element.100.gate, f32[4096,1024]{1,0:T(8,128)} %get-tuple-element.101.up), custom_call_target="tpu_custom_call" | custom-call | bytes 90000000 | tf_op jit(solution)/shard_map/pallas_call | solution.py:1265
  583.3 24.4 %convolution_convert_fusion.4.grad_a = bf16[2048,1024]{1,0:T(8,128)(2,1)} fusion(bf16[4096,2048]{1,0:T(8,128)(2,1)} %get-tuple-element.91.normed, bf16[4096,1024]{1,0:T(8,128)(2,1)} %get-tuple-element.103.d_gate), kind=kOutput, calls=%fused_computation.11 | convolution fusion | flops 17181966336 | bytes 29360128 | tf_op jit(solution)/shard_map/dot_general | solution.py:20
  607.6 21.3 %convolution_convert_fusion.3.grad_b = bf16[2048,1024]{1,0:T(8,128)(2,1)} fusion(bf16[4096,2048]{1,0:T(8,128)(2,1)} %get-tuple-element.91.normed, bf16[4096,1024]{1,0:T(8,128)(2,1)S(1)} %copy-done.3), kind=kOutput, calls=%fused_computation.10 | convolution fusion | flops 17181966336 | bytes 29360128 | tf_op jit(solution)/shard_map/dot_general | solution.py:20
  629.0 4.0 reduce-scatter.3.cloned.1.call-done
  633.0 166.9 %shard_map.208 = (f32[512,2048]{1,0:T(8,128)}, f32[8,2048]{1,0:T(8,128)}, bf16[4096,2048]{1,0:T(8,128)(2,1)}, bf16[2048,256]{1,0:T(8,128)(2,1)}, bf16[2048,256]{...) custom-call(bf16[4096,1024]{1,0:T(8,128)(2,1)} %get-tuple-element.10, ...), custom_call_target="tpu_custom_call" | custom-call | bytes 450000000 | tf_op jit(solution)/shard_map/pallas_call | solution.py:889
  799.9 10.2 convolution_convert_fusion.2.grads
  810.1 1.1 copy-done
  811.2 0.6 copy-done.1
  811.8 5.5 convolution_convert_fusion.6.out_grad
  817.2 2.1 add_convert_fusion.mixed
  819.3 92.9 %shard_map.209 = (bf16[4096,768]{1,0:T(8,128)(2,1)}, bf16[4,64,2048]{2,1,0:T(8,128)(2,1)}, bf16[512,2048]{1,0:T(8,128)(2,1)}) custom-call(s32[8]{0:T(128)} %bitcast.80, bf16[4096,768]{1,0:T(8,128)(2,1)} %convolution_convert_fusion.1.qkv, bf16[4096,256]{1,0:T(8,128)(2,1)} %convolution_convert_fusion.2.grads, ...), custom_call_target="tpu_custom_call" | custom-call | bytes 300000000 | tf_op jit(solution)/shard_map/pallas_call | solution.py:1296
  912.3 19.8 %fusion.6 = bf16[2048,768]{1,0:T(8,128)(2,1)S(1)} fusion(bf16[4096,768]{1,0:T(8,128)(2,1)} %get-tuple-element.109.d_qkv, bf16[4096,2048]{1,0:T(8,128)(2,1)} %get-tuple-element.84.x_whole, f32[2048]{0:T(1024)S(1)} %copy-done.19, f32[4096]{0:T(1024)S(1)} %copy-done.17), kind=kOutput, calls=%fused_computation.13 | convolution fusion | flops 12920029184 | bytes 26238976 | tf_op jit(solution)/shard_map/dot_general | solution.py:20
  932.1 1.9 copy.27
  934.1 0.7 reshape_squeeze.11.gain
  934.8 3.5 add_add_fusion
  938.3 142.3 %shard_map.210 = (bf16[512,2048]{1,0:T(8,128)(2,1)}, f32[2,8,128]{2,1,0:T(8,128)}) custom-call(bf16[4096,768]{1,0:T(8,128)(2,1)} %get-tuple-element.109.d_qkv, bf16[2048,768]{1,0:T(8,128)(2,1)} %bitcast.63, bf16[4096,2048]{1,0:T(8,128)(2,1)} %get-tuple-element.84.x_whole, f32[512,2048]{1,0:T(8,128)} %get-tuple-element.110.d_resid, ...), custom_call_target="tpu_custom_call" | custom-call | bytes 350000000 | tf_op jit(solution)/shard_map/pallas_call | solution.py:1020
  1080.6 0.7 reduce_sum.29
  1081.3 0.1 reshape.206
  1081.4 0.9 convert_reduce_fusion
  1082.4 4.3 bitcast_convert_fusion
  1086.7 3.8 all-to-all-start
  1090.5 0.5 fusion.11
  1091.0 4.9 convert_add_fusion
  1095.9 6.6 all-to-all-done
  1102.5 0.9 reshape.210
  1103.4 1.5 fusion.13
  1104.9 0.3 copy.28
  1105.2 1.0 copy.31
  1106.1 0.3 copy.29
  1106.4 1.0 copy.32
  1107.4 0.3 copy.30
  1107.7 1.0 copy.33
  1108.7 1.3 copy.37
  (52 shorter events, 0.3 us)
Async XLA Ops:
  7.2 202.3 %all-gather.6.cloned.1.call-start = ((), (), s32[]{:S(2)}) async-start(), calls=%async_computation.6 | async-start | bytes 1310720 | tf_op jit(solution)/shard_map/all_gather | solution.py:1356
  9.5 0.6 copy-start.15
  140.1 117.3 %collective-permute-start = (bf16[1,512,2048]{2,1,0:T(8,128)(2,1)}, bf16[1,512,2048]{2,1,0:T(8,128)(2,1)S(1)}, u32[]{:S(2)}, u32[]{:S(2)}) collective-permute-start(bf16[1,512,2048]{2,1,0:T(8,128)(2,1)} %param.20), channel_id=1, source_target_pairs={{0,0},{1,1},{2,16},{3,17},{4,8},{5,9},{6,24},{7,25},{8,4},{9,5},{1... | collective-permute-start | bytes 6291464 | tf_op jit(solution)/shard_map/ppermute | solution.py:1331
  142.4 352.4 %all-gather.4.cloned.1.call-start = ((), (), s32[]{:S(2)}) async-start(), calls=%async_computation.3 | async-start | bytes 5242880 | tf_op jit(solution)/shard_map/all_gather | solution.py:1368
  144.1 7.5 copy-start.18
  144.1 7.5 copy-start.7
  151.6 19.0 %copy-start.16 = (f32[4096]{0:T(1024)}, f32[4096]{0:T(1024)S(1)}, u32[]{:S(2)}) copy-start(f32[4096]{0:T(1024)S(1)} %add_rsqrt_fusion) | copy-start | bytes 49156
  211.4 46.0 %collective-permute-start.1 = (bf16[2,64,2048]{2,1,0:T(8,128)(2,1)}, bf16[2,64,2048]{2,1,0:T(8,128)(2,1)}, u32[]{:S(2)}, u32[]{:S(2)}) collective-permute-start(bf16[2,64,2048]{2,1,0:T(8,128)(2,1)} %constant_dynamic-slice_fusion.5), channel_id=1, source_target_pairs={{0,1},{1,0},{2,3},{3,2},{4,5},{5,4},{6,7},{7,6},{8,9},{9,8},{10,11... | collective-permute-start | bytes 1572872 | tf_op jit(solution)/shard_map/ppermute | solution.py:1361
  214.9 42.5 %copy-start.11 = (bf16[256,2048]{1,0:T(8,128)(2,1)S(1)}, bf16[256,2048]{1,0:T(8,128)(2,1)}, u32[]{:S(2)}) copy-start(bf16[256,2048]{1,0:T(8,128)(2,1)} %all-gather.6.cloned.1.call-done) | copy-start | bytes 3145732
  257.4 156.7 %copy-start.4 = (bf16[1,512,2048]{2,1,0:T(8,128)(2,1)}, bf16[1,512,2048]{2,1,0:T(8,128)(2,1)S(1)}, u32[]{:S(2)}) copy-start(bf16[1,512,2048]{2,1,0:T(8,128)(2,1)S(1)} %collective-permute-done) | copy-start | bytes 6291460
  414.1 218.9 %reduce-scatter.3.cloned.1.call-start = ((), (), s32[]{:S(2)}) async-start(), calls=%async_computation.4 | async-start | bytes 18874368 | tf_op jit(solution)/shard_map/reduce_scatter | solution.py:1371
  518.2 568.4 %reduce-scatter.5.cloned.1.call-start = ((), (), s32[]{:S(2)}) async-start(), calls=%async_computation.5 | async-start | bytes 3932160 | tf_op jit(solution)/shard_map/reduce_scatter | solution.py:1407
  541.8 2.0 copy-start.6
  545.5 83.4 %collective-permute-start.2 = (bf16[256,2048]{1,0:T(8,128)(2,1)}, bf16[256,2048]{1,0:T(8,128)(2,1)S(1)}, u32[]{:S(2)}, u32[]{:S(2)}) collective-permute-start(bf16[256,2048]{1,0:T(8,128)(2,1)} %get-tuple-element.123), channel_id=1, source_target_pairs={{0,2},{2,4},{4,6},{6,0},{1,3},{3,5},{5,7},{7,1},{8,10},{10,12},{12... | collective-permute-start | bytes 3145736 | tf_op jit(solution)/shard_map/ppermute | solution.py:1378
  546.3 82.6 %collective-permute-start.3 = (bf16[256,2048]{1,0:T(8,128)(2,1)}, bf16[256,2048]{1,0:T(8,128)(2,1)S(1)}, u32[]{:S(2)}, u32[]{:S(2)}) collective-permute-start(bf16[256,2048]{1,0:T(8,128)(2,1)} %get-tuple-element.122), channel_id=1, source_target_pairs={{0,4},{2,6},{4,0},{6,2},{1,5},{3,7},{5,1},{7,3},{8,12},{10,14},{12... | collective-permute-start | bytes 3145736 | tf_op jit(solution)/shard_map/ppermute | solution.py:1378
  547.6 81.3 %collective-permute-start.4 = (bf16[256,2048]{1,0:T(8,128)(2,1)}, bf16[256,2048]{1,0:T(8,128)(2,1)}, u32[]{:S(2)}, u32[]{:S(2)}) collective-permute-start(bf16[256,2048]{1,0:T(8,128)(2,1)} %get-tuple-element.121), channel_id=1, source_target_pairs={{0,6},{2,0},{4,2},{6,4},{1,7},{3,1},{5,3},{7,5},{8,14},{10,8},{12,... | collective-permute-start | bytes 3145736 | tf_op jit(solution)/shard_map/ppermute | solution.py:1378
  583.3 24.4 %copy-start.3 = (bf16[4096,1024]{1,0:T(8,128)(2,1)S(1)}, bf16[4096,1024]{1,0:T(8,128)(2,1)}, u32[]{:S(2)}) copy-start(bf16[4096,1024]{1,0:T(8,128)(2,1)} %get-tuple-element.104.d_up) | copy-start | bytes 25165828
  628.9 170.9 %copy-start.5 = (bf16[2,2,64,2048]{3,2,1,0:T(8,128)(2,1)S(1)}, bf16[2,2,64,2048]{3,2,1,0:T(8,128)(2,1)}, u32[]{:S(2)}) copy-start(bf16[2,2,64,2048]{3,2,1,0:T(8,128)(2,1)} %pad_maximum_fusion) | copy-start | bytes 3145732
  799.9 11.3 %copy-start = (bf16[4096,2048]{1,0:T(8,128)(2,1)S(1)}, bf16[4096,2048]{1,0:T(8,128)(2,1)}, u32[]{:S(2)}) copy-start(bf16[4096,2048]{1,0:T(8,128)(2,1)} %get-tuple-element.105) | copy-start | bytes 50331652
  799.9 11.9 %copy-start.1 = (bf16[4096,256]{1,0:T(8,128)(2,1)S(1)}, bf16[4096,256]{1,0:T(8,128)(2,1)}, u32[]{:S(2)}) copy-start(bf16[4096,256]{1,0:T(8,128)(2,1)} %shard_map.204.attended) | copy-start | bytes 6291460
  811.8 5.5 copy-start.2
  811.8 5.5 copy-start.9
  819.3 92.9 %copy-start.17 = (f32[4096]{0:T(1024)S(1)}, f32[4096]{0:T(1024)}, u32[]{:S(2)}) copy-start(f32[4096]{0:T(1024)} %copy-done.16) | copy-start | bytes 49156
  819.3 92.9 %copy-start.19 = (f32[2048]{0:T(1024)S(1)}, f32[2048]{0:T(1024)}, u32[]{:S(2)}) copy-start(f32[2048]{0:T(1024)} %copy-done.18) | copy-start | bytes 24580
  932.1 2.0 copy-start.14
  938.3 143.1 %copy-start.10 = (bf16[4,64,2048]{2,1,0:T(8,128)(2,1)S(1)}, bf16[4,64,2048]{2,1,0:T(8,128)(2,1)}, u32[]{:S(2)}) copy-start(bf16[4,64,2048]{2,1,0:T(8,128)(2,1)} %get-tuple-element.113) | copy-start | bytes 3145732
  1082.4 8.6 copy-start.12
  1082.4 8.6 copy-start.13
  1086.7 15.8 %all-to-all-start = ((bf16[8,64,768]{2,1,0:T(8,128)(2,1)}), bf16[8,64,768]{2,1,0:T(8,128)(2,1)S(1)}, u32[]{:S(2)}, u32[]{:S(2)}) async-start(bf16[8,64,768]{2,1,0:T(8,128)(2,1)} %bitcast.73), calls=%async_computation.2 | async-start | bytes 1572864 | tf_op jit(solution)/shard_map/all_to_all | solution.py:1408
  1103.4 5.3 copy-start.8
Sparse Core Ops, SparseCore 0:
  142.5 66.9 all-gather.5
  414.2 79.3 all-gather.3
  518.4 114.5 reduce-scatter.2
  934.2 98.0 reduce-scatter.4

commit v10 on v9

--- a/solution.py
+++ b/solution.py
@@ -441,14 +441,9 @@
 
 
 class Fold:
-    def __init__(self, whole, far, near_part, cross, mine, theirs, send, recv, local):
+    def __init__(self, slab, far, near_part, cross, mine, theirs, send, recv, local):
         y, c, z, x = spot()
         a, b = z // 2, lax.rem(z, 2)
-        size = whole.shape[1] // 4
-
-        def slab(at):
-            return whole.at[:, pl.ds(pl.multiple_of(at * size, size), size)]
-
         pair, middle = (y, c, 2 * a + 1 - b, x), (y, c, 2 * (1 - a) + b, x)
         self.far = remote(slab(2 * (1 - a) + 1 - b), far, send.at[0], recv.at[0], pair)
         self.near = remote(slab(2 * a + 1 - b), near_part, send.at[1], recv.at[1], pair)
@@ -477,6 +472,11 @@
             copy.wait_recv()
         for copy in (self.far, self.near, self.cross):
             copy.wait_send()
+
+
+def columns_of_layer(whole):
+    size = whole.shape[1] // 4
+    return lambda at: whole.at[:, pl.ds(pl.multiple_of(at * size, size), size)]
 
 
 def fold_peers():
@@ -606,21 +606,24 @@
     barrier, count = greet_neighbours(layer)
     pl.semaphore_wait(barrier, count + trade.greet(barrier, True))
 
-    shard, width = w_query.shape
-    owned = width // 8
+    shard = w_query.shape[0]
     for half in (0, 1):
         trade.start(half)
     spread = [
         remote(facts, facts_whole.at[row, z, x], fact_send.at[k], fact_recv.at[k], peer) for k, peer in enumerate(layer)
     ]
-    kept = [pltpu.make_async_copy(facts, facts_whole.at[row, z, x], local.at[3])]
-    for m, source in enumerate((w_query, w_key, w_value)):
-        dst = w_qkv.at[row, z, pl.ds(pl.multiple_of(x * shard, shard), shard), pl.ds(m * owned, owned)]
+    kept = [pltpu.make_async_copy(facts, facts_whole.at[row, z, x], local.at[6])]
+    for m in range(6):
+        source, slot = (w_query, w_key, w_value)[m // 2], m % 2
+
+        def columns_of(at):
+            head = 4 * (2 * at[0] + at[1]) + (3 - at[3] if slot else at[3])
+            return source.at[:, pl.ds(pl.multiple_of(head * HD, HD), HD)]
+
+        dst = w_qkv.at[row, z, pl.ds(pl.multiple_of(x * shard, shard), shard), pl.ds(m * HD, HD)]
         for k, peer in enumerate(layer):
-            columns = pl.ds(pl.multiple_of((4 * peer[0] + 2 * peer[1] + peer[3]) * owned, owned), owned)
-            spread.append(remote(source.at[:, columns], dst, w_send.at[m, k], w_recv.at[m, k], peer))
-        columns = pl.ds(pl.multiple_of((4 * y + 2 * c + x) * owned, owned), owned)
-        kept.append(pltpu.make_async_copy(source.at[:, columns], dst, local.at[m]))
+            spread.append(remote(columns_of(peer), dst, w_send.at[m, k], w_recv.at[m, k], peer))
+        kept.append(pltpu.make_async_copy(columns_of((y, c, z, x)), dst, local.at[m]))
     for copy in spread + kept:
         copy.start()
 
@@ -688,7 +691,7 @@
         in_specs=[in_vmem()] + [anywhere()] * 4,
         out_specs=[anywhere()] * 3,
         scratch_shapes=[
-            dma(GATHER_COPIES), dma(GATHER_COPIES), dma(3, 7), dma(3, 7), dma(7), dma(7), dma(4),
+            dma(GATHER_COPIES), dma(GATHER_COPIES), dma(6, 7), dma(6, 7), dma(7), dma(7), dma(7),
             *trade_scratch(2, block // 2, width), *chain_sems(2),
         ],
         compiler_params=remote_params(1),
@@ -836,8 +839,8 @@
         copy.start()
     greet(near() + fold_peers())
     folds = [
-        Fold(*refs, mine.at[k], theirs, fold_send.at[k], fold_recv.at[k], fold_local.at[k])
-        for k, refs in enumerate(((grad_a, far_a, near_a, cross_a), (grad_b, far_b, near_b, cross_b)))
+        Fold(columns_of_layer(grad), *refs, mine.at[k], theirs, fold_send.at[k], fold_recv.at[k], fold_local.at[k])
+        for k, (grad, *refs) in enumerate(((grad_a, far_a, near_a, cross_a), (grad_b, far_b, near_b, cross_b)))
     ]
     for fold in folds:
         fold.start()
@@ -905,8 +908,11 @@
     )(d_gate, d_up, w_gate, w_up, resid, upstream, gain, *grads)
 
 
-def close_layer_kernel(d_qkv, w_qkv, x_whole, d_resid, gain, mlp_term, grad_low, gain_grads, own, terms, layer_terms, part, column_terms, *scratch):
-    scatter, (send, recv, term_send, term_recv, line_send, line_recv, x_own, x_sem) = scratch[:7], scratch[7:]
+def close_layer_kernel(
+    d_qkv, w_qkv, x_whole, d_resid, gain, mlp_term, grad, grad_low, gain_grads, far, near_part, cross, grad_parts, own, terms, layer_terms, part, column_terms, *scratch
+):
+    scatter, (send, recv, term_send, term_recv, line_send, line_recv, x_own, x_sem, *rest) = scratch[:7], scratch[7:]
+    mine, theirs, fold_send, fold_recv, fold_local, part_send, part_recv = rest
     y, c, z, x = spot()
     fetch_x = pltpu.make_async_copy(x_whole.at[place_of(y, c, x)], x_own, x_sem.at[0])
     fetch_x.start()
@@ -940,10 +946,13 @@
 
         return Scatter(produce, *scatter, part=piece, start=piece * size, size=size)
 
+    fold = Fold(lambda at: grad.at[at], far, near_part, cross, mine, theirs, fold_send, fold_recv, fold_local)
+    fold.start()
     sums = [part_of(piece) for piece in range(PIECES)]
     sums[0].begin()
     sums[0].relay()
     sums[1].begin()
+    fold.fold()
     total, landed = scatter[2], scatter[4]
     terms[1] = mlp_term[...]
     terms[0] = jnp.zeros_like(mlp_term)
@@ -975,6 +984,32 @@
             sums[piece + 1].relay()
         if piece + 2 < PIECES:
             sums[piece + 2].begin()
+
+    fold.finish()
+    for source, target, k in ((grad.at[z], mine, 0), (near_part, theirs, 1)):
+        pltpu.make_async_copy(source, target, fold_local.at[k]).start()
+    for source, target, k in ((grad.at[z], mine, 0), (near_part, theirs, 1)):
+        pltpu.make_async_copy(source, target, fold_local.at[k]).wait()
+    add_rows(mine, 0, theirs, 0, mine.shape[0])
+    last = pltpu.make_async_copy(cross, theirs, fold_local.at[1])
+    last.start()
+    last.wait()
+    add_rows(mine, 0, theirs, 0, mine.shape[0])
+    shard = mine.shape[0] // 8
+    index = 4 * y + 2 * c + x
+    parts = [
+        remote(
+            mine.at[pl.ds(pl.multiple_of((4 * peer[0] + 2 * peer[1] + peer[3]) * shard, shard), shard)],
+            grad_parts.at[index],
+            part_send.at[k],
+            part_recv.at[k],
+            peer,
+        )
+        for k, peer in enumerate(layer)
+    ]
+    kept = pltpu.make_async_copy(mine.at[pl.ds(pl.multiple_of(index * shard, shard), shard)], grad_parts.at[index], fold_local.at[0])
+    for copy in parts + [kept]:
+        copy.start()
 
     def columns_of(row, layers):
         return pl.ds(pl.multiple_of((4 * row) * HD, HD), layers * HD)
@@ -1003,6 +1038,8 @@
         copy.wait_send()
     for part_sum in sums:
         part_sum.finish()
+    for copy in parts + [kept]:
+        copy.wait()
 
     @pl.when(moves)
     def _():
@@ -1015,13 +1052,18 @@
             copy.wait()
 
 
-def close_layer(d_qkv, w_qkv, x_whole, d_resid, gain, mlp_term):
+def close_layer(d_qkv, w_qkv, x_whole, d_resid, gain, mlp_term, grad):
     block, width = d_resid.shape
     return pl.pallas_call(
         close_layer_kernel,
-        out_shape=(jax.ShapeDtypeStruct((block, width), LOW), jax.ShapeDtypeStruct((2, 8, width // 16), jnp.float32)),
-        in_specs=[in_vmem(), in_vmem(), anywhere()] + [in_vmem()] * 3,
-        out_specs=[anywhere(), in_vmem()],
+        out_shape=(
+            jax.ShapeDtypeStruct((block, width), LOW),
+            jax.ShapeDtypeStruct((2, 8, width // 16), jnp.float32),
+            *[jax.ShapeDtypeStruct(grad.shape[1:], LOW)] * 3,
+            jax.ShapeDtypeStruct((8, grad.shape[1] // 8, grad.shape[2]), LOW),
+        ),
+        in_specs=[in_vmem(), in_vmem(), anywhere()] + [in_vmem()] * 3 + [anywhere()],
+        out_specs=[anywhere(), in_vmem()] + [anywhere()] * 4,
         scratch_shapes=[
             pltpu.VMEM((block, width), LOW),
             pltpu.VMEM((2, 8, width), jnp.float32),
@@ -1030,10 +1072,12 @@
             pltpu.VMEM((3, 2, 8, width // 16), jnp.float32),
         ]
         + scatter_scratch(width, PIECES)
-        + [dma(PIECES), dma(PIECES), dma(7), dma(7), dma(3), dma(3), pltpu.VMEM((block, width), LOW), dma(1)],
+        + [dma(PIECES), dma(PIECES), dma(7), dma(7), dma(3), dma(3), pltpu.VMEM((block, width), LOW), dma(1)]
+        + [pltpu.VMEM(grad.shape[1:], LOW)] * 2
+        + [dma(3), dma(3), dma(2), dma(7), dma(7)],
         compiler_params=remote_params(4),
         cost_estimate=pl.CostEstimate(flops=0, bytes_accessed=350_000_000, transcendentals=0),
-    )(d_qkv, w_qkv, x_whole, d_resid, gain, mlp_term)
+    )(d_qkv, w_qkv, x_whole, d_resid, gain, mlp_term, grad)
 
 
 def doc_start(ends, place):
@@ -1141,8 +1185,10 @@
 
 def out_turns():
     y, c, z, x = spot()
-    owners = [((y, c, 2 * x + j // 2, j % 2), (z == 2 * x + j // 2) & (x == j % 2)) for j in range(4)]
-    holders = [((y, c, j, z // 2), (z == j) & (x == z // 2)) for j in range(4)]
+    layers = (x, x, 3 - x, 3 - x)
+    owners = [((y, c, layers[j], j % 2), (z == layers[j]) & (x == j % 2)) for j in range(4)]
+    side = lax.rem((z + 1) // 2, 2)
+    holders = [((y, c, j, side), (z == j) & (x == side)) for j in range(4)]
     return owners, holders
 
 
@@ -1174,7 +1220,7 @@
             def _():
                 pl.semaphore_signal(barrier, inc=1, device_id=peer, device_id_type=MESH_ID)
 
-        pl.semaphore_wait(barrier, 4 - (x == z // 2).astype(jnp.int32) + trade.greet(barrier, False))
+        pl.semaphore_wait(barrier, 4 - (x == lax.rem((z + 1) // 2, 2)).astype(jnp.int32) + trade.greet(barrier, False))
         for half in (0, 1):
             trade.start(half)
         for turn in range(4):
@@ -1353,16 +1399,14 @@
     own_lengths = lax.dynamic_slice(own_lengths, (layer % 2, layer // 2, 0), (1, 1, own_lengths.shape[2]))[0, 0]
     ends = jnp.cumsum(own_lengths.astype(jnp.int32))
     layer_normed = norm_forward(layer_x.astype(jnp.float32), full_gain_attn)[0].astype(LOW)
-    line = lax.all_gather(after(facts, w_out), "z", axis=0)
+    here = lax.axis_index("x")
+    out_rows = lax.all_gather(after(facts, w_out), ("z", "x"), axis=0, tiled=True)
+    w_out_own = [lax.dynamic_slice_in_dim(out_rows, head * HD, HD, 0) for head in (here, 3 - here)]
+    w_out_own = jnp.concatenate(w_out_own, axis=0)
+
     qkv = dot_wide(layer_normed, w_qkv).astype(LOW)
-    here = lax.axis_index("x")
-    line = after(qkv, line)
-    to_neighbour = lax.dynamic_slice_in_dim(line, 2 * (1 - here), 2, 0)
-    mine, theirs = lax.dynamic_slice_in_dim(line, 2 * here, 2, 0), lax.ppermute(to_neighbour, "x", [(0, 1), (1, 0)])
-    w_out_own = jnp.stack((jnp.where(here == 0, mine, theirs), jnp.where(here == 0, theirs, mine)), axis=1)
-    w_out_own = w_out_own.reshape(owned, width)
     upstream = trade(after(facts, cotangent)).reshape(block, width)
-    attended = attend(ends, after(to_neighbour, qkv))
+    attended = attend(ends, qkv)
     resid, layer_mlp, own_gate, own_up = close_attention(after(upstream, attended), w_out_own, layer_x, full_gain_mlp, w_gate, w_up)
 
     own_down = lax.all_gather(after(resid, w_down), "z", axis=0, tiled=True)
@@ -1397,17 +1441,15 @@
     grad_gate, grad_up = own_part(gate_term, *parts[1:3]), own_part(up_term, *parts[4:6])
     grad_out = jnp.sum(out_parts.astype(jnp.float32), axis=0)
     qkv_term = contract_rows(layer_normed, d_qkv).astype(LOW)
-    grad_low, gain_grads = close_layer(
-        after(qkv_term, d_qkv), w_qkv, layer_x, d_resid, full_gain_attn, gain_mlp_term
+    qkv_term = qkv_term.reshape(4, layers, 2 * shard, 3 * owned).transpose(1, 0, 2, 3)
+    qkv_term = qkv_term.reshape(layers, members * shard, 3 * owned)
+    grad_low, gain_grads, *_, parts = close_layer(
+        d_qkv, w_qkv, layer_x, d_resid, full_gain_attn, gain_mlp_term, qkv_term
     )
     grad_tokens = grad_low.astype(jnp.float32).reshape(rows_here, block, width)
-
-    qkv_term = qkv_term.reshape(4, layers, 2 * shard, 3 * owned).transpose(1, 0, 2, 3)
-    qkv_term = qkv_term.reshape(layers * members * shard, 3 * owned)
-    qkv_term = lax.psum_scatter(qkv_term, "z", scatter_dimension=0, tiled=True)
-    qkv_term = lax.all_to_all(qkv_term.reshape(members, shard, 3 * owned), LAYER, 0, 0)
-    qkv_term = qkv_term.reshape(members, shard, 3, owned).transpose(2, 1, 0, 3).astype(jnp.float32)
-    grad_query, grad_key, grad_value = qkv_term.reshape(3, shard, width)
+    parts = parts.reshape(4, 2, shard, 3, 2, HD)
+    parts = jnp.stack((parts[:, 0, :, :, 0], parts[:, 1, :, :, 0], parts[:, 1, :, :, 1], parts[:, 0, :, :, 1]), axis=1)
+    grad_query, grad_key, grad_value = parts.transpose(3, 2, 0, 1, 4).astype(jnp.float32).reshape(3, shard, width)
     gain_grads = lax.dynamic_index_in_dim(jnp.sum(gain_grads, axis=1).reshape(2, 2, shard), lax.axis_index("x"), 1, False)
     return (
         mixed,

time: 1130 us -> 1100 us (0.973)
  waiting for transfers between devices: 49.6 us -> 10.3 us
  Pallas kernels: 843 us -> 865 us
    all_gather x1, waiting for transfers between devices: 38.9 us -> 10.2 us  [body_layers(): lax.all_gather(after(facts, w_out), ('z', 'x'), axis=0, tiled=True)]
    pallas_call x1, Pallas kernels: 154 us -> 167 us  [close_attention(): pl.pallas_call(close_attention_kernel, out_shape=(jax.ShapeDtypeStruct((b...]
    pallas_call x1, Pallas kernels: 142 us -> 155 us  [close_layer(): pl.pallas_call(close_layer_kernel, out_shape=(jax.ShapeDtypeStruct((block...]
  transfers between devices with their start and end apart: 10 -> 7, of which waited for: 3 -> 1; matrix products, arithmetic and copies ran while one was open for 11% -> 10% of each run, Pallas kernels for 27% -> 14%
where the time goes in v10:
time: 1100 us; the launch traced here: 1090 us
  Pallas kernels  865 us (79%)
  matrix products  148 us (13%)
  other arithmetic  27.5 us (2%)
  local copies, waits for them, and re-layouts  20.7 us (2%)
  between operations  14.3 us (1%)
    pallas_call x1, Pallas kernels, close_mlp(): pl.pallas_call(close_mlp_kernel, out_shape=(jax.ShapeDtypeStruct((block,...  171 us
    pallas_call x1, Pallas kernels, close_attention(): pl.pallas_call(close_attention_kernel, out_shape=(jax.ShapeDtypeStruct((b...  167 us
    pallas_call x1, Pallas kernels, close_layer(): pl.pallas_call(close_layer_kernel, out_shape=(jax.ShapeDtypeStruct((block...  155 us
    pallas_call x1, Pallas kernels, begin(): pl.pallas_call(begin_kernel, out_shape=(jax.ShapeDtypeStruct((8 * block,...  130 us
    dot_general x5, matrix products, contract_rows(): lax.dot_general(left, right, (((0,), (0,)), ((), ())), preferred_element_...  94.7 us
    pallas_call x1, Pallas kernels, attend_back(): pl.pallas_call(attend_back_kernel, out_shape=(jax.ShapeDtypeStruct((place...  84.6 us
    pallas_call x1, Pallas kernels, open_mlp(): pl.pallas_call(open_mlp_kernel, out_shape=(jax.ShapeDtypeStruct((places,...  80.8 us
    dot_general x2, matrix products, dot_wide(): return jnp.dot(left, right, preferred_element_type=jnp.float32)  43.5 us
  transfers between devices with their start and end apart: 7, of which 1 were waited for; matrix products, arithmetic and copies ran while one was open for 10% of the time, Pallas kernels for 14%

profile of v10, /device:TPU:0, one launch (start us, length us, event | category | flops | bytes accessed | tf_op | source)
XLA Modules:
  0.0 1092.9 jit_solution(259979053645263300)
XLA Ops:
  7.2 0.0 all-gather.3.cloned.1.call-start
  7.2 0.7 pad_convert_fusion
  7.9 0.7 bitcast_convert_fusion.1
  8.5 0.7 convert_element_type.95
  9.2 0.1 scatter.19
  9.3 0.2 scatter.20.facts
  9.5 0.6 copy-done.10
  10.1 130.4 %shard_map.203 = (bf16[4096,2048]{1,0:T(8,128)(2,1)}, bf16[4,4,128,768]{3,2,1,0:T(8,128)(2,1)}, f32[4,4,2,8,128]{4,3,2,1,0:T(8,128)}) custom-call(bf16[2,256,2048]{2,1,0:T(8,128)(2,1)} %bitcast.55, bf16[64,2048]{1,0:T(8,128)(2,1)} %w_query.1, bf16[64,2048]{1,0:T(8,128)(2,1)} %w_key.1, bf16[64,2048]{1,0:T(8,128)(2,1)} %w_value.1, f32[8,128]{1,0:T(8,128)} %copy-done.10), custom_call_target="tpu_custom_call" | custom-call | bytes 350000000 | tf_op jit(solution)/shard_map/pallas_call | solution.py:684
  140.5 2.3 collective-permute-start
  142.8 0.2 all-gather.5.cloned.1.call-start
  143.0 0.7 slice.86
  143.8 7.2 fusion
  151.0 0.7 reduce-window.9
  151.7 1.1 slice_reduce_fusion
  152.7 0.1 mul.44
  152.8 0.7 reshape_squeeze.10.gain
  153.5 20.1 %convolution_convert_fusion.1.qkv = bf16[4096,768]{1,0:T(8,128)(2,1)} fusion(bf16[2048,768]{1,0:T(8,128)(2,1)} %bitcast.52, bf16[4096,2048]{1,0:T(8,128)(2,1)} %get-tuple-element.82.x_whole, f32[2048]{0:T(1024)S(1)} %mul.44, f32[4096]{0:T(1024)S(1)} %add_rsqrt_fusion), kind=kOutput, calls=%fused_computation.6 | convolution fusion | flops 12921602048 | bytes 26238976 | tf_op jit(solution)/shard_map/dot_general | solution.py:86
  173.6 42.4 %shard_map.204.attended = bf16[4096,256]{1,0:T(8,128)(2,1)} custom-call(s32[8]{0:T(128)} %bitcast.61, bf16[4096,768]{1,0:T(8,128)(2,1)} %convolution_convert_fusion.1.qkv), custom_call_target="tpu_custom_call" | custom-call | bytes 150000000 | tf_op jit(solution)/shard_map/pallas_call | solution.py:1326
  216.0 10.2 all-gather.3.cloned.1.call-done
  226.2 1.3 constant_dynamic-slice_fusion.6
  227.5 1.0 pad_maximum_fusion.w_out
  228.5 167.3 %shard_map.205 = (f32[512,2048]{1,0:T(8,128)}, bf16[4096,2048]{1,0:T(8,128)(2,1)}, bf16[2048,1024]{1,0:T(8,128)(2,1)}, bf16[2048,1024]{1,0:T(8,128)(2,1)}) custom-call(bf16[4096,256]{1,0:T(8,128)(2,1)} %shard_map.204.attended, bf16[256,2048]{1,0:T(8,128)(2,1)} %pad_maximum_fusion.w_out, bf16[4096,2048]{1,0:T(8,128)(2,1)} %get-tuple-element.82.x_whole, ...), custom_call_target="tpu_custom_call" | custom-call | bytes 450000000 | tf_op jit(solution)/shard_map/pallas_call | solution.py:787
  395.9 0.0 all-gather.5.cloned.1.call-update
  395.9 0.0 reduce-scatter.2.cloned.1.call-start
  395.9 80.8 %shard_map.206 = (f32[4096,1024]{1,0:T(8,128)}, f32[4096,1024]{1,0:T(8,128)}, bf16[4096,1024]{1,0:T(8,128)(2,1)}, bf16[4096,2048]{1,0:T(8,128)(2,1)}) custom-call(bf16[4096,2048]{1,0:T(8,128)(2,1)} %get-tuple-element.87.normed, bf16[2048,1024]{1,0:T(8,128)(2,1)} %get-tuple-element.88.w_gate, bf16[2048,1024]{1,0:T(8,128)(2,1)} %get-tuple-element.89.w_up, ...), custom_call_target="tpu_custom_call" | custom-call | bytes 250000000 | tf_op jit(solution)/shard_map/pallas_call | solution.py:1169
  476.7 0.0 all-gather.5.cloned.1.call-done.w_down
  476.8 23.5 %convolution_convert_fusion = bf16[4096,2048]{1,0:T(8,128)(2,1)} fusion(bf16[4096,1024]{1,0:T(8,128)(2,1)} %get-tuple-element.93, bf16[1024,2048]{1,0:T(8,128)(2,1)} %all-gather.5.cloned.1.call-done.w_down), kind=kOutput, calls=%fused_computation.5 | convolution fusion | flops 17188257792 | bytes 29360128 | tf_op jit(solution)/shard_map/dot_general | solution.py:86
  500.3 0.7 reshape_squeeze.11.gain
  501.0 23.9 %convolution_convert_fusion.5 = bf16[1024,2048]{1,0:T(8,128)(2,1)S(1)} fusion(bf16[4096,1024]{1,0:T(8,128)(2,1)} %get-tuple-element.93, bf16[4096,2048]{1,0:T(8,128)(2,1)} %get-tuple-element.95.upstream), kind=kOutput, calls=%fused_computation.12 | convolution fusion | flops 17181966336 | bytes 29360128 | tf_op jit(solution)/shard_map/dot_general | solution.py:20
  524.9 2.0 copy-done.5
  526.9 1.8 constant_dynamic-slice_fusion.2
  528.6 0.6 collective-permute-start.2
  529.2 3.6 collective-permute-start.3
  532.8 33.5 %shard_map.207 = (bf16[4096,1024]{1,0:T(8,128)(2,1)}, bf16[4096,1024]{1,0:T(8,128)(2,1)}) custom-call(bf16[4096,2048]{1,0:T(8,128)(2,1)} %get-tuple-element.95.upstream, bf16[1024,2048]{1,0:T(8,128)(2,1)} %all-gather.5.cloned.1.call-done.w_down, f32[4096,1024]{1,0:T(8,128)} %get-tuple-element.96.gate, f32[4096,1024]{1,0:T(8,128)} %get-tuple-element.97.up), custom_call_target="tpu_custom_call" | custom-call | bytes 90000000 | tf_op jit(solution)/shard_map/pallas_call | solution.py:1311
  566.3 24.2 %convolution_convert_fusion.4.grad_a = bf16[2048,1024]{1,0:T(8,128)(2,1)} fusion(bf16[4096,2048]{1,0:T(8,128)(2,1)} %get-tuple-element.87.normed, bf16[4096,1024]{1,0:T(8,128)(2,1)} %get-tuple-element.99.d_gate), kind=kOutput, calls=%fused_computation.11 | convolution fusion | flops 17181966336 | bytes 29360128 | tf_op jit(solution)/shard_map/dot_general | solution.py:20
  590.5 21.3 %convolution_convert_fusion.3.grad_b = bf16[2048,1024]{1,0:T(8,128)(2,1)} fusion(bf16[4096,2048]{1,0:T(8,128)(2,1)} %get-tuple-element.87.normed, bf16[4096,1024]{1,0:T(8,128)(2,1)S(1)} %copy-done.3), kind=kOutput, calls=%fused_computation.10 | convolution fusion | flops 17181966336 | bytes 29360128 | tf_op jit(solution)/shard_map/dot_general | solution.py:20
  611.8 3.6 add_add_fusion
  615.3 171.0 %shard_map.208 = (f32[512,2048]{1,0:T(8,128)}, f32[8,2048]{1,0:T(8,128)}, bf16[4096,2048]{1,0:T(8,128)(2,1)}, bf16[2048,256]{1,0:T(8,128)(2,1)}, bf16[2048,256]{...) custom-call(bf16[4096,1024]{1,0:T(8,128)(2,1)} %get-tuple-element.99, ...), custom_call_target="tpu_custom_call" | custom-call | bytes 450000000 | tf_op jit(solution)/shard_map/pallas_call | solution.py:892
  786.3 10.0 convolution_convert_fusion.2.grads
  796.4 1.2 copy-done
  797.6 0.6 copy-done.1
  798.2 5.5 convolution_convert_fusion.6.out_grad
  803.7 2.1 add_convert_fusion.mixed
  805.8 84.6 %shard_map.209 = (bf16[4096,768]{1,0:T(8,128)(2,1)}, bf16[4,64,2048]{2,1,0:T(8,128)(2,1)}, bf16[512,2048]{1,0:T(8,128)(2,1)}) custom-call(s32[8]{0:T(128)} %bitcast.62, bf16[4096,768]{1,0:T(8,128)(2,1)} %convolution_convert_fusion.1.qkv, bf16[4096,256]{1,0:T(8,128)(2,1)} %convolution_convert_fusion.2.grads, ...), custom_call_target="tpu_custom_call" | custom-call | bytes 300000000 | tf_op jit(solution)/shard_map/pallas_call | solution.py:1342
  890.4 19.9 %fusion.6 = bf16[2048,768]{1,0:T(8,128)(2,1)S(1)} fusion(bf16[4096,768]{1,0:T(8,128)(2,1)} %get-tuple-element.104.d_qkv, bf16[4096,2048]{1,0:T(8,128)(2,1)} %get-tuple-element.82.x_whole, f32[2048]{0:T(1024)S(1)} %copy-done.14, f32[4096]{0:T(1024)S(1)} %copy-done.12), kind=kOutput, calls=%fused_computation.13 | convolution fusion | flops 12920029184 | bytes 26238976 | tf_op jit(solution)/shard_map/dot_general | solution.py:20
  910.3 1.9 copy.35
  912.2 155.1 %shard_map.210 = (bf16[512,2048]{1,0:T(8,128)(2,1)}, f32[2,8,128]{2,1,0:T(8,128)}, bf16[512,768]{1,0:T(8,128)(2,1)}, bf16[512,768]{1,0:T(8,128)(2,1)}, bf16[512,...) custom-call(bf16[4096,768]{1,0:T(8,128)(2,1)} %get-tuple-element.104.d_qkv, bf16[2048,768]{1,0:T(8,128)(2,1)} %bitcast.53, ...), custom_call_target="tpu_custom_call" | custom-call | bytes 350000000 | tf_op jit(solution)/shard_map/pallas_call | solution.py:1057
  1067.3 4.2 bitcast_convert_fusion
  1071.5 0.2 reshape.198
  1071.7 1.3 fusion.14
  1073.1 0.1 copy_bitcast_fusion.1
  1073.2 0.1 convert_bitcast_fusion
  1073.4 0.2 fusion.13
  1073.6 0.3 copy.40
  1073.9 1.0 unstack.19
  1074.9 0.3 copy.41
  1075.3 1.0 unstack.21
  1076.3 0.3 copy.42
  1076.6 1.0 unstack.23
  1077.6 0.9 convert_reduce_fusion
  1078.6 0.1 reshape.199
  1078.7 0.5 fusion.11
  1079.2 5.6 convert_add_fusion
  1084.9 1.3 copy.56
  (41 shorter events, 0.2 us)
Async XLA Ops:
  7.2 219.0 %all-gather.3.cloned.1.call-start = ((), (), s32[]{:S(2)}) async-start(), calls=%async_computation.1 | async-start | bytes 2359296 | tf_op jit(solution)/shard_map/all_gather | solution.py:1403
  9.5 0.6 copy-start.10
  140.5 75.5 %collective-permute-start = (bf16[1,512,2048]{2,1,0:T(8,128)(2,1)}, bf16[1,512,2048]{2,1,0:T(8,128)(2,1)S(1)}, u32[]{:S(2)}, u32[]{:S(2)}) collective-permute-start(bf16[1,512,2048]{2,1,0:T(8,128)(2,1)} %param.20), channel_id=1, source_target_pairs={{0,0},{1,1},{2,16},{3,17},{4,8},{5,9},{6,24},{7,25},{8,4},{9,5},{1... | collective-permute-start | bytes 6291464 | tf_op jit(solution)/shard_map/ppermute | solution.py:1377
  142.8 333.9 %all-gather.5.cloned.1.call-start = ((), (), s32[]{:S(2)}) async-start(), calls=%async_computation.2 | async-start | bytes 5242880 | tf_op jit(solution)/shard_map/all_gather | solution.py:1412
  152.8 20.8 %copy-start.13 = (f32[2048]{0:T(1024)}, f32[2048]{0:T(1024)S(1)}, u32[]{:S(2)}) copy-start(f32[2048]{0:T(1024)S(1)} %mul.44) | copy-start | bytes 24580
  153.5 20.1 %copy-start.11 = (f32[4096]{0:T(1024)}, f32[4096]{0:T(1024)S(1)}, u32[]{:S(2)}) copy-start(f32[4096]{0:T(1024)S(1)} %add_rsqrt_fusion) | copy-start | bytes 49156
  216.0 179.8 %copy-start.4 = (bf16[1,512,2048]{2,1,0:T(8,128)(2,1)}, bf16[1,512,2048]{2,1,0:T(8,128)(2,1)S(1)}, u32[]{:S(2)}) copy-start(bf16[1,512,2048]{2,1,0:T(8,128)(2,1)S(1)} %collective-permute-done) | copy-start | bytes 6291460
  395.9 219.5 %reduce-scatter.2.cloned.1.call-start = ((), (), s32[]{:S(2)}) async-start(), calls=%async_computation.3 | async-start | bytes 18874368 | tf_op jit(solution)/shard_map/reduce_scatter | solution.py:1415
  524.9 2.0 copy-start.5
  528.6 83.2 %collective-permute-start.1 = (bf16[256,2048]{1,0:T(8,128)(2,1)}, bf16[256,2048]{1,0:T(8,128)(2,1)S(1)}, u32[]{:S(2)}, u32[]{:S(2)}) collective-permute-start(bf16[256,2048]{1,0:T(8,128)(2,1)} %get-tuple-element.119), channel_id=1, source_target_pairs={{0,2},{2,4},{4,6},{6,0},{1,3},{3,5},{5,7},{7,1},{8,10},{10,12},{12... | collective-permute-start | bytes 3145736 | tf_op jit(solution)/shard_map/ppermute | solution.py:1422
  528.6 83.2 %collective-permute-start.2 = (bf16[256,2048]{1,0:T(8,128)(2,1)}, bf16[256,2048]{1,0:T(8,128)(2,1)S(1)}, u32[]{:S(2)}, u32[]{:S(2)}) collective-permute-start(bf16[256,2048]{1,0:T(8,128)(2,1)} %get-tuple-element.118), channel_id=1, source_target_pairs={{0,4},{2,6},{4,0},{6,2},{1,5},{3,7},{5,1},{7,3},{8,12},{10,14},{12... | collective-permute-start | bytes 3145736 | tf_op jit(solution)/shard_map/ppermute | solution.py:1422
  529.2 82.5 %collective-permute-start.3 = (bf16[256,2048]{1,0:T(8,128)(2,1)}, bf16[256,2048]{1,0:T(8,128)(2,1)}, u32[]{:S(2)}, u32[]{:S(2)}) collective-permute-start(bf16[256,2048]{1,0:T(8,128)(2,1)} %get-tuple-element.117), channel_id=1, source_target_pairs={{0,6},{2,0},{4,2},{6,4},{1,7},{3,1},{5,3},{7,5},{8,14},{10,8},{12,... | collective-permute-start | bytes 3145736 | tf_op jit(solution)/shard_map/ppermute | solution.py:1422
  566.3 24.2 %copy-start.3 = (bf16[4096,1024]{1,0:T(8,128)(2,1)S(1)}, bf16[4096,1024]{1,0:T(8,128)(2,1)}, u32[]{:S(2)}) copy-start(bf16[4096,1024]{1,0:T(8,128)(2,1)} %get-tuple-element.100.d_up) | copy-start | bytes 25165828
  786.3 11.3 %copy-start = (bf16[4096,2048]{1,0:T(8,128)(2,1)S(1)}, bf16[4096,2048]{1,0:T(8,128)(2,1)}, u32[]{:S(2)}) copy-start(bf16[4096,2048]{1,0:T(8,128)(2,1)} %get-tuple-element.101) | copy-start | bytes 50331652
  786.3 11.9 %copy-start.1 = (bf16[4096,256]{1,0:T(8,128)(2,1)S(1)}, bf16[4096,256]{1,0:T(8,128)(2,1)}, u32[]{:S(2)}) copy-start(bf16[4096,256]{1,0:T(8,128)(2,1)} %shard_map.204.attended) | copy-start | bytes 6291460
  798.2 5.5 copy-start.2
  798.2 5.5 copy-start.7
  805.8 84.6 %copy-start.12 = (f32[4096]{0:T(1024)S(1)}, f32[4096]{0:T(1024)}, u32[]{:S(2)}) copy-start(f32[4096]{0:T(1024)} %copy-done.11) | copy-start | bytes 49156
  805.8 84.6 %copy-start.14 = (f32[2048]{0:T(1024)S(1)}, f32[2048]{0:T(1024)}, u32[]{:S(2)}) copy-start(f32[2048]{0:T(1024)} %copy-done.13) | copy-start | bytes 24580
  1067.3 4.2 copy-start.9
  1073.4 4.2 copy-start.8
  1073.6 5.0 copy-start.15
  1079.2 5.7 copy-start.6
Sparse Core Ops, SparseCore 0:
  142.9 83.2 all-gather.2
  396.0 78.5 all-gather.4
  500.4 113.5 reduce-scatter.1

commit v11 on v10

--- a/solution.py
+++ b/solution.py
@@ -593,16 +593,14 @@
 
 
 def begin_kernel(
-    x_own, w_query, w_key, w_value, facts, x_whole, w_qkv, facts_whole,
-    gather_send, gather_recv, w_send, w_recv, fact_send, fact_recv, local, *scratch
+    x_source, w_query, w_key, w_value, facts, normed_whole, x_own, w_qkv, facts_whole,
+    held, normed, gather_send, gather_recv, w_send, w_recv, fact_send, fact_recv, local, *scratch
 ):
     y, c, z, x = spot()
     row = 2 * y + c
     layer = others()
     trade_parts, sems = scratch[:5], scratch[5:]
-    trade = Trade(
-        [x_own.at[half] for half in (0, 1)], lambda half, at: x_whole.at[place_of(at[0], at[1], at[3], half)], *trade_parts, detour=False
-    )
+    trade = Trade([x_source.at[half] for half in (0, 1)], lambda half, at: held.at[half], *trade_parts, detour=False)
     barrier, count = greet_neighbours(layer)
     pl.semaphore_wait(barrier, count + trade.greet(barrier, True))
 
@@ -627,11 +625,23 @@
     for copy in spread + kept:
         copy.start()
 
-    gather = GatherWhole(lambda half: x_whole.at[place_of(y, c, x, half)], x_whole, gather_send, gather_recv)
+    gather = GatherWhole(lambda half: normed.at[half], normed_whole, gather_send, gather_recv)
+    outs = []
     for half in (0, 1):
-        trade.forward(half)
         trade.arrive(half)
+
+        def step(i, carry):
+            here = pl.ds(pl.multiple_of(i * CHUNK, CHUNK), CHUNK)
+            value = held[half, here, :].astype(jnp.float32)
+            normed[half, here, :] = (value * inverse_of(value)).astype(LOW)
+            return carry
+
+        lax.fori_loop(0, HALF // CHUNK, step, 0)
         gather.start(half)
+        outs.append(pltpu.make_async_copy(held.at[half], x_own.at[pl.ds(half * HALF, HALF)], local.at[7 + half]))
+        outs.append(pltpu.make_async_copy(normed.at[half], normed_whole.at[place_of(y, c, x, half)], local.at[9 + half]))
+        outs[-2].start()
+        outs[-1].start()
 
     for copy in kept:
         copy.wait()
@@ -660,6 +670,8 @@
         copy.wait_send()
     for chain in chains:
         chain.finish()
+    for copy in outs:
+        copy.wait()
 
 
 def anywhere():
@@ -678,26 +690,30 @@
     return pltpu.CompilerParams(collective_id=number, has_side_effects=True, vmem_limit_bytes=VMEM_LIMIT)
 
 
-def begin(x_own, w_query, w_key, w_value, facts):
-    block, width = x_own.shape
+def begin(x_source, w_query, w_key, w_value, facts):
+    block, width = x_source.shape
     shard = w_query.shape[0]
-    x_whole, w_qkv, facts_whole = pl.pallas_call(
+    whole_facts = (4, 4, 2, *facts.shape)
+    normed_whole, x_own, w_qkv, facts_whole = pl.pallas_call(
         begin_kernel,
         out_shape=(
             jax.ShapeDtypeStruct((8 * block, width), LOW),
+            jax.ShapeDtypeStruct((block, width), LOW),
             jax.ShapeDtypeStruct((4, 4, 2 * shard, 3 * width // 8), LOW),
-            jax.ShapeDtypeStruct((4, 4, 2, *facts.shape), jnp.float32),
+            jax.ShapeDtypeStruct(whole_facts, jnp.float32),
         ),
         in_specs=[in_vmem()] + [anywhere()] * 4,
-        out_specs=[anywhere()] * 3,
+        out_specs=[anywhere()] * 4,
         scratch_shapes=[
-            dma(GATHER_COPIES), dma(GATHER_COPIES), dma(6, 7), dma(6, 7), dma(7), dma(7), dma(7),
+            pltpu.VMEM((2, block // 2, width), LOW),
+            pltpu.VMEM((2, block // 2, width), LOW),
+            dma(14), dma(14), dma(6, 7), dma(6, 7), dma(7), dma(7), dma(11),
             *trade_scratch(2, block // 2, width), *chain_sems(2),
         ],
         compiler_params=remote_params(1),
         cost_estimate=pl.CostEstimate(flops=0, bytes_accessed=350_000_000, transcendentals=0),
-    )(x_own.reshape(2, block // 2, width), w_query, w_key, w_value, facts)
-    return x_whole, w_qkv.reshape(width, 3 * width // 8), facts_whole
+    )(x_source.reshape(2, block // 2, width), w_query, w_key, w_value, facts)
+    return normed_whole, x_own, w_qkv.reshape(width, 3 * width // 8), facts_whole
 
 
 def summed(total, landed, here):
@@ -721,10 +737,10 @@
     return lax.rsqrt(jnp.mean(value * value, axis=-1, keepdims=True) + EPSILON)
 
 
-def close_attention_kernel(attended, w_out, x_whole, gain, w_gate, w_up, resid, normed, own_gate, own_up, own, x_own, *scratch):
+def close_attention_kernel(attended, w_out, x_home, gain, w_gate, w_up, resid, normed, own_gate, own_up, own, x_own, *scratch):
     scatter, (send, recv, local), sems = scratch[:7], scratch[7:10], scratch[10:]
     y, c, z, x = spot()
-    fetch_x = pltpu.make_async_copy(x_whole.at[place_of(y, c, x)], x_own, local.at[0])
+    fetch_x = pltpu.make_async_copy(x_home, x_own, local.at[0])
     fetch_x.start()
     width = w_out.shape[1]
     hidden = w_gate.shape[1]
@@ -781,8 +797,8 @@
         copy.wait()
 
 
-def close_attention(attended, w_out, x_whole, gain, w_gate, w_up):
-    block, width = x_whole.shape[0] // 8, x_whole.shape[1]
+def close_attention(attended, w_out, x_home, gain, w_gate, w_up):
+    block, width = x_home.shape
     hidden = w_gate.shape[1]
     return pl.pallas_call(
         close_attention_kernel,
@@ -799,7 +815,7 @@
         + [dma(GATHER_COPIES), dma(GATHER_COPIES), dma(3), *chain_sems(2)],
         compiler_params=remote_params(2),
         cost_estimate=pl.CostEstimate(flops=0, bytes_accessed=450_000_000, transcendentals=0),
-    )(attended, w_out, x_whole, gain, w_gate, w_up)
+    )(attended, w_out, x_home, gain, w_gate, w_up)
 
 
 def norm_back(value, gain, upstream):
@@ -909,12 +925,12 @@
 
 
 def close_layer_kernel(
-    d_qkv, w_qkv, x_whole, d_resid, gain, mlp_term, grad, grad_low, gain_grads, far, near_part, cross, grad_parts, own, terms, layer_terms, part, column_terms, *scratch
+    d_qkv, w_qkv, x_home, d_resid, gain, mlp_term, grad, grad_low, gain_grads, far, near_part, cross, grad_parts, own, terms, layer_terms, part, column_terms, *scratch
 ):
     scatter, (send, recv, term_send, term_recv, line_send, line_recv, x_own, x_sem, *rest) = scratch[:7], scratch[7:]
     mine, theirs, fold_send, fold_recv, fold_local, part_send, part_recv = rest
     y, c, z, x = spot()
-    fetch_x = pltpu.make_async_copy(x_whole.at[place_of(y, c, x)], x_own, x_sem.at[0])
+    fetch_x = pltpu.make_async_copy(x_home, x_own, x_sem.at[0])
     fetch_x.start()
     partner = partner_of(y, c, z, x)
     moves = z != 2 * c + y
@@ -948,6 +964,34 @@
 
     fold = Fold(lambda at: grad.at[at], far, near_part, cross, mine, theirs, fold_send, fold_recv, fold_local)
     fold.start()
+    def end_fold():
+        fold.finish()
+        for source, target, k in ((grad.at[z], mine, 0), (near_part, theirs, 1)):
+            pltpu.make_async_copy(source, target, fold_local.at[k]).start()
+        for source, target, k in ((grad.at[z], mine, 0), (near_part, theirs, 1)):
+            pltpu.make_async_copy(source, target, fold_local.at[k]).wait()
+        add_rows(mine, 0, theirs, 0, mine.shape[0])
+        last = pltpu.make_async_copy(cross, theirs, fold_local.at[1])
+        last.start()
+        last.wait()
+        add_rows(mine, 0, theirs, 0, mine.shape[0])
+        shard = mine.shape[0] // 8
+        index = 4 * y + 2 * c + x
+        parts = [
+            remote(
+                mine.at[pl.ds(pl.multiple_of((4 * peer[0] + 2 * peer[1] + peer[3]) * shard, shard), shard)],
+                grad_parts.at[index],
+                part_send.at[k],
+                part_recv.at[k],
+                peer,
+            )
+            for k, peer in enumerate(layer)
+        ]
+        kept = pltpu.make_async_copy(mine.at[pl.ds(pl.multiple_of(index * shard, shard), shard)], grad_parts.at[index], fold_local.at[0])
+        for copy in parts + [kept]:
+            copy.start()
+        return parts + [kept]
+
     sums = [part_of(piece) for piece in range(PIECES)]
     sums[0].begin()
     sums[0].relay()
@@ -960,7 +1004,10 @@
     trades = [remote(own.at[at], grad_low.at[at], send.at[k], recv.at[k], partner) for k, at in enumerate(pieces)]
     keeps = [pltpu.make_async_copy(own.at[at], grad_low.at[at], recv.at[k]) for k, at in enumerate(pieces)]
     fetch_x.wait()
+    to_peers = []
     for piece in range(PIECES):
+        if piece == PIECES - 1:
+            to_peers = end_fold()
         sums[piece].arrive()
 
         def step(i, carry):
@@ -984,32 +1031,6 @@
             sums[piece + 1].relay()
         if piece + 2 < PIECES:
             sums[piece + 2].begin()
-
-    fold.finish()
-    for source, target, k in ((grad.at[z], mine, 0), (near_part, theirs, 1)):
-        pltpu.make_async_copy(source, target, fold_local.at[k]).start()
-    for source, target, k in ((grad.at[z], mine, 0), (near_part, theirs, 1)):
-        pltpu.make_async_copy(source, target, fold_local.at[k]).wait()
-    add_rows(mine, 0, theirs, 0, mine.shape[0])
-    last = pltpu.make_async_copy(cross, theirs, fold_local.at[1])
-    last.start()
-    last.wait()
-    add_rows(mine, 0, theirs, 0, mine.shape[0])
-    shard = mine.shape[0] // 8
-    index = 4 * y + 2 * c + x
-    parts = [
-        remote(
-            mine.at[pl.ds(pl.multiple_of((4 * peer[0] + 2 * peer[1] + peer[3]) * shard, shard), shard)],
-            grad_parts.at[index],
-            part_send.at[k],
-            part_recv.at[k],
-            peer,
-        )
-        for k, peer in enumerate(layer)
-    ]
-    kept = pltpu.make_async_copy(mine.at[pl.ds(pl.multiple_of(index * shard, shard), shard)], grad_parts.at[index], fold_local.at[0])
-    for copy in parts + [kept]:
-        copy.start()
 
     def columns_of(row, layers):
         return pl.ds(pl.multiple_of((4 * row) * HD, HD), layers * HD)
@@ -1038,7 +1059,7 @@
         copy.wait_send()
     for part_sum in sums:
         part_sum.finish()
-    for copy in parts + [kept]:
+    for copy in to_peers:
         copy.wait()
 
     @pl.when(moves)
@@ -1052,7 +1073,7 @@
             copy.wait()
 
 
-def close_layer(d_qkv, w_qkv, x_whole, d_resid, gain, mlp_term, grad):
+def close_layer(d_qkv, w_qkv, x_home, d_resid, gain, mlp_term, grad):
     block, width = d_resid.shape
     return pl.pallas_call(
         close_layer_kernel,
@@ -1077,7 +1098,7 @@
         + [dma(3), dma(3), dma(2), dma(7), dma(7)],
         compiler_params=remote_params(4),
         cost_estimate=pl.CostEstimate(flops=0, bytes_accessed=350_000_000, transcendentals=0),
-    )(d_qkv, w_qkv, x_whole, d_resid, gain, mlp_term, grad)
+    )(d_qkv, w_qkv, x_home, d_resid, gain, mlp_term, grad)
 
 
 def doc_start(ends, place):
@@ -1389,17 +1410,19 @@
     layers = lax.axis_size("z")
     shard = w_query.shape[0]
     owned = width // members
-    facts = jnp.zeros((8, 2 * shard), jnp.float32)
-    facts = facts.at[0, :shard].set(gain_attn.astype(jnp.float32)).at[1, :shard].set(gain_mlp.astype(jnp.float32))
-    facts = facts.at[2, : lengths.shape[1]].set(lengths[0].astype(jnp.float32))
-    layer_x, w_qkv, facts = begin(tokens.reshape(block, width), w_query, w_key, w_value, facts)
-    full_gain_attn, full_gain_mlp = facts[:, :, :, 0, :shard].reshape(1, width), facts[:, :, :, 1, :shard].reshape(1, width)
+    here = lax.axis_index("x")
+    gains = jnp.stack((gain_attn, gain_mlp)).astype(jnp.float32)
+    gains = jnp.concatenate((jnp.where(here == 0, gains, 0.0), jnp.where(here == 1, gains, 0.0)), axis=1)
+    lengths_row = jnp.pad(lengths.astype(jnp.float32), ((0, 0), (0, 2 * shard - lengths.shape[1])))
+    facts = jnp.concatenate((gains, lengths_row, jnp.zeros((5, 2 * shard), jnp.float32)), axis=0)
+    layer_scaled, x_own, w_qkv, facts = begin(tokens.reshape(block, width), w_query, w_key, w_value, facts)
+    gains = facts[:, :, 0] + facts[:, :, 1]
+    full_gain_attn, full_gain_mlp = gains[:, :, 0].reshape(1, width), gains[:, :, 1].reshape(1, width)
+    layer_normed = (layer_scaled.astype(jnp.float32) * full_gain_attn).astype(LOW)
     layer = lax.axis_index("z")
     own_lengths = facts[:, 0, 0, 2, : lengths.shape[1]].reshape(2, 2, -1)
     own_lengths = lax.dynamic_slice(own_lengths, (layer % 2, layer // 2, 0), (1, 1, own_lengths.shape[2]))[0, 0]
     ends = jnp.cumsum(own_lengths.astype(jnp.int32))
-    layer_normed = norm_forward(layer_x.astype(jnp.float32), full_gain_attn)[0].astype(LOW)
-    here = lax.axis_index("x")
     out_rows = lax.all_gather(after(facts, w_out), ("z", "x"), axis=0, tiled=True)
     w_out_own = [lax.dynamic_slice_in_dim(out_rows, head * HD, HD, 0) for head in (here, 3 - here)]
     w_out_own = jnp.concatenate(w_out_own, axis=0)
@@ -1407,7 +1430,7 @@
     qkv = dot_wide(layer_normed, w_qkv).astype(LOW)
     upstream = trade(after(facts, cotangent)).reshape(block, width)
     attended = attend(ends, qkv)
-    resid, layer_mlp, own_gate, own_up = close_attention(after(upstream, attended), w_out_own, layer_x, full_gain_mlp, w_gate, w_up)
+    resid, layer_mlp, own_gate, own_up = close_attention(after(upstream, attended), w_out_own, x_own, full_gain_mlp, w_gate, w_up)
 
     own_down = lax.all_gather(after(resid, w_down), "z", axis=0, tiled=True)
     gate, up_part, hidden, layer_upstream = open_mlp(layer_mlp, own_gate, own_up, upstream)
@@ -1444,7 +1467,7 @@
     qkv_term = qkv_term.reshape(4, layers, 2 * shard, 3 * owned).transpose(1, 0, 2, 3)
     qkv_term = qkv_term.reshape(layers, members * shard, 3 * owned)
     grad_low, gain_grads, *_, parts = close_layer(
-        d_qkv, w_qkv, layer_x, d_resid, full_gain_attn, gain_mlp_term, qkv_term
+        d_qkv, w_qkv, x_own, d_resid, full_gain_attn, gain_mlp_term, qkv_term
     )
     grad_tokens = grad_low.astype(jnp.float32).reshape(rows_here, block, width)
     parts = parts.reshape(4, 2, shard, 3, 2, HD)

time: 1100 us -> 1090 us (level)
  Pallas kernels: 865 us -> 847 us
  transfers between devices with their start and end apart: 7 -> 7, of which waited for: 1 -> 1; matrix products, arithmetic and copies ran while one was open for 10% -> 9% of each run, Pallas kernels for 14% -> 14%
where the time goes in v11:
time: 1090 us; the launch traced here: 1080 us
  Pallas kernels  847 us (78%)
  matrix products  147 us (13%)
  other arithmetic  21.2 us (2%)
  waiting for transfers between devices  18.6 us (2%)
  local copies, waits for them, and re-layouts  17.8 us (2%)
  starting transfers between devices  14.6 us (1%)
  between operations  14.3 us (1%)
    pallas_call x1, Pallas kernels, close_attention(): pl.pallas_call(close_attention_kernel, out_shape=(jax.ShapeDtypeStruct((b...  168 us
    pallas_call x1, Pallas kernels, close_mlp(): pl.pallas_call(close_mlp_kernel, out_shape=(jax.ShapeDtypeStruct((block,...  163 us
    pallas_call x1, Pallas kernels, close_layer(): pl.pallas_call(close_layer_kernel, out_shape=(jax.ShapeDtypeStruct((block...  145 us
    pallas_call x1, Pallas kernels, begin(): pl.pallas_call(begin_kernel, out_shape=(jax.ShapeDtypeStruct((8 * block,...  130 us
    dot_general x5, matrix products, contract_rows(): lax.dot_general(left, right, (((0,), (0,)), ((), ())), preferred_element_...  93.6 us
    pallas_call x1, Pallas kernels, attend_back(): pl.pallas_call(attend_back_kernel, out_shape=(jax.ShapeDtypeStruct((place...  84.5 us
    pallas_call x1, Pallas kernels, open_mlp(): pl.pallas_call(open_mlp_kernel, out_shape=(jax.ShapeDtypeStruct((places,...  80.8 us
    dot_general x2, matrix products, dot_wide(): return jnp.dot(left, right, preferred_element_type=jnp.float32)  42.9 us
  transfers between devices with their start and end apart: 7, of which 1 were waited for; matrix products, arithmetic and copies ran while one was open for 9% of the time, Pallas kernels for 14%

profile of v11, /device:TPU:0, one launch (start us, length us, event | category | flops | bytes accessed | tf_op | source)
XLA Modules:
  0.0 1080.3 jit_solution(14252669951116031507)
XLA Ops:
  7.2 0.0 all-gather.3.cloned.1.call-start
  7.2 0.7 convert_element_type.98
  7.9 0.1 pad.14.clone
  8.0 0.7 convert_select_fusion.1
  8.6 0.7 fusion.4.facts
  9.3 130.4 %shard_map.203 = (bf16[4096,2048]{1,0:T(8,128)(2,1)}, bf16[512,2048]{1,0:T(8,128)(2,1)}, bf16[4,4,128,768]{3,2,1,0:T(8,128)(2,1)}, f32[4,4,2,8,128]{4,3,2,1,0:T(8,128)}) custom-call(bf16[2,256,2048]{2,1,0:T(8,128)(2,1)} %bitcast.57, bf16[64,2048]{1,0:T(8,128)(2,1)} %w_query.1, bf16[64,2048]{1,0:T(8,128)(2,1)} %w_key.1, bf16[64,2048]{1,0:T(8,128)(2,1)} %w_value.1, ...), custom_call_target="tpu_custom_call" | custom-call | bytes 350000000 | tf_op jit(solution)/shard_map/pallas_call | solution.py:697
  139.7 2.3 collective-permute-start
  142.0 0.0 all-gather.3.cloned.1.call-update
  142.0 0.0 all-gather.5.cloned.1.call-start
  142.1 0.7 slice.38
  142.8 0.7 reduce-window.9
  143.5 0.9 add_bitcast_fusion
  144.4 0.6 fusion.12
  145.0 19.4 %fusion.2.qkv = bf16[4096,768]{1,0:T(8,128)(2,1)} fusion(bf16[2048,768]{1,0:T(8,128)(2,1)} %bitcast.55, bf16[4096,2048]{1,0:T(8,128)(2,1)} %get-tuple-element.47, f32[2048]{0:T(1024)S(1)} %bitcast.63), kind=kOutput, calls=%fused_computation.4 | convolution fusion | flops 12913213440 | bytes 26222592 | tf_op jit(solution)/shard_map/dot_general | solution.py:86
  164.4 42.4 %shard_map.204.attended = bf16[4096,256]{1,0:T(8,128)(2,1)} custom-call(s32[8]{0:T(128)} %bitcast.67, bf16[4096,768]{1,0:T(8,128)(2,1)} %fusion.2.qkv), custom_call_target="tpu_custom_call" | custom-call | bytes 150000000 | tf_op jit(solution)/shard_map/pallas_call | solution.py:1347
  206.8 0.0 collective-permute-done
  206.8 18.5 %all-gather.3.cloned.1.call-done = bf16[512,2048]{1,0:T(8,128)(2,1)} async-done(((bf16[64,2048]{1,0:T(8,128)(2,1)}), bf16[512,2048]{1,0:T(8,128)(2,1)}) %all-gather.3.cloned.1.call-update) | async-done | bytes 2097168 | tf_op jit(solution)/shard_map/all_gather | solution.py:1426
  225.3 1.3 constant_dynamic-slice_fusion.6
  226.6 1.0 pad_maximum_fusion.w_out
  227.6 167.7 %shard_map.205 = (f32[512,2048]{1,0:T(8,128)}, bf16[4096,2048]{1,0:T(8,128)(2,1)}, bf16[2048,1024]{1,0:T(8,128)(2,1)}, bf16[2048,1024]{1,0:T(8,128)(2,1)}) custom-call(bf16[4096,256]{1,0:T(8,128)(2,1)} %shard_map.204.attended, bf16[256,2048]{1,0:T(8,128)(2,1)} %pad_maximum_fusion.w_out, bf16[512,2048]{1,0:T(8,128)(2,1)} %get-tuple-element.52.x_home, ...), custom_call_target="tpu_custom_call" | custom-call | bytes 450000000 | tf_op jit(solution)/shard_map/pallas_call | solution.py:803
  395.4 0.0 all-gather.5.cloned.1.call-update
  395.4 0.0 reduce-scatter.2.cloned.1.call-start
  395.4 80.8 %shard_map.206 = (f32[4096,1024]{1,0:T(8,128)}, f32[4096,1024]{1,0:T(8,128)}, bf16[4096,1024]{1,0:T(8,128)(2,1)}, bf16[4096,2048]{1,0:T(8,128)(2,1)}) custom-call(bf16[4096,2048]{1,0:T(8,128)(2,1)} %get-tuple-element.53.normed, bf16[2048,1024]{1,0:T(8,128)(2,1)} %get-tuple-element.54.w_gate, bf16[2048,1024]{1,0:T(8,128)(2,1)} %get-tuple-element.55.w_up, ...), custom_call_target="tpu_custom_call" | custom-call | bytes 250000000 | tf_op jit(solution)/shard_map/pallas_call | solution.py:1190
  476.2 0.0 all-gather.5.cloned.1.call-done.w_down
  476.3 23.5 %convolution_convert_fusion = bf16[4096,2048]{1,0:T(8,128)(2,1)} fusion(bf16[4096,1024]{1,0:T(8,128)(2,1)} %get-tuple-element.59, bf16[1024,2048]{1,0:T(8,128)(2,1)} %all-gather.5.cloned.1.call-done.w_down), kind=kOutput, calls=%fused_computation.1 | convolution fusion | flops 17188257792 | bytes 29360128 | tf_op jit(solution)/shard_map/dot_general | solution.py:86
  499.7 0.0 reduce-scatter.2.cloned.1.call-update
  499.8 23.6 %convolution_convert_fusion.4 = bf16[1024,2048]{1,0:T(8,128)(2,1)S(1)} fusion(bf16[4096,1024]{1,0:T(8,128)(2,1)} %get-tuple-element.59, bf16[4096,2048]{1,0:T(8,128)(2,1)} %get-tuple-element.61.upstream), kind=kOutput, calls=%fused_computation.9 | convolution fusion | flops 17181966336 | bytes 29360128 | tf_op jit(solution)/shard_map/dot_general | solution.py:20
  523.4 0.0 copy-start.5
  523.4 2.0 copy-done.5
  525.4 1.7 constant_dynamic-slice_fusion.2
  527.2 0.5 collective-permute-start.2
  527.7 11.8 %collective-permute-start.3 = (bf16[256,2048]{1,0:T(8,128)(2,1)}, bf16[256,2048]{1,0:T(8,128)(2,1)}, u32[]{:S(2)}, u32[]{:S(2)}) collective-permute-start(bf16[256,2048]{1,0:T(8,128)(2,1)} %get-tuple-element.81), channel_id=1, source_target_pairs={{0,6},{2,0},{4,2},{6,4},{1,7},{3,1},{5,3},{7,5},{8,14},{10,8},{12,... | collective-permute-start | bytes 3145736 | tf_op jit(solution)/shard_map/ppermute | solution.py:1445
  539.4 33.1 %shard_map.207 = (bf16[4096,1024]{1,0:T(8,128)(2,1)}, bf16[4096,1024]{1,0:T(8,128)(2,1)}) custom-call(bf16[4096,2048]{1,0:T(8,128)(2,1)} %get-tuple-element.61.upstream, bf16[1024,2048]{1,0:T(8,128)(2,1)} %all-gather.5.cloned.1.call-done.w_down, f32[4096,1024]{1,0:T(8,128)} %get-tuple-element.62.gate, f32[4096,1024]{1,0:T(8,128)} %get-tuple-element.63.up), custom_call_target="tpu_custom_call" | custom-call | bytes 90000000 | tf_op jit(solution)/shard_map/pallas_call | solution.py:1332
  572.5 24.0 %convolution_convert_fusion.3.grad_a = bf16[2048,1024]{1,0:T(8,128)(2,1)} fusion(bf16[4096,2048]{1,0:T(8,128)(2,1)} %get-tuple-element.53.normed, bf16[4096,1024]{1,0:T(8,128)(2,1)} %get-tuple-element.65.d_gate), kind=kOutput, calls=%fused_computation.8 | convolution fusion | flops 17181966336 | bytes 29360128 | tf_op jit(solution)/shard_map/dot_general | solution.py:20
  596.5 21.3 %convolution_convert_fusion.2.grad_b = bf16[2048,1024]{1,0:T(8,128)(2,1)} fusion(bf16[4096,2048]{1,0:T(8,128)(2,1)} %get-tuple-element.53.normed, bf16[4096,1024]{1,0:T(8,128)(2,1)S(1)} %copy-done.3), kind=kOutput, calls=%fused_computation.7 | convolution fusion | flops 17181966336 | bytes 29360128 | tf_op jit(solution)/shard_map/dot_general | solution.py:20
  617.8 3.6 add_add_fusion
  621.4 163.5 %shard_map.208 = (f32[512,2048]{1,0:T(8,128)}, f32[8,2048]{1,0:T(8,128)}, bf16[4096,2048]{1,0:T(8,128)(2,1)}, bf16[2048,256]{1,0:T(8,128)(2,1)}, bf16[2048,256]{...) custom-call(bf16[4096,1024]{1,0:T(8,128)(2,1)} %get-tuple-element.65, ...), custom_call_target="tpu_custom_call" | custom-call | bytes 450000000 | tf_op jit(solution)/shard_map/pallas_call | solution.py:908
  784.9 0.0 copy-start.1
  784.9 10.2 convolution_convert_fusion.1.grads
  795.1 1.1 copy-done
  796.2 0.6 copy-done.1
  796.8 5.5 convolution_convert_fusion.5.out_grad
  802.3 2.1 add_convert_fusion.mixed
  804.4 84.5 %shard_map.209 = (bf16[4096,768]{1,0:T(8,128)(2,1)}, bf16[4,64,2048]{2,1,0:T(8,128)(2,1)}, bf16[512,2048]{1,0:T(8,128)(2,1)}) custom-call(s32[8]{0:T(128)} %bitcast.68, bf16[4096,768]{1,0:T(8,128)(2,1)} %fusion.2.qkv, bf16[4096,256]{1,0:T(8,128)(2,1)} %convolution_convert_fusion.1.grads, bf16[256,2048]{1,0:T(8,128)(2,1)} %convolution_convert_fusion.5.out_grad, ...), custom_call_target="tpu_custom_call" | custom-call | bytes 300000000 | tf_op jit(solution)/shard_map/pallas_call | solution.py:1363
  888.9 19.2 %fusion.3 = bf16[2048,768]{1,0:T(8,128)(2,1)S(1)} fusion(bf16[4096,768]{1,0:T(8,128)(2,1)} %get-tuple-element.70.d_qkv, bf16[4096,2048]{1,0:T(8,128)(2,1)} %get-tuple-element.47, f32[2048]{0:T(1024)S(1)} %bitcast.65), kind=kOutput, calls=%fused_computation.10 | convolution fusion | flops 12911640576 | bytes 26222592 | tf_op jit(solution)/shard_map/dot_general | solution.py:20
  908.1 1.9 copy.35
  910.0 144.6 %shard_map.210 = (bf16[512,2048]{1,0:T(8,128)(2,1)}, f32[2,8,128]{2,1,0:T(8,128)}, bf16[512,768]{1,0:T(8,128)(2,1)}, bf16[512,768]{1,0:T(8,128)(2,1)}, bf16[512,...) custom-call(bf16[4096,768]{1,0:T(8,128)(2,1)} %get-tuple-element.70.d_qkv, bf16[2048,768]{1,0:T(8,128)(2,1)} %bitcast.56, ...), custom_call_target="tpu_custom_call" | custom-call | bytes 350000000 | tf_op jit(solution)/shard_map/pallas_call | solution.py:1078
  1054.6 4.2 bitcast_convert_fusion
  1058.8 0.2 reshape.101
  1059.0 1.3 fusion.11
  1060.4 0.1 copy_bitcast_fusion.1
  1060.5 0.1 convert_bitcast_fusion
  1060.7 0.2 fusion.10
  1060.9 0.3 copy.40
  1061.2 1.0 unstack.19
  1062.2 0.3 copy.41
  1062.6 1.0 unstack.21
  1063.6 0.3 copy.42
  1063.9 1.0 unstack.23
  1064.9 0.9 convert_reduce_fusion
  1065.9 0.1 reshape.102
  1066.0 0.5 fusion.8
  1066.5 5.6 convert_add_fusion
  1072.2 1.3 copy.54
  (31 shorter events, 0.2 us)
Async XLA Ops:
  7.2 218.1 %all-gather.3.cloned.1.call-start = ((), (), s32[]{:S(2)}) async-start(), calls=%async_computation.1 | async-start | bytes 2359296 | tf_op jit(solution)/shard_map/all_gather | solution.py:1426
  139.7 67.1 %collective-permute-start = (bf16[1,512,2048]{2,1,0:T(8,128)(2,1)}, bf16[1,512,2048]{2,1,0:T(8,128)(2,1)S(1)}, u32[]{:S(2)}, u32[]{:S(2)}) collective-permute-start(bf16[1,512,2048]{2,1,0:T(8,128)(2,1)} %param.14), channel_id=1, source_target_pairs={{0,0},{1,1},{2,16},{3,17},{4,8},{5,9},{6,24},{7,25},{8,4},{9,5},{1... | collective-permute-start | bytes 6291464 | tf_op jit(solution)/shard_map/ppermute | solution.py:1398
  142.0 334.2 %all-gather.5.cloned.1.call-start = ((), (), s32[]{:S(2)}) async-start(), calls=%async_computation.2 | async-start | bytes 5242880 | tf_op jit(solution)/shard_map/all_gather | solution.py:1435
  145.0 19.4 %copy-start.10 = (f32[4,4,1,128]{3,2,1,0:T(1,128)}, f32[4,4,1,128]{3,2,1,0:T(1,128)S(1)}, u32[]{:S(2)}) copy-start(f32[4,4,1,128]{3,2,1,0:T(1,128)S(1)} %get-tuple-element.94) | copy-start | bytes 24580
  206.8 188.5 %copy-start.4 = (bf16[1,512,2048]{2,1,0:T(8,128)(2,1)}, bf16[1,512,2048]{2,1,0:T(8,128)(2,1)S(1)}, u32[]{:S(2)}) copy-start(bf16[1,512,2048]{2,1,0:T(8,128)(2,1)S(1)} %collective-permute-done) | copy-start | bytes 6291460
  395.4 226.0 %reduce-scatter.2.cloned.1.call-start = ((), (), s32[]{:S(2)}) async-start(), calls=%async_computation.3 | async-start | bytes 18874368 | tf_op jit(solution)/shard_map/reduce_scatter | solution.py:1438
  523.4 2.0 copy-start.5
  527.2 90.7 %collective-permute-start.1 = (bf16[256,2048]{1,0:T(8,128)(2,1)}, bf16[256,2048]{1,0:T(8,128)(2,1)S(1)}, u32[]{:S(2)}, u32[]{:S(2)}) collective-permute-start(bf16[256,2048]{1,0:T(8,128)(2,1)} %get-tuple-element.83), channel_id=1, source_target_pairs={{0,2},{2,4},{4,6},{6,0},{1,3},{3,5},{5,7},{7,1},{8,10},{10,12},{12... | collective-permute-start | bytes 3145736 | tf_op jit(solution)/shard_map/ppermute | solution.py:1445
  527.2 90.7 %collective-permute-start.2 = (bf16[256,2048]{1,0:T(8,128)(2,1)}, bf16[256,2048]{1,0:T(8,128)(2,1)S(1)}, u32[]{:S(2)}, u32[]{:S(2)}) collective-permute-start(bf16[256,2048]{1,0:T(8,128)(2,1)} %get-tuple-element.82), channel_id=1, source_target_pairs={{0,4},{2,6},{4,0},{6,2},{1,5},{3,7},{5,1},{7,3},{8,12},{10,14},{12... | collective-permute-start | bytes 3145736 | tf_op jit(solution)/shard_map/ppermute | solution.py:1445
  527.7 90.2 %collective-permute-start.3 = (bf16[256,2048]{1,0:T(8,128)(2,1)}, bf16[256,2048]{1,0:T(8,128)(2,1)}, u32[]{:S(2)}, u32[]{:S(2)}) collective-permute-start(bf16[256,2048]{1,0:T(8,128)(2,1)} %get-tuple-element.81), channel_id=1, source_target_pairs={{0,6},{2,0},{4,2},{6,4},{1,7},{3,1},{5,3},{7,5},{8,14},{10,8},{12,... | collective-permute-start | bytes 3145736 | tf_op jit(solution)/shard_map/ppermute | solution.py:1445
  572.5 24.0 %copy-start.3 = (bf16[4096,1024]{1,0:T(8,128)(2,1)S(1)}, bf16[4096,1024]{1,0:T(8,128)(2,1)}, u32[]{:S(2)}) copy-start(bf16[4096,1024]{1,0:T(8,128)(2,1)} %get-tuple-element.66.d_up) | copy-start | bytes 25165828
  784.9 11.3 %copy-start = (bf16[4096,2048]{1,0:T(8,128)(2,1)S(1)}, bf16[4096,2048]{1,0:T(8,128)(2,1)}, u32[]{:S(2)}) copy-start(bf16[4096,2048]{1,0:T(8,128)(2,1)} %get-tuple-element.67) | copy-start | bytes 50331652
  784.9 11.9 %copy-start.1 = (bf16[4096,256]{1,0:T(8,128)(2,1)S(1)}, bf16[4096,256]{1,0:T(8,128)(2,1)}, u32[]{:S(2)}) copy-start(bf16[4096,256]{1,0:T(8,128)(2,1)} %shard_map.204.attended) | copy-start | bytes 6291460
  796.8 5.5 copy-start.2
  796.8 5.5 copy-start.7
  804.4 84.5 %copy-start.11 = (f32[4,4,1,128]{3,2,1,0:T(1,128)S(1)}, f32[4,4,1,128]{3,2,1,0:T(1,128)}, u32[]{:S(2)}) copy-start(f32[4,4,1,128]{3,2,1,0:T(1,128)} %copy-done.10) | copy-start | bytes 24580
  1054.6 4.2 copy-start.9
  1060.7 4.2 copy-start.8
  1060.9 5.0 copy-start.12
  1066.5 5.7 copy-start.6
Sparse Core Ops, SparseCore 0:
  142.1 83.1 all-gather.2
  395.5 78.1 all-gather.4
  499.9 113.2 reduce-scatter.1

commit v12 on v10

--- a/solution.py
+++ b/solution.py
@@ -815,10 +815,14 @@
 
 
 def close_mlp_kernel(
-    d_gate, d_up, w_gate, w_up, resid, upstream, gain, grad_a, grad_b, d_resid, gain_term, d_resid_whole,
+    d_gate, d_up, w_gate, w_up, resid_home, upstream_home, gain, grad_a, grad_b, d_resid, gain_term, d_resid_whole,
     far_a, near_a, cross_a, far_b, near_b, cross_b, own, blocks, *scratch
 ):
-    scatter, (send, recv, local, fetched, fold_send, fold_recv, fold_local, mine, theirs) = scratch[:7], scratch[7:]
+    scatter, (send, recv, local, fetched, fold_send, fold_recv, fold_local, mine, theirs, resid, upstream, row_sems) = scratch[:7], scratch[7:]
+    rows_fetched = [
+        pltpu.make_async_copy(source, target, row_sems.at[k])
+        for k, (source, target) in enumerate(((resid_home, resid), (upstream_home, upstream)))
+    ]
     y, c, z, x = spot()
     width = w_gate.shape[0]
     order = [
@@ -835,7 +839,7 @@
             for m, source in enumerate((d_gate, d_up))
         ]
 
-    for copy in fetch(0):
+    for copy in fetch(0) + rows_fetched:
         copy.start()
     greet(near() + fold_peers())
     folds = [
@@ -875,6 +879,9 @@
         fold_rows(gain_term, terms)
 
     def rows_of_half(half):
+        if half == 0:
+            for copy in rows_fetched:
+                copy.wait()
         over_chunks(chunk, half)
 
     gather = Gather(own_halves(own), d_resid_whole, send, recv)
@@ -897,12 +904,13 @@
             jax.ShapeDtypeStruct((8 * block, width), LOW),
             *[jax.ShapeDtypeStruct((width, hidden // 4), LOW)] * 6,
         ),
-        in_specs=[anywhere()] * 2 + [in_vmem()] * 5 + [anywhere()] * 2,
+        in_specs=[anywhere()] * 2 + [in_vmem()] * 2 + [anywhere()] * 2 + [in_vmem()] + [anywhere()] * 2,
         out_specs=[in_vmem(), in_vmem()] + [anywhere()] * 7,
         scratch_shapes=[pltpu.VMEM((block, width), LOW), pltpu.VMEM((2, 2, block // 2, hidden), LOW)]
         + scatter_scratch(width, 2)
         + [dma(GATHER_COPIES), dma(GATHER_COPIES), dma(1), dma(2, 2), dma(2, 3), dma(2, 3), dma(2, 2)]
-        + [pltpu.VMEM((2, width, hidden // 4), LOW), pltpu.VMEM((width, hidden // 4), LOW)],
+        + [pltpu.VMEM((2, width, hidden // 4), LOW), pltpu.VMEM((width, hidden // 4), LOW)]
+        + [pltpu.VMEM((block, width), jnp.float32), pltpu.VMEM((block, width), LOW), dma(2)],
         compiler_params=remote_params(3),
         cost_estimate=pl.CostEstimate(flops=0, bytes_accessed=450_000_000, transcendentals=0),
     )(d_gate, d_up, w_gate, w_up, resid, upstream, gain, *grads)
@@ -948,6 +956,34 @@
 
     fold = Fold(lambda at: grad.at[at], far, near_part, cross, mine, theirs, fold_send, fold_recv, fold_local)
     fold.start()
+    def end_fold():
+        fold.finish()
+        for source, target, k in ((grad.at[z], mine, 0), (near_part, theirs, 1)):
+            pltpu.make_async_copy(source, target, fold_local.at[k]).start()
+        for source, target, k in ((grad.at[z], mine, 0), (near_part, theirs, 1)):
+            pltpu.make_async_copy(source, target, fold_local.at[k]).wait()
+        add_rows(mine, 0, theirs, 0, mine.shape[0])
+        last = pltpu.make_async_copy(cross, theirs, fold_local.at[1])
+        last.start()
+        last.wait()
+        add_rows(mine, 0, theirs, 0, mine.shape[0])
+        shard = mine.shape[0] // 8
+        index = 4 * y + 2 * c + x
+        parts = [
+            remote(
+                mine.at[pl.ds(pl.multiple_of((4 * peer[0] + 2 * peer[1] + peer[3]) * shard, shard), shard)],
+                grad_parts.at[index],
+                part_send.at[k],
+                part_recv.at[k],
+                peer,
+            )
+            for k, peer in enumerate(layer)
+        ]
+        kept = pltpu.make_async_copy(mine.at[pl.ds(pl.multiple_of(index * shard, shard), shard)], grad_parts.at[index], fold_local.at[0])
+        for copy in parts + [kept]:
+            copy.start()
+        return parts + [kept]
+
     sums = [part_of(piece) for piece in range(PIECES)]
     sums[0].begin()
     sums[0].relay()
@@ -960,7 +996,10 @@
     trades = [remote(own.at[at], grad_low.at[at], send.at[k], recv.at[k], partner) for k, at in enumerate(pieces)]
     keeps = [pltpu.make_async_copy(own.at[at], grad_low.at[at], recv.at[k]) for k, at in enumerate(pieces)]
     fetch_x.wait()
+    to_peers = []
     for piece in range(PIECES):
+        if piece == PIECES - 1:
+            to_peers = end_fold()
         sums[piece].arrive()
 
         def step(i, carry):
@@ -984,32 +1023,6 @@
             sums[piece + 1].relay()
         if piece + 2 < PIECES:
             sums[piece + 2].begin()
-
-    fold.finish()
-    for source, target, k in ((grad.at[z], mine, 0), (near_part, theirs, 1)):
-        pltpu.make_async_copy(source, target, fold_local.at[k]).start()
-    for source, target, k in ((grad.at[z], mine, 0), (near_part, theirs, 1)):
-        pltpu.make_async_copy(source, target, fold_local.at[k]).wait()
-    add_rows(mine, 0, theirs, 0, mine.shape[0])
-    last = pltpu.make_async_copy(cross, theirs, fold_local.at[1])
-    last.start()
-    last.wait()
-    add_rows(mine, 0, theirs, 0, mine.shape[0])
-    shard = mine.shape[0] // 8
-    index = 4 * y + 2 * c + x
-    parts = [
-        remote(
-            mine.at[pl.ds(pl.multiple_of((4 * peer[0] + 2 * peer[1] + peer[3]) * shard, shard), shard)],
-            grad_parts.at[index],
-            part_send.at[k],
-            part_recv.at[k],
-            peer,
-        )
-        for k, peer in enumerate(layer)
-    ]
-    kept = pltpu.make_async_copy(mine.at[pl.ds(pl.multiple_of(index * shard, shard), shard)], grad_parts.at[index], fold_local.at[0])
-    for copy in parts + [kept]:
-        copy.start()
 
     def columns_of(row, layers):
         return pl.ds(pl.multiple_of((4 * row) * HD, HD), layers * HD)
@@ -1038,7 +1051,7 @@
         copy.wait_send()
     for part_sum in sums:
         part_sum.finish()
-    for copy in parts + [kept]:
+    for copy in to_peers:
         copy.wait()
 
     @pl.when(moves)
@@ -1423,7 +1436,7 @@
     d_gate, d_up = back_mlp(after(down_term, layer_upstream), own_down, gate, up_part)
     gate_term, up_term = contract_rows(layer_mlp, d_gate).astype(LOW), contract_rows(layer_mlp, d_up).astype(LOW)
     d_resid, gain_mlp_term, layer_d_resid, *parts = close_mlp(
-        after((mixed_sum, *down_parts), d_gate), d_up, own_gate, own_up, resid, upstream, full_gain_mlp, gate_term, up_term
+        after(mixed_sum, d_gate), d_up, own_gate, own_up, resid, upstream, full_gain_mlp, gate_term, up_term
     )
 
     def own_part(whole, near_part, cross):
@@ -1432,7 +1445,7 @@
 
     mixed = (resid + after(layer_d_resid, mixed_sum).astype(jnp.float32)).astype(LOW)
     grad_down = lax.dynamic_slice_in_dim(down_term, layer * down_rows, down_rows, 0).astype(jnp.float32)
-    grad_down = grad_down + sum(slab.astype(jnp.float32) for slab in down_parts)
+    grad_down = grad_down + sum(slab.astype(jnp.float32) for slab in after(layer_d_resid, down_parts))
 
     out_term = contract_rows(attended, layer_d_resid).astype(LOW)
     d_attended = contract_cols(layer_d_resid, w_out_own).astype(LOW)

time: 1100 us -> 1080 us (0.982)
  Pallas kernels: 865 us -> 846 us
  transfers between devices with their start and end apart: 7 -> 7, of which waited for: 1 -> 2; matrix products, arithmetic and copies ran while one was open for 10% -> 14% of each run, Pallas kernels for 14% -> 51%
where the time goes in v12:
time: 1080 us
  Pallas kernels  846 us (78%)
  matrix products  148 us (14%)
  other arithmetic  26.8 us (2%)
  local copies, waits for them, and re-layouts  24.5 us (2%)
  between operations  14.3 us (1%)
  waiting for transfers between devices  12.5 us (1%)
    pallas_call x1, Pallas kernels, close_attention(): pl.pallas_call(close_attention_kernel, out_shape=(jax.ShapeDtypeStruct((b...  167 us
    pallas_call x1, Pallas kernels, close_mlp(): pl.pallas_call(close_mlp_kernel, out_shape=(jax.ShapeDtypeStruct((block,...  160 us
    pallas_call x1, Pallas kernels, close_layer(): pl.pallas_call(close_layer_kernel, out_shape=(jax.ShapeDtypeStruct((block...  145 us
    pallas_call x1, Pallas kernels, begin(): pl.pallas_call(begin_kernel, out_shape=(jax.ShapeDtypeStruct((8 * block,...  130 us
    dot_general x5, matrix products, contract_rows(): lax.dot_general(left, right, (((0,), (0,)), ((), ())), preferred_element_...  94.7 us
    pallas_call x1, Pallas kernels, attend_back(): pl.pallas_call(attend_back_kernel, out_shape=(jax.ShapeDtypeStruct((place...  86.3 us
    pallas_call x1, Pallas kernels, open_mlp(): pl.pallas_call(open_mlp_kernel, out_shape=(jax.ShapeDtypeStruct((places,...  80.8 us
    dot_general x2, matrix products, dot_wide(): return jnp.dot(left, right, preferred_element_type=jnp.float32)  43.5 us
  transfers between devices with their start and end apart: 7, of which 2 were waited for; matrix products, arithmetic and copies ran while one was open for 14% of the time, Pallas kernels for 51%

profile of v12, /device:TPU:0, one launch (start us, length us, event | category | flops | bytes accessed | tf_op | source)
XLA Modules:
  0.0 1078.8 jit_solution(9943168953301440392)
XLA Ops:
  7.2 0.0 all-gather.3.cloned.1.call-start
  7.2 0.7 pad_convert_fusion
  7.9 0.7 bitcast_convert_fusion.1
  8.5 0.7 convert_element_type.95
  9.2 0.1 scatter.19
  9.3 0.2 scatter.20.facts
  9.5 0.6 copy-done.13
  10.1 130.4 %shard_map.203 = (bf16[4096,2048]{1,0:T(8,128)(2,1)}, bf16[4,4,128,768]{3,2,1,0:T(8,128)(2,1)}, f32[4,4,2,8,128]{4,3,2,1,0:T(8,128)}) custom-call(bf16[2,256,2048]{2,1,0:T(8,128)(2,1)} %bitcast.55, bf16[64,2048]{1,0:T(8,128)(2,1)} %w_query.1, bf16[64,2048]{1,0:T(8,128)(2,1)} %w_key.1, bf16[64,2048]{1,0:T(8,128)(2,1)} %w_value.1, f32[8,128]{1,0:T(8,128)} %copy-done.13), custom_call_target="tpu_custom_call" | custom-call | bytes 350000000 | tf_op jit(solution)/shard_map/pallas_call | solution.py:684
  140.5 2.3 collective-permute-start
  142.8 0.2 all-gather.5.cloned.1.call-start
  143.0 0.7 slice.86
  143.8 7.2 fusion
  151.0 0.7 reduce-window.9
  151.7 1.1 slice_reduce_fusion
  152.7 0.1 mul.44
  152.8 0.7 reshape_squeeze.10.gain
  153.5 20.1 %convolution_convert_fusion.1.qkv = bf16[4096,768]{1,0:T(8,128)(2,1)} fusion(bf16[2048,768]{1,0:T(8,128)(2,1)} %bitcast.52, bf16[4096,2048]{1,0:T(8,128)(2,1)} %get-tuple-element.85.x_whole, f32[2048]{0:T(1024)S(1)} %mul.44, f32[4096]{0:T(1024)S(1)} %add_rsqrt_fusion), kind=kOutput, calls=%fused_computation.6 | convolution fusion | flops 12921602048 | bytes 26238976 | tf_op jit(solution)/shard_map/dot_general | solution.py:86
  173.6 42.4 %shard_map.204.attended = bf16[4096,256]{1,0:T(8,128)(2,1)} custom-call(s32[8]{0:T(128)} %bitcast.61, bf16[4096,768]{1,0:T(8,128)(2,1)} %convolution_convert_fusion.1.qkv), custom_call_target="tpu_custom_call" | custom-call | bytes 150000000 | tf_op jit(solution)/shard_map/pallas_call | solution.py:1339
  216.0 10.2 all-gather.3.cloned.1.call-done
  226.2 1.3 constant_dynamic-slice_fusion.6
  227.5 1.0 pad_maximum_fusion.w_out
  228.5 167.4 %shard_map.205 = (f32[512,2048]{1,0:T(8,128)}, bf16[4096,2048]{1,0:T(8,128)(2,1)}, bf16[2048,1024]{1,0:T(8,128)(2,1)}, bf16[2048,1024]{1,0:T(8,128)(2,1)}) custom-call(bf16[4096,256]{1,0:T(8,128)(2,1)} %shard_map.204.attended, bf16[256,2048]{1,0:T(8,128)(2,1)} %pad_maximum_fusion.w_out, bf16[4096,2048]{1,0:T(8,128)(2,1)} %get-tuple-element.85.x_whole, ...), custom_call_target="tpu_custom_call" | custom-call | bytes 450000000 | tf_op jit(solution)/shard_map/pallas_call | solution.py:787
  396.0 0.0 reduce-scatter.2.cloned.1.call-start
  396.0 80.8 %shard_map.206 = (f32[4096,1024]{1,0:T(8,128)}, f32[4096,1024]{1,0:T(8,128)}, bf16[4096,1024]{1,0:T(8,128)(2,1)}, bf16[4096,2048]{1,0:T(8,128)(2,1)}) custom-call(bf16[4096,2048]{1,0:T(8,128)(2,1)} %get-tuple-element.90.normed, bf16[2048,1024]{1,0:T(8,128)(2,1)} %get-tuple-element.91.w_gate, bf16[2048,1024]{1,0:T(8,128)(2,1)} %get-tuple-element.92.w_up, ...), custom_call_target="tpu_custom_call" | custom-call | bytes 250000000 | tf_op jit(solution)/shard_map/pallas_call | solution.py:1182
  476.8 0.0 all-gather.5.cloned.1.call-done.w_down
  476.8 23.5 %convolution_convert_fusion = bf16[4096,2048]{1,0:T(8,128)(2,1)} fusion(bf16[4096,1024]{1,0:T(8,128)(2,1)} %get-tuple-element.96, bf16[1024,2048]{1,0:T(8,128)(2,1)} %all-gather.5.cloned.1.call-done.w_down), kind=kOutput, calls=%fused_computation.5 | convolution fusion | flops 17188257792 | bytes 29360128 | tf_op jit(solution)/shard_map/dot_general | solution.py:86
  500.3 0.7 reshape_squeeze.11.gain
  501.0 23.9 %convolution_convert_fusion.5 = bf16[1024,2048]{1,0:T(8,128)(2,1)S(1)} fusion(bf16[4096,1024]{1,0:T(8,128)(2,1)} %get-tuple-element.96, bf16[4096,2048]{1,0:T(8,128)(2,1)} %get-tuple-element.98.upstream), kind=kOutput, calls=%fused_computation.12 | convolution fusion | flops 17181966336 | bytes 29360128 | tf_op jit(solution)/shard_map/dot_general | solution.py:20
  524.9 2.0 copy-done.5
  526.9 1.7 constant_dynamic-slice_fusion.2
  528.6 0.7 collective-permute-start.2
  529.3 3.5 collective-permute-start.3
  532.8 33.5 %shard_map.207 = (bf16[4096,1024]{1,0:T(8,128)(2,1)}, bf16[4096,1024]{1,0:T(8,128)(2,1)}) custom-call(bf16[4096,2048]{1,0:T(8,128)(2,1)} %get-tuple-element.98.upstream, bf16[1024,2048]{1,0:T(8,128)(2,1)} %all-gather.5.cloned.1.call-done.w_down, f32[4096,1024]{1,0:T(8,128)} %get-tuple-element.99.gate, f32[4096,1024]{1,0:T(8,128)} %get-tuple-element.100.up), custom_call_target="tpu_custom_call" | custom-call | bytes 90000000 | tf_op jit(solution)/shard_map/pallas_call | solution.py:1324
  566.3 24.2 %convolution_convert_fusion.4.grad_a = bf16[2048,1024]{1,0:T(8,128)(2,1)} fusion(bf16[4096,2048]{1,0:T(8,128)(2,1)} %get-tuple-element.90.normed, bf16[4096,1024]{1,0:T(8,128)(2,1)} %get-tuple-element.102.d_gate), kind=kOutput, calls=%fused_computation.11 | convolution fusion | flops 17181966336 | bytes 29360128 | tf_op jit(solution)/shard_map/dot_general | solution.py:20
  590.4 21.3 %convolution_convert_fusion.3.grad_b = bf16[2048,1024]{1,0:T(8,128)(2,1)} fusion(bf16[4096,2048]{1,0:T(8,128)(2,1)} %get-tuple-element.90.normed, bf16[4096,1024]{1,0:T(8,128)(2,1)S(1)} %copy-done.3), kind=kOutput, calls=%fused_computation.10 | convolution fusion | flops 17181966336 | bytes 29360128 | tf_op jit(solution)/shard_map/dot_general | solution.py:20
  611.7 2.3 reduce-scatter.2.cloned.1.call-done
  614.0 160.0 %shard_map.208 = (f32[512,2048]{1,0:T(8,128)}, f32[8,2048]{1,0:T(8,128)}, bf16[4096,2048]{1,0:T(8,128)(2,1)}, bf16[2048,256]{1,0:T(8,128)(2,1)}, bf16[2048,256]{...) custom-call(bf16[4096,1024]{1,0:T(8,128)(2,1)} %get-tuple-element.10, ...), custom_call_target="tpu_custom_call" | custom-call | bytes 450000000 | tf_op jit(solution)/shard_map/pallas_call | solution.py:899
  774.0 10.0 convolution_convert_fusion.2.grads
  784.0 1.2 copy-done
  785.3 0.6 copy-done.1
  785.9 5.5 convolution_convert_fusion.6.out_grad
  791.4 2.1 add_convert_fusion.mixed
  793.5 86.3 %shard_map.209 = (bf16[4096,768]{1,0:T(8,128)(2,1)}, bf16[4,64,2048]{2,1,0:T(8,128)(2,1)}, bf16[512,2048]{1,0:T(8,128)(2,1)}) custom-call(s32[8]{0:T(128)} %bitcast.62, bf16[4096,768]{1,0:T(8,128)(2,1)} %convolution_convert_fusion.1.qkv, bf16[4096,256]{1,0:T(8,128)(2,1)} %convolution_convert_fusion.2.grads, ...), custom_call_target="tpu_custom_call" | custom-call | bytes 300000000 | tf_op jit(solution)/shard_map/pallas_call | solution.py:1355
  879.8 19.9 %fusion.6 = bf16[2048,768]{1,0:T(8,128)(2,1)S(1)} fusion(bf16[4096,768]{1,0:T(8,128)(2,1)} %get-tuple-element.107.d_qkv, bf16[4096,2048]{1,0:T(8,128)(2,1)} %get-tuple-element.85.x_whole, f32[2048]{0:T(1024)S(1)} %copy-done.17, f32[4096]{0:T(1024)S(1)} %copy-done.15), kind=kOutput, calls=%fused_computation.13 | convolution fusion | flops 12920029184 | bytes 26238976 | tf_op jit(solution)/shard_map/dot_general | solution.py:20
  899.7 1.9 copy.35
  901.6 144.9 %shard_map.210 = (bf16[512,2048]{1,0:T(8,128)(2,1)}, f32[2,8,128]{2,1,0:T(8,128)}, bf16[512,768]{1,0:T(8,128)(2,1)}, bf16[512,768]{1,0:T(8,128)(2,1)}, bf16[512,...) custom-call(bf16[4096,768]{1,0:T(8,128)(2,1)} %get-tuple-element.107.d_qkv, bf16[2048,768]{1,0:T(8,128)(2,1)} %bitcast.53, ...), custom_call_target="tpu_custom_call" | custom-call | bytes 350000000 | tf_op jit(solution)/shard_map/pallas_call | solution.py:1070
  1046.5 2.2 reshape.198
  1048.7 1.3 fusion.14
  1050.1 0.1 copy_bitcast_fusion.1
  1050.2 0.1 convert_bitcast_fusion
  1050.4 0.9 fusion.13
  1051.3 0.3 copy.40
  1051.7 1.0 unstack.19
  1052.7 1.4 copy.41
  1054.1 1.0 unstack.21
  1055.1 0.3 copy.42
  1055.4 1.0 unstack.23
  1056.4 2.2 convert_reduce_fusion
  1058.6 2.5 bitcast_convert_fusion
  1061.2 0.1 reshape.199
  1061.3 0.5 fusion.11
  1061.8 4.5 add_add_fusion
  1066.4 4.4 convert_add_fusion
  1070.8 1.3 copy.56
  (47 shorter events, 0.3 us)
Async XLA Ops:
  7.2 219.0 %all-gather.3.cloned.1.call-start = ((), (), s32[]{:S(2)}) async-start(), calls=%async_computation.1 | async-start | bytes 2359296 | tf_op jit(solution)/shard_map/all_gather | solution.py:1416
  9.5 0.6 copy-start.13
  140.5 75.5 %collective-permute-start = (bf16[1,512,2048]{2,1,0:T(8,128)(2,1)}, bf16[1,512,2048]{2,1,0:T(8,128)(2,1)S(1)}, u32[]{:S(2)}, u32[]{:S(2)}) collective-permute-start(bf16[1,512,2048]{2,1,0:T(8,128)(2,1)} %param.20), channel_id=1, source_target_pairs={{0,0},{1,1},{2,16},{3,17},{4,8},{5,9},{6,24},{7,25},{8,4},{9,5},{1... | collective-permute-start | bytes 6291464 | tf_op jit(solution)/shard_map/ppermute | solution.py:1390
  142.8 334.0 %all-gather.5.cloned.1.call-start = ((), (), s32[]{:S(2)}) async-start(), calls=%async_computation.2 | async-start | bytes 5242880 | tf_op jit(solution)/shard_map/all_gather | solution.py:1425
  152.8 20.8 %copy-start.16 = (f32[2048]{0:T(1024)}, f32[2048]{0:T(1024)S(1)}, u32[]{:S(2)}) copy-start(f32[2048]{0:T(1024)S(1)} %mul.44) | copy-start | bytes 24580
  153.5 20.1 %copy-start.14 = (f32[4096]{0:T(1024)}, f32[4096]{0:T(1024)S(1)}, u32[]{:S(2)}) copy-start(f32[4096]{0:T(1024)S(1)} %add_rsqrt_fusion) | copy-start | bytes 49156
  216.0 179.9 %copy-start.4 = (bf16[1,512,2048]{2,1,0:T(8,128)(2,1)}, bf16[1,512,2048]{2,1,0:T(8,128)(2,1)S(1)}, u32[]{:S(2)}) copy-start(bf16[1,512,2048]{2,1,0:T(8,128)(2,1)S(1)} %collective-permute-done) | copy-start | bytes 6291460
  396.0 218.0 %reduce-scatter.2.cloned.1.call-start = ((), (), s32[]{:S(2)}) async-start(), calls=%async_computation.3 | async-start | bytes 18874368 | tf_op jit(solution)/shard_map/reduce_scatter | solution.py:1428
  524.9 2.0 copy-start.5
  528.6 532.6 %collective-permute-start.1 = (bf16[256,2048]{1,0:T(8,128)(2,1)}, bf16[256,2048]{1,0:T(8,128)(2,1)}, u32[]{:S(2)}, u32[]{:S(2)}) collective-permute-start(bf16[256,2048]{1,0:T(8,128)(2,1)} %get-tuple-element.125), channel_id=1, source_target_pairs={{0,2},{2,4},{4,6},{6,0},{1,3},{3,5},{5,7},{7,1},{8,10},{10,12},{12... | collective-permute-start | bytes 3145736 | tf_op jit(solution)/shard_map/ppermute | solution.py:1435
  528.6 532.6 %collective-permute-start.2 = (bf16[256,2048]{1,0:T(8,128)(2,1)}, bf16[256,2048]{1,0:T(8,128)(2,1)}, u32[]{:S(2)}, u32[]{:S(2)}) collective-permute-start(bf16[256,2048]{1,0:T(8,128)(2,1)} %get-tuple-element.124), channel_id=1, source_target_pairs={{0,4},{2,6},{4,0},{6,2},{1,5},{3,7},{5,1},{7,3},{8,12},{10,14},{12... | collective-permute-start | bytes 3145736 | tf_op jit(solution)/shard_map/ppermute | solution.py:1435
  529.3 531.9 %collective-permute-start.3 = (bf16[256,2048]{1,0:T(8,128)(2,1)}, bf16[256,2048]{1,0:T(8,128)(2,1)}, u32[]{:S(2)}, u32[]{:S(2)}) collective-permute-start(bf16[256,2048]{1,0:T(8,128)(2,1)} %get-tuple-element.123), channel_id=1, source_target_pairs={{0,6},{2,0},{4,2},{6,4},{1,7},{3,1},{5,3},{7,5},{8,14},{10,8},{12,... | collective-permute-start | bytes 3145736 | tf_op jit(solution)/shard_map/ppermute | solution.py:1435
  566.3 24.2 %copy-start.3 = (bf16[4096,1024]{1,0:T(8,128)(2,1)S(1)}, bf16[4096,1024]{1,0:T(8,128)(2,1)}, u32[]{:S(2)}) copy-start(bf16[4096,1024]{1,0:T(8,128)(2,1)} %get-tuple-element.103.d_up) | copy-start | bytes 25165828
  774.0 11.3 %copy-start = (bf16[4096,2048]{1,0:T(8,128)(2,1)S(1)}, bf16[4096,2048]{1,0:T(8,128)(2,1)}, u32[]{:S(2)}) copy-start(bf16[4096,2048]{1,0:T(8,128)(2,1)} %get-tuple-element.104) | copy-start | bytes 50331652
  774.0 11.9 %copy-start.1 = (bf16[4096,256]{1,0:T(8,128)(2,1)S(1)}, bf16[4096,256]{1,0:T(8,128)(2,1)}, u32[]{:S(2)}) copy-start(bf16[4096,256]{1,0:T(8,128)(2,1)} %shard_map.204.attended) | copy-start | bytes 6291460
  785.9 5.5 copy-start.2
  785.9 5.5 copy-start.8
  793.4 86.3 %copy-start.15 = (f32[4096]{0:T(1024)S(1)}, f32[4096]{0:T(1024)}, u32[]{:S(2)}) copy-start(f32[4096]{0:T(1024)} %copy-done.14) | copy-start | bytes 49156
  793.5 86.3 %copy-start.17 = (f32[2048]{0:T(1024)S(1)}, f32[2048]{0:T(1024)}, u32[]{:S(2)}) copy-start(f32[2048]{0:T(1024)} %copy-done.16) | copy-start | bytes 24580
  1051.3 7.3 copy-start.6
  1056.4 4.8 copy-start.18
  1061.2 5.2 copy-start.9
  1061.2 5.2 copy-start.10
  1061.2 5.2 copy-start.11
  1061.3 5.0 copy-start.12
  1066.4 4.4 copy-start.7
Sparse Core Ops, SparseCore 0:
  142.9 83.2 all-gather.2
  396.1 78.5 all-gather.4
  500.4 113.5 reduce-scatter.1

commit v13 on v12

--- a/solution.py
+++ b/solution.py
@@ -1380,14 +1380,31 @@
 ALL = ("y", "c", "z", "x")
 
 
-def trade(part):
+def trade_start(part, beside):
+    y, c, z = (lax.axis_index(name) for name in ("y", "c", "z"))
     pairs = []
-    for y in range(2):
-        for c in range(2):
-            for z in range(4):
-                for x in range(2):
-                    pairs.append((((y * 2 + c) * 4 + z) * 2 + x, (((z % 2) * 2 + z // 2) * 4 + 2 * c + y) * 2 + x))
-    return lax.ppermute(part, ALL, pairs)
+    for at in range(2):
+        for x in range(2):
+            owner = ((at * 2 + at) * 4 + 1 + at) * 2 + x
+            across = (((1 - at) * 2 + at) * 4 + 1 + at) * 2 + x
+            pairs.append((owner, across))
+    passes = (1 - y == c) & (z == 2 - y)
+    return jnp.where(passes, after(beside, lax.ppermute(part, ALL, pairs)), part)
+
+
+def trade_end(started, part):
+    y, c, z = (lax.axis_index(name) for name in ("y", "c", "z"))
+    pairs = []
+    for y_ in range(2):
+        for c_ in range(2):
+            for z_ in range(4):
+                for x_ in range(2):
+                    if z_ == 2 * c_ + y_:
+                        continue
+                    from_y = 1 - y_ if y_ == c_ and z_ == 1 + y_ else y_
+                    owner = ((from_y * 2 + c_) * 4 + z_) * 2 + x_
+                    pairs.append((owner, (((z_ % 2) * 2 + z_ // 2) * 4 + 2 * c_ + y_) * 2 + x_))
+    return jnp.where(z == 2 * c + y, part, lax.ppermute(started, ALL, pairs))
 
 
 def after(first, then):
@@ -1412,14 +1429,16 @@
     own_lengths = lax.dynamic_slice(own_lengths, (layer % 2, layer // 2, 0), (1, 1, own_lengths.shape[2]))[0, 0]
     ends = jnp.cumsum(own_lengths.astype(jnp.int32))
     layer_normed = norm_forward(layer_x.astype(jnp.float32), full_gain_attn)[0].astype(LOW)
+    out_rows = lax.all_gather(after(facts, w_out), ("z", "x"), axis=0, tiled=True)
+    qkv = dot_wide(layer_normed, w_qkv).astype(LOW)
+    ready = after(facts, cotangent)
+    started = trade_start(ready, qkv)
+    attended = attend(ends, after(started, qkv))
     here = lax.axis_index("x")
-    out_rows = lax.all_gather(after(facts, w_out), ("z", "x"), axis=0, tiled=True)
+    out_rows = after(attended, out_rows)
     w_out_own = [lax.dynamic_slice_in_dim(out_rows, head * HD, HD, 0) for head in (here, 3 - here)]
     w_out_own = jnp.concatenate(w_out_own, axis=0)
-
-    qkv = dot_wide(layer_normed, w_qkv).astype(LOW)
-    upstream = trade(after(facts, cotangent)).reshape(block, width)
-    attended = attend(ends, qkv)
+    upstream = trade_end(started, ready).reshape(block, width)
     resid, layer_mlp, own_gate, own_up = close_attention(after(upstream, attended), w_out_own, layer_x, full_gain_mlp, w_gate, w_up)
 
     own_down = lax.all_gather(after(resid, w_down), "z", axis=0, tiled=True)

time: 1080 us -> 1100 us (1.019)
  Pallas kernels: 846 us -> 859 us
    pallas_call x1, Pallas kernels: 167 us -> 181 us  [close_attention(): pl.pallas_call(close_attention_kernel, out_shape=(jax.ShapeDtypeStruct((b...]
  transfers between devices with their start and end apart: 7 -> 8, of which waited for: 2 -> 2; matrix products, arithmetic and copies ran while one was open for 14% -> 15% of each run, Pallas kernels for 51% -> 50%
where the time goes in v13:
time: 1100 us; the launch traced here: 1090 us
  Pallas kernels  859 us (78%)
  matrix products  147 us (13%)
  other arithmetic  30.1 us (3%)
  local copies, waits for them, and re-layouts  24.6 us (2%)
  between operations  14.4 us (1%)
    pallas_call x1, Pallas kernels, close_attention(): pl.pallas_call(close_attention_kernel, out_shape=(jax.ShapeDtypeStruct((b...  181 us
    pallas_call x1, Pallas kernels, close_mlp(): pl.pallas_call(close_mlp_kernel, out_shape=(jax.ShapeDtypeStruct((block,...  160 us
    pallas_call x1, Pallas kernels, close_layer(): pl.pallas_call(close_layer_kernel, out_shape=(jax.ShapeDtypeStruct((block...  145 us
    pallas_call x1, Pallas kernels, begin(): pl.pallas_call(begin_kernel, out_shape=(jax.ShapeDtypeStruct((8 * block,...  130 us
    dot_general x5, matrix products, contract_rows(): lax.dot_general(left, right, (((0,), (0,)), ((), ())), preferred_element_...  93.8 us
    pallas_call x1, Pallas kernels, attend_back(): pl.pallas_call(attend_back_kernel, out_shape=(jax.ShapeDtypeStruct((place...  86.3 us
    pallas_call x1, Pallas kernels, open_mlp(): pl.pallas_call(open_mlp_kernel, out_shape=(jax.ShapeDtypeStruct((places,...  80.1 us
    dot_general x2, matrix products, dot_wide(): return jnp.dot(left, right, preferred_element_type=jnp.float32)  42.5 us
  transfers between devices with their start and end apart: 8, of which 2 were waited for; matrix products, arithmetic and copies ran while one was open for 15% of the time, Pallas kernels for 50%

profile of v13, /device:TPU:0, one launch (start us, length us, event | category | flops | bytes accessed | tf_op | source)
XLA Modules:
  0.0 1089.6 jit_solution(17451525193200119785)
XLA Ops:
  7.2 0.7 pad_convert_fusion
  7.9 0.7 bitcast_convert_fusion.1
  8.5 0.7 convert_element_type.95
  9.2 0.1 scatter.19
  9.3 0.2 scatter.20.facts
  9.5 0.6 copy-done.14
  10.1 130.4 %shard_map.203 = (bf16[4096,2048]{1,0:T(8,128)(2,1)}, bf16[4,4,128,768]{3,2,1,0:T(8,128)(2,1)}, f32[4,4,2,8,128]{4,3,2,1,0:T(8,128)}) custom-call(bf16[2,256,2048]{2,1,0:T(8,128)(2,1)} %bitcast.54, bf16[64,2048]{1,0:T(8,128)(2,1)} %w_query.1, bf16[64,2048]{1,0:T(8,128)(2,1)} %w_key.1, bf16[64,2048]{1,0:T(8,128)(2,1)} %w_value.1, f32[8,128]{1,0:T(8,128)} %copy-done.14), custom_call_target="tpu_custom_call" | custom-call | bytes 350000000 | tf_op jit(solution)/shard_map/pallas_call | solution.py:684
  140.5 2.0 collective-permute-start
  142.6 1.1 slice_reduce_fusion
  143.7 0.1 mul.47
  143.8 7.4 fusion
  151.3 19.1 %convolution_convert_fusion.1.qkv = bf16[4096,768]{1,0:T(8,128)(2,1)} fusion(bf16[2048,768]{1,0:T(8,128)(2,1)S(1)} %bitcast.52, bf16[4096,2048]{1,0:T(8,128)(2,1)} %get-tuple-element.88.x_whole, f32[2048]{0:T(1024)S(1)} %mul.47, f32[4096]{0:T(1024)S(1)} %add_rsqrt_fusion), kind=kOutput, calls=%fused_computation.6 | convolution fusion | flops 12921602048 | bytes 26238976 | tf_op jit(solution)/shard_map/dot_general | solution.py:86
  170.4 1.5 broadcast_select_fusion
  171.9 2.4 collective-permute-start.1
  174.4 0.7 slice.86
  175.1 0.7 reduce-window.9
  175.8 0.7 reshape_squeeze.10.gain
  176.5 42.4 %shard_map.204.attended = bf16[4096,256]{1,0:T(8,128)(2,1)} custom-call(s32[8]{0:T(128)} %bitcast.60, bf16[4096,768]{1,0:T(8,128)(2,1)} %convolution_convert_fusion.1.qkv), custom_call_target="tpu_custom_call" | custom-call | bytes 150000000 | tf_op jit(solution)/shard_map/pallas_call | solution.py:1339
  218.9 1.3 constant_dynamic-slice_fusion.6
  220.1 1.0 pad_maximum_fusion.w_out
  221.2 1.5 select_bitcast_fusion.upstream.upstream_home
  222.7 181.4 %shard_map.205 = (f32[512,2048]{1,0:T(8,128)}, bf16[4096,2048]{1,0:T(8,128)(2,1)}, bf16[2048,1024]{1,0:T(8,128)(2,1)}, bf16[2048,1024]{1,0:T(8,128)(2,1)}) custom-call(bf16[4096,256]{1,0:T(8,128)(2,1)} %shard_map.204.attended, bf16[256,2048]{1,0:T(8,128)(2,1)} %pad_maximum_fusion.w_out, bf16[4096,2048]{1,0:T(8,128)(2,1)} %get-tuple-element.88.x_whole, ...), custom_call_target="tpu_custom_call" | custom-call | bytes 450000000 | tf_op jit(solution)/shard_map/pallas_call | solution.py:787
  404.2 0.0 reduce-scatter.2.cloned.1.call-start
  404.2 80.1 %shard_map.206 = (f32[4096,1024]{1,0:T(8,128)}, f32[4096,1024]{1,0:T(8,128)}, bf16[4096,1024]{1,0:T(8,128)(2,1)}, bf16[4096,2048]{1,0:T(8,128)(2,1)}) custom-call(bf16[4096,2048]{1,0:T(8,128)(2,1)} %get-tuple-element.96.normed, bf16[2048,1024]{1,0:T(8,128)(2,1)} %get-tuple-element.97.w_gate, bf16[2048,1024]{1,0:T(8,128)(2,1)} %get-tuple-element.98.w_up, ...), custom_call_target="tpu_custom_call" | custom-call | bytes 250000000 | tf_op jit(solution)/shard_map/pallas_call | solution.py:1182
  484.4 1.2 all-gather.5.cloned.1.call-done.w_down
  485.6 23.4 %convolution_convert_fusion = bf16[4096,2048]{1,0:T(8,128)(2,1)} fusion(bf16[4096,1024]{1,0:T(8,128)(2,1)} %get-tuple-element.102, bf16[1024,2048]{1,0:T(8,128)(2,1)} %all-gather.5.cloned.1.call-done.w_down), kind=kOutput, calls=%fused_computation.5 | convolution fusion | flops 17188257792 | bytes 29360128 | tf_op jit(solution)/shard_map/dot_general | solution.py:86
  509.1 0.7 reshape_squeeze.11.gain
  509.8 22.9 %convolution_convert_fusion.5 = bf16[1024,2048]{1,0:T(8,128)(2,1)S(1)} fusion(bf16[4096,1024]{1,0:T(8,128)(2,1)} %get-tuple-element.102, bf16[4096,2048]{1,0:T(8,128)(2,1)} %get-tuple-element.104.upstream), kind=kOutput, calls=%fused_computation.12 | convolution fusion | flops 17181966336 | bytes 29360128 | tf_op jit(solution)/shard_map/dot_general | solution.py:20
  532.7 2.2 copy-done.5
  534.9 1.7 constant_dynamic-slice_fusion.2
  536.7 3.2 collective-permute-start.2
  539.8 3.0 collective-permute-start.4
  542.8 33.5 %shard_map.207 = (bf16[4096,1024]{1,0:T(8,128)(2,1)}, bf16[4096,1024]{1,0:T(8,128)(2,1)}) custom-call(bf16[4096,2048]{1,0:T(8,128)(2,1)} %get-tuple-element.104.upstream, bf16[1024,2048]{1,0:T(8,128)(2,1)} %all-gather.5.cloned.1.call-done.w_down, f32[4096,1024]{1,0:T(8,128)} %get-tuple-element.105.gate, f32[4096,1024]{1,0:T(8,128)} %get-tuple-element.106.up), custom_call_target="tpu_custom_call" | custom-call | bytes 90000000 | tf_op jit(solution)/shard_map/pallas_call | solution.py:1324
  576.3 24.3 %convolution_convert_fusion.4.grad_a = bf16[2048,1024]{1,0:T(8,128)(2,1)} fusion(bf16[4096,2048]{1,0:T(8,128)(2,1)} %get-tuple-element.96.normed, bf16[4096,1024]{1,0:T(8,128)(2,1)} %get-tuple-element.108.d_gate), kind=kOutput, calls=%fused_computation.11 | convolution fusion | flops 17181966336 | bytes 29360128 | tf_op jit(solution)/shard_map/dot_general | solution.py:20
  600.6 21.3 %convolution_convert_fusion.3.grad_b = bf16[2048,1024]{1,0:T(8,128)(2,1)} fusion(bf16[4096,2048]{1,0:T(8,128)(2,1)} %get-tuple-element.96.normed, bf16[4096,1024]{1,0:T(8,128)(2,1)S(1)} %copy-done.4), kind=kOutput, calls=%fused_computation.10 | convolution fusion | flops 17181966336 | bytes 29360128 | tf_op jit(solution)/shard_map/dot_general | solution.py:20
  621.9 3.0 reduce-scatter.2.cloned.1.call-done
  624.9 160.0 %shard_map.208 = (f32[512,2048]{1,0:T(8,128)}, f32[8,2048]{1,0:T(8,128)}, bf16[4096,2048]{1,0:T(8,128)(2,1)}, bf16[2048,256]{1,0:T(8,128)(2,1)}, bf16[2048,256]{...) custom-call(bf16[4096,1024]{1,0:T(8,128)(2,1)} %get-tuple-element.10, ...), custom_call_target="tpu_custom_call" | custom-call | bytes 450000000 | tf_op jit(solution)/shard_map/pallas_call | solution.py:899
  785.0 10.2 convolution_convert_fusion.2.grads
  795.2 1.1 copy-done
  796.3 0.6 copy-done.1
  796.9 5.5 convolution_convert_fusion.6.out_grad
  802.3 2.1 add_convert_fusion.mixed
  804.4 86.3 %shard_map.209 = (bf16[4096,768]{1,0:T(8,128)(2,1)}, bf16[4,64,2048]{2,1,0:T(8,128)(2,1)}, bf16[512,2048]{1,0:T(8,128)(2,1)}) custom-call(s32[8]{0:T(128)} %bitcast.61, bf16[4096,768]{1,0:T(8,128)(2,1)} %convolution_convert_fusion.1.qkv, bf16[4096,256]{1,0:T(8,128)(2,1)} %convolution_convert_fusion.2.grads, ...), custom_call_target="tpu_custom_call" | custom-call | bytes 300000000 | tf_op jit(solution)/shard_map/pallas_call | solution.py:1355
  890.7 19.8 %fusion.6 = bf16[2048,768]{1,0:T(8,128)(2,1)S(1)} fusion(bf16[4096,768]{1,0:T(8,128)(2,1)} %get-tuple-element.113.d_qkv, bf16[4096,2048]{1,0:T(8,128)(2,1)} %get-tuple-element.88.x_whole, f32[2048]{0:T(1024)S(1)} %copy-done.18, f32[4096]{0:T(1024)S(1)} %copy-done.16), kind=kOutput, calls=%fused_computation.13 | convolution fusion | flops 12920029184 | bytes 26238976 | tf_op jit(solution)/shard_map/dot_general | solution.py:20
  910.6 1.9 copy.35
  912.5 144.6 %shard_map.210 = (bf16[512,2048]{1,0:T(8,128)(2,1)}, f32[2,8,128]{2,1,0:T(8,128)}, bf16[512,768]{1,0:T(8,128)(2,1)}, bf16[512,768]{1,0:T(8,128)(2,1)}, bf16[512,...) custom-call(bf16[4096,768]{1,0:T(8,128)(2,1)} %get-tuple-element.113.d_qkv, bf16[2048,768]{1,0:T(8,128)(2,1)} %bitcast.51, ...), custom_call_target="tpu_custom_call" | custom-call | bytes 350000000 | tf_op jit(solution)/shard_map/pallas_call | solution.py:1070
  1057.1 2.3 reshape.198
  1059.4 1.3 fusion.14
  1060.8 0.1 copy_bitcast_fusion.1
  1060.9 0.1 convert_bitcast_fusion
  1061.0 0.9 fusion.13
  1062.0 0.3 copy.40
  1062.3 1.0 unstack.19
  1063.3 1.4 copy.41
  1064.7 1.0 unstack.21
  1065.7 0.3 copy.42
  1066.1 1.0 unstack.23
  1067.1 2.2 convert_reduce_fusion
  1069.3 2.5 bitcast_convert_fusion
  1071.9 0.1 reshape.199
  1072.0 0.5 fusion.11
  1072.5 4.5 add_add_fusion
  1077.0 4.4 convert_add_fusion
  1081.4 1.3 copy.56
  (53 shorter events, 0.3 us)
Async XLA Ops:
  7.2 211.7 %all-gather.3.cloned.1.call-start = ((), (), s32[]{:S(2)}) async-start(), calls=%async_computation.1 | async-start | bytes 2359296 | tf_op jit(solution)/shard_map/all_gather | solution.py:1432
  9.5 0.6 copy-start.14
  140.5 29.8 %collective-permute-start = (bf16[1,512,2048]{2,1,0:T(8,128)(2,1)}, bf16[1,512,2048]{2,1,0:T(8,128)(2,1)}, u32[]{:S(2)}, u32[]{:S(2)}) collective-permute-start(bf16[1,512,2048]{2,1,0:T(8,128)(2,1)} %param.20), channel_id=1, source_target_pairs={{2,18},{3,19},{28,12},{29,13}} | collective-permute-start | bytes 6291464 | tf_op jit(solution)/shard_map/ppermute | solution.py:1392
  142.6 343.0 %all-gather.5.cloned.1.call-start = ((), (), s32[]{:S(2)}) async-start(), calls=%async_computation.2 | async-start | bytes 5242880 | tf_op jit(solution)/shard_map/all_gather | solution.py:1444
  143.8 7.5 copy-start.17
  143.8 7.5 copy-start.6
  151.3 19.1 %copy-start.15 = (f32[4096]{0:T(1024)}, f32[4096]{0:T(1024)S(1)}, u32[]{:S(2)}) copy-start(f32[4096]{0:T(1024)S(1)} %add_rsqrt_fusion) | copy-start | bytes 49156
  151.3 19.1 %copy-start.3 = (bf16[1,512,2048]{2,1,0:T(8,128)(2,1)S(1)}, bf16[1,512,2048]{2,1,0:T(8,128)(2,1)}, u32[]{:S(2)}) copy-start(bf16[1,512,2048]{2,1,0:T(8,128)(2,1)} %param.20) | copy-start | bytes 6291460
  171.9 49.2 %collective-permute-start.1 = (bf16[1,512,2048]{2,1,0:T(8,128)(2,1)}, bf16[1,512,2048]{2,1,0:T(8,128)(2,1)}, u32[]{:S(2)}, u32[]{:S(2)}) collective-permute-start(bf16[1,512,2048]{2,1,0:T(8,128)(2,1)} %broadcast_select_fusion), channel_id=1, source_target_pairs={{18,16},{19,17},{4,8},{5,9},{6,24},{7,25},{8,4},{9,5},{10,20},{11,... | collective-permute-start | bytes 6291464 | tf_op jit(solution)/shard_map/ppermute | solution.py:1407
  404.2 220.7 %reduce-scatter.2.cloned.1.call-start = ((), (), s32[]{:S(2)}) async-start(), calls=%async_computation.3 | async-start | bytes 18874368 | tf_op jit(solution)/shard_map/reduce_scatter | solution.py:1447
  532.7 2.2 copy-start.5
  536.7 535.2 %collective-permute-start.2 = (bf16[256,2048]{1,0:T(8,128)(2,1)}, bf16[256,2048]{1,0:T(8,128)(2,1)}, u32[]{:S(2)}, u32[]{:S(2)}) collective-permute-start(bf16[256,2048]{1,0:T(8,128)(2,1)} %get-tuple-element.131), channel_id=1, source_target_pairs={{0,2},{2,4},{4,6},{6,0},{1,3},{3,5},{5,7},{7,1},{8,10},{10,12},{12... | collective-permute-start | bytes 3145736 | tf_op jit(solution)/shard_map/ppermute | solution.py:1454
  539.8 532.0 %collective-permute-start.3 = (bf16[256,2048]{1,0:T(8,128)(2,1)}, bf16[256,2048]{1,0:T(8,128)(2,1)}, u32[]{:S(2)}, u32[]{:S(2)}) collective-permute-start(bf16[256,2048]{1,0:T(8,128)(2,1)} %get-tuple-element.130), channel_id=1, source_target_pairs={{0,4},{2,6},{4,0},{6,2},{1,5},{3,7},{5,1},{7,3},{8,12},{10,14},{12... | collective-permute-start | bytes 3145736 | tf_op jit(solution)/shard_map/ppermute | solution.py:1454
  539.8 532.0 %collective-permute-start.4 = (bf16[256,2048]{1,0:T(8,128)(2,1)}, bf16[256,2048]{1,0:T(8,128)(2,1)}, u32[]{:S(2)}, u32[]{:S(2)}) collective-permute-start(bf16[256,2048]{1,0:T(8,128)(2,1)} %get-tuple-element.129), channel_id=1, source_target_pairs={{0,6},{2,0},{4,2},{6,4},{1,7},{3,1},{5,3},{7,5},{8,14},{10,8},{12,... | collective-permute-start | bytes 3145736 | tf_op jit(solution)/shard_map/ppermute | solution.py:1454
  576.3 24.3 %copy-start.4 = (bf16[4096,1024]{1,0:T(8,128)(2,1)S(1)}, bf16[4096,1024]{1,0:T(8,128)(2,1)}, u32[]{:S(2)}) copy-start(bf16[4096,1024]{1,0:T(8,128)(2,1)} %get-tuple-element.109.d_up) | copy-start | bytes 25165828
  785.0 11.3 %copy-start = (bf16[4096,2048]{1,0:T(8,128)(2,1)S(1)}, bf16[4096,2048]{1,0:T(8,128)(2,1)}, u32[]{:S(2)}) copy-start(bf16[4096,2048]{1,0:T(8,128)(2,1)} %get-tuple-element.110) | copy-start | bytes 50331652
  785.0 11.9 %copy-start.1 = (bf16[4096,256]{1,0:T(8,128)(2,1)S(1)}, bf16[4096,256]{1,0:T(8,128)(2,1)}, u32[]{:S(2)}) copy-start(bf16[4096,256]{1,0:T(8,128)(2,1)} %shard_map.204.attended) | copy-start | bytes 6291460
  796.9 5.5 copy-start.2
  796.9 5.5 copy-start.9
  804.4 86.3 %copy-start.16 = (f32[4096]{0:T(1024)S(1)}, f32[4096]{0:T(1024)}, u32[]{:S(2)}) copy-start(f32[4096]{0:T(1024)} %copy-done.15) | copy-start | bytes 49156
  804.4 86.3 %copy-start.18 = (f32[2048]{0:T(1024)S(1)}, f32[2048]{0:T(1024)}, u32[]{:S(2)}) copy-start(f32[2048]{0:T(1024)} %copy-done.17) | copy-start | bytes 24580
  1062.0 7.3 copy-start.7
  1067.1 4.8 copy-start.19
  1071.8 5.2 copy-start.10
  1071.8 5.2 copy-start.11
  1071.8 5.2 copy-start.12
  1072.0 5.0 copy-start.13
  1077.0 4.4 copy-start.8
Sparse Core Ops, SparseCore 0:
  142.7 60.0 all-gather.2
  404.3 81.2 all-gather.4
  509.2 115.6 reduce-scatter.1

commit v14 on v12

--- a/solution.py
+++ b/solution.py
@@ -917,10 +917,12 @@
 
 
 def close_layer_kernel(
-    d_qkv, w_qkv, x_whole, d_resid, gain, mlp_term, grad, grad_low, gain_grads, far, near_part, cross, grad_parts, own, terms, layer_terms, part, column_terms, *scratch
+    d_qkv, w_qkv, x_whole, d_resid_home, gain, mlp_term, grad, grad_low, gain_grads, far, near_part, cross, grad_parts, own, terms, layer_terms, part, column_terms, *scratch
 ):
     scatter, (send, recv, term_send, term_recv, line_send, line_recv, x_own, x_sem, *rest) = scratch[:7], scratch[7:]
-    mine, theirs, fold_send, fold_recv, fold_local, part_send, part_recv = rest
+    mine, theirs, fold_send, fold_recv, fold_local, part_send, part_recv, d_resid = rest
+    fetch_d_resid = pltpu.make_async_copy(d_resid_home, d_resid, x_sem.at[1])
+    fetch_d_resid.start()
     y, c, z, x = spot()
     fetch_x = pltpu.make_async_copy(x_whole.at[place_of(y, c, x)], x_own, x_sem.at[0])
     fetch_x.start()
@@ -996,6 +998,7 @@
     trades = [remote(own.at[at], grad_low.at[at], send.at[k], recv.at[k], partner) for k, at in enumerate(pieces)]
     keeps = [pltpu.make_async_copy(own.at[at], grad_low.at[at], recv.at[k]) for k, at in enumerate(pieces)]
     fetch_x.wait()
+    fetch_d_resid.wait()
     to_peers = []
     for piece in range(PIECES):
         if piece == PIECES - 1:
@@ -1075,7 +1078,7 @@
             *[jax.ShapeDtypeStruct(grad.shape[1:], LOW)] * 3,
             jax.ShapeDtypeStruct((8, grad.shape[1] // 8, grad.shape[2]), LOW),
         ),
-        in_specs=[in_vmem(), in_vmem(), anywhere()] + [in_vmem()] * 3 + [anywhere()],
+        in_specs=[in_vmem(), in_vmem(), anywhere(), anywhere(), in_vmem(), in_vmem(), anywhere()],
         out_specs=[anywhere(), in_vmem()] + [anywhere()] * 4,
         scratch_shapes=[
             pltpu.VMEM((block, width), LOW),
@@ -1085,9 +1088,9 @@
             pltpu.VMEM((3, 2, 8, width // 16), jnp.float32),
         ]
         + scatter_scratch(width, PIECES)
-        + [dma(PIECES), dma(PIECES), dma(7), dma(7), dma(3), dma(3), pltpu.VMEM((block, width), LOW), dma(1)]
+        + [dma(PIECES), dma(PIECES), dma(7), dma(7), dma(3), dma(3), pltpu.VMEM((block, width), LOW), dma(2)]
         + [pltpu.VMEM(grad.shape[1:], LOW)] * 2
-        + [dma(3), dma(3), dma(2), dma(7), dma(7)],
+        + [dma(3), dma(3), dma(2), dma(7), dma(7), pltpu.VMEM((block, width), jnp.float32)],
         compiler_params=remote_params(4),
         cost_estimate=pl.CostEstimate(flops=0, bytes_accessed=350_000_000, transcendentals=0),
     )(d_qkv, w_qkv, x_whole, d_resid, gain, mlp_term, grad)
@@ -1436,7 +1439,7 @@
     d_gate, d_up = back_mlp(after(down_term, layer_upstream), own_down, gate, up_part)
     gate_term, up_term = contract_rows(layer_mlp, d_gate).astype(LOW), contract_rows(layer_mlp, d_up).astype(LOW)
     d_resid, gain_mlp_term, layer_d_resid, *parts = close_mlp(
-        after(mixed_sum, d_gate), d_up, own_gate, own_up, resid, upstream, full_gain_mlp, gate_term, up_term
+        d_gate, d_up, own_gate, own_up, resid, upstream, full_gain_mlp, gate_term, up_term
     )
 
     def own_part(whole, near_part, cross):

time: 1080 us -> 1080 us (level)
  transfers between devices with their start and end apart: 7 -> 7, of which waited for: 2 -> 1; matrix products, arithmetic and copies ran while one was open for 14% -> 12% of each run, Pallas kernels for 51% -> 29%
where the time goes in v14:
time: 1080 us
  Pallas kernels  843 us (78%)
  matrix products  148 us (14%)
  other arithmetic  30.5 us (3%)
  local copies, waits for them, and re-layouts  23.8 us (2%)
  between operations  14.5 us (1%)
    pallas_call x1, Pallas kernels, close_attention(): pl.pallas_call(close_attention_kernel, out_shape=(jax.ShapeDtypeStruct((b...  167 us
    pallas_call x1, Pallas kernels, close_mlp(): pl.pallas_call(close_mlp_kernel, out_shape=(jax.ShapeDtypeStruct((block,...  160 us
    pallas_call x1, Pallas kernels, close_layer(): pl.pallas_call(close_layer_kernel, out_shape=(jax.ShapeDtypeStruct((block...  144 us
    pallas_call x1, Pallas kernels, begin(): pl.pallas_call(begin_kernel, out_shape=(jax.ShapeDtypeStruct((8 * block,...  130 us
    dot_general x5, matrix products, contract_rows(): lax.dot_general(left, right, (((0,), (0,)), ((), ())), preferred_element_...  99 us
    pallas_call x1, Pallas kernels, attend_back(): pl.pallas_call(attend_back_kernel, out_shape=(jax.ShapeDtypeStruct((place...  85.1 us
    pallas_call x1, Pallas kernels, open_mlp(): pl.pallas_call(open_mlp_kernel, out_shape=(jax.ShapeDtypeStruct((places,...  80.7 us
    dot_general x2, matrix products, dot_wide(): return jnp.dot(left, right, preferred_element_type=jnp.float32)  43.2 us
  transfers between devices with their start and end apart: 7, of which 1 were waited for; matrix products, arithmetic and copies ran while one was open for 12% of the time, Pallas kernels for 29%

profile of v14, /device:TPU:0, one launch (start us, length us, event | category | flops | bytes accessed | tf_op | source)
XLA Modules:
  0.0 1075.4 jit_solution(16412638672389084132)
XLA Ops:
  7.2 0.0 all-gather.3.cloned.1.call-start
  7.2 0.7 convert_element_type.95
  7.9 0.7 bitcast_convert_fusion.1
  8.5 0.7 pad_convert_fusion
  9.2 0.1 scatter.19
  9.3 0.2 scatter.20.facts
  9.5 0.6 copy-done.10
  10.1 130.4 %shard_map.203 = (bf16[4096,2048]{1,0:T(8,128)(2,1)}, bf16[4,4,128,768]{3,2,1,0:T(8,128)(2,1)}, f32[4,4,2,8,128]{4,3,2,1,0:T(8,128)}) custom-call(bf16[2,256,2048]{2,1,0:T(8,128)(2,1)} %bitcast.57, bf16[64,2048]{1,0:T(8,128)(2,1)} %w_query.1, bf16[64,2048]{1,0:T(8,128)(2,1)} %w_key.1, bf16[64,2048]{1,0:T(8,128)(2,1)} %w_value.1, f32[8,128]{1,0:T(8,128)} %copy-done.10), custom_call_target="tpu_custom_call" | custom-call | bytes 350000000 | tf_op jit(solution)/shard_map/pallas_call | solution.py:684
  140.6 0.0 all-gather.5.cloned.1.call-start
  140.6 2.5 collective-permute-start
  143.2 0.7 slice.86
  143.9 7.2 fusion
  151.1 1.1 slice_reduce_fusion
  152.2 0.7 reshape_squeeze.10.gain
  152.9 0.7 reduce-window.9
  153.6 0.1 mul.44
  153.7 19.8 %convolution_convert_fusion.1.qkv = bf16[4096,768]{1,0:T(8,128)(2,1)} fusion(bf16[2048,768]{1,0:T(8,128)(2,1)} %bitcast.54, bf16[4096,2048]{1,0:T(8,128)(2,1)} %get-tuple-element.84.x_whole, f32[2048]{0:T(1024)S(1)} %mul.44, f32[4096]{0:T(1024)S(1)} %add_rsqrt_fusion), kind=kOutput, calls=%fused_computation.6 | convolution fusion | flops 12921602048 | bytes 26238976 | tf_op jit(solution)/shard_map/dot_general | solution.py:86
  173.5 42.4 %shard_map.204.attended = bf16[4096,256]{1,0:T(8,128)(2,1)} custom-call(s32[8]{0:T(128)} %bitcast.63, bf16[4096,768]{1,0:T(8,128)(2,1)} %convolution_convert_fusion.1.qkv), custom_call_target="tpu_custom_call" | custom-call | bytes 150000000 | tf_op jit(solution)/shard_map/pallas_call | solution.py:1342
  215.9 10.4 all-gather.3.cloned.1.call-done
  226.3 1.3 constant_dynamic-slice_fusion.6
  227.6 0.8 copy-done.6
  228.4 0.2 copy-done.8
  228.5 1.1 pad_maximum_fusion.w_out
  229.6 167.3 %shard_map.205 = (f32[512,2048]{1,0:T(8,128)}, bf16[4096,2048]{1,0:T(8,128)(2,1)}, bf16[2048,1024]{1,0:T(8,128)(2,1)}, bf16[2048,1024]{1,0:T(8,128)(2,1)}) custom-call(bf16[4096,256]{1,0:T(8,128)(2,1)} %shard_map.204.attended, bf16[256,2048]{1,0:T(8,128)(2,1)} %pad_maximum_fusion.w_out, bf16[4096,2048]{1,0:T(8,128)(2,1)} %get-tuple-element.84.x_whole, ...), custom_call_target="tpu_custom_call" | custom-call | bytes 450000000 | tf_op jit(solution)/shard_map/pallas_call | solution.py:787
  397.0 0.0 reduce-scatter.2.cloned.1.call-start
  397.0 80.7 %shard_map.206 = (f32[4096,1024]{1,0:T(8,128)}, f32[4096,1024]{1,0:T(8,128)}, bf16[4096,1024]{1,0:T(8,128)(2,1)}, bf16[4096,2048]{1,0:T(8,128)(2,1)}) custom-call(bf16[4096,2048]{1,0:T(8,128)(2,1)} %get-tuple-element.89.normed, bf16[2048,1024]{1,0:T(8,128)(2,1)} %get-tuple-element.90.w_gate, bf16[2048,1024]{1,0:T(8,128)(2,1)} %get-tuple-element.91.w_up, ...), custom_call_target="tpu_custom_call" | custom-call | bytes 250000000 | tf_op jit(solution)/shard_map/pallas_call | solution.py:1185
  477.8 0.0 all-gather.5.cloned.1.call-done.w_down
  477.8 23.5 %convolution_convert_fusion = bf16[4096,2048]{1,0:T(8,128)(2,1)} fusion(bf16[4096,1024]{1,0:T(8,128)(2,1)} %get-tuple-element.95, bf16[1024,2048]{1,0:T(8,128)(2,1)} %all-gather.5.cloned.1.call-done.w_down), kind=kOutput, calls=%fused_computation.5 | convolution fusion | flops 17188257792 | bytes 29360128 | tf_op jit(solution)/shard_map/dot_general | solution.py:86
  501.3 0.7 reshape_squeeze.11.gain
  502.0 23.9 %convolution_convert_fusion.5 = bf16[1024,2048]{1,0:T(8,128)(2,1)S(1)} fusion(bf16[4096,1024]{1,0:T(8,128)(2,1)} %get-tuple-element.95, bf16[4096,2048]{1,0:T(8,128)(2,1)} %get-tuple-element.97.upstream), kind=kOutput, calls=%fused_computation.12 | convolution fusion | flops 17181966336 | bytes 29360128 | tf_op jit(solution)/shard_map/dot_general | solution.py:20
  525.9 2.0 copy-done.3
  527.9 1.7 constant_dynamic-slice_fusion.2
  529.7 0.1 collective-permute-start.3
  529.7 2.1 collective-permute-start.1
  531.8 33.3 %shard_map.207 = (bf16[4096,1024]{1,0:T(8,128)(2,1)}, bf16[4096,1024]{1,0:T(8,128)(2,1)}) custom-call(bf16[4096,2048]{1,0:T(8,128)(2,1)} %get-tuple-element.97.upstream, bf16[1024,2048]{1,0:T(8,128)(2,1)} %all-gather.5.cloned.1.call-done.w_down, f32[4096,1024]{1,0:T(8,128)} %get-tuple-element.98.gate, f32[4096,1024]{1,0:T(8,128)} %get-tuple-element.99.up), custom_call_target="tpu_custom_call" | custom-call | bytes 90000000 | tf_op jit(solution)/shard_map/pallas_call | solution.py:1327
  565.2 24.3 %convolution_convert_fusion.4.grad_a = bf16[2048,1024]{1,0:T(8,128)(2,1)} fusion(bf16[4096,2048]{1,0:T(8,128)(2,1)} %get-tuple-element.89.normed, bf16[4096,1024]{1,0:T(8,128)(2,1)} %get-tuple-element.100.d_gate), kind=kOutput, calls=%fused_computation.11 | convolution fusion | flops 17181966336 | bytes 29360128 | tf_op jit(solution)/shard_map/dot_general | solution.py:20
  589.5 21.3 %convolution_convert_fusion.3.grad_b = bf16[2048,1024]{1,0:T(8,128)(2,1)} fusion(bf16[4096,2048]{1,0:T(8,128)(2,1)} %get-tuple-element.89.normed, bf16[4096,1024]{1,0:T(8,128)(2,1)S(1)} %copy-done.1), kind=kOutput, calls=%fused_computation.10 | convolution fusion | flops 17181966336 | bytes 29360128 | tf_op jit(solution)/shard_map/dot_general | solution.py:20
  610.8 160.3 %shard_map.208 = (f32[512,2048]{1,0:T(8,128)}, f32[8,2048]{1,0:T(8,128)}, bf16[4096,2048]{1,0:T(8,128)(2,1)}, bf16[2048,256]{1,0:T(8,128)(2,1)}, bf16[2048,256]{...) custom-call(bf16[4096,1024]{1,0:T(8,128)(2,1)} %get-tuple-element.10, ...), custom_call_target="tpu_custom_call" | custom-call | bytes 450000000 | tf_op jit(solution)/shard_map/pallas_call | solution.py:899
  771.1 5.8 convert_add_fusion
  776.9 9.9 convolution_convert_fusion.6.out_grad
  786.9 5.9 convolution_convert_fusion.2.grads
  792.9 3.2 add_add_fusion
  796.1 4.9 add_convert_fusion.mixed
  801.0 85.1 %shard_map.209 = (bf16[4096,768]{1,0:T(8,128)(2,1)}, bf16[4,64,2048]{2,1,0:T(8,128)(2,1)}, bf16[512,2048]{1,0:T(8,128)(2,1)}) custom-call(s32[8]{0:T(128)} %bitcast.64, bf16[4096,768]{1,0:T(8,128)(2,1)} %convolution_convert_fusion.1.qkv, bf16[4096,256]{1,0:T(8,128)(2,1)} %convolution_convert_fusion.2.grads, ...), custom_call_target="tpu_custom_call" | custom-call | bytes 300000000 | tf_op jit(solution)/shard_map/pallas_call | solution.py:1358
  886.2 2.2 convert_reduce_fusion
  888.4 19.7 %fusion.6 = bf16[2048,768]{1,0:T(8,128)(2,1)S(1)} fusion(bf16[4096,768]{1,0:T(8,128)(2,1)} %get-tuple-element.105.d_qkv, bf16[4096,2048]{1,0:T(8,128)(2,1)} %get-tuple-element.84.x_whole, f32[2048]{0:T(1024)S(1)} %copy-done.14, f32[4096]{0:T(1024)S(1)} %copy-done.12), kind=kOutput, calls=%fused_computation.13 | convolution fusion | flops 12920029184 | bytes 26238976 | tf_op jit(solution)/shard_map/dot_general | solution.py:20
  908.1 1.9 copy.35
  909.9 143.5 %shard_map.210 = (bf16[512,2048]{1,0:T(8,128)(2,1)}, f32[2,8,128]{2,1,0:T(8,128)}, bf16[512,768]{1,0:T(8,128)(2,1)}, bf16[512,768]{1,0:T(8,128)(2,1)}, bf16[512,...) custom-call(bf16[4096,768]{1,0:T(8,128)(2,1)} %get-tuple-element.105.d_qkv, bf16[2048,768]{1,0:T(8,128)(2,1)} %bitcast.55, ...), custom_call_target="tpu_custom_call" | custom-call | bytes 350000000 | tf_op jit(solution)/shard_map/pallas_call | solution.py:1073
  1053.5 0.7 reduce_sum.29
  1054.2 0.1 reshape.199
  1054.3 2.3 reshape.198
  1056.5 1.3 fusion.14
  1057.9 0.1 copy_bitcast_fusion.1
  1058.1 0.1 convert_bitcast_fusion
  1058.2 0.9 fusion.13
  1059.2 0.3 copy.42
  1059.5 1.0 unstack.23
  1060.5 1.4 copy.41
  1061.9 1.0 unstack.21
  1062.9 0.3 copy.40
  1063.2 1.0 unstack.19
  1064.2 2.5 bitcast_convert_fusion
  1066.8 0.5 fusion.11
  1067.3 1.3 copy.56
  (48 shorter events, 0.2 us)
Async XLA Ops:
  7.2 219.1 %all-gather.3.cloned.1.call-start = ((), (), s32[]{:S(2)}) async-start(), calls=%async_computation.1 | async-start | bytes 2359296 | tf_op jit(solution)/shard_map/all_gather | solution.py:1419
  9.5 0.6 copy-start.10
  140.6 337.2 %all-gather.5.cloned.1.call-start = ((), (), s32[]{:S(2)}) async-start(), calls=%async_computation.2 | async-start | bytes 5242880 | tf_op jit(solution)/shard_map/all_gather | solution.py:1428
  140.6 75.2 %collective-permute-start = (bf16[1,512,2048]{2,1,0:T(8,128)(2,1)}, bf16[1,512,2048]{2,1,0:T(8,128)(2,1)S(1)}, u32[]{:S(2)}, u32[]{:S(2)}) collective-permute-start(bf16[1,512,2048]{2,1,0:T(8,128)(2,1)} %param.20), channel_id=1, source_target_pairs={{0,0},{1,1},{2,16},{3,17},{4,8},{5,9},{6,24},{7,25},{8,4},{9,5},{1... | collective-permute-start | bytes 6291464 | tf_op jit(solution)/shard_map/ppermute | solution.py:1393
  153.6 19.8 %copy-start.13 = (f32[2048]{0:T(1024)}, f32[2048]{0:T(1024)S(1)}, u32[]{:S(2)}) copy-start(f32[2048]{0:T(1024)S(1)} %mul.44) | copy-start | bytes 24580
  153.7 19.8 %copy-start.11 = (f32[4096]{0:T(1024)}, f32[4096]{0:T(1024)S(1)}, u32[]{:S(2)}) copy-start(f32[4096]{0:T(1024)S(1)} %add_rsqrt_fusion) | copy-start | bytes 49156
  215.9 181.1 %copy-start.2 = (bf16[1,512,2048]{2,1,0:T(8,128)(2,1)}, bf16[1,512,2048]{2,1,0:T(8,128)(2,1)S(1)}, u32[]{:S(2)}) copy-start(bf16[1,512,2048]{2,1,0:T(8,128)(2,1)S(1)} %collective-permute-done) | copy-start | bytes 6291460
  227.6 0.8 copy-start.6
  227.6 1.0 copy-start.8
  397.0 399.2 %reduce-scatter.2.cloned.1.call-start = ((), (), s32[]{:S(2)}) async-start(), calls=%async_computation.3 | async-start | bytes 18874368 | tf_op jit(solution)/shard_map/reduce_scatter | solution.py:1431
  525.9 2.0 copy-start.3
  529.7 263.2 %collective-permute-start.3 = (bf16[256,2048]{1,0:T(8,128)(2,1)}, bf16[256,2048]{1,0:T(8,128)(2,1)S(1)}, u32[]{:S(2)}, u32[]{:S(2)}) collective-permute-start(bf16[256,2048]{1,0:T(8,128)(2,1)} %get-tuple-element.121), channel_id=1, source_target_pairs={{0,6},{2,0},{4,2},{6,4},{1,7},{3,1},{5,3},{7,5},{8,14},{10,8},{12,... | collective-permute-start | bytes 3145736 | tf_op jit(solution)/shard_map/ppermute | solution.py:1438
  529.7 263.1 %collective-permute-start.2 = (bf16[256,2048]{1,0:T(8,128)(2,1)}, bf16[256,2048]{1,0:T(8,128)(2,1)S(1)}, u32[]{:S(2)}, u32[]{:S(2)}) collective-permute-start(bf16[256,2048]{1,0:T(8,128)(2,1)} %get-tuple-element.122), channel_id=1, source_target_pairs={{0,4},{2,6},{4,0},{6,2},{1,5},{3,7},{5,1},{7,3},{8,12},{10,14},{12... | collective-permute-start | bytes 3145736 | tf_op jit(solution)/shard_map/ppermute | solution.py:1438
  529.7 263.1 %collective-permute-start.1 = (bf16[256,2048]{1,0:T(8,128)(2,1)}, bf16[256,2048]{1,0:T(8,128)(2,1)S(1)}, u32[]{:S(2)}, u32[]{:S(2)}) collective-permute-start(bf16[256,2048]{1,0:T(8,128)(2,1)} %get-tuple-element.123), channel_id=1, source_target_pairs={{0,2},{2,4},{4,6},{6,0},{1,3},{3,5},{5,7},{7,1},{8,10},{10,12},{12... | collective-permute-start | bytes 3145736 | tf_op jit(solution)/shard_map/ppermute | solution.py:1438
  565.2 24.3 %copy-start.1 = (bf16[4096,1024]{1,0:T(8,128)(2,1)S(1)}, bf16[4096,1024]{1,0:T(8,128)(2,1)}, u32[]{:S(2)}) copy-start(bf16[4096,1024]{1,0:T(8,128)(2,1)} %get-tuple-element.101.d_up) | copy-start | bytes 25165828
  771.1 5.8 copy-start
  771.1 15.8 %slice-start = ((s8[16777216]{0:T(1024)(128)(4,1)}), s8[4194304]{0:T(1024)(128)(4,1)S(1)}, s32[]{:S(2)}) async-start(s8[16777216]{0:T(1024)(128)(4,1)} %bitcast.49), calls=%async_computation.4 | async-start | bytes 8388608
  771.1 15.8 %slice-start.1 = ((s8[16777216]{0:T(1024)(128)(4,1)}), s8[4194304]{0:T(1024)(128)(4,1)S(1)}, s32[]{:S(2)}) async-start(s8[16777216]{0:T(1024)(128)(4,1)} %bitcast.49), calls=%async_computation.5 | async-start | bytes 8388608
  776.9 10.0 slice-start.2
  776.9 10.0 slice-start.3
  776.9 10.0 copy-start.7
  776.9 10.0 copy-start.9
  801.0 87.4 %copy-start.12 = (f32[4096]{0:T(1024)S(1)}, f32[4096]{0:T(1024)}, u32[]{:S(2)}) copy-start(f32[4096]{0:T(1024)} %copy-done.11) | copy-start | bytes 49156
  801.0 87.4 %copy-start.14 = (f32[2048]{0:T(1024)S(1)}, f32[2048]{0:T(1024)}, u32[]{:S(2)}) copy-start(f32[2048]{0:T(1024)} %copy-done.13) | copy-start | bytes 24580
  1058.2 6.0 copy-start.4
  1064.2 3.1 copy-start.5
Sparse Core Ops, SparseCore 0:
  140.7 85.5 all-gather.2
  397.1 78.5 all-gather.4
  501.4 113.5 reduce-scatter.1

commit v15 on v14

--- a/solution.py
+++ b/solution.py
@@ -772,7 +772,7 @@
         over_chunks(chunk, half)
 
     gather = Gather(own_halves(own), normed, send, recv)
-    sum_and_gather(part_of, rows_of_half, gather, lambda turn: arrive(turn - 1) if turn > 0 else None)
+    sum_and_gather(part_of, rows_of_half, gather, lambda turn: arrive((0, None, 1, 2)[turn]) if turn != 1 else None)
     keep = pltpu.make_async_copy(own, normed.at[place_of(y, c, x)], local.at[0])
     keep.start()
     for chain in chains:

time: 1080 us -> 1080 us (level)
  no operation moved by 1% of the time
where the time goes in v15:
time: 1080 us
  Pallas kernels  843 us (78%)
  matrix products  148 us (14%)
  other arithmetic  30.5 us (3%)
  local copies, waits for them, and re-layouts  23.8 us (2%)
  between operations  14.5 us (1%)
    pallas_call x1, Pallas kernels, close_attention(): pl.pallas_call(close_attention_kernel, out_shape=(jax.ShapeDtypeStruct((b...  167 us
    pallas_call x1, Pallas kernels, close_mlp(): pl.pallas_call(close_mlp_kernel, out_shape=(jax.ShapeDtypeStruct((block,...  160 us
    pallas_call x1, Pallas kernels, close_layer(): pl.pallas_call(close_layer_kernel, out_shape=(jax.ShapeDtypeStruct((block...  143 us
    pallas_call x1, Pallas kernels, begin(): pl.pallas_call(begin_kernel, out_shape=(jax.ShapeDtypeStruct((8 * block,...  130 us
    dot_general x5, matrix products, contract_rows(): lax.dot_general(left, right, (((0,), (0,)), ((), ())), preferred_element_...  99.2 us
    pallas_call x1, Pallas kernels, attend_back(): pl.pallas_call(attend_back_kernel, out_shape=(jax.ShapeDtypeStruct((place...  85.3 us
    pallas_call x1, Pallas kernels, open_mlp(): pl.pallas_call(open_mlp_kernel, out_shape=(jax.ShapeDtypeStruct((places,...  80.8 us
    dot_general x2, matrix products, dot_wide(): return jnp.dot(left, right, preferred_element_type=jnp.float32)  43.2 us
  transfers between devices with their start and end apart: 7, of which 1 were waited for; matrix products, arithmetic and copies ran while one was open for 12% of the time, Pallas kernels for 29%

profile of v15, /device:TPU:0, one launch (start us, length us, event | category | flops | bytes accessed | tf_op | source)
XLA Modules:
  0.0 1075.8 jit_solution(13450211269778285388)
XLA Ops:
  7.2 0.0 all-gather.3.cloned.1.call-start
  7.2 0.7 convert_element_type.95
  7.9 0.7 bitcast_convert_fusion.1
  8.5 0.7 pad_convert_fusion
  9.2 0.1 scatter.19
  9.3 0.2 scatter.20.facts
  9.5 0.6 copy-done.10
  10.1 130.4 %shard_map.203 = (bf16[4096,2048]{1,0:T(8,128)(2,1)}, bf16[4,4,128,768]{3,2,1,0:T(8,128)(2,1)}, f32[4,4,2,8,128]{4,3,2,1,0:T(8,128)}) custom-call(bf16[2,256,2048]{2,1,0:T(8,128)(2,1)} %bitcast.57, bf16[64,2048]{1,0:T(8,128)(2,1)} %w_query.1, bf16[64,2048]{1,0:T(8,128)(2,1)} %w_key.1, bf16[64,2048]{1,0:T(8,128)(2,1)} %w_value.1, f32[8,128]{1,0:T(8,128)} %copy-done.10), custom_call_target="tpu_custom_call" | custom-call | bytes 350000000 | tf_op jit(solution)/shard_map/pallas_call | solution.py:684
  140.6 0.0 all-gather.5.cloned.1.call-start
  140.6 2.5 collective-permute-start
  143.2 0.7 slice.86
  143.9 7.2 fusion
  151.1 1.1 slice_reduce_fusion
  152.2 0.7 reshape_squeeze.10.gain
  152.9 0.7 reduce-window.9
  153.6 0.1 mul.44
  153.7 19.8 %convolution_convert_fusion.1.qkv = bf16[4096,768]{1,0:T(8,128)(2,1)} fusion(bf16[2048,768]{1,0:T(8,128)(2,1)} %bitcast.54, bf16[4096,2048]{1,0:T(8,128)(2,1)} %get-tuple-element.84.x_whole, f32[2048]{0:T(1024)S(1)} %mul.44, f32[4096]{0:T(1024)S(1)} %add_rsqrt_fusion), kind=kOutput, calls=%fused_computation.6 | convolution fusion | flops 12921602048 | bytes 26238976 | tf_op jit(solution)/shard_map/dot_general | solution.py:86
  173.5 42.4 %shard_map.204.attended = bf16[4096,256]{1,0:T(8,128)(2,1)} custom-call(s32[8]{0:T(128)} %bitcast.63, bf16[4096,768]{1,0:T(8,128)(2,1)} %convolution_convert_fusion.1.qkv), custom_call_target="tpu_custom_call" | custom-call | bytes 150000000 | tf_op jit(solution)/shard_map/pallas_call | solution.py:1342
  215.9 10.4 all-gather.3.cloned.1.call-done
  226.3 1.3 constant_dynamic-slice_fusion.6
  227.6 0.8 copy-done.6
  228.4 0.2 copy-done.8
  228.5 1.1 pad_maximum_fusion.w_out
  229.6 167.3 %shard_map.205 = (f32[512,2048]{1,0:T(8,128)}, bf16[4096,2048]{1,0:T(8,128)(2,1)}, bf16[2048,1024]{1,0:T(8,128)(2,1)}, bf16[2048,1024]{1,0:T(8,128)(2,1)}) custom-call(bf16[4096,256]{1,0:T(8,128)(2,1)} %shard_map.204.attended, bf16[256,2048]{1,0:T(8,128)(2,1)} %pad_maximum_fusion.w_out, bf16[4096,2048]{1,0:T(8,128)(2,1)} %get-tuple-element.84.x_whole, ...), custom_call_target="tpu_custom_call" | custom-call | bytes 450000000 | tf_op jit(solution)/shard_map/pallas_call | solution.py:787
  397.0 0.0 reduce-scatter.2.cloned.1.call-start
  397.0 80.8 %shard_map.206 = (f32[4096,1024]{1,0:T(8,128)}, f32[4096,1024]{1,0:T(8,128)}, bf16[4096,1024]{1,0:T(8,128)(2,1)}, bf16[4096,2048]{1,0:T(8,128)(2,1)}) custom-call(bf16[4096,2048]{1,0:T(8,128)(2,1)} %get-tuple-element.89.normed, bf16[2048,1024]{1,0:T(8,128)(2,1)} %get-tuple-element.90.w_gate, bf16[2048,1024]{1,0:T(8,128)(2,1)} %get-tuple-element.91.w_up, ...), custom_call_target="tpu_custom_call" | custom-call | bytes 250000000 | tf_op jit(solution)/shard_map/pallas_call | solution.py:1185
  477.8 0.0 all-gather.5.cloned.1.call-done.w_down
  477.8 23.5 %convolution_convert_fusion = bf16[4096,2048]{1,0:T(8,128)(2,1)} fusion(bf16[4096,1024]{1,0:T(8,128)(2,1)} %get-tuple-element.95, bf16[1024,2048]{1,0:T(8,128)(2,1)} %all-gather.5.cloned.1.call-done.w_down), kind=kOutput, calls=%fused_computation.5 | convolution fusion | flops 17188257792 | bytes 29360128 | tf_op jit(solution)/shard_map/dot_general | solution.py:86
  501.4 0.7 reshape_squeeze.11.gain
  502.0 24.0 %convolution_convert_fusion.5 = bf16[1024,2048]{1,0:T(8,128)(2,1)S(1)} fusion(bf16[4096,1024]{1,0:T(8,128)(2,1)} %get-tuple-element.95, bf16[4096,2048]{1,0:T(8,128)(2,1)} %get-tuple-element.97.upstream), kind=kOutput, calls=%fused_computation.12 | convolution fusion | flops 17181966336 | bytes 29360128 | tf_op jit(solution)/shard_map/dot_general | solution.py:20
  526.1 2.0 copy-done.3
  528.1 1.7 constant_dynamic-slice_fusion.2
  529.8 0.2 collective-permute-start.2
  530.1 1.9 collective-permute-start.1
  532.0 33.3 %shard_map.207 = (bf16[4096,1024]{1,0:T(8,128)(2,1)}, bf16[4096,1024]{1,0:T(8,128)(2,1)}) custom-call(bf16[4096,2048]{1,0:T(8,128)(2,1)} %get-tuple-element.97.upstream, bf16[1024,2048]{1,0:T(8,128)(2,1)} %all-gather.5.cloned.1.call-done.w_down, f32[4096,1024]{1,0:T(8,128)} %get-tuple-element.98.gate, f32[4096,1024]{1,0:T(8,128)} %get-tuple-element.99.up), custom_call_target="tpu_custom_call" | custom-call | bytes 90000000 | tf_op jit(solution)/shard_map/pallas_call | solution.py:1327
  565.3 24.4 %convolution_convert_fusion.4.grad_a = bf16[2048,1024]{1,0:T(8,128)(2,1)} fusion(bf16[4096,2048]{1,0:T(8,128)(2,1)} %get-tuple-element.89.normed, bf16[4096,1024]{1,0:T(8,128)(2,1)} %get-tuple-element.100.d_gate), kind=kOutput, calls=%fused_computation.11 | convolution fusion | flops 17181966336 | bytes 29360128 | tf_op jit(solution)/shard_map/dot_general | solution.py:20
  589.6 21.3 %convolution_convert_fusion.3.grad_b = bf16[2048,1024]{1,0:T(8,128)(2,1)} fusion(bf16[4096,2048]{1,0:T(8,128)(2,1)} %get-tuple-element.89.normed, bf16[4096,1024]{1,0:T(8,128)(2,1)S(1)} %copy-done.1), kind=kOutput, calls=%fused_computation.10 | convolution fusion | flops 17181966336 | bytes 29360128 | tf_op jit(solution)/shard_map/dot_general | solution.py:20
  610.9 160.4 %shard_map.208 = (f32[512,2048]{1,0:T(8,128)}, f32[8,2048]{1,0:T(8,128)}, bf16[4096,2048]{1,0:T(8,128)(2,1)}, bf16[2048,256]{1,0:T(8,128)(2,1)}, bf16[2048,256]{...) custom-call(bf16[4096,1024]{1,0:T(8,128)(2,1)} %get-tuple-element.10, ...), custom_call_target="tpu_custom_call" | custom-call | bytes 450000000 | tf_op jit(solution)/shard_map/pallas_call | solution.py:899
  771.4 5.8 convert_add_fusion
  777.2 9.9 convolution_convert_fusion.6.out_grad
  787.2 5.9 convolution_convert_fusion.2.grads
  793.1 3.2 add_add_fusion
  796.4 4.9 add_convert_fusion.mixed
  801.3 85.3 %shard_map.209 = (bf16[4096,768]{1,0:T(8,128)(2,1)}, bf16[4,64,2048]{2,1,0:T(8,128)(2,1)}, bf16[512,2048]{1,0:T(8,128)(2,1)}) custom-call(s32[8]{0:T(128)} %bitcast.64, bf16[4096,768]{1,0:T(8,128)(2,1)} %convolution_convert_fusion.1.qkv, bf16[4096,256]{1,0:T(8,128)(2,1)} %convolution_convert_fusion.2.grads, ...), custom_call_target="tpu_custom_call" | custom-call | bytes 300000000 | tf_op jit(solution)/shard_map/pallas_call | solution.py:1358
  886.6 2.2 convert_reduce_fusion
  888.8 19.7 %fusion.6 = bf16[2048,768]{1,0:T(8,128)(2,1)S(1)} fusion(bf16[4096,768]{1,0:T(8,128)(2,1)} %get-tuple-element.105.d_qkv, bf16[4096,2048]{1,0:T(8,128)(2,1)} %get-tuple-element.84.x_whole, f32[2048]{0:T(1024)S(1)} %copy-done.14, f32[4096]{0:T(1024)S(1)} %copy-done.12), kind=kOutput, calls=%fused_computation.13 | convolution fusion | flops 12920029184 | bytes 26238976 | tf_op jit(solution)/shard_map/dot_general | solution.py:20
  908.5 1.9 copy.35
  910.4 143.4 %shard_map.210 = (bf16[512,2048]{1,0:T(8,128)(2,1)}, f32[2,8,128]{2,1,0:T(8,128)}, bf16[512,768]{1,0:T(8,128)(2,1)}, bf16[512,768]{1,0:T(8,128)(2,1)}, bf16[512,...) custom-call(bf16[4096,768]{1,0:T(8,128)(2,1)} %get-tuple-element.105.d_qkv, bf16[2048,768]{1,0:T(8,128)(2,1)} %bitcast.55, ...), custom_call_target="tpu_custom_call" | custom-call | bytes 350000000 | tf_op jit(solution)/shard_map/pallas_call | solution.py:1073
  1053.8 0.7 reduce_sum.29
  1054.5 0.1 reshape.199
  1054.6 2.3 reshape.198
  1056.9 1.3 fusion.14
  1058.3 0.1 copy_bitcast_fusion.1
  1058.4 0.1 convert_bitcast_fusion
  1058.5 0.9 fusion.13
  1059.5 0.3 copy.42
  1059.8 1.0 unstack.23
  1060.8 1.4 copy.41
  1062.2 1.0 unstack.21
  1063.2 0.3 copy.40
  1063.6 1.0 unstack.19
  1064.6 2.5 bitcast_convert_fusion
  1067.1 0.5 fusion.11
  1067.6 1.3 copy.56
  (48 shorter events, 0.2 us)
Async XLA Ops:
  7.2 219.1 %all-gather.3.cloned.1.call-start = ((), (), s32[]{:S(2)}) async-start(), calls=%async_computation.1 | async-start | bytes 2359296 | tf_op jit(solution)/shard_map/all_gather | solution.py:1419
  9.5 0.6 copy-start.10
  140.6 337.2 %all-gather.5.cloned.1.call-start = ((), (), s32[]{:S(2)}) async-start(), calls=%async_computation.2 | async-start | bytes 5242880 | tf_op jit(solution)/shard_map/all_gather | solution.py:1428
  140.6 75.2 %collective-permute-start = (bf16[1,512,2048]{2,1,0:T(8,128)(2,1)}, bf16[1,512,2048]{2,1,0:T(8,128)(2,1)S(1)}, u32[]{:S(2)}, u32[]{:S(2)}) collective-permute-start(bf16[1,512,2048]{2,1,0:T(8,128)(2,1)} %param.20), channel_id=1, source_target_pairs={{0,0},{1,1},{2,16},{3,17},{4,8},{5,9},{6,24},{7,25},{8,4},{9,5},{1... | collective-permute-start | bytes 6291464 | tf_op jit(solution)/shard_map/ppermute | solution.py:1393
  153.6 19.8 %copy-start.13 = (f32[2048]{0:T(1024)}, f32[2048]{0:T(1024)S(1)}, u32[]{:S(2)}) copy-start(f32[2048]{0:T(1024)S(1)} %mul.44) | copy-start | bytes 24580
  153.7 19.8 %copy-start.11 = (f32[4096]{0:T(1024)}, f32[4096]{0:T(1024)S(1)}, u32[]{:S(2)}) copy-start(f32[4096]{0:T(1024)S(1)} %add_rsqrt_fusion) | copy-start | bytes 49156
  215.9 181.1 %copy-start.2 = (bf16[1,512,2048]{2,1,0:T(8,128)(2,1)}, bf16[1,512,2048]{2,1,0:T(8,128)(2,1)S(1)}, u32[]{:S(2)}) copy-start(bf16[1,512,2048]{2,1,0:T(8,128)(2,1)S(1)} %collective-permute-done) | copy-start | bytes 6291460
  227.6 0.8 copy-start.6
  227.6 1.0 copy-start.8
  397.0 399.4 %reduce-scatter.2.cloned.1.call-start = ((), (), s32[]{:S(2)}) async-start(), calls=%async_computation.3 | async-start | bytes 18874368 | tf_op jit(solution)/shard_map/reduce_scatter | solution.py:1431
  526.1 2.0 copy-start.3
  529.8 263.3 %collective-permute-start.3 = (bf16[256,2048]{1,0:T(8,128)(2,1)}, bf16[256,2048]{1,0:T(8,128)(2,1)S(1)}, u32[]{:S(2)}, u32[]{:S(2)}) collective-permute-start(bf16[256,2048]{1,0:T(8,128)(2,1)} %get-tuple-element.121), channel_id=1, source_target_pairs={{0,6},{2,0},{4,2},{6,4},{1,7},{3,1},{5,3},{7,5},{8,14},{10,8},{12,... | collective-permute-start | bytes 3145736 | tf_op jit(solution)/shard_map/ppermute | solution.py:1438
  529.8 263.3 %collective-permute-start.2 = (bf16[256,2048]{1,0:T(8,128)(2,1)}, bf16[256,2048]{1,0:T(8,128)(2,1)S(1)}, u32[]{:S(2)}, u32[]{:S(2)}) collective-permute-start(bf16[256,2048]{1,0:T(8,128)(2,1)} %get-tuple-element.122), channel_id=1, source_target_pairs={{0,4},{2,6},{4,0},{6,2},{1,5},{3,7},{5,1},{7,3},{8,12},{10,14},{12... | collective-permute-start | bytes 3145736 | tf_op jit(solution)/shard_map/ppermute | solution.py:1438
  530.1 263.0 %collective-permute-start.1 = (bf16[256,2048]{1,0:T(8,128)(2,1)}, bf16[256,2048]{1,0:T(8,128)(2,1)S(1)}, u32[]{:S(2)}, u32[]{:S(2)}) collective-permute-start(bf16[256,2048]{1,0:T(8,128)(2,1)} %get-tuple-element.123), channel_id=1, source_target_pairs={{0,2},{2,4},{4,6},{6,0},{1,3},{3,5},{5,7},{7,1},{8,10},{10,12},{12... | collective-permute-start | bytes 3145736 | tf_op jit(solution)/shard_map/ppermute | solution.py:1438
  565.3 24.4 %copy-start.1 = (bf16[4096,1024]{1,0:T(8,128)(2,1)S(1)}, bf16[4096,1024]{1,0:T(8,128)(2,1)}, u32[]{:S(2)}) copy-start(bf16[4096,1024]{1,0:T(8,128)(2,1)} %get-tuple-element.101.d_up) | copy-start | bytes 25165828
  771.3 5.8 copy-start
  771.3 15.8 %slice-start = ((s8[16777216]{0:T(1024)(128)(4,1)}), s8[4194304]{0:T(1024)(128)(4,1)S(1)}, s32[]{:S(2)}) async-start(s8[16777216]{0:T(1024)(128)(4,1)} %bitcast.49), calls=%async_computation.4 | async-start | bytes 8388608
  771.4 15.8 %slice-start.1 = ((s8[16777216]{0:T(1024)(128)(4,1)}), s8[4194304]{0:T(1024)(128)(4,1)S(1)}, s32[]{:S(2)}) async-start(s8[16777216]{0:T(1024)(128)(4,1)} %bitcast.49), calls=%async_computation.5 | async-start | bytes 8388608
  777.2 10.0 slice-start.2
  777.2 10.0 slice-start.3
  777.2 10.0 copy-start.7
  777.2 10.0 copy-start.9
  801.3 87.6 %copy-start.12 = (f32[4096]{0:T(1024)S(1)}, f32[4096]{0:T(1024)}, u32[]{:S(2)}) copy-start(f32[4096]{0:T(1024)} %copy-done.11) | copy-start | bytes 49156
  801.3 87.6 %copy-start.14 = (f32[2048]{0:T(1024)S(1)}, f32[2048]{0:T(1024)}, u32[]{:S(2)}) copy-start(f32[2048]{0:T(1024)} %copy-done.13) | copy-start | bytes 24580
  1058.5 6.0 copy-start.4
  1064.6 3.1 copy-start.5
Sparse Core Ops, SparseCore 0:
  140.7 85.5 all-gather.2
  397.1 78.4 all-gather.4
  501.4 113.4 reduce-scatter.1
